TPU v7x, 32 devices: a whole 2x2x4 slice. The times are simulated.
32 devices in a mesh: grp: 2 (over y), blk: 4 (over z), mpo: 2 (over x), rep: 2 (over core).
Axes of the slice: x: 2, y: 2, z: 4, core: 2. Of those that a mesh axis runs over, the one named last changes fastest.
Arguments:
- wavefunction: float32 [64, 64, 1024], P(('grp', 'blk')), parts along dimension 0, may hold values from -4000 to 4000
- environment: float32 [48, 32, 64, 128], P(('grp', 'mpo', 'rep'), None, 'blk'), parts along dimension 0, may hold values from -0.75 to 0.75
- bond_terms: float32 [48, 16, 16], P(('grp', 'mpo', 'rep')), parts along dimension 0, may hold values from -0.3125 to 0.3125
- diagonal: float32 [64, 64, 1024], P(('grp', 'blk'), None, ('mpo', 'rep')), parts along dimension 0, may hold values from 0.5 to 4
- term_slot: int32 [48, 32], P(('grp', 'mpo', 'rep'), 'blk'), parts along dimension 0, may hold values from 0 to 7, as said below
- slot_block: int32 [8, 8], P('grp', 'blk'), parts along dimension 0, may hold values from 0 to 7
Outputs:
- first_image: float32 [64, 64, 1024], P(('grp', 'blk'), None, ('mpo', 'rep')), parts along dimension 0
- second_vector: float32 [64, 64, 1024], P(('grp', 'blk'), None, ('mpo', 'rep')), parts along dimension 0
- second_image: float32 [64, 64, 1024], P(('grp', 'blk'), None, ('mpo', 'rep')), parts along dimension 0
There are 2 independent parts, one for each index of `grp`. A program takes and returns all parts, laid end to end along the dimension named above; each array names one. Nothing has to cross between parts.
Inputs may be any that keep to these rules, and one draw needn't show every extreme that they name: `term_slot`: slot t of the device that owns block j sends to the owner t // 2.
All inputs are finite; a program needn't handle non-finite values.
Results may differ from a plain program's by a relative error of at most 0.00014.
Values sent between devices are 32-bit elements; how exact they have to be, the bound alone decides.
No kernel may reach another device: no remote copies, remote signals or barrier semaphores. Data moves between devices by JAX's collectives and lax.ppermute only.
A program may use at most 128 MiB of HBM per device.

v0:
```python
import jax
import jax.numpy as jnp
from jax import lax
from jax.sharding import PartitionSpec as P


def bond_apply(vector_full, environment, bond_terms, term_slot, slot_block, diagonal):
    block_count, block_rows, block_width = vector_full.shape
    phys_size = bond_terms.shape[-1]
    right_rows = block_width // phys_size
    slot_count = slot_block.shape[0] * slot_block.shape[1]
    blocks = vector_full.reshape(block_count, block_rows, right_rows, phys_size)
    ordered = jnp.transpose(blocks, (0, 3, 1, 2))
    left_env = environment[:, :, :, :block_rows]
    right_env = environment[:, :, :, block_rows:]
    left_done = jnp.einsum("wjab,jsac->wjsbc", left_env, ordered, precision=lax.Precision.HIGHEST)
    right_done = jnp.einsum(
        "wjsbc,wjcd->wjsbd", left_done, right_env, precision=lax.Precision.HIGHEST
    )
    right_done = right_done.reshape(
        environment.shape[0], block_count, phys_size, block_rows * right_rows
    )
    bond_term = jnp.einsum(
        "wjsx,wst->wjtx", right_done, bond_terms, precision=lax.Precision.HIGHEST
    )
    bond_term = bond_term.reshape(environment.shape[0], block_count, block_rows * block_width)
    slot_table = (
        term_slot[:, None, :] == jnp.arange(slot_count, dtype=jnp.int32)[None, :, None]
    ).astype(jnp.float32)
    slot_buffer = jnp.einsum("wsj,wjx->sx", slot_table, bond_term, precision=lax.Precision.HIGHEST)
    slot_buffer = slot_buffer.reshape(slot_count, phys_size, block_rows, right_rows)
    slot_buffer = jnp.transpose(slot_buffer, (0, 2, 3, 1)).reshape(
        slot_count, block_rows, block_width
    )
    owners = slot_block.reshape(-1)
    selector = (owners[None, :] == jnp.arange(block_count, dtype=jnp.int32)[:, None]).astype(
        jnp.float32
    )
    column_width = block_width // lax.axis_size(("mpo", "rep"))
    column_start = lax.axis_index(("mpo", "rep")) * column_width
    own_part = lax.dynamic_slice_in_dim(vector_full, column_start, column_width, 2)
    shares = lax.psum_scatter(slot_buffer, ("mpo", "rep"), scatter_dimension=2, tiled=True)
    arrived = lax.all_to_all(shares, "blk", split_axis=0, concat_axis=0, tiled=True)
    result = jnp.einsum("ks,sbc->kbc", selector, arrived, precision=lax.Precision.HIGHEST)
    return (result + diagonal * own_part, own_part)


def per_device(wavefunction, environment, bond_terms, diagonal, term_slot, slot_block):
    arranged = lax.all_to_all(environment, "blk", split_axis=1, concat_axis=2, tiled=True)
    entries = float(
        wavefunction.shape[0] * lax.axis_size("blk") * wavefunction.shape[1] * wavefunction.shape[2]
    )
    square_sum = lax.psum(jnp.sum(wavefunction * wavefunction), "blk")
    first_vector = wavefunction * lax.rsqrt(square_sum / entries + 1e-06)
    first_image, first_part = bond_apply(
        first_vector, arranged, bond_terms, term_slot, slot_block, diagonal
    )
    rayleigh = lax.psum(jnp.sum(first_part * first_image), ("blk", "mpo", "rep")) / entries
    residual = first_image - rayleigh * first_part
    resid_sum = lax.psum(jnp.sum(residual * residual), ("blk", "mpo", "rep"))
    second_vector = residual * lax.rsqrt(resid_sum / entries + 1e-06)
    second_full = lax.all_gather(second_vector, ("mpo", "rep"), axis=2, tiled=True)
    second_image, unused = bond_apply(
        second_full, arranged, bond_terms, term_slot, slot_block, diagonal
    )
    return (first_image, second_vector, second_image)


def solution(mesh):
    return jax.shard_map(
        per_device,
        mesh=mesh,
        in_specs=(
            P(("grp", "blk"), None, None),
            P(("grp", "mpo", "rep"), None, "blk", None),
            P(("grp", "mpo", "rep"), None, None),
            P(("grp", "blk"), None, ("mpo", "rep")),
            P(("grp", "mpo", "rep"), "blk"),
            P("grp", "blk"),
        ),
        out_specs=(
            P(("grp", "blk"), None, ("mpo", "rep")),
            P(("grp", "blk"), None, ("mpo", "rep")),
            P(("grp", "blk"), None, ("mpo", "rep")),
        ),
        check_vma=False,
    )
```

profile of v0, /device:TPU:0, one launch (start us, length us, event | category | flops | bytes accessed | tf_op | source)
XLA Modules:
  0.0 640.3 jit_solution(11333163537945294832)
XLA Ops:
  10.2 6.3 all-to-all-start
  17.6 31.0 %psum.21 = f32[]{:T(128)} all-reduce(f32[]{:T(128)} %multiply_reduce_fusion), channel_id=1, replica_groups=mesh['grp'=2,'blk'=4,'mpo'=2,'rep'=2] {'blk'}, use_global_device_ids=true, to_apply=%region_1.0 | all-reduce | flops 1 | bytes 8 | tf_op jit(solution)/shard_map/psum | solution.py:53
  56.5 23.1 %fusion.10 = f32[8,16,64,6,64]{4,2,1,0,3:T(8,128)S(1)} fusion(f32[8,16,64,64]{2,1,3,0:T(8,128)} %bitcast.94, f32[6,8,64,128]{3,2,1,0:T(8,128)S(1)} %bitcast.88), kind=kOutput, calls=%fused_computation.12 | convolution fusion | flops 2415919104 | bytes 16252928 | tf_op jit(solution)/shard_map/wjab,jsac->wjsbc/dot_general | solution.py:16
  79.7 45.0 %fusion.2 = f32[6,8,16,64,64]{4,3,2,1,0:T(8,128)} fusion(f32[8,16,64,6,64]{4,2,1,0,3:T(8,128)S(1)} %fusion.10, f32[6,8,64,128]{3,2,1,0:T(8,128)S(1)} %bitcast.89), kind=kOutput, calls=%fused_computation.2 | convolution fusion | flops 2415919104 | bytes 26738688 | tf_op jit(solution)/shard_map/wjsbc,wjcd->wjsbd/dot_general | solution.py:17
  124.6 20.8 %reshape.37 = f32[6,8,16,4096]{3,2,1,0:T(8,128)} reshape(f32[6,8,16,64,64]{4,3,2,1,0:T(8,128)} %fusion.2) | data formatting | bytes 25165824 | tf_op jit(solution)/shard_map/reshape | solution.py:20
  145.5 18.3 %convolution_bitcast_fusion.1 = f32[6,8,16,4096]{3,2,1,0:T(8,128)} fusion(f32[6,8,16,4096]{3,2,1,0:T(8,128)} %reshape.37, f32[6,16,16]{2,1,0:T(8,128)S(1)} %copy-done), kind=kOutput, calls=%fused_computation.9 | convolution fusion | flops 603979776 | bytes 25171968 | tf_op jit(solution)/shard_map/wjsx,wst->wjtx/dot_general | solution.py:23
  163.8 11.1 %reshape.38 = f32[6,8,65536]{2,1,0:T(8,128)} reshape(f32[6,8,16,4096]{3,2,1,0:T(8,128)} %convolution_bitcast_fusion.1) | data formatting | bytes 25165824 | tf_op jit(solution)/shard_map/reshape | solution.py:26
  174.9 17.1 %dot_general.42 = f32[16,64,64,8,6]{2,1,0,3,4:T(8,128)} reshape(f32[65536,8,6]{0,1,2:T(8,128)} %bitcast.86) | data formatting | bytes 25165824 | tf_op jit(solution)/shard_map/wsj,wjx->sx/dot_general | solution.py:30
  192.0 32.0 %fusion.14 = f32[8,64,64,16]{2,0,1,3:T(8,128)} fusion(f32[16,64,64,8,6]{2,1,0,3,4:T(8,128)} %dot_general.42, s32[6,8]{1,0:T(8,128)S(1)} %copy-done.5), kind=kOutput, calls=%fused_computation.16 | convolution fusion | flops 301990272 | bytes 14680256 | tf_op jit(solution)/shard_map/wsj,wjx->sx/dot_general | solution.py:30
  228.4 51.5 %reduce-scatter.3.cloned.1.call-done = f32[8,64,256]{1,2,0:T(8,128)} async-done(((f32[8,64,1024]{1,2,0:T(8,128)}), f32[8,64,256]{1,2,0:T(8,128)}) %reduce-scatter.3.cloned.1.call-update) | async-done | bytes 524304 | tf_op jit(solution)/shard_map/reduce_scatter | solution.py:42
  282.3 4.6 all-to-all-start.1
  287.1 14.3 %all-to-all-done.1 = f32[8,64,256]{2,1,0:T(8,128)S(1)} async-done(((f32[8,64,256]{2,1,0:T(8,128)}), f32[8,64,256]{2,1,0:T(8,128)S(1)}, u32[]{:S(2)}, u32[]{:S(2)}) %all-to-all-start.1) | async-done | bytes 524320 | tf_op jit(solution)/shard_map/all_to_all | solution.py:43
  303.9 30.1 %psum.22 = f32[]{:T(128)} all-reduce(f32[]{:T(128)} %get-tuple-element.12), channel_id=1, replica_groups=mesh['grp'=2,'blk'=4,'mpo'=2,'rep'=2] {'blk','mpo','rep'}, use_global_device_ids=true, to_apply=%region_4.0 | all-reduce | flops 1 | bytes 8 | tf_op jit(solution)/shard_map/psum | solution.py:58
  336.5 30.1 %psum.23 = f32[]{:T(128)} all-reduce(f32[]{:T(128)} %multiply_reduce_fusion.1), channel_id=1, replica_groups=mesh['grp'=2,'blk'=4,'mpo'=2,'rep'=2] {'blk','mpo','rep'}, use_global_device_ids=true, to_apply=%region_6.0 | all-reduce | flops 1 | bytes 8 | tf_op jit(solution)/shard_map/psum | solution.py:60
  369.2 19.9 %all-gather.2.cloned.1.call-done = f32[8,64,1024]{2,0,1:T(8,128)} async-done(((f32[8,64,256]{2,0,1:T(8,128)}), f32[8,64,1024]{2,0,1:T(8,128)}) %all-gather.2.cloned.1.call-update) | async-done | bytes 2097168 | tf_op jit(solution)/shard_map/all_gather | solution.py:62
  393.2 23.1 %fusion.8 = f32[8,16,64,6,64]{4,2,1,0,3:T(8,128)S(1)} fusion(f32[8,64,64,16]{1,3,2,0:T(8,128)} %bitcast.95, f32[6,8,64,128]{3,2,1,0:T(8,128)S(1)} %bitcast.90), kind=kOutput, calls=%fused_computation.10 | convolution fusion | flops 2415919104 | bytes 16252928 | tf_op jit(solution)/shard_map/wjab,jsac->wjsbc/dot_general | solution.py:16
  416.3 44.5 %fusion = f32[6,8,16,64,64]{4,3,2,1,0:T(8,128)} fusion(f32[8,16,64,6,64]{4,2,1,0,3:T(8,128)S(1)} %fusion.8, f32[6,8,64,128]{3,2,1,0:T(8,128)S(1)} %bitcast.91), kind=kOutput, calls=%fused_computation | convolution fusion | flops 2415919104 | bytes 26738688 | tf_op jit(solution)/shard_map/wjsbc,wjcd->wjsbd/dot_general | solution.py:17
  460.8 20.8 %reshape.41 = f32[6,8,16,4096]{3,2,1,0:T(8,128)} reshape(f32[6,8,16,64,64]{4,3,2,1,0:T(8,128)} %fusion) | data formatting | bytes 25165824 | tf_op jit(solution)/shard_map/reshape | solution.py:20
  481.7 18.6 %convolution_bitcast_fusion = f32[6,8,16,4096]{3,2,1,0:T(8,128)} fusion(f32[6,8,16,4096]{3,2,1,0:T(8,128)} %reshape.41, f32[6,16,16]{2,1,0:T(8,128)S(1)} %copy-done), kind=kOutput, calls=%fused_computation.8 | convolution fusion | flops 603979776 | bytes 25171968 | tf_op jit(solution)/shard_map/wjsx,wst->wjtx/dot_general | solution.py:23
  500.2 11.1 %reshape.42 = f32[6,8,65536]{2,1,0:T(8,128)} reshape(f32[6,8,16,4096]{3,2,1,0:T(8,128)} %convolution_bitcast_fusion) | data formatting | bytes 25165824 | tf_op jit(solution)/shard_map/reshape | solution.py:26
  511.3 17.1 %dot_general.49 = f32[16,64,64,8,6]{2,1,0,3,4:T(8,128)} reshape(f32[65536,8,6]{0,1,2:T(8,128)} %bitcast.87) | data formatting | bytes 25165824 | tf_op jit(solution)/shard_map/wsj,wjx->sx/dot_general | solution.py:30
  528.4 31.8 %fusion.17 = f32[8,64,64,16]{2,0,1,3:T(8,128)} fusion(f32[16,64,64,8,6]{2,1,0,3,4:T(8,128)} %dot_general.49, s32[6,8]{1,0:T(8,128)S(1)} %copy-done.5), kind=kOutput, calls=%fused_computation.17 | convolution fusion | flops 301990272 | bytes 14680256 | tf_op jit(solution)/shard_map/wsj,wjx->sx/dot_general | solution.py:30
  564.6 44.7 %reduce-scatter.5.cloned.1.call-done = f32[8,64,256]{1,2,0:T(8,128)} async-done(((f32[8,64,1024]{1,2,0:T(8,128)}), f32[8,64,256]{1,2,0:T(8,128)}) %reduce-scatter.5.cloned.1.call-update) | async-done | bytes 524304 | tf_op jit(solution)/shard_map/reduce_scatter | solution.py:42
  618.1 12.6 %all-to-all-done.2 = f32[8,64,256]{2,1,0:T(8,128)S(1)} async-done(((f32[8,64,256]{2,1,0:T(8,128)}), f32[8,64,256]{2,1,0:T(8,128)S(1)}, u32[]{:S(2)}, u32[]{:S(2)}) %all-to-all-start.2) | async-done | bytes 524320 | tf_op jit(solution)/shard_map/all_to_all | solution.py:43
  (41 shorter events, 44.7 us)
Async XLA Ops:
  7.2 138.3 %copy-start = (f32[6,16,16]{2,1,0:T(8,128)S(1)}, f32[6,16,16]{2,1,0:T(8,128)}, u32[]{:S(2)}) copy-start(f32[6,16,16]{2,1,0:T(8,128)} %param.8) | copy-start | bytes 18436
  7.2 9.3 %copy-start.2 = (f32[8,64,1024]{2,1,0:T(8,128)S(1)}, f32[8,64,1024]{2,1,0:T(8,128)}, u32[]{:S(2)}) copy-start(f32[8,64,1024]{2,1,0:T(8,128)} %param.6) | copy-start | bytes 6291460
  10.2 44.7 %all-to-all-start = ((f32[6,32,16,128]{3,2,0,1:T(8,128)}), f32[6,32,16,128]{3,2,0,1:T(8,128)}, u32[]{:S(2)}, u32[]{:S(2)}) async-start(f32[6,32,16,128]{3,2,0,1:T(8,128)} %copy.40), calls=%async_computation | async-start | bytes 3145728 | tf_op jit(solution)/shard_map/all_to_all | solution.py:49
  16.5 263.5 %reduce-scatter.3.cloned.1.call-start = ((), (), s32[]{:S(2)}) async-start(), calls=%async_computation.5 | async-start | bytes 5242880 | tf_op jit(solution)/shard_map/reduce_scatter | solution.py:42
  52.1 2.8 copy-start.1
  174.9 17.1 %copy-start.5 = (s32[6,8]{1,0:T(8,128)S(1)}, s32[6,8]{1,0:T(8,128)}, u32[]{:S(2)}) copy-start(s32[6,8]{1,0:T(8,128)} %param.10) | copy-start | bytes 580
  228.4 58.5 %copy-start.6 = (s32[4,2]{0,1:T(2,128)S(1)}, s32[4,2]{0,1:T(2,128)}, u32[]{:S(2)}) copy-start(s32[4,2]{0,1:T(2,128)} %param.11) | copy-start | bytes 100
  228.4 73.0 %copy-start.4 = (f32[8,64,256]{2,1,0:T(8,128)S(1)}, f32[8,64,256]{2,1,0:T(8,128)}, u32[]{:S(2)}) copy-start(f32[8,64,256]{2,1,0:T(8,128)} %param.9) | copy-start | bytes 1572868
  282.3 19.1 %all-to-all-start.1 = ((f32[8,64,256]{2,1,0:T(8,128)}), f32[8,64,256]{2,1,0:T(8,128)S(1)}, u32[]{:S(2)}, u32[]{:S(2)}) async-start(f32[8,64,256]{2,1,0:T(8,128)} %copy.47), calls=%async_computation.2 | async-start | bytes 1048576 | tf_op jit(solution)/shard_map/all_to_all | solution.py:43
  286.9 102.3 %all-gather.2.cloned.1.call-start = ((), (), s32[]{:S(2)}) async-start(), calls=%async_computation.6 | async-start | bytes 2621440 | tf_op jit(solution)/shard_map/all_gather | solution.py:62
  369.2 240.1 %reduce-scatter.5.cloned.1.call-start = ((), (), s32[]{:S(2)}) async-start(), calls=%async_computation.7 | async-start | bytes 5242880 | tf_op jit(solution)/shard_map/reduce_scatter | solution.py:42
  564.6 52.6 %copy-start.3 = (f32[8,64,256]{2,0,1:T(8,128)S(1)}, f32[8,64,256]{2,0,1:T(8,128)}, u32[]{:S(2)}) copy-start(f32[8,64,256]{2,0,1:T(8,128)} %broadcast_multiply_fusion) | copy-start | bytes 1572868
  611.6 19.1 %all-to-all-start.2 = ((f32[8,64,256]{2,1,0:T(8,128)}), f32[8,64,256]{2,1,0:T(8,128)S(1)}, u32[]{:S(2)}, u32[]{:S(2)}) async-start(f32[8,64,256]{2,1,0:T(8,128)} %copy.56), calls=%async_computation.4 | async-start | bytes 1048576 | tf_op jit(solution)/shard_map/all_to_all | solution.py:43
Sparse Core Ops, SparseCore 0:
  228.6 51.3 reduce-scatter.2
  369.3 19.8 all-gather.1
  564.7 44.5 reduce-scatter.4
where the time goes:
time: 648 us; the launch traced here: 640 us
  matrix products  241 us (37%)
  waiting for transfers between devices  143 us (22%)
  local copies, waits for them, and re-layouts  126 us (19%)
  blocking collectives  91.2 us (14%)
  between operations  16 us (2%)
  starting transfers between devices  15.5 us (2%)
  other arithmetic  7.65 us (1%)
    reduce_scatter x2, waiting for transfers between devices, bond_apply(): lax.psum_scatter(slot_buffer, ('mpo', 'rep'), scatter_dimension=2, tiled=...  96.2 us
    dot_general x2, matrix products, bond_apply(): jnp.einsum('wjsbc,wjcd->wjsbd', left_done, right_env, precision=lax.Preci...  89.5 us
    dot_general x2, matrix products, bond_apply(): jnp.einsum('wsj,wjx->sx', slot_table, bond_term, precision=lax.Precision....  63.8 us
    dot_general x2, matrix products, bond_apply(): jnp.einsum('wjab,jsac->wjsbc', left_env, ordered, precision=lax.Precision...  46.3 us
    reshape x2, local copies, waits for them, and re-layouts, bond_apply(): right_done.reshape(environment.shape[0], block_count, phys_size, block_ro...  41.7 us
    dot_general x2, matrix products, bond_apply(): jnp.einsum('wjsx,wst->wjtx', right_done, bond_terms, precision=lax.Precis...  36.9 us
    dot_general x2, local copies, waits for them, and re-layouts, bond_apply(): jnp.einsum('wsj,wjx->sx', slot_table, bond_term, precision=lax.Precision....  34.1 us
    psum x1, blocking collectives, per_device(): square_sum = lax.psum(jnp.sum(wavefunction * wavefunction), 'blk')  31 us
  transfers between devices with their start and end apart: 6, of which 5 were waited for; matrix products, arithmetic and copies ran while one was open for 1% of the time, Pallas kernels for 0%

commit v1 on v0

--- a/solution.py
+++ b/solution.py
@@ -1,10 +1,20 @@
+import functools
+import math
+
 import jax
 import jax.numpy as jnp
 from jax import lax
+from jax.experimental import pallas as pl
+from jax.experimental.pallas import tpu as pltpu
 from jax.sharding import PartitionSpec as P
 
-
-def bond_apply(vector_full, environment, bond_terms, term_slot, slot_block, diagonal):
+LANES = 128
+SUB = 8
+GROUPS = 3
+VMEM_LIMIT = 56 * 1024 * 1024
+
+
+def plain_apply(vector_full, environment, bond_terms, term_slot, slot_block, diagonal):
     block_count, block_rows, block_width = vector_full.shape
     phys_size = bond_terms.shape[-1]
     right_rows = block_width // phys_size
@@ -45,14 +55,14 @@
     return (result + diagonal * own_part, own_part)
 
 
-def per_device(wavefunction, environment, bond_terms, diagonal, term_slot, slot_block):
+def plain_device(wavefunction, environment, bond_terms, diagonal, term_slot, slot_block):
     arranged = lax.all_to_all(environment, "blk", split_axis=1, concat_axis=2, tiled=True)
     entries = float(
         wavefunction.shape[0] * lax.axis_size("blk") * wavefunction.shape[1] * wavefunction.shape[2]
     )
     square_sum = lax.psum(jnp.sum(wavefunction * wavefunction), "blk")
     first_vector = wavefunction * lax.rsqrt(square_sum / entries + 1e-06)
-    first_image, first_part = bond_apply(
+    first_image, first_part = plain_apply(
         first_vector, arranged, bond_terms, term_slot, slot_block, diagonal
     )
     rayleigh = lax.psum(jnp.sum(first_part * first_image), ("blk", "mpo", "rep")) / entries
@@ -60,15 +70,313 @@
     resid_sum = lax.psum(jnp.sum(residual * residual), ("blk", "mpo", "rep"))
     second_vector = residual * lax.rsqrt(resid_sum / entries + 1e-06)
     second_full = lax.all_gather(second_vector, ("mpo", "rep"), axis=2, tiled=True)
-    second_image, unused = bond_apply(
+    second_image, unused = plain_apply(
         second_full, arranged, bond_terms, term_slot, slot_block, diagonal
     )
     return (first_image, second_vector, second_image)
 
 
+def split_two(x):
+    high = x.astype(jnp.bfloat16)
+    low = (x - high.astype(jnp.float32)).astype(jnp.bfloat16)
+    return high, low
+
+
+def prepare_kernel(place_ref, *refs):
+    sources = refs[:-3]
+    left_high, left_low, right_out = refs[-3:]
+    zs, per, blocks, rows, lanes = sources[0].shape
+    half = lanes // 2
+    lane = lax.broadcasted_iota(jnp.int32, (half, lanes), 1)
+    first = place_ref[0]
+    pairs = [(s, k) for s in range(len(sources)) for k in range(per)]
+    count = lanes // 16
+    for j in range(blocks):
+        for base in range(0, len(pairs), count):
+            group = pairs[base : base + count]
+            columns = jnp.zeros((half, lanes), jnp.float32)
+            for at, (s, k) in enumerate(group):
+                block = jnp.concatenate([sources[s][z, k, j] for z in range(zs)], axis=0)
+                turned = pltpu.roll(block, half, 1)
+                both = jnp.where(lane < half, block, turned)
+                high, low = split_two(both)
+                left_high[base + at, j] = high
+                left_low[base + at, j] = low
+                shift = (16 * at + lanes - half - first) % lanes
+                moved = pltpu.roll(block, lax.rem(shift, lanes), 1)
+                columns = jnp.where(lane // 16 == at, moved, columns)
+            upright = columns.T
+            pieces = []
+            for at in range(len(group)):
+                a = upright[16 * at : 16 * at + 8]
+                b = upright[16 * at + 8 : 16 * at + 16]
+                pieces.append(jnp.concatenate([a, b], axis=1))
+            packed = jnp.concatenate(pieces, axis=0)
+            high, low = split_two(packed)
+            where = pl.ds(SUB * base, SUB * len(group))
+            right_out[j, where, 0:lanes] = high
+            right_out[j, where, lanes : 2 * lanes] = high
+            right_out[j, where, 2 * lanes : 3 * lanes] = low
+
+
+def prepare(environments, first_column):
+    zs, per, blocks, rows, lanes = environments[0].shape
+    total = per * len(environments)
+    half = lanes // 2
+    step = 2
+    return pl.pallas_call(
+        prepare_kernel,
+        grid_spec=pltpu.PrefetchScalarGridSpec(
+            num_scalar_prefetch=1,
+            grid=(blocks // step,),
+            in_specs=[
+                pl.BlockSpec((zs, per, step, rows, lanes), lambda i, p: (0, 0, i, 0, 0))
+                for _ in environments
+            ],
+            out_specs=[
+                pl.BlockSpec((total, step, half, lanes), lambda i, p: (0, i, 0, 0)),
+                pl.BlockSpec((total, step, half, lanes), lambda i, p: (0, i, 0, 0)),
+                pl.BlockSpec((step, total * SUB, 3 * lanes), lambda i, p: (i, 0, 0)),
+            ],
+        ),
+        out_shape=[
+            jax.ShapeDtypeStruct((total, blocks, half, lanes), jnp.bfloat16),
+            jax.ShapeDtypeStruct((total, blocks, half, lanes), jnp.bfloat16),
+            jax.ShapeDtypeStruct((blocks, total * SUB, 3 * lanes), jnp.bfloat16),
+        ],
+        compiler_params=pltpu.CompilerParams(vmem_limit_bytes=VMEM_LIMIT),
+        name="prepare",
+    )(first_column.reshape(1), *environments)
+
+
+def apply_kernel(slot_ref, place_ref, *refs):
+    parts = refs[:4]
+    left_high, left_low, right_ref, mix_ref, before, out_ref, vec, mid = refs[4:]
+    step = parts[0].shape[0]
+    total = left_high.shape[0]
+    lanes = LANES
+    half = lanes // 2
+    phys = 16
+    lane = lax.broadcasted_iota(jnp.int32, (16, lanes), 1)
+    lane64 = lax.broadcasted_iota(jnp.int32, (half, lanes), 1)
+    zero16 = jnp.zeros((16, lanes), jnp.float32)
+    zero64 = jnp.zeros((half, lanes), jnp.bfloat16)
+
+    @pl.when(pl.program_id(0) == 0)
+    def _():
+        out_ref[...] = before[...]
+
+    for j in range(step):
+        for s in range(phys):
+            for g in range(4):
+                x = parts[g][j, pl.ds(s, SUB, stride=phys), :]
+                y = pltpu.roll(x, half, 1)
+                xy = jnp.concatenate([x, y], axis=0)
+                yx = jnp.concatenate([y, x], axis=0)
+                top_high, top_low = split_two(jnp.where(lane < half, xy, zero16))
+                low_high, low_low = split_two(jnp.where(lane < half, zero16, yx))
+                row = pl.multiple_of(place_ref[g] * 16, 16)
+                columns = slice(s * lanes, (s + 1) * lanes)
+                vec[pl.ds(row, 16), columns] = top_high
+                vec[pl.ds(row + half, 16), columns] = low_high
+                vec[pl.ds(row + lanes, 16), columns] = top_low
+                vec[pl.ds(row + lanes + half, 16), columns] = low_low
+        mid[j] = jnp.dot(
+            right_ref[j, :, 0 : 2 * lanes], vec[...], preferred_element_type=jnp.float32
+        ) + jnp.dot(
+            right_ref[j, :, 2 * lanes :], vec[0:lanes, :], preferred_element_type=jnp.float32
+        )
+
+    def one_bond(w):
+        highs, lows = [], []
+        for j in range(step):
+            rows = pl.ds(pl.multiple_of(w * SUB, SUB), SUB)
+            t = jnp.concatenate(
+                [mid[j, rows, s * lanes : (s + 1) * lanes] for s in range(phys)], axis=0
+            )
+            t_high, t_low = split_two(t)
+            lh, ll = left_high[w, j], left_low[w, j]
+            wide_high = jnp.concatenate(
+                [jnp.where(lane64 < half, lh, zero64), jnp.where(lane64 < half, zero64, lh)], axis=0
+            )
+            wide_low = jnp.concatenate(
+                [jnp.where(lane64 < half, ll, zero64), jnp.where(lane64 < half, zero64, ll)], axis=0
+            )
+            z = jnp.dot(
+                jnp.concatenate([t_high, t_low], axis=1),
+                jnp.concatenate([wide_high, wide_high], axis=0),
+                preferred_element_type=jnp.float32,
+            ) + jnp.dot(t_high, wide_low, preferred_element_type=jnp.float32)
+            z_high, z_low = split_two(z)
+            highs.append(z_high)
+            lows.append(z_low)
+        z_high = jnp.concatenate(highs, axis=1)
+        z_low = jnp.concatenate(lows, axis=1)
+        mix_high = mix_ref[w, :, 0:lanes]
+        mix_low = mix_ref[w, :, lanes:]
+        mixed = jnp.dot(
+            jnp.concatenate([mix_high, mix_high], axis=1),
+            jnp.concatenate([z_high, z_low], axis=0),
+            preferred_element_type=jnp.float32,
+        ) + jnp.dot(mix_low, z_high, preferred_element_type=jnp.float32)
+        for j in range(step):
+            slot = slot_ref[w, pl.program_id(0) * step + j]
+            out_ref[slot] += mixed[:, j * lanes : (j + 1) * lanes]
+
+    unroll = 4 if total % 4 == 0 else 1
+
+    def several(i, carry):
+        for k in range(unroll):
+            one_bond(i * unroll + k)
+        return carry
+
+    lax.fori_loop(0, total // unroll, several, 0)
+
+
+def apply_bonds(parts, places, operands, mixing, slots, before):
+    left_high, left_low, right = operands
+    total, blocks, half, lanes = left_high.shape
+    step = 2
+    whole = lambda *shape: pl.BlockSpec(shape, lambda i, *_: (0,) * len(shape))
+    flops = 2 * blocks * total * SUB * lanes * (3 * lanes * 16 + 3 * lanes * 16 + 3 * lanes * 16)
+    return pl.pallas_call(
+        apply_kernel,
+        grid_spec=pltpu.PrefetchScalarGridSpec(
+            num_scalar_prefetch=2,
+            grid=(blocks // step,),
+            in_specs=[
+                pl.BlockSpec((step, lanes, lanes), lambda i, *_: (i, 0, 0)) for _ in parts
+            ]
+            + [
+                pl.BlockSpec((total, step, half, lanes), lambda i, *_: (0, i, 0, 0)),
+                pl.BlockSpec((total, step, half, lanes), lambda i, *_: (0, i, 0, 0)),
+                pl.BlockSpec((step, total * SUB, 3 * lanes), lambda i, *_: (i, 0, 0)),
+                whole(*mixing.shape),
+                whole(*before.shape),
+            ],
+            out_specs=whole(*before.shape),
+            scratch_shapes=[
+                pltpu.VMEM((2 * lanes, 16 * lanes), jnp.bfloat16),
+                pltpu.VMEM((step, total * SUB, 16 * lanes), jnp.float32),
+            ],
+        ),
+        out_shape=jax.ShapeDtypeStruct(before.shape, jnp.float32),
+        compiler_params=pltpu.CompilerParams(vmem_limit_bytes=VMEM_LIMIT),
+        cost_estimate=pl.CostEstimate(
+            flops=flops, bytes_accessed=12 * 1024 * 1024, transcendentals=0
+        ),
+        name="apply_bonds",
+    )(slots, places, *parts, left_high, left_low, right, mixing, before)
+
+
+def swap(x, axis):
+    return lax.ppermute(x, axis, [(0, 1), (1, 0)])
+
+
+def gathered(x):
+    across = swap(x, "mpo")
+    return [x, across, swap(x, "rep"), swap(across, "rep")]
+
+
+def to_packed(x):
+    blocks, rows, width = x.shape
+    x = x.reshape(blocks, rows, 2, width // 2)
+    return jnp.transpose(x, (0, 3, 2, 1)).reshape(blocks, width // 2, 2 * rows)
+
+
+def from_packed(x):
+    blocks, width, rows = x.shape
+    x = x.reshape(blocks, width, 2, rows // 2)
+    return jnp.transpose(x, (0, 3, 2, 1)).reshape(blocks, rows // 2, 2 * width)
+
+
+def mixing_operand(bond_terms):
+    count, phys, _ = bond_terms.shape
+    eye = jnp.eye(SUB, dtype=jnp.float32)
+    wide = jnp.transpose(bond_terms, (0, 2, 1))[:, None, :, :, None] * eye[None, :, None, None, :]
+    wide = wide.reshape(count, SUB * phys, phys * SUB)
+    high = lax.reduce_precision(wide, 8, 7)
+    return jnp.concatenate([high, wide - high], axis=2).astype(jnp.bfloat16)
+
+
+def owner_sum(slot_sums, slot_block):
+    arrived = lax.all_to_all(slot_sums, "blk", split_axis=0, concat_axis=0, tiled=True)
+    owners = slot_block.reshape(-1)
+    blocks = slot_sums.shape[0]
+    total = []
+    selector = owners[None, :] == jnp.arange(blocks, dtype=jnp.int32)[:, None]
+    return jnp.einsum(
+        "ks,sbc->kbc",
+        selector.astype(jnp.float32),
+        arrived,
+        precision=lax.Precision.HIGHEST,
+    )
+
+
+def per_device(wavefunction, environment, bond_terms, diagonal, term_slot, slot_block):
+    blocks, rows, width = wavefunction.shape
+    zs = lax.axis_size("blk")
+    mpo, rep = lax.axis_index("mpo"), lax.axis_index("rep")
+    place = lambda m, r: 2 * m + r
+    places = jnp.stack(
+        [place(mpo, rep), place(1 - mpo, rep), place(mpo, 1 - rep), place(1 - mpo, 1 - rep)]
+    ).astype(jnp.int32)
+    own = places[0]
+    bonds = environment.shape[0]
+    per = bonds // GROUPS
+    entries = float(blocks * zs * rows * width)
+
+    operands = []
+    for group in range(GROUPS):
+        piece = environment[group * per : (group + 1) * per]
+        piece = piece.reshape(per, zs, blocks, rows // zs, 2 * rows)
+        piece = jnp.transpose(piece, (1, 0, 2, 3, 4))
+        piece = lax.all_to_all(piece, "blk", split_axis=0, concat_axis=0, tiled=True)
+        operands.append(prepare(gathered(piece), 16 * own))
+
+    terms = gathered(bond_terms)
+    slots = gathered(term_slot)
+
+    def of_group(items, group):
+        return jnp.concatenate([x[group * per : (group + 1) * per] for x in items], axis=0)
+
+    mixings = [mixing_operand(of_group(terms, group)) for group in range(GROUPS)]
+    slot_tables = [of_group(slots, group) for group in range(GROUPS)]
+
+    quarters = wavefunction.reshape(blocks, rows, 4, 2, width // 8)
+    quarters = jnp.transpose(quarters, (2, 0, 4, 3, 1)).reshape(4, blocks, width // 8, 2 * rows)
+    in_order = jnp.arange(4, dtype=jnp.int32)
+    own_first = lax.dynamic_index_in_dim(quarters, own, 0, keepdims=False)
+    diagonal_packed = to_packed(diagonal)
+
+    def apply(parts, where):
+        total = jnp.zeros((zs * slot_block.shape[1], width // 8, 2 * rows), jnp.float32)
+        for group in range(GROUPS):
+            total = apply_bonds(
+                parts, where, operands[group], mixings[group], slot_tables[group], total
+            )
+        return owner_sum(total, slot_block)
+
+    image = apply([quarters[q] for q in range(4)], in_order) + diagonal_packed * own_first
+    second = apply(gathered(image), places) + diagonal_packed * image
+
+    square_sum = lax.psum(jnp.sum(wavefunction * wavefunction), "blk")
+    cross_sum = lax.psum(jnp.sum(own_first * image), ("blk", "mpo", "rep"))
+    scale = lax.rsqrt(square_sum / entries + 1e-06)
+    rayleigh = cross_sum * scale * scale / entries
+    residual = scale * (image - rayleigh * own_first)
+    resid_sum = lax.psum(jnp.sum(residual * residual), ("blk", "mpo", "rep"))
+    second_scale = lax.rsqrt(resid_sum / entries + 1e-06)
+    first_image = scale * image
+    second_vector = second_scale * residual
+    second_image = second_scale * scale * (second - rayleigh * image)
+    return tuple(from_packed(x) for x in (first_image, second_vector, second_image))
+
+
 def solution(mesh):
+    packed = mesh.shape["mpo"] == 2 and mesh.shape["rep"] == 2
     return jax.shard_map(
-        per_device,
+        per_device if packed else plain_device,
         mesh=mesh,
         in_specs=(
             P(("grp", "blk"), None, None),

time: 648 us -> 349 us (0.54)
  matrix products: 241 us -> 2.34 us
  Pallas kernels: 0 us -> 117 us
  waiting for transfers between devices: 143 us -> 45.1 us
  local copies, waits for them, and re-layouts: 126 us -> 57.7 us
  starting transfers between devices: 15.5 us -> 33.9 us
  blocking collectives: 91.2 us -> 76.9 us
  between operations: 16 us -> 3.11 us
    dot_general x10 -> x2, matrix products: 241 us -> 2.34 us  [owner_sum(): jnp.einsum('ks,sbc->kbc', selector.astype(jnp.float32), arrived, precisio...]
    pallas_call x0 -> x9, Pallas kernels: none -> 117 us  [the longest x6 101 us: apply_bonds(): pl.pallas_call(apply_kernel, grid_spec=pltpu.PrefetchScalarGridSpec(num_s...]
    reduce_scatter x2 -> x0, waiting for transfers between devices: 96.2 us -> none  [bond_apply(): lax.psum_scatter(slot_buffer, ('mpo', 'rep'), scatter_dimension=2, tiled=...]
    reshape x4 -> x9, local copies, waits for them, and re-layouts: 63.8 us -> 10.6 us  [the longest x3 4.64 us: per_device(): piece = piece.reshape(per, zs, blocks, rows // zs, 2 * rows)]
    dot_general x2 -> x0, local copies, waits for them, and re-layouts: 34.1 us -> none  [bond_apply(): jnp.einsum('wsj,wjx->sx', slot_table, bond_term, precision=lax.Precision....]
    mul x1 -> x15, local copies, waits for them, and re-layouts: 2.76 us -> 25.7 us  [the longest x12 25.1 us: mixing_operand(): jnp.transpose(bond_terms, (0, 2, 1))[:, None, :, :, None]]
    ppermute x0 -> x18, waiting for transfers between devices: none -> 21.1 us  [swap(): return lax.ppermute(x, axis, [(0, 1), (1, 0)])]
    all_gather x1 -> x0, waiting for transfers between devices: 19.9 us -> none  [per_device(): lax.all_gather(second_vector, ('mpo', 'rep'), axis=2, tiled=True)]
  transfers between devices with their start and end apart: 6 -> 23, of which waited for: 5 -> 5; matrix products, arithmetic and copies ran while one was open for 1% -> 17% of each run, Pallas kernels for 0% -> 13%
where the time goes in v1:
time: 349 us; the launch traced here: 347 us
  Pallas kernels  117 us (34%)
  blocking collectives  76.9 us (22%)
  local copies, waits for them, and re-layouts  57.7 us (17%)
  waiting for transfers between devices  45.1 us (13%)
  starting transfers between devices  33.9 us (10%)
  other arithmetic  11 us (3%)
    pallas_call x6, Pallas kernels, apply_bonds(): pl.pallas_call(apply_kernel, grid_spec=pltpu.PrefetchScalarGridSpec(num_s...  101 us
    psum x1, blocking collectives, per_device(): cross_sum = lax.psum(jnp.sum(own_first * image), ('blk', 'mpo', 'rep'))  32.2 us
    psum x1, blocking collectives, per_device(): resid_sum = lax.psum(jnp.sum(residual * residual), ('blk', 'mpo', 'rep'))  30.1 us
    mul x12, local copies, waits for them, and re-layouts, mixing_operand(): jnp.transpose(bond_terms, (0, 2, 1))[:, None, :, :, None]  25.1 us
    ppermute x18, waiting for transfers between devices, swap(): return lax.ppermute(x, axis, [(0, 1), (1, 0)])  21.1 us
    pallas_call x3, Pallas kernels, prepare(): pl.pallas_call(prepare_kernel, grid_spec=pltpu.PrefetchScalarGridSpec(num...  15.7 us
    psum x1, blocking collectives, per_device(): square_sum = lax.psum(jnp.sum(wavefunction * wavefunction), 'blk')  14.7 us
    all_to_all x3, starting transfers between devices, per_device(): lax.all_to_all(piece, 'blk', split_axis=0, concat_axis=0, tiled=True)  14.5 us
  transfers between devices with their start and end apart: 23, of which 5 were waited for; matrix products, arithmetic and copies ran while one was open for 17% of the time, Pallas kernels for 13%

profile of v1, /device:TPU:0, one launch (start us, length us, event | category | flops | bytes accessed | tf_op | source)
XLA Modules:
  0.0 347.1 jit_solution(17066200961766632828)
XLA Ops:
  7.5 5.1 %all-to-all-start.1 = ((f32[4,2,8,16,128]{4,3,2,1,0:T(8,128)}), f32[4,2,8,16,128]{4,3,2,1,0:T(8,128)S(1)}, u32[]{:S(2)}, u32[]{:S(2)}) async-start(f32[4,2,8,16,128]{4,3,2,1,0:T(8,128)} %bitcast.87), calls=%async_computation.1 | async-start | bytes 1048576 | tf_op jit(solution)/shard_map/all_to_all | solution.py:334
  29.1 5.1 %all-to-all-start.2 = ((f32[4,2,8,16,128]{4,3,2,1,0:T(8,128)}), f32[4,2,8,16,128]{4,3,2,1,0:T(8,128)S(1)}, u32[]{:S(2)}, u32[]{:S(2)}) async-start(f32[4,2,8,16,128]{4,3,2,1,0:T(8,128)} %bitcast.93), calls=%async_computation.2 | async-start | bytes 1048576 | tf_op jit(solution)/shard_map/all_to_all | solution.py:334
  36.2 13.1 %all-to-all-done.2.refs_0_ = f32[4,2,8,16,128]{4,3,2,1,0:T(8,128)S(1)} async-done(((f32[4,2,8,16,128]{4,3,2,1,0:T(8,128)}), f32[4,2,8,16,128]{4,3,2,1,0:T(8,128)S(1)}, u32[]{:S(2)}, u32[]{:S(2)}) %all-to-all-start.2) | async-done | bytes 524320 | tf_op jit(solution)/shard_map/all_to_all | solution.py:334
  49.3 4.3 %all-to-all-start = ((f32[4,2,8,16,128]{4,3,2,1,0:T(8,128)}), f32[4,2,8,16,128]{4,3,2,1,0:T(8,128)}, u32[]{:S(2)}, u32[]{:S(2)}) async-start(f32[4,2,8,16,128]{4,3,2,1,0:T(8,128)} %bitcast.92), calls=%async_computation | async-start | bytes 1048576 | tf_op jit(solution)/shard_map/all_to_all | solution.py:334
  58.0 3.9 %mul.143 = f32[8,128,128]{1,2,0:T(8,128)} reshape(f32[8,8,16,16,8]{2,1,4,3,0:T(8,128)} %mul.142) | data formatting | bytes 1048576 | tf_op jit(solution)/shard_map/mul | solution.py:296
  66.3 3.9 %mul.140 = f32[8,128,128]{1,2,0:T(8,128)} reshape(f32[8,8,16,16,8]{2,1,4,3,0:T(8,128)} %mul.139) | data formatting | bytes 1048576 | tf_op jit(solution)/shard_map/mul | solution.py:296
  74.5 3.9 %mul.134 = f32[8,128,128]{1,2,0:T(8,128)} reshape(f32[8,8,16,16,8]{2,1,4,3,0:T(8,128)} %mul.133) | data formatting | bytes 1048576 | tf_op jit(solution)/shard_map/mul | solution.py:296
  86.6 8.5 %collective-permute-done.3.refs_1_ = f32[4,2,8,16,128]{4,3,2,1,0:T(8,128)S(1)} collective-permute-done((f32[4,2,8,16,128]{4,3,2,1,0:T(8,128)}, f32[4,2,8,16,128]{4,3,2,1,0:T(8,128)S(1)}, u32[]{:S(2)}, u32[]{:S(2)}) %collective-permute-start.3) | collective-permute-done | bytes 524320 | tf_op jit(solution)/shard_map/ppermute | solution.py:273
  97.3 5.2 %prepare.4 = (bf16[8,8,64,128]{3,2,1,0:T(8,128)(2,1)}, bf16[8,8,64,128]{3,2,1,0:T(8,128)(2,1)}, bf16[8,64,384]{2,1,0:T(8,128)(2,1)}) custom-call(s32[1]{0:T(128)} %bitcast.6.place_ref, f32[4,2,8,16,128]{4,3,2,1,0:T(8,128)} %copy-done.3, f32[4,2,8,16,128]{4,3,2,1,0:T(8,128)} %collective-permute-done.9.refs_1_, ...), custom_call_target="tpu_custom_call" | custom-call | tf_op jit(solution)/shard_map/prepare/pallas_call | solution.py:127
  103.3 5.2 %prepare.5 = (bf16[8,8,64,128]{3,2,1,0:T(8,128)(2,1)}, bf16[8,8,64,128]{3,2,1,0:T(8,128)(2,1)}, bf16[8,64,384]{2,1,0:T(8,128)(2,1)}) custom-call(s32[1]{0:T(128)} %bitcast.6.place_ref, f32[4,2,8,16,128]{4,3,2,1,0:T(8,128)} %copy-done.4, f32[4,2,8,16,128]{4,3,2,1,0:T(8,128)} %collective-permute-done.12.refs_1_, ...), custom_call_target="tpu_custom_call" | custom-call | tf_op jit(solution)/shard_map/prepare/pallas_call | solution.py:127
  110.0 16.9 %apply_bonds.6.refs_8_ = f32[8,128,128]{2,1,0:T(8,128)} custom-call(s32[8,8]{1,0:T(8,128)} %pad_add_fusion.2.slot_ref, s32[4]{0:T(128)} %iota.46.place_ref, f32[8,128,128]{2,1,0:T(8,128)} %copy.72.refs_0_, f32[8,128,128]{2,1,0:T(8,128)} %copy.73.refs_1_, f32[8,128,128]{2,1,0:T(8,128)} %copy.74.refs_2_, f32[8,128,128]{2,1,0:T(8,128)} %copy.75.refs_3_, ...), custom_call_target="tpu_custom_call" | custom-call | flops 2415919104 | bytes 12582912 | tf_op jit(solution)/shard_map/apply_bonds/pallas_call | solution.py:242
  127.5 16.9 %apply_bonds.7.refs_8_ = f32[8,128,128]{2,1,0:T(8,128)} custom-call(s32[8,8]{1,0:T(8,128)} %pad_add_fusion.1.slot_ref, s32[4]{0:T(128)} %iota.45.place_ref, f32[8,128,128]{2,1,0:T(8,128)} %copy.72.refs_0_, f32[8,128,128]{2,1,0:T(8,128)} %copy.73.refs_1_, f32[8,128,128]{2,1,0:T(8,128)} %copy.74.refs_2_, f32[8,128,128]{2,1,0:T(8,128)} %copy.75.refs_3_, ...), custom_call_target="tpu_custom_call" | custom-call | flops 2415919104 | bytes 12582912 | tf_op jit(solution)/shard_map/apply_bonds/pallas_call | solution.py:242
  146.0 5.2 %prepare.3 = (bf16[8,8,64,128]{3,2,1,0:T(8,128)(2,1)}, bf16[8,8,64,128]{3,2,1,0:T(8,128)(2,1)}, bf16[8,64,384]{2,1,0:T(8,128)(2,1)}) custom-call(s32[1]{0:T(128)} %bitcast.6.place_ref, f32[4,2,8,16,128]{4,3,2,1,0:T(8,128)} %all-to-all-done.refs_0_, f32[4,2,8,16,128]{4,3,2,1,0:T(8,128)} %copy-done.5, f32[4,2,8,16,128]{4,3,2,1,0:T(8,128)} %copy-done.6, ...), custom_call_target="tpu_custom_call" | custom-call | tf_op jit(solution)/shard_map/prepare/pallas_call | solution.py:127
  151.7 16.9 %apply_bonds.8 = f32[8,128,128]{2,1,0:T(8,128)} custom-call(s32[8,8]{1,0:T(8,128)} %pad_add_fusion.slot_ref, s32[4]{0:T(128)} %iota.42.place_ref, f32[8,128,128]{2,1,0:T(8,128)} %copy.72.refs_0_, f32[8,128,128]{2,1,0:T(8,128)} %copy.73.refs_1_, f32[8,128,128]{2,1,0:T(8,128)} %copy.74.refs_2_, f32[8,128,128]{2,1,0:T(8,128)} %copy.75.refs_3_, ...), custom_call_target="tpu_custom_call" | custom-call | flops 2415919104 | bytes 12582912 | tf_op jit(solution)/shard_map/apply_bonds/pallas_call | solution.py:242
  168.6 4.8 %all-to-all-start.3 = ((f32[8,128,128]{2,1,0:T(8,128)}), f32[8,128,128]{2,1,0:T(8,128)S(1)}, u32[]{:S(2)}, u32[]{:S(2)}) async-start(f32[8,128,128]{2,1,0:T(8,128)} %apply_bonds.8), calls=%async_computation.3 | async-start | bytes 1048576 | tf_op jit(solution)/shard_map/all_to_all | solution.py:303
  177.2 10.9 %all-to-all-done.3 = f32[8,128,128]{2,1,0:T(8,128)S(1)} async-done(((f32[8,128,128]{2,1,0:T(8,128)}), f32[8,128,128]{2,1,0:T(8,128)S(1)}, u32[]{:S(2)}, u32[]{:S(2)}) %all-to-all-start.3) | async-done | bytes 524320 | tf_op jit(solution)/shard_map/all_to_all | solution.py:303
  191.1 11.4 %collective-permute-done.15.refs_1_ = f32[8,128,128]{2,1,0:T(8,128)S(1)} collective-permute-done((f32[8,128,128]{2,1,0:T(8,128)S(1)}, f32[8,128,128]{2,1,0:T(8,128)S(1)}, u32[]{:S(2)}, u32[]{:S(2)}) %collective-permute-start.15) | collective-permute-done | bytes 524320 | tf_op jit(solution)/shard_map/ppermute | solution.py:273
  205.2 16.9 %apply_bonds.9.refs_8_ = f32[8,128,128]{2,1,0:T(8,128)} custom-call(s32[8,8]{1,0:T(8,128)} %pad_add_fusion.2.slot_ref, s32[4]{0:T(128)} %pad_add_fusion.3.place_ref, f32[8,128,128]{2,1,0:T(8,128)} %copy-done.1, f32[8,128,128]{2,1,0:T(8,128)} %copy-done.14, f32[8,128,128]{2,1,0:T(8,128)} %copy-done.15, f32[8,128,128]{2,1,0:T(8,128)} %copy-done.16, ...), custom_call_target="tpu_custom_call" | custom-call | flops 2415919104 | bytes 12582912 | tf_op jit(solution)/shard_map/apply_bonds/pallas_call | solution.py:242
  222.1 16.9 %apply_bonds.10.refs_8_ = f32[8,128,128]{2,1,0:T(8,128)} custom-call(s32[8,8]{1,0:T(8,128)} %pad_add_fusion.1.slot_ref, s32[4]{0:T(128)} %pad_add_fusion.3.place_ref, f32[8,128,128]{2,1,0:T(8,128)} %copy-done.1, f32[8,128,128]{2,1,0:T(8,128)} %copy-done.14, f32[8,128,128]{2,1,0:T(8,128)} %copy-done.15, f32[8,128,128]{2,1,0:T(8,128)} %copy-done.16, ...), custom_call_target="tpu_custom_call" | custom-call | flops 2415919104 | bytes 12582912 | tf_op jit(solution)/shard_map/apply_bonds/pallas_call | solution.py:242
  239.0 17.0 %apply_bonds.11 = f32[8,128,128]{2,1,0:T(8,128)} custom-call(s32[8,8]{1,0:T(8,128)} %pad_add_fusion.slot_ref, s32[4]{0:T(128)} %pad_add_fusion.3.place_ref, f32[8,128,128]{2,1,0:T(8,128)} %copy-done.1, f32[8,128,128]{2,1,0:T(8,128)} %copy-done.14, f32[8,128,128]{2,1,0:T(8,128)} %copy-done.15, f32[8,128,128]{2,1,0:T(8,128)} %copy-done.16, ...), custom_call_target="tpu_custom_call" | custom-call | flops 2415919104 | bytes 12582912 | tf_op jit(solution)/shard_map/apply_bonds/pallas_call | solution.py:242
  256.0 4.1 %all-to-all-start.4 = ((f32[8,128,128]{2,1,0:T(8,128)}), f32[8,128,128]{2,1,0:T(8,128)}, u32[]{:S(2)}, u32[]{:S(2)}) async-start(f32[8,128,128]{2,1,0:T(8,128)} %apply_bonds.11), calls=%async_computation.4 | async-start | bytes 1048576 | tf_op jit(solution)/shard_map/all_to_all | solution.py:303
  261.3 14.7 %psum.21 = f32[]{:T(128)} all-reduce(f32[]{:T(128)} %multiply_reduce_fusion), channel_id=1, replica_groups=mesh['grp'=2,'blk'=4,'mpo'=2,'rep'=2] {'blk'}, use_global_device_ids=true, to_apply=%region_1.2 | all-reduce | flops 1 | bytes 8 | tf_op jit(solution)/shard_map/psum | solution.py:363
  276.6 32.2 %psum.22 = f32[]{:T(128)} all-reduce(f32[]{:T(128)} %get-tuple-element.21), channel_id=1, replica_groups=mesh['grp'=2,'blk'=4,'mpo'=2,'rep'=2] {'blk','mpo','rep'}, use_global_device_ids=true, to_apply=%region_3.4 | all-reduce | flops 1 | bytes 8 | tf_op jit(solution)/shard_map/psum | solution.py:364
  311.3 30.1 %psum.23 = f32[]{:T(128)} all-reduce(f32[]{:T(128)} %multiply_reduce_fusion.1), channel_id=1, replica_groups=mesh['grp'=2,'blk'=4,'mpo'=2,'rep'=2] {'blk','mpo','rep'}, use_global_device_ids=true, to_apply=%region_5.6 | all-reduce | flops 1 | bytes 8 | tf_op jit(solution)/shard_map/psum | solution.py:368
  (137 shorter events, 70.8 us)
Async XLA Ops:
  0.6 28.3 %collective-permute-start = (s32[6,8]{1,0:T(8,128)}, s32[6,8]{1,0:T(8,128)S(1)}, u32[]{:S(2)}, u32[]{:S(2)}) collective-permute-start(s32[6,8]{1,0:T(8,128)} %param.10), channel_id=1, source_target_pairs={{0,2},{2,0},{1,3},{3,1},{4,6},{6,4},{5,7},{7,5},{8,10},{10,8},{9,1... | collective-permute-start | bytes 584 | tf_op jit(solution)/shard_map/ppermute | solution.py:273
  3.6 30.6 %collective-permute-start.1 = (s32[6,8]{1,0:T(8,128)}, s32[6,8]{1,0:T(8,128)S(1)}, u32[]{:S(2)}, u32[]{:S(2)}) collective-permute-start(s32[6,8]{1,0:T(8,128)} %param.10), channel_id=1, source_target_pairs={{0,1},{1,0},{2,3},{3,2},{4,5},{5,4},{6,7},{7,6},{8,9},{9,8},{10,11... | collective-permute-start | bytes 584 | tf_op jit(solution)/shard_map/ppermute | solution.py:273
  3.6 32.4 %collective-permute-start.6 = (f32[6,16,16]{2,1,0:T(8,128)}, f32[6,16,16]{2,1,0:T(8,128)S(1)}, u32[]{:S(2)}, u32[]{:S(2)}) collective-permute-start(f32[6,16,16]{2,1,0:T(8,128)} %param.8), channel_id=1, source_target_pairs={{0,2},{2,0},{1,3},{3,1},{4,6},{6,4},{5,7},{7,5},{8,10},{10,8},{9,1... | collective-permute-start | bytes 18440 | tf_op jit(solution)/shard_map/ppermute | solution.py:273
  3.8 52.0 %collective-permute-start.7 = (f32[6,16,16]{2,1,0:T(8,128)}, f32[6,16,16]{2,1,0:T(8,128)S(1)}, u32[]{:S(2)}, u32[]{:S(2)}) collective-permute-start(f32[6,16,16]{2,1,0:T(8,128)} %param.8), channel_id=1, source_target_pairs={{0,1},{1,0},{2,3},{3,2},{4,5},{5,4},{6,7},{7,6},{8,9},{9,8},{10,11... | collective-permute-start | bytes 18440 | tf_op jit(solution)/shard_map/ppermute | solution.py:273
  7.5 21.6 %all-to-all-start.1 = ((f32[4,2,8,16,128]{4,3,2,1,0:T(8,128)}), f32[4,2,8,16,128]{4,3,2,1,0:T(8,128)S(1)}, u32[]{:S(2)}, u32[]{:S(2)}) async-start(f32[4,2,8,16,128]{4,3,2,1,0:T(8,128)} %bitcast.87), calls=%async_computation.1 | async-start | bytes 1048576 | tf_op jit(solution)/shard_map/all_to_all | solution.py:334
  29.0 5.2 %collective-permute-start.2 = (s32[6,8]{1,0:T(8,128)S(1)}, s32[6,8]{1,0:T(8,128)S(1)}, u32[]{:S(2)}, u32[]{:S(2)}) collective-permute-start(s32[6,8]{1,0:T(8,128)S(1)} %collective-permute-done), channel_id=1, source_target_pairs={{0,1},{1,0},{2,3},{3,2},{4,5},{5,4},{6,7},{7,6},{8,9},{9,8},{10,11... | collective-permute-start | bytes 584 | tf_op jit(solution)/shard_map/ppermute | solution.py:273
  29.1 20.2 %all-to-all-start.2 = ((f32[4,2,8,16,128]{4,3,2,1,0:T(8,128)}), f32[4,2,8,16,128]{4,3,2,1,0:T(8,128)S(1)}, u32[]{:S(2)}, u32[]{:S(2)}) async-start(f32[4,2,8,16,128]{4,3,2,1,0:T(8,128)} %bitcast.93), calls=%async_computation.2 | async-start | bytes 1048576 | tf_op jit(solution)/shard_map/all_to_all | solution.py:334
  36.0 19.7 %collective-permute-start.8 = (f32[6,16,16]{2,1,0:T(8,128)S(1)}, f32[6,16,16]{2,1,0:T(8,128)S(1)}, u32[]{:S(2)}, u32[]{:S(2)}) collective-permute-start(f32[6,16,16]{2,1,0:T(8,128)S(1)} %collective-permute-done.6), channel_id=1, source_target_pairs={{0,1},{1,0},{2,3},{3,2},{4,5},{5,4},{6,7},{7,6},{8,9},{9,8},{10,11... | collective-permute-start | bytes 18440 | tf_op jit(solution)/shard_map/ppermute | solution.py:273
  49.3 31.7 %all-to-all-start = ((f32[4,2,8,16,128]{4,3,2,1,0:T(8,128)}), f32[4,2,8,16,128]{4,3,2,1,0:T(8,128)}, u32[]{:S(2)}, u32[]{:S(2)}) async-start(f32[4,2,8,16,128]{4,3,2,1,0:T(8,128)} %bitcast.92), calls=%async_computation | async-start | bytes 1048576 | tf_op jit(solution)/shard_map/all_to_all | solution.py:334
  53.7 28.9 %collective-permute-start.9 = (f32[4,2,8,16,128]{4,3,2,1,0:T(8,128)S(1)}, f32[4,2,8,16,128]{4,3,2,1,0:T(8,128)}, u32[]{:S(2)}, u32[]{:S(2)}) collective-permute-start(f32[4,2,8,16,128]{4,3,2,1,0:T(8,128)S(1)} %all-to-all-done.1.refs_0_), channel_id=1, source_target_pairs={{0,2},{2,0},{1,3},{3,1},{4,6},{6,4},{5,7},{7,5},{8,10},{10,8},{9,1... | collective-permute-start | bytes 1572872 | tf_op jit(solution)/shard_map/ppermute | solution.py:273
  55.2 27.3 %collective-permute-start.12 = (f32[4,2,8,16,128]{4,3,2,1,0:T(8,128)S(1)}, f32[4,2,8,16,128]{4,3,2,1,0:T(8,128)}, u32[]{:S(2)}, u32[]{:S(2)}) collective-permute-start(f32[4,2,8,16,128]{4,3,2,1,0:T(8,128)S(1)} %all-to-all-done.2.refs_0_), channel_id=1, source_target_pairs={{0,2},{2,0},{1,3},{3,1},{4,6},{6,4},{5,7},{7,5},{8,10},{10,8},{9,1... | collective-permute-start | bytes 1572872 | tf_op jit(solution)/shard_map/ppermute | solution.py:273
  80.5 14.6 %collective-permute-start.10 = (f32[4,2,8,16,128]{4,3,2,1,0:T(8,128)S(1)}, f32[4,2,8,16,128]{4,3,2,1,0:T(8,128)}, u32[]{:S(2)}, u32[]{:S(2)}) collective-permute-start(f32[4,2,8,16,128]{4,3,2,1,0:T(8,128)S(1)} %all-to-all-done.1.refs_0_), channel_id=1, source_target_pairs={{0,1},{1,0},{2,3},{3,2},{4,5},{5,4},{6,7},{7,6},{8,9},{9,8},{10,11... | collective-permute-start | bytes 1572872 | tf_op jit(solution)/shard_map/ppermute | solution.py:273
  80.5 22.0 %collective-permute-start.13 = (f32[4,2,8,16,128]{4,3,2,1,0:T(8,128)S(1)}, f32[4,2,8,16,128]{4,3,2,1,0:T(8,128)}, u32[]{:S(2)}, u32[]{:S(2)}) collective-permute-start(f32[4,2,8,16,128]{4,3,2,1,0:T(8,128)S(1)} %all-to-all-done.2.refs_0_), channel_id=1, source_target_pairs={{0,1},{1,0},{2,3},{3,2},{4,5},{5,4},{6,7},{7,6},{8,9},{9,8},{10,11... | collective-permute-start | bytes 1572872 | tf_op jit(solution)/shard_map/ppermute | solution.py:273
  81.0 14.1 %collective-permute-start.3 = (f32[4,2,8,16,128]{4,3,2,1,0:T(8,128)}, f32[4,2,8,16,128]{4,3,2,1,0:T(8,128)S(1)}, u32[]{:S(2)}, u32[]{:S(2)}) collective-permute-start(f32[4,2,8,16,128]{4,3,2,1,0:T(8,128)} %all-to-all-done.refs_0_), channel_id=1, source_target_pairs={{0,2},{2,0},{1,3},{3,1},{4,6},{6,4},{5,7},{7,5},{8,10},{10,8},{9,1... | collective-permute-start | bytes 1572872 | tf_op jit(solution)/shard_map/ppermute | solution.py:273
  82.5 14.0 %collective-permute-start.11 = (f32[4,2,8,16,128]{4,3,2,1,0:T(8,128)}, f32[4,2,8,16,128]{4,3,2,1,0:T(8,128)S(1)}, u32[]{:S(2)}, u32[]{:S(2)}) collective-permute-start(f32[4,2,8,16,128]{4,3,2,1,0:T(8,128)} %collective-permute-done.9.refs_1_), channel_id=1, source_target_pairs={{0,1},{1,0},{2,3},{3,2},{4,5},{5,4},{6,7},{7,6},{8,9},{9,8},{10,11... | collective-permute-start | bytes 1572872 | tf_op jit(solution)/shard_map/ppermute | solution.py:273
  82.5 20.0 %collective-permute-start.14 = (f32[4,2,8,16,128]{4,3,2,1,0:T(8,128)}, f32[4,2,8,16,128]{4,3,2,1,0:T(8,128)S(1)}, u32[]{:S(2)}, u32[]{:S(2)}) collective-permute-start(f32[4,2,8,16,128]{4,3,2,1,0:T(8,128)} %collective-permute-done.12.refs_1_), channel_id=1, source_target_pairs={{0,1},{1,0},{2,3},{3,2},{4,5},{5,4},{6,7},{7,6},{8,9},{9,8},{10,11... | collective-permute-start | bytes 1572872 | tf_op jit(solution)/shard_map/ppermute | solution.py:273
  95.1 49.2 %collective-permute-start.4 = (f32[4,2,8,16,128]{4,3,2,1,0:T(8,128)}, f32[4,2,8,16,128]{4,3,2,1,0:T(8,128)S(1)}, u32[]{:S(2)}, u32[]{:S(2)}) collective-permute-start(f32[4,2,8,16,128]{4,3,2,1,0:T(8,128)} %all-to-all-done.refs_0_), channel_id=1, source_target_pairs={{0,1},{1,0},{2,3},{3,2},{4,5},{5,4},{6,7},{7,6},{8,9},{9,8},{10,11... | collective-permute-start | bytes 1572872 | tf_op jit(solution)/shard_map/ppermute | solution.py:273
  95.1 49.2 %collective-permute-start.5 = (f32[4,2,8,16,128]{4,3,2,1,0:T(8,128)S(1)}, f32[4,2,8,16,128]{4,3,2,1,0:T(8,128)S(1)}, u32[]{:S(2)}, u32[]{:S(2)}) collective-permute-start(f32[4,2,8,16,128]{4,3,2,1,0:T(8,128)S(1)} %collective-permute-done.3.refs_1_), channel_id=1, source_target_pairs={{0,1},{1,0},{2,3},{3,2},{4,5},{5,4},{6,7},{7,6},{8,9},{9,8},{10,11... | collective-permute-start | bytes 1572872 | tf_op jit(solution)/shard_map/ppermute | solution.py:273
  168.6 19.5 %all-to-all-start.3 = ((f32[8,128,128]{2,1,0:T(8,128)}), f32[8,128,128]{2,1,0:T(8,128)S(1)}, u32[]{:S(2)}, u32[]{:S(2)}) async-start(f32[8,128,128]{2,1,0:T(8,128)} %apply_bonds.8), calls=%async_computation.3 | async-start | bytes 1048576 | tf_op jit(solution)/shard_map/all_to_all | solution.py:303
  189.6 12.9 %collective-permute-start.15 = (f32[8,128,128]{2,1,0:T(8,128)S(1)}, f32[8,128,128]{2,1,0:T(8,128)S(1)}, u32[]{:S(2)}, u32[]{:S(2)}) collective-permute-start(f32[8,128,128]{2,1,0:T(8,128)S(1)} %get-tuple-element.22.refs_0_), channel_id=1, source_target_pairs={{0,2},{2,0},{1,3},{3,1},{4,6},{6,4},{5,7},{7,5},{8,10},{10,8},{9,1... | collective-permute-start | bytes 1572872 | tf_op jit(solution)/shard_map/ppermute | solution.py:273
  191.1 12.2 %collective-permute-start.16 = (f32[8,128,128]{2,1,0:T(8,128)S(1)}, f32[8,128,128]{2,1,0:T(8,128)S(1)}, u32[]{:S(2)}, u32[]{:S(2)}) collective-permute-start(f32[8,128,128]{2,1,0:T(8,128)S(1)} %get-tuple-element.22.refs_0_), channel_id=1, source_target_pairs={{0,1},{1,0},{2,3},{3,2},{4,5},{5,4},{6,7},{7,6},{8,9},{9,8},{10,11... | collective-permute-start | bytes 1572872 | tf_op jit(solution)/shard_map/ppermute | solution.py:273
  202.5 1.9 collective-permute-start.17
  256.0 86.1 %all-to-all-start.4 = ((f32[8,128,128]{2,1,0:T(8,128)}), f32[8,128,128]{2,1,0:T(8,128)}, u32[]{:S(2)}, u32[]{:S(2)}) async-start(f32[8,128,128]{2,1,0:T(8,128)} %apply_bonds.11), calls=%async_computation.4 | async-start | bytes 1048576 | tf_op jit(solution)/shard_map/all_to_all | solution.py:303
  261.3 82.5 %copy-start.2 = (f32[8,128,128]{2,1,0:T(8,128)S(1)}, f32[8,128,128]{2,1,0:T(8,128)}, u32[]{:S(2)}) copy-start(f32[8,128,128]{2,1,0:T(8,128)} %copy-done.1) | copy-start | bytes 1572868
  (16 other events, 151.8 us)

commit v2 on v0

--- a/solution.py
+++ b/solution.py
@@ -1,10 +1,20 @@
+import functools
+
 import jax
 import jax.numpy as jnp
 from jax import lax
+from jax.experimental import pallas as pl
+from jax.experimental.pallas import tpu as pltpu
 from jax.sharding import PartitionSpec as P
 
-
-def bond_apply(vector_full, environment, bond_terms, term_slot, slot_block, diagonal):
+LANES = 128
+SUB = 8
+PHYS = 16
+GROUPS = 2
+VMEM_LIMIT = 56 * 1024 * 1024
+
+
+def plain_apply(vector_full, environment, bond_terms, term_slot, slot_block, diagonal):
     block_count, block_rows, block_width = vector_full.shape
     phys_size = bond_terms.shape[-1]
     right_rows = block_width // phys_size
@@ -45,14 +55,14 @@
     return (result + diagonal * own_part, own_part)
 
 
-def per_device(wavefunction, environment, bond_terms, diagonal, term_slot, slot_block):
+def plain_device(wavefunction, environment, bond_terms, diagonal, term_slot, slot_block):
     arranged = lax.all_to_all(environment, "blk", split_axis=1, concat_axis=2, tiled=True)
     entries = float(
         wavefunction.shape[0] * lax.axis_size("blk") * wavefunction.shape[1] * wavefunction.shape[2]
     )
     square_sum = lax.psum(jnp.sum(wavefunction * wavefunction), "blk")
     first_vector = wavefunction * lax.rsqrt(square_sum / entries + 1e-06)
-    first_image, first_part = bond_apply(
+    first_image, first_part = plain_apply(
         first_vector, arranged, bond_terms, term_slot, slot_block, diagonal
     )
     rayleigh = lax.psum(jnp.sum(first_part * first_image), ("blk", "mpo", "rep")) / entries
@@ -60,15 +70,502 @@
     resid_sum = lax.psum(jnp.sum(residual * residual), ("blk", "mpo", "rep"))
     second_vector = residual * lax.rsqrt(resid_sum / entries + 1e-06)
     second_full = lax.all_gather(second_vector, ("mpo", "rep"), axis=2, tiled=True)
-    second_image, unused = bond_apply(
+    second_image, unused = plain_apply(
         second_full, arranged, bond_terms, term_slot, slot_block, diagonal
     )
     return (first_image, second_vector, second_image)
 
 
+def split_two(x):
+    high = x.astype(jnp.bfloat16)
+    low = (x - high.astype(jnp.float32)).astype(jnp.bfloat16)
+    return high, low
+
+
+def lane_is_first(rows):
+    return lax.broadcasted_iota(jnp.int32, (rows, LANES), 1) < LANES // 2
+
+
+def whole(*shape):
+    return pl.BlockSpec(shape, lambda i, *_: (0,) * len(shape))
+
+
+def pack_tile(x):
+    return jnp.concatenate([x[:, :LANES], x[:, LANES:]], axis=0).T
+
+
+def unpack_tile(x):
+    upright = x.T
+    return jnp.concatenate([upright[: LANES // 2], upright[LANES // 2 :]], axis=1)
+
+
+def store_vector(parts, j, rows_of, put):
+    first = lane_is_first(SUB)
+    for pair in range(PHYS // 2):
+        for part, row in zip(parts, rows_of):
+            even = part[j, pl.ds(2 * pair, SUB, stride=PHYS), :]
+            odd = part[j, pl.ds(2 * pair + 1, SUB, stride=PHYS), :]
+            upper = jnp.where(first, even, pltpu.roll(odd, LANES // 2, 1))
+            lower = jnp.where(first, pltpu.roll(even, LANES // 2, 1), odd)
+            high, low = split_two(jnp.concatenate([upper, lower], axis=0))
+            put(row, pair, high, low)
+
+
+def pack_kernel(info_ref, wave_ref, own_wave_ref, diag_ref, vec_ref, own_ref, diag_out, tiles):
+    half = LANES // 2
+    for j in range(wave_ref.shape[0]):
+        own_ref[j] = pack_tile(own_wave_ref[j])
+        diag_out[j] = pack_tile(diag_ref[j])
+        for q in range(4):
+            tiles[q, j] = pack_tile(wave_ref[j, :, 2 * LANES * q : 2 * LANES * (q + 1)])
+
+        def put(row, pair, high, low):
+            columns = slice(pair * LANES, (pair + 1) * LANES)
+            vec_ref[j, row : row + 16, columns] = high
+            vec_ref[j, row + half : row + half + 16, columns] = low
+
+        store_vector([tiles.at[q] for q in range(4)], j, [16 * q for q in range(4)], put)
+
+
+def pack(info, wavefunction, diagonal):
+    blocks, rows, width = wavefunction.shape
+    step = 2
+    tile = pl.BlockSpec((step, LANES, LANES), lambda i, *_: (i, 0, 0))
+    return pl.pallas_call(
+        pack_kernel,
+        grid_spec=pltpu.PrefetchScalarGridSpec(
+            num_scalar_prefetch=1,
+            grid=(blocks // step,),
+            in_specs=[
+                pl.BlockSpec((step, rows, width), lambda i, *_: (i, 0, 0)),
+                pl.BlockSpec((step, rows, width // 4), lambda i, info: (i, 0, info[0])),
+                pl.BlockSpec((step, rows, width // 4), lambda i, *_: (i, 0, 0)),
+            ],
+            out_specs=[pl.BlockSpec((step, LANES, width), lambda i, *_: (i, 0, 0)), tile, tile],
+            scratch_shapes=[pltpu.VMEM((4, step, LANES, LANES), jnp.float32)],
+        ),
+        out_shape=[
+            jax.ShapeDtypeStruct((blocks, LANES, width), jnp.bfloat16),
+            jax.ShapeDtypeStruct((blocks, LANES, LANES), jnp.float32),
+            jax.ShapeDtypeStruct((blocks, LANES, LANES), jnp.float32),
+        ],
+        compiler_params=pltpu.CompilerParams(vmem_limit_bytes=VMEM_LIMIT),
+        name="pack",
+    )(info, wavefunction, wavefunction, diagonal)
+
+
+def mixing_kernel(*refs):
+    sources, out_ref = refs[:-1], refs[-1]
+    spread = (
+        lax.broadcasted_iota(jnp.int32, (PHYS, LANES), 1) // SUB
+        == lax.broadcasted_iota(jnp.int32, (PHYS, LANES), 0)
+    ).astype(jnp.bfloat16)
+    row = lax.broadcasted_iota(jnp.int32, (LANES, LANES), 0) // PHYS
+    column = lax.broadcasted_iota(jnp.int32, (LANES, LANES), 1) % SUB
+    same = row == column
+    per = sources[0].shape[0] // GROUPS
+    at = 0
+    for group in range(GROUPS):
+        for source in sources:
+            for k in range(per):
+                for place, term in enumerate(split_two(source[group * per + k].T)):
+                    wide = jnp.dot(term, spread, preferred_element_type=jnp.float32)
+                    tall = jnp.concatenate([wide] * SUB, axis=0)
+                    out_ref[at, :, place * LANES : (place + 1) * LANES] = jnp.where(
+                        same, tall, 0.0
+                    ).astype(jnp.bfloat16)
+                at += 1
+
+
+def mixing_operand(sources):
+    count = sources[0].shape[0] * len(sources)
+    return pl.pallas_call(
+        mixing_kernel,
+        out_shape=jax.ShapeDtypeStruct((count, LANES, 2 * LANES), jnp.bfloat16),
+        compiler_params=pltpu.CompilerParams(vmem_limit_bytes=VMEM_LIMIT),
+        name="mixing",
+    )(*sources)
+
+
+def prepare_kernel(info_ref, *refs):
+    sources, (left_high, left_low, right_out, blocks_ref) = refs[:-4], refs[-4:]
+    zs = 4
+    per, blocks, rows, lanes = sources[0].shape
+    half = lanes // 2
+    first = lane_is_first(half)
+    lane = lax.broadcasted_iota(jnp.int32, (half, lanes), 1)
+    start = info_ref[0] * 16
+    count = lanes // 16
+    pairs = [(s, k) for s in range(len(sources) // zs) for k in range(per)]
+    for j in range(blocks):
+        for base in range(0, len(pairs), count):
+            group = pairs[base : base + count]
+            columns = jnp.zeros((half, lanes), jnp.float32)
+            for at, (s, k) in enumerate(group):
+                for z in range(zs):
+                    row = pl.multiple_of((info_ref[4] ^ z) * rows, rows)
+                    blocks_ref[base + at, j, pl.ds(row, rows), :] = sources[s * zs + z][k, j]
+                block = blocks_ref[base + at, j]
+                high, low = split_two(jnp.where(first, block, pltpu.roll(block, half, 1)))
+                left_high[base + at, j] = high
+                left_low[base + at, j] = low
+                shift = lax.rem(16 * at + lanes + half - start, lanes)
+                columns = jnp.where(lane // 16 == at, pltpu.roll(block, shift, 1), columns)
+            upright = columns.T[: 16 * len(group)]
+            high, low = split_two(upright)
+            where = pl.ds(16 * base, 16 * len(group))
+            right_out[j, where, 0:lanes] = jnp.concatenate([high, high], axis=1)
+            right_out[j, where, lanes : 2 * lanes] = jnp.concatenate([low, low], axis=1)
+
+
+def prepare(info, sources):
+    per, blocks, rows, lanes = sources[0].shape
+    total = per * len(sources) // 4
+    half = lanes // 2
+    step = 2
+    return pl.pallas_call(
+        prepare_kernel,
+        grid_spec=pltpu.PrefetchScalarGridSpec(
+            num_scalar_prefetch=1,
+            grid=(blocks // step,),
+            in_specs=[
+                pl.BlockSpec((per, step, rows, lanes), lambda i, *_: (0, i, 0, 0))
+                for _ in sources
+            ],
+            out_specs=[
+                pl.BlockSpec((total, step, half, lanes), lambda i, *_: (0, i, 0, 0)),
+                pl.BlockSpec((total, step, half, lanes), lambda i, *_: (0, i, 0, 0)),
+                pl.BlockSpec((step, total * 16, 2 * lanes), lambda i, *_: (i, 0, 0)),
+            ],
+            scratch_shapes=[pltpu.VMEM((total, step, half, lanes), jnp.float32)],
+        ),
+        out_shape=[
+            jax.ShapeDtypeStruct((total, blocks, half, lanes), jnp.bfloat16),
+            jax.ShapeDtypeStruct((total, blocks, half, lanes), jnp.bfloat16),
+            jax.ShapeDtypeStruct((blocks, total * 16, 2 * lanes), jnp.bfloat16),
+        ],
+        compiler_params=pltpu.CompilerParams(vmem_limit_bytes=VMEM_LIMIT),
+        name="prepare",
+    )(info, *sources)
+
+
+def apply_kernel(plan, info_ref, *refs):
+    groups, parts_given, before_given, pieces = plan
+    refs = list(refs)
+    take = lambda n: [refs.pop(0) for _ in range(n)]
+    slots = take(4)
+    vector = take(4 if parts_given else 1)
+    operands = [take(4) for _ in groups]
+    before = take(1) if before_given else None
+    outs = take(4 if pieces else 1)
+    total_ref, vec, mid = refs
+    step = vector[0].shape[0]
+    lanes, half = LANES, LANES // 2
+    first = lane_is_first(SUB)
+    first_half = lane_is_first(half)
+    keep_first = jnp.where(first_half, 1.0, 0.0).astype(jnp.bfloat16)
+    keep_second = jnp.where(first_half, 0.0, 1.0).astype(jnp.bfloat16)
+    me = info_ref[4]
+
+    @pl.when(pl.program_id(0) == 0)
+    def _():
+        total_ref[...] = before[0][...] if before_given else jnp.zeros_like(total_ref)
+
+    for j in range(step):
+        if parts_given:
+
+            def put(row, pair, high, low):
+                columns = slice(pair * lanes, (pair + 1) * lanes)
+                vec[j, pl.ds(row, 16), columns] = high
+                vec[j, pl.ds(row + half, 16), columns] = low
+
+            rows_of = [pl.multiple_of(info_ref[g] * 16, 16) for g in range(4)]
+            store_vector(vector, j, rows_of, put)
+            source = vec[j]
+        else:
+            source = vector[0][j]
+        source = jnp.concatenate([source, source], axis=0)
+        at = 0
+        for left_high, left_low, right, mix in operands:
+            count = right.shape[1]
+            mid[j, at : at + count, :] = jnp.dot(
+                right[j], source, preferred_element_type=jnp.float32
+            )
+            at += count
+
+    def one_bond(refs_of, w, slot_of, base):
+        left_high, left_low, right, mix = refs_of
+        highs, lows = [], []
+        for j in range(step):
+            row = pl.multiple_of((base + w) * 16, 16)
+            tiles = []
+            for pair in range(PHYS // 2):
+                columns = slice(pair * lanes, (pair + 1) * lanes)
+                upper = mid[j, pl.ds(row, SUB), columns]
+                lower = mid[j, pl.ds(row + SUB, SUB), columns]
+                tiles.append(jnp.where(first, upper, pltpu.roll(lower, half, 1)))
+                tiles.append(jnp.where(first, pltpu.roll(upper, half, 1), lower))
+            t_high, t_low = split_two(jnp.concatenate(tiles, axis=0))
+            lh, ll = left_high[w, j], left_low[w, j]
+            wide_high = jnp.concatenate([lh * keep_first, lh * keep_second], axis=0)
+            wide_low = jnp.concatenate([ll * keep_first, ll * keep_second], axis=0)
+            z = jnp.dot(
+                jnp.concatenate([t_high, t_low], axis=1),
+                jnp.concatenate([wide_high, wide_high], axis=0),
+                preferred_element_type=jnp.float32,
+            ) + jnp.dot(t_high, wide_low, preferred_element_type=jnp.float32)
+            z_high, z_low = split_two(z)
+            highs.append(z_high)
+            lows.append(z_low)
+        z_high = jnp.concatenate(highs, axis=1)
+        z_low = jnp.concatenate(lows, axis=1)
+        mix_high = mix[w, :, 0:lanes]
+        mix_low = mix[w, :, lanes:]
+        mixed = jnp.dot(
+            jnp.concatenate([mix_high, mix_high], axis=1),
+            jnp.concatenate([z_high, z_low], axis=0),
+            preferred_element_type=jnp.float32,
+        ) + jnp.dot(mix_low, z_high, preferred_element_type=jnp.float32)
+        for j in range(step):
+            slot = slot_of(pl.program_id(0) * step + j)
+            slot = ((slot >> 1) ^ me) * 2 + (slot & 1)
+            total_ref[slot] += mixed[:, j * lanes : (j + 1) * lanes]
+
+    base = 0
+    for group, refs_of in zip(groups, operands):
+        count = refs_of[0].shape[0]
+        per = count // 4
+        for s in range(4):
+            table = slots[s]
+
+            def some(k, carry):
+                one_bond(
+                    refs_of, s * per + k, lambda j: table[group * per + k, j], base
+                )
+                return carry
+
+            for k in range(per):
+                some(k, 0)
+        base += count
+
+    @pl.when(pl.program_id(0) == pl.num_programs(0) - 1)
+    def _():
+        if pieces:
+            for k in range(4):
+                outs[k][...] = total_ref[2 * k : 2 * k + 2]
+        else:
+            outs[0][...] = total_ref[...]
+
+
+def apply_bonds(info, slots, vector, groups, operands, mixing, before, pieces):
+    blocks, half, lanes = operands[0][0].shape[1:]
+    counts = [x[0].shape[0] for x in operands]
+    per_group = mixing.shape[0] // GROUPS
+    step = 2
+    flops = 2 * blocks * sum(counts) * SUB * lanes * (3 * lanes * 16 * 3)
+    in_specs = [pl.BlockSpec((step,) + x.shape[1:], lambda i, *_: (i, 0, 0)) for x in vector]
+    arguments = list(vector)
+    for group, (left_high, left_low, right), count in zip(groups, operands, counts):
+        in_specs += [
+            pl.BlockSpec((count, step, half, lanes), lambda i, *_: (0, i, 0, 0)),
+            pl.BlockSpec((count, step, half, lanes), lambda i, *_: (0, i, 0, 0)),
+            pl.BlockSpec((step,) + right.shape[1:], lambda i, *_: (i, 0, 0)),
+            pl.BlockSpec((per_group,) + mixing.shape[1:], lambda i, *_, g=group: (g, 0, 0)),
+        ]
+        arguments += [left_high, left_low, right, mixing]
+    if before is not None:
+        in_specs.append(whole(*before.shape))
+        arguments.append(before)
+    shapes = [(2, lanes, lanes)] * 4 if pieces else [(8, lanes, lanes)]
+    plan = (tuple(groups), len(vector) == 4, before is not None, pieces)
+    return pl.pallas_call(
+        functools.partial(apply_kernel, plan),
+        grid_spec=pltpu.PrefetchScalarGridSpec(
+            num_scalar_prefetch=5,
+            grid=(blocks // step,),
+            in_specs=in_specs,
+            out_specs=[whole(*shape) for shape in shapes],
+            scratch_shapes=[
+                pltpu.VMEM((8, lanes, lanes), jnp.float32),
+                pltpu.VMEM((step, lanes, PHYS * half), jnp.bfloat16),
+                pltpu.VMEM((step, sum(counts) * 16, PHYS * half), jnp.float32),
+            ],
+        ),
+        out_shape=[jax.ShapeDtypeStruct(shape, jnp.float32) for shape in shapes],
+        compiler_params=pltpu.CompilerParams(vmem_limit_bytes=VMEM_LIMIT),
+        cost_estimate=pl.CostEstimate(
+            flops=flops, bytes_accessed=12 * 1024 * 1024, transcendentals=0
+        ),
+        name="apply_bonds",
+    )(info, *slots, *arguments)
+
+
+def folded(x):
+    return jnp.sum(x.reshape(-1, SUB, LANES), axis=0)
+
+
+def add_arrived(info_ref, owner_ref, arrived, total):
+    for k in range(4):
+        for i in range(2):
+            total[owner_ref[info_ref[4] ^ k, i]] += arrived[k][i]
+
+
+def image_kernel(info_ref, owner_ref, a0, a1, a2, a3, diag_ref, own_ref, image_ref, sums_ref):
+    image_ref[...] = diag_ref[...] * own_ref[...]
+    add_arrived(info_ref, owner_ref, (a0, a1, a2, a3), image_ref)
+    own = own_ref[...]
+    sums_ref[0:SUB] = folded(own * image_ref[...])
+    sums_ref[SUB:] = folded(own * own)
+
+
+def owner_image(info, owners, arrived, diagonal, own):
+    return pl.pallas_call(
+        image_kernel,
+        grid_spec=pltpu.PrefetchScalarGridSpec(
+            num_scalar_prefetch=2,
+            grid=(1,),
+            in_specs=[whole(*x.shape) for x in (*arrived, diagonal, own)],
+            out_specs=[whole(*own.shape), whole(2 * SUB, LANES)],
+        ),
+        out_shape=[
+            jax.ShapeDtypeStruct(own.shape, jnp.float32),
+            jax.ShapeDtypeStruct((2 * SUB, LANES), jnp.float32),
+        ],
+        compiler_params=pltpu.CompilerParams(vmem_limit_bytes=VMEM_LIMIT),
+        name="owner_image",
+    )(info, owners, *arrived, diagonal, own)
+
+
+def scalars_of(sums, entries):
+    cross = jnp.sum(sums[0:SUB], keepdims=True) / entries
+    square = jnp.sum(sums[SUB:], keepdims=True) / entries
+    scale = lax.rsqrt(square + 1e-06)
+    return scale, cross * scale * scale
+
+
+def residual_kernel(entries, sums_ref, image_ref, own_ref, first_ref, resid_ref):
+    scale, rayleigh = scalars_of(sums_ref[...], entries)
+    total = jnp.zeros((SUB, LANES), jnp.float32)
+    for k in range(image_ref.shape[0]):
+        image = image_ref[k]
+        residual = scale * (image - rayleigh * own_ref[k])
+        total += folded(residual * residual)
+        first_ref[k] = unpack_tile(scale * image)
+    resid_ref[...] = total
+
+
+def first_outputs(sums, image, own, entries):
+    blocks = image.shape[0]
+    return pl.pallas_call(
+        functools.partial(residual_kernel, entries),
+        out_shape=[
+            jax.ShapeDtypeStruct((blocks, LANES // 2, 2 * LANES), jnp.float32),
+            jax.ShapeDtypeStruct((SUB, LANES), jnp.float32),
+        ],
+        compiler_params=pltpu.CompilerParams(vmem_limit_bytes=VMEM_LIMIT),
+        name="first_outputs",
+    )(sums, image, own)
+
+
+def final_kernel(
+    entries, info_ref, owner_ref, a0, a1, a2, a3, diag_ref, own_ref, image_ref, sums_ref, resid_ref,
+    vector_ref, second_ref, total,
+):
+    scale, rayleigh = scalars_of(sums_ref[...], entries)
+    mean = jnp.sum(resid_ref[...], keepdims=True) / entries
+    scale = scale * lax.rsqrt(mean + 1e-06)
+    total[...] = (diag_ref[...] - rayleigh) * image_ref[...]
+    add_arrived(info_ref, owner_ref, (a0, a1, a2, a3), total)
+    for k in range(image_ref.shape[0]):
+        vector_ref[k] = unpack_tile(scale * (image_ref[k] - rayleigh * own_ref[k]))
+        second_ref[k] = unpack_tile(scale * total[k])
+
+
+def second_outputs(info, owners, arrived, diagonal, own, image, sums, resid, entries):
+    shape = (own.shape[0], LANES // 2, 2 * LANES)
+    arguments = (*arrived, diagonal, own, image, sums, resid)
+    return pl.pallas_call(
+        functools.partial(final_kernel, entries),
+        grid_spec=pltpu.PrefetchScalarGridSpec(
+            num_scalar_prefetch=2,
+            grid=(1,),
+            in_specs=[whole(*x.shape) for x in arguments],
+            out_specs=[whole(*shape), whole(*shape)],
+            scratch_shapes=[pltpu.VMEM(own.shape, jnp.float32)],
+        ),
+        out_shape=[jax.ShapeDtypeStruct(shape, jnp.float32)] * 2,
+        compiler_params=pltpu.CompilerParams(vmem_limit_bytes=VMEM_LIMIT),
+        name="second_outputs",
+    )(info, owners, *arguments)
+
+
+def partner(x, axis, k):
+    size = lax.axis_size(axis)
+    return lax.ppermute(x, axis, [(i, i ^ k) for i in range(size)])
+
+
+def gathered(x):
+    across = partner(x, "mpo", 1)
+    return [x, across, partner(x, "rep", 1), partner(across, "rep", 1)]
+
+
+def summed(x, axes):
+    return x + partner(x, axes, 1) + partner(x, axes, 2) + partner(x, axes, 3)
+
+
+def exchanged(pieces):
+    return [pieces[0]] + [partner(pieces[k], "blk", k) for k in range(1, 4)]
+
+
+def per_device(wavefunction, environment, bond_terms, diagonal, term_slot, slot_block):
+    blocks, rows, width = wavefunction.shape
+    zs = lax.axis_size("blk")
+    mpo, rep, blk = lax.axis_index("mpo"), lax.axis_index("rep"), lax.axis_index("blk")
+    place = 2 * mpo + rep
+    info = jnp.stack([place, place ^ 2, place ^ 1, place ^ 3, blk]).astype(jnp.int32)
+    bonds = environment.shape[0]
+    per = bonds // GROUPS
+    entries = float(blocks * zs * rows * width)
+
+    by_owner = environment.reshape(bonds, zs, blocks, rows // zs, 2 * rows)
+    operands = []
+    for group in range(GROUPS):
+        mine = by_owner[group * per : (group + 1) * per]
+        pieces = exchanged(
+            [lax.dynamic_index_in_dim(mine, blk ^ k, 1, keepdims=False) for k in range(4)]
+        )
+        by_source = list(zip(*[gathered(piece) for piece in pieces]))
+        operands.append(prepare(info, [piece for source in by_source for piece in source]))
+
+    mixing = mixing_operand(gathered(bond_terms))
+    slots = gathered(term_slot)
+    vector, own, diagonal_packed = pack(info, wavefunction, diagonal)
+
+    total = None
+    for group in range(GROUPS):
+        last = group == GROUPS - 1
+        out = apply_bonds(
+            info, slots, [vector], [group], [operands[group]], mixing, total, last
+        )
+        total = None if last else out[0]
+    image, sums = owner_image(info, slot_block, exchanged(out), diagonal_packed, own)
+
+    out = apply_bonds(
+        info, slots, gathered(image), list(range(GROUPS)), operands, mixing, None, True
+    )
+    sums = summed(summed(sums, ("mpo", "rep")), "blk")
+    first_image, resid = first_outputs(sums, image, own, entries)
+    resid = summed(summed(resid, ("mpo", "rep")), "blk")
+    second_vector, second_image = second_outputs(
+        info, slot_block, exchanged(out), diagonal_packed, own, image, sums, resid, entries
+    )
+    return (first_image, second_vector, second_image)
+
+
 def solution(mesh):
+    packed = mesh.shape["mpo"] == 2 and mesh.shape["rep"] == 2 and mesh.shape["blk"] == 4
     return jax.shard_map(
-        per_device,
+        per_device if packed else plain_device,
         mesh=mesh,
         in_specs=(
             P(("grp", "blk"), None, None),

time: 648 us -> 227 us (0.35)
  matrix products: 241 us -> 0 us
  local copies, waits for them, and re-layouts: 126 us -> 8.79 us
  Pallas kernels: 0 us -> 92.8 us
  blocking collectives: 91.2 us -> 0 us
  waiting for transfers between devices: 143 us -> 63.8 us
  starting transfers between devices: 15.5 us -> 56.1 us
  between operations: 16 us -> 1.15 us
    dot_general x10 -> x0, matrix products: 241 us -> none  [the longest x2 89.5 us: bond_apply(): jnp.einsum('wjsbc,wjcd->wjsbd', left_done, right_env, precision=lax.Preci...]
    reduce_scatter x2 -> x0, waiting for transfers between devices: 96.2 us -> none  [bond_apply(): lax.psum_scatter(slot_buffer, ('mpo', 'rep'), scatter_dimension=2, tiled=...]
    pallas_call x0 -> x10, Pallas kernels: none -> 92.8 us  [the longest x3 59.9 us: apply_bonds(): pl.pallas_call(functools.partial(apply_kernel, plan), grid_spec=pltpu.Pre...]
    psum x3 -> x0, blocking collectives: 91.2 us -> none  [the longest x1 31 us: per_device(): square_sum = lax.psum(jnp.sum(wavefunction * wavefunction), 'blk')]
    reshape x4 -> x0, local copies, waits for them, and re-layouts: 63.8 us -> none  [the longest x2 41.7 us: bond_apply(): right_done.reshape(environment.shape[0], block_count, phys_size, block_ro...]
    ppermute x0 -> x57, waiting for transfers between devices: none -> 63.8 us  [partner(): return lax.ppermute(x, axis, [(i, i ^ k) for i in range(size)])]
    ppermute x0 -> x57, starting transfers between devices: none -> 56.1 us  [partner(): return lax.ppermute(x, axis, [(i, i ^ k) for i in range(size)])]
    dot_general x2 -> x0, local copies, waits for them, and re-layouts: 34.1 us -> none  [bond_apply(): jnp.einsum('wsj,wjx->sx', slot_table, bond_term, precision=lax.Precision....]
  transfers between devices with their start and end apart: 6 -> 57, of which waited for: 5 -> 17; matrix products, arithmetic and copies ran while one was open for 1% -> 2% of each run, Pallas kernels for 0% -> 28%
where the time goes in v2:
time: 227 us; the launch traced here: 225 us
  Pallas kernels  92.8 us (41%)
  waiting for transfers between devices  63.8 us (28%)
  starting transfers between devices  56.1 us (25%)
  local copies, waits for them, and re-layouts  8.79 us (4%)
  other arithmetic  2.61 us (1%)
    ppermute x57, waiting for transfers between devices, partner(): return lax.ppermute(x, axis, [(i, i ^ k) for i in range(size)])  63.8 us
    pallas_call x3, Pallas kernels, apply_bonds(): pl.pallas_call(functools.partial(apply_kernel, plan), grid_spec=pltpu.Pre...  59.9 us
    ppermute x57, starting transfers between devices, partner(): return lax.ppermute(x, axis, [(i, i ^ k) for i in range(size)])  56.1 us
    pallas_call x2, Pallas kernels, prepare(): pl.pallas_call(prepare_kernel, grid_spec=pltpu.PrefetchScalarGridSpec(num...  15.5 us
    unnamed x87, local copies, waits for them, and re-layouts  6.6 us
    pallas_call x1, Pallas kernels, pack(): pl.pallas_call(pack_kernel, grid_spec=pltpu.PrefetchScalarGridSpec(num_sc...  5.76 us
  transfers between devices with their start and end apart: 57, of which 17 were waited for; matrix products, arithmetic and copies ran while one was open for 2% of the time, Pallas kernels for 28%

profile of v2, /device:TPU:0, one launch (start us, length us, event | category | flops | bytes accessed | tf_op | source)
XLA Modules:
  0.0 225.2 jit_solution(13623796936834922057)
XLA Ops:
  1.1 2.6 %collective-permute-start = (s32[6,8]{1,0:T(8,128)}, s32[6,8]{1,0:T(8,128)S(1)}, u32[]{:S(2)}, u32[]{:S(2)}) collective-permute-start(s32[6,8]{1,0:T(8,128)} %refs_0_.7), channel_id=1, source_target_pairs={{0,2},{2,0},{1,3},{3,1},{4,6},{6,4},{5,7},{7,5},{8,10},{10,8},{9,1... | collective-permute-start | bytes 584 | tf_op jit(solution)/shard_map/ppermute | solution.py:504
  5.5 4.0 %collective-permute-start.5 = (f32[3,8,16,128]{3,2,1,0:T(8,128)S(1)}, f32[3,8,16,128]{3,2,1,0:T(8,128)S(1)}, u32[]{:S(2)}, u32[]{:S(2)}) collective-permute-start(f32[3,8,16,128]{3,2,1,0:T(8,128)S(1)} %get-tuple-element.55), channel_id=1, source_target_pairs={{0,12},{4,8},{8,4},{12,0},{1,13},{5,9},{9,5},{13,1},{2,14},{6,10},... | collective-permute-start | bytes 589832 | tf_op jit(solution)/shard_map/ppermute | solution.py:504
  15.5 8.1 %collective-permute-start.21 = (f32[3,8,16,128]{3,2,1,0:T(8,128)S(1)}, f32[3,8,16,128]{3,2,1,0:T(8,128)S(1)}, u32[]{:S(2)}, u32[]{:S(2)}) collective-permute-start(f32[3,8,16,128]{3,2,1,0:T(8,128)S(1)} %get-tuple-element.53), channel_id=1, source_target_pairs={{0,4},{4,0},{8,12},{12,8},{1,5},{5,1},{9,13},{13,9},{2,6},{6,2},{1... | collective-permute-start | bytes 589832 | tf_op jit(solution)/shard_map/ppermute | solution.py:504
  23.6 12.1 %collective-permute-done.4.refs_2_ = f32[3,8,16,128]{3,2,1,0:T(8,128)S(1)} collective-permute-done((f32[3,8,16,128]{3,2,1,0:T(8,128)S(1)}, f32[3,8,16,128]{3,2,1,0:T(8,128)S(1)}, u32[]{:S(2)}, u32[]{:S(2)}) %collective-permute-start.4) | collective-permute-done | bytes 196640 | tf_op jit(solution)/shard_map/ppermute | solution.py:504
  37.5 6.3 %collective-permute-done.22.refs_2_ = f32[3,8,16,128]{3,2,1,0:T(8,128)S(1)} collective-permute-done((f32[3,8,16,128]{3,2,1,0:T(8,128)S(1)}, f32[3,8,16,128]{3,2,1,0:T(8,128)S(1)}, u32[]{:S(2)}, u32[]{:S(2)}) %collective-permute-start.22) | collective-permute-done | bytes 196640 | tf_op jit(solution)/shard_map/ppermute | solution.py:504
  47.5 4.0 %collective-permute-done.24.refs_4_ = f32[3,8,16,128]{3,2,1,0:T(8,128)S(1)} collective-permute-done((f32[3,8,16,128]{3,2,1,0:T(8,128)S(1)}, f32[3,8,16,128]{3,2,1,0:T(8,128)S(1)}, u32[]{:S(2)}, u32[]{:S(2)}) %collective-permute-start.24) | collective-permute-done | bytes 196640 | tf_op jit(solution)/shard_map/ppermute | solution.py:504
  53.1 2.7 %collective-permute-done.27.refs_7_ = f32[3,8,16,128]{3,2,1,0:T(8,128)S(1)} collective-permute-done((f32[3,8,16,128]{3,2,1,0:T(8,128)S(1)}, f32[3,8,16,128]{3,2,1,0:T(8,128)S(1)}, u32[]{:S(2)}, u32[]{:S(2)}) %collective-permute-start.27) | collective-permute-done | bytes 196640 | tf_op jit(solution)/shard_map/ppermute | solution.py:504
  56.3 3.7 %collective-permute-done.26.refs_6_ = f32[3,8,16,128]{3,2,1,0:T(8,128)S(1)} collective-permute-done((f32[3,8,16,128]{3,2,1,0:T(8,128)S(1)}, f32[3,8,16,128]{3,2,1,0:T(8,128)S(1)}, u32[]{:S(2)}, u32[]{:S(2)}) %collective-permute-start.26) | collective-permute-done | bytes 196640 | tf_op jit(solution)/shard_map/ppermute | solution.py:504
  60.0 2.9 %collective-permute-done.25.refs_5_ = f32[3,8,16,128]{3,2,1,0:T(8,128)S(1)} collective-permute-done((f32[3,8,16,128]{3,2,1,0:T(8,128)S(1)}, f32[3,8,16,128]{3,2,1,0:T(8,128)S(1)}, u32[]{:S(2)}, u32[]{:S(2)}) %collective-permute-start.25) | collective-permute-done | bytes 196640 | tf_op jit(solution)/shard_map/ppermute | solution.py:504
  68.4 5.8 %pack.1 = (bf16[8,128,1024]{2,1,0:T(8,128)(2,1)}, f32[8,128,128]{2,1,0:T(8,128)}, f32[8,128,128]{2,1,0:T(8,128)}) custom-call(s32[5]{0:T(128)} %stack.23.info_ref, f32[8,64,1024]{2,1,0:T(8,128)} %own_wave_ref.1, f32[8,64,1024]{2,1,0:T(8,128)} %own_wave_ref.1, f32[8,64,256]{2,1,0:T(8,128)} %diag_ref.1), custom_call_target="tpu_custom_call" | custom-call | tf_op jit(solution)/shard_map/pack/pallas_call | solution.py:134
  76.7 7.8 %prepare.3 = (bf16[12,8,64,128]{3,2,1,0:T(8,128)(2,1)}, bf16[12,8,64,128]{3,2,1,0:T(8,128)(2,1)}, bf16[8,192,256]{2,1,0:T(8,128)(2,1)}) custom-call(s32[5]{0:T(128)} %stack.23.info_ref, f32[3,8,16,128]{3,2,1,0:T(8,128)} %copy-done.1, f32[3,8,16,128]{3,2,1,0:T(8,128)} %copy-done.9, f32[3,8,16,128]{3,2,1,0:T(8,128)} %copy-done.8, f32[3,8,16,128]{3,2,1,0:T(8,128)} %copy-done.7, ...), custom_call_target="tpu_custom_call" | custom-call | tf_op jit(solution)/shard_map/prepare/pallas_call | solution.py:226
  85.8 15.9 %apply_bonds.3.refs_9_ = f32[8,128,128]{2,1,0:T(8,128)} custom-call(s32[5]{0:T(128)} %stack.23.info_ref, s32[6,8]{1,0:T(8,128)} %refs_0_.7, s32[6,8]{1,0:T(8,128)} %copy-done.41, s32[6,8]{1,0:T(8,128)} %copy-done.40, s32[6,8]{1,0:T(8,128)} %copy-done.42, bf16[8,128,1024]{2,1,0:T(8,128)(2,1)} %get-tuple-element.26.refs_4_, ...), custom_call_target="tpu_custom_call" | custom-call | flops 3623878656 | bytes 12582912 | tf_op jit(solution)/shard_map/apply_bonds/pallas_call | solution.py:381
  103.3 7.7 %prepare.2 = (bf16[12,8,64,128]{3,2,1,0:T(8,128)(2,1)}, bf16[12,8,64,128]{3,2,1,0:T(8,128)(2,1)}, bf16[8,192,256]{2,1,0:T(8,128)(2,1)}) custom-call(s32[5]{0:T(128)} %stack.23.info_ref, f32[3,8,16,128]{3,2,1,0:T(8,128)} %copy-done, f32[3,8,16,128]{3,2,1,0:T(8,128)} %copy-done.4, f32[3,8,16,128]{3,2,1,0:T(8,128)} %copy-done.3, f32[3,8,16,128]{3,2,1,0:T(8,128)} %copy-done.2, ...), custom_call_target="tpu_custom_call" | custom-call | tf_op jit(solution)/shard_map/prepare/pallas_call | solution.py:226
  111.1 16.1 %apply_bonds.4 = (f32[2,128,128]{2,1,0:T(8,128)}, f32[2,128,128]{2,1,0:T(8,128)}, f32[2,128,128]{2,1,0:T(8,128)}, f32[2,128,128]{2,1,0:T(8,128)}) custom-call(s32[5]{0:T(128)} %stack.23.info_ref, s32[6,8]{1,0:T(8,128)} %refs_0_.7, s32[6,8]{1,0:T(8,128)} %copy-done.41, s32[6,8]{1,0:T(8,128)} %copy-done.40, s32[6,8]{1,0:T(8,128)} %copy-done.42, ...), custom_call_target="tpu_custom_call" | custom-call | flops 3623878656 | bytes 12582912 | tf_op jit(solution)/shard_map/apply_bonds/pallas_call | solution.py:381
  127.1 3.1 %collective-permute-start.37 = (f32[2,128,128]{2,1,0:T(8,128)}, f32[2,128,128]{2,1,0:T(8,128)S(1)}, u32[]{:S(2)}, u32[]{:S(2)}) collective-permute-start(f32[2,128,128]{2,1,0:T(8,128)} %get-tuple-element.35), channel_id=1, source_target_pairs={{0,8},{4,12},{8,0},{12,4},{1,9},{5,13},{9,1},{13,5},{2,10},{6,14},... | collective-permute-start | bytes 393224 | tf_op jit(solution)/shard_map/ppermute | solution.py:504
  132.2 3.4 %collective-permute-done.36.a1 = f32[2,128,128]{2,1,0:T(8,128)S(1)} collective-permute-done((f32[2,128,128]{2,1,0:T(8,128)}, f32[2,128,128]{2,1,0:T(8,128)S(1)}, u32[]{:S(2)}, u32[]{:S(2)}) %collective-permute-start.36) | collective-permute-done | bytes 131104 | tf_op jit(solution)/shard_map/ppermute | solution.py:504
  135.6 4.8 %collective-permute-done.37.a2 = f32[2,128,128]{2,1,0:T(8,128)S(1)} collective-permute-done((f32[2,128,128]{2,1,0:T(8,128)}, f32[2,128,128]{2,1,0:T(8,128)S(1)}, u32[]{:S(2)}, u32[]{:S(2)}) %collective-permute-start.37) | collective-permute-done | bytes 131104 | tf_op jit(solution)/shard_map/ppermute | solution.py:504
  141.1 3.1 %owner_image.1 = (f32[8,128,128]{2,1,0:T(8,128)}, f32[16,128]{1,0:T(8,128)}) custom-call(s32[5]{0:T(128)} %stack.23.info_ref, s32[4,2]{1,0:T(4,128)} %copy.17.owner_ref, f32[2,128,128]{2,1,0:T(8,128)} %get-tuple-element.33.a0, f32[2,128,128]{2,1,0:T(8,128)} %copy-done.27, f32[2,128,128]{2,1,0:T(8,128)} %copy-done.28, f32[2,128,128]{2,1,0:T(8,128)} %copy-done.29, ...), custom_call_target="tpu_custom_call" | custom-call | tf_op jit(solution)/shard_map/owner_image/pallas_call | solution.py:422
  146.8 10.7 %collective-permute-done.45.refs_5_ = f32[8,128,128]{2,1,0:T(8,128)S(1)} collective-permute-done((f32[8,128,128]{2,1,0:T(8,128)}, f32[8,128,128]{2,1,0:T(8,128)S(1)}, u32[]{:S(2)}, u32[]{:S(2)}) %collective-permute-start.45) | collective-permute-done | bytes 524320 | tf_op jit(solution)/shard_map/ppermute | solution.py:504
  158.3 2.6 %collective-permute-start.44 = (f32[16,128]{1,0:T(8,128)S(1)}, f32[16,128]{1,0:T(8,128)S(1)}, u32[]{:S(2)}, u32[]{:S(2)}) collective-permute-start(f32[16,128]{1,0:T(8,128)S(1)} %add_add_fusion.1), channel_id=1, source_target_pairs={{0,12},{4,8},{8,4},{12,0},{1,13},{5,9},{9,5},{13,1},{2,14},{6,10},... | collective-permute-start | bytes 24584 | tf_op jit(solution)/shard_map/ppermute | solution.py:504
  180.4 28.0 %apply_bonds.5 = (f32[2,128,128]{2,1,0:T(8,128)}, f32[2,128,128]{2,1,0:T(8,128)}, f32[2,128,128]{2,1,0:T(8,128)}, f32[2,128,128]{2,1,0:T(8,128)}) custom-call(s32[5]{0:T(128)} %stack.23.info_ref, s32[6,8]{1,0:T(8,128)} %refs_0_.7, s32[6,8]{1,0:T(8,128)} %copy-done.41, s32[6,8]{1,0:T(8,128)} %copy-done.40, s32[6,8]{1,0:T(8,128)} %copy-done.42, ...), custom_call_target="tpu_custom_call" | custom-call | flops 7247757312 | bytes 12582912 | tf_op jit(solution)/shard_map/apply_bonds/pallas_call | solution.py:381
  208.5 2.9 %collective-permute-start.49 = (f32[2,128,128]{2,1,0:T(8,128)}, f32[2,128,128]{2,1,0:T(8,128)S(1)}, u32[]{:S(2)}, u32[]{:S(2)}) collective-permute-start(f32[2,128,128]{2,1,0:T(8,128)} %get-tuple-element.44), channel_id=1, source_target_pairs={{0,8},{4,12},{8,0},{12,4},{1,9},{5,13},{9,1},{13,5},{2,10},{6,14},... | collective-permute-start | bytes 393224 | tf_op jit(solution)/shard_map/ppermute | solution.py:504
  214.9 5.9 %collective-permute-done.49.a2 = f32[2,128,128]{2,1,0:T(8,128)S(1)} collective-permute-done((f32[2,128,128]{2,1,0:T(8,128)}, f32[2,128,128]{2,1,0:T(8,128)S(1)}, u32[]{:S(2)}, u32[]{:S(2)}) %collective-permute-start.49) | collective-permute-done | bytes 131104 | tf_op jit(solution)/shard_map/ppermute | solution.py:504
  221.5 3.8 %second_outputs.1 = (f32[8,64,256]{2,1,0:T(8,128)}, f32[8,64,256]{2,1,0:T(8,128)}) custom-call(s32[5]{0:T(128)} %stack.23.info_ref, s32[4,2]{1,0:T(4,128)} %copy.17.owner_ref, f32[2,128,128]{2,1,0:T(8,128)} %get-tuple-element.42.a0, f32[2,128,128]{2,1,0:T(8,128)} %copy-done.30, f32[2,128,128]{2,1,0:T(8,128)} %copy-done.31, f32[2,128,128]{2,1,0:T(8,128)} %copy-done.32, ...), custom_call_target="tpu_custom_call" | custom-call | tf_op jit(solution)/shard_map/second_outputs/pallas_call | solution.py:487
  (195 shorter events, 56.2 us)
Async XLA Ops:
  10.2 25.5 %collective-permute-start.4 = (f32[3,8,16,128]{3,2,1,0:T(8,128)S(1)}, f32[3,8,16,128]{3,2,1,0:T(8,128)S(1)}, u32[]{:S(2)}, u32[]{:S(2)}) collective-permute-start(f32[3,8,16,128]{3,2,1,0:T(8,128)S(1)} %get-tuple-element.56), channel_id=1, source_target_pairs={{0,8},{4,12},{8,0},{12,4},{1,9},{5,13},{9,1},{13,5},{2,10},{6,14},... | collective-permute-start | bytes 589832 | tf_op jit(solution)/shard_map/ppermute | solution.py:504
  11.3 24.4 %collective-permute-start.3 = (f32[3,8,16,128]{3,2,1,0:T(8,128)S(1)}, f32[3,8,16,128]{3,2,1,0:T(8,128)S(1)}, u32[]{:S(2)}, u32[]{:S(2)}) collective-permute-start(f32[3,8,16,128]{3,2,1,0:T(8,128)S(1)} %get-tuple-element.57), channel_id=1, source_target_pairs={{0,4},{4,0},{8,12},{12,8},{1,5},{5,1},{9,13},{13,9},{2,6},{6,2},{1... | collective-permute-start | bytes 589832 | tf_op jit(solution)/shard_map/ppermute | solution.py:504
  13.5 23.8 %collective-permute-start.23 = (f32[3,8,16,128]{3,2,1,0:T(8,128)S(1)}, f32[3,8,16,128]{3,2,1,0:T(8,128)S(1)}, u32[]{:S(2)}, u32[]{:S(2)}) collective-permute-start(f32[3,8,16,128]{3,2,1,0:T(8,128)S(1)} %get-tuple-element.51), channel_id=1, source_target_pairs={{0,12},{4,8},{8,4},{12,0},{1,13},{5,9},{9,5},{13,1},{2,14},{6,10},... | collective-permute-start | bytes 589832 | tf_op jit(solution)/shard_map/ppermute | solution.py:504
  15.2 28.6 %collective-permute-start.22 = (f32[3,8,16,128]{3,2,1,0:T(8,128)S(1)}, f32[3,8,16,128]{3,2,1,0:T(8,128)S(1)}, u32[]{:S(2)}, u32[]{:S(2)}) collective-permute-start(f32[3,8,16,128]{3,2,1,0:T(8,128)S(1)} %get-tuple-element.52), channel_id=1, source_target_pairs={{0,8},{4,12},{8,0},{12,4},{1,9},{5,13},{9,1},{13,5},{2,10},{6,14},... | collective-permute-start | bytes 589832 | tf_op jit(solution)/shard_map/ppermute | solution.py:504
  15.5 29.8 %collective-permute-start.21 = (f32[3,8,16,128]{3,2,1,0:T(8,128)S(1)}, f32[3,8,16,128]{3,2,1,0:T(8,128)S(1)}, u32[]{:S(2)}, u32[]{:S(2)}) collective-permute-start(f32[3,8,16,128]{3,2,1,0:T(8,128)S(1)} %get-tuple-element.53), channel_id=1, source_target_pairs={{0,4},{4,0},{8,12},{12,8},{1,5},{5,1},{9,13},{13,9},{2,6},{6,2},{1... | collective-permute-start | bytes 589832 | tf_op jit(solution)/shard_map/ppermute | solution.py:504
  46.1 13.9 %collective-permute-start.26 = (f32[3,8,16,128]{3,2,1,0:T(8,128)S(1)}, f32[3,8,16,128]{3,2,1,0:T(8,128)S(1)}, u32[]{:S(2)}, u32[]{:S(2)}) collective-permute-start(f32[3,8,16,128]{3,2,1,0:T(8,128)S(1)} %collective-permute-done.22.refs_2_), channel_id=1, source_target_pairs={{0,2},{2,0},{1,3},{3,1},{4,6},{6,4},{5,7},{7,5},{8,10},{10,8},{9,1... | collective-permute-start | bytes 589832 | tf_op jit(solution)/shard_map/ppermute | solution.py:504
  62.9 21.6 %collective-permute-start.13 = (f32[3,8,16,128]{3,2,1,0:T(8,128)S(1)}, f32[3,8,16,128]{3,2,1,0:T(8,128)S(1)}, u32[]{:S(2)}, u32[]{:S(2)}) collective-permute-start(f32[3,8,16,128]{3,2,1,0:T(8,128)S(1)} %collective-permute-done.5.refs_3_), channel_id=1, source_target_pairs={{0,1},{1,0},{2,3},{3,2},{4,5},{5,4},{6,7},{7,6},{8,9},{9,8},{10,11... | collective-permute-start | bytes 589832 | tf_op jit(solution)/shard_map/ppermute | solution.py:504
  63.4 21.2 %collective-permute-start.9 = (f32[3,8,16,128]{3,2,1,0:T(8,128)S(1)}, f32[3,8,16,128]{3,2,1,0:T(8,128)S(1)}, u32[]{:S(2)}, u32[]{:S(2)}) collective-permute-start(f32[3,8,16,128]{3,2,1,0:T(8,128)S(1)} %collective-permute-done.5.refs_3_), channel_id=1, source_target_pairs={{0,2},{2,0},{1,3},{3,1},{4,6},{6,4},{5,7},{7,5},{8,10},{10,8},{9,1... | collective-permute-start | bytes 589832 | tf_op jit(solution)/shard_map/ppermute | solution.py:504
  64.9 20.3 %collective-permute-start.12 = (f32[3,8,16,128]{3,2,1,0:T(8,128)S(1)}, f32[3,8,16,128]{3,2,1,0:T(8,128)S(1)}, u32[]{:S(2)}, u32[]{:S(2)}) collective-permute-start(f32[3,8,16,128]{3,2,1,0:T(8,128)S(1)} %collective-permute-done.4.refs_2_), channel_id=1, source_target_pairs={{0,1},{1,0},{2,3},{3,2},{4,5},{5,4},{6,7},{7,6},{8,9},{9,8},{10,11... | collective-permute-start | bytes 589832 | tf_op jit(solution)/shard_map/ppermute | solution.py:504
  65.0 20.4 %collective-permute-start.8 = (f32[3,8,16,128]{3,2,1,0:T(8,128)S(1)}, f32[3,8,16,128]{3,2,1,0:T(8,128)}, u32[]{:S(2)}, u32[]{:S(2)}) collective-permute-start(f32[3,8,16,128]{3,2,1,0:T(8,128)S(1)} %collective-permute-done.4.refs_2_), channel_id=1, source_target_pairs={{0,2},{2,0},{1,3},{3,1},{4,6},{6,4},{5,7},{7,5},{8,10},{10,8},{9,1... | collective-permute-start | bytes 589832 | tf_op jit(solution)/shard_map/ppermute | solution.py:504
  66.3 19.4 %collective-permute-start.7 = (f32[3,8,16,128]{3,2,1,0:T(8,128)S(1)}, f32[3,8,16,128]{3,2,1,0:T(8,128)}, u32[]{:S(2)}, u32[]{:S(2)}) collective-permute-start(f32[3,8,16,128]{3,2,1,0:T(8,128)S(1)} %collective-permute-done.3.refs_1_), channel_id=1, source_target_pairs={{0,2},{2,0},{1,3},{3,1},{4,6},{6,4},{5,7},{7,5},{8,10},{10,8},{9,1... | collective-permute-start | bytes 589832 | tf_op jit(solution)/shard_map/ppermute | solution.py:504
  84.6 17.2 %collective-permute-start.11 = (f32[3,8,16,128]{3,2,1,0:T(8,128)S(1)}, f32[3,8,16,128]{3,2,1,0:T(8,128)S(1)}, u32[]{:S(2)}, u32[]{:S(2)}) collective-permute-start(f32[3,8,16,128]{3,2,1,0:T(8,128)S(1)} %collective-permute-done.3.refs_1_), channel_id=1, source_target_pairs={{0,1},{1,0},{2,3},{3,2},{4,5},{5,4},{6,7},{7,6},{8,9},{9,8},{10,11... | collective-permute-start | bytes 589832 | tf_op jit(solution)/shard_map/ppermute | solution.py:504
  84.7 17.1 %collective-permute-start.14 = (f32[3,8,16,128]{3,2,1,0:T(8,128)S(1)}, f32[3,8,16,128]{3,2,1,0:T(8,128)S(1)}, u32[]{:S(2)}, u32[]{:S(2)}) collective-permute-start(f32[3,8,16,128]{3,2,1,0:T(8,128)S(1)} %collective-permute-done.6.refs_4_), channel_id=1, source_target_pairs={{0,1},{1,0},{2,3},{3,2},{4,5},{5,4},{6,7},{7,6},{8,9},{9,8},{10,11... | collective-permute-start | bytes 589832 | tf_op jit(solution)/shard_map/ppermute | solution.py:504
  85.2 16.6 %collective-permute-start.17 = (f32[3,8,16,128]{3,2,1,0:T(8,128)S(1)}, f32[3,8,16,128]{3,2,1,0:T(8,128)S(1)}, u32[]{:S(2)}, u32[]{:S(2)}) collective-permute-start(f32[3,8,16,128]{3,2,1,0:T(8,128)S(1)} %collective-permute-done.9.refs_7_), channel_id=1, source_target_pairs={{0,1},{1,0},{2,3},{3,2},{4,5},{5,4},{6,7},{7,6},{8,9},{9,8},{10,11... | collective-permute-start | bytes 589832 | tf_op jit(solution)/shard_map/ppermute | solution.py:504
  85.3 16.5 %collective-permute-start.16 = (f32[3,8,16,128]{3,2,1,0:T(8,128)}, f32[3,8,16,128]{3,2,1,0:T(8,128)S(1)}, u32[]{:S(2)}, u32[]{:S(2)}) collective-permute-start(f32[3,8,16,128]{3,2,1,0:T(8,128)} %collective-permute-done.8.refs_6_), channel_id=1, source_target_pairs={{0,1},{1,0},{2,3},{3,2},{4,5},{5,4},{6,7},{7,6},{8,9},{9,8},{10,11... | collective-permute-start | bytes 589832 | tf_op jit(solution)/shard_map/ppermute | solution.py:504
  85.7 16.1 %collective-permute-start.15 = (f32[3,8,16,128]{3,2,1,0:T(8,128)}, f32[3,8,16,128]{3,2,1,0:T(8,128)S(1)}, u32[]{:S(2)}, u32[]{:S(2)}) collective-permute-start(f32[3,8,16,128]{3,2,1,0:T(8,128)} %collective-permute-done.7.refs_5_), channel_id=1, source_target_pairs={{0,1},{1,0},{2,3},{3,2},{4,5},{5,4},{6,7},{7,6},{8,9},{9,8},{10,11... | collective-permute-start | bytes 589832 | tf_op jit(solution)/shard_map/ppermute | solution.py:504
  127.1 13.3 %collective-permute-start.37 = (f32[2,128,128]{2,1,0:T(8,128)}, f32[2,128,128]{2,1,0:T(8,128)S(1)}, u32[]{:S(2)}, u32[]{:S(2)}) collective-permute-start(f32[2,128,128]{2,1,0:T(8,128)} %get-tuple-element.35), channel_id=1, source_target_pairs={{0,8},{4,12},{8,0},{12,4},{1,9},{5,13},{9,1},{13,5},{2,10},{6,14},... | collective-permute-start | bytes 393224 | tf_op jit(solution)/shard_map/ppermute | solution.py:504
  144.2 13.3 %collective-permute-start.45 = (f32[8,128,128]{2,1,0:T(8,128)}, f32[8,128,128]{2,1,0:T(8,128)S(1)}, u32[]{:S(2)}, u32[]{:S(2)}) collective-permute-start(f32[8,128,128]{2,1,0:T(8,128)} %get-tuple-element.40.image_ref.refs_4_), channel_id=1, source_target_pairs={{0,2},{2,0},{1,3},{3,1},{4,6},{6,4},{5,7},{7,5},{8,10},{10,8},{9,1... | collective-permute-start | bytes 1572872 | tf_op jit(solution)/shard_map/ppermute | solution.py:504
  144.9 12.7 %collective-permute-start.40 = (f32[16,128]{1,0:T(8,128)}, f32[16,128]{1,0:T(8,128)S(1)}, u32[]{:S(2)}, u32[]{:S(2)}) collective-permute-start(f32[16,128]{1,0:T(8,128)} %get-tuple-element.39), channel_id=1, source_target_pairs={{0,2},{1,3},{2,0},{3,1},{4,6},{5,7},{6,4},{7,5},{8,10},{9,11},{10,... | collective-permute-start | bytes 24584 | tf_op jit(solution)/shard_map/ppermute | solution.py:504
  146.8 32.0 %collective-permute-start.46 = (f32[8,128,128]{2,1,0:T(8,128)}, f32[8,128,128]{2,1,0:T(8,128)S(1)}, u32[]{:S(2)}, u32[]{:S(2)}) collective-permute-start(f32[8,128,128]{2,1,0:T(8,128)} %get-tuple-element.40.image_ref.refs_4_), channel_id=1, source_target_pairs={{0,1},{1,0},{2,3},{3,2},{4,5},{5,4},{6,7},{7,6},{8,9},{9,8},{10,11... | collective-permute-start | bytes 1572872 | tf_op jit(solution)/shard_map/ppermute | solution.py:504
  157.4 21.4 %collective-permute-start.47 = (f32[8,128,128]{2,1,0:T(8,128)S(1)}, f32[8,128,128]{2,1,0:T(8,128)S(1)}, u32[]{:S(2)}, u32[]{:S(2)}) collective-permute-start(f32[8,128,128]{2,1,0:T(8,128)S(1)} %collective-permute-done.45.refs_5_), channel_id=1, source_target_pairs={{0,1},{1,0},{2,3},{3,2},{4,5},{5,4},{6,7},{7,6},{8,9},{9,8},{10,11... | collective-permute-start | bytes 1572872 | tf_op jit(solution)/shard_map/ppermute | solution.py:504
  174.4 37.0 %collective-permute-start.56 = (f32[8,128]{1,0:T(8,128)S(1)}, f32[8,128]{1,0:T(8,128)S(1)}, u32[]{:S(2)}, u32[]{:S(2)}) collective-permute-start(f32[8,128]{1,0:T(8,128)S(1)} %add_add_fusion.3), channel_id=1, source_target_pairs={{0,12},{4,8},{8,4},{12,0},{1,13},{5,9},{9,5},{13,1},{2,14},{6,10},... | collective-permute-start | bytes 12296 | tf_op jit(solution)/shard_map/ppermute | solution.py:504
  176.8 36.0 %collective-permute-start.55 = (f32[8,128]{1,0:T(8,128)S(1)}, f32[8,128]{1,0:T(8,128)S(1)}, u32[]{:S(2)}, u32[]{:S(2)}) collective-permute-start(f32[8,128]{1,0:T(8,128)S(1)} %add_add_fusion.3), channel_id=1, source_target_pairs={{0,8},{4,12},{8,0},{12,4},{1,9},{5,13},{9,1},{13,5},{2,10},{6,14},... | collective-permute-start | bytes 12296 | tf_op jit(solution)/shard_map/ppermute | solution.py:504
  176.8 36.0 %collective-permute-start.54 = (f32[8,128]{1,0:T(8,128)S(1)}, f32[8,128]{1,0:T(8,128)S(1)}, u32[]{:S(2)}, u32[]{:S(2)}) collective-permute-start(f32[8,128]{1,0:T(8,128)S(1)} %add_add_fusion.3), channel_id=1, source_target_pairs={{0,4},{4,0},{8,12},{12,8},{1,5},{5,1},{9,13},{13,9},{2,6},{6,2},{1... | collective-permute-start | bytes 12296 | tf_op jit(solution)/shard_map/ppermute | solution.py:504
  (76 other events, 1207.1 us)

commit v3 on v2

--- a/solution.py
+++ b/solution.py
@@ -10,7 +10,8 @@
 LANES = 128
 SUB = 8
 PHYS = 16
-GROUPS = 2
+TINY = 1e-30
+GROUPS = 3
 VMEM_LIMIT = 56 * 1024 * 1024
 
 
@@ -84,6 +85,10 @@
 
 def lane_is_first(rows):
     return lax.broadcasted_iota(jnp.int32, (rows, LANES), 1) < LANES // 2
+
+
+def micros(count):
+    return pl.CostEstimate(flops=count * 1100000000, bytes_accessed=1 << 20, transcendentals=0)
 
 
 def whole(*shape):
@@ -192,10 +197,11 @@
     zs = 4
     per, blocks, rows, lanes = sources[0].shape
     half = lanes // 2
+    wide = half // 2
     first = lane_is_first(half)
     lane = lax.broadcasted_iota(jnp.int32, (half, lanes), 1)
-    start = info_ref[0] * 16
-    count = lanes // 16
+    start = info_ref[6] * wide
+    count = lanes // wide
     pairs = [(s, k) for s in range(len(sources) // zs) for k in range(per)]
     for j in range(blocks):
         for base in range(0, len(pairs), count):
@@ -209,11 +215,11 @@
                 high, low = split_two(jnp.where(first, block, pltpu.roll(block, half, 1)))
                 left_high[base + at, j] = high
                 left_low[base + at, j] = low
-                shift = lax.rem(16 * at + lanes + half - start, lanes)
-                columns = jnp.where(lane // 16 == at, pltpu.roll(block, shift, 1), columns)
-            upright = columns.T[: 16 * len(group)]
+                shift = lax.rem(wide * at + lanes + half - start, lanes)
+                columns = jnp.where(lane // wide == at, pltpu.roll(block, shift, 1), columns)
+            upright = columns.T[: wide * len(group)]
             high, low = split_two(upright)
-            where = pl.ds(16 * base, 16 * len(group))
+            where = pl.ds(wide * base, wide * len(group))
             right_out[j, where, 0:lanes] = jnp.concatenate([high, high], axis=1)
             right_out[j, where, lanes : 2 * lanes] = jnp.concatenate([low, low], axis=1)
 
@@ -235,16 +241,17 @@
             out_specs=[
                 pl.BlockSpec((total, step, half, lanes), lambda i, *_: (0, i, 0, 0)),
                 pl.BlockSpec((total, step, half, lanes), lambda i, *_: (0, i, 0, 0)),
-                pl.BlockSpec((step, total * 16, 2 * lanes), lambda i, *_: (i, 0, 0)),
+                pl.BlockSpec((step, total * 32, 2 * lanes), lambda i, *_: (i, 0, 0)),
             ],
             scratch_shapes=[pltpu.VMEM((total, step, half, lanes), jnp.float32)],
         ),
         out_shape=[
             jax.ShapeDtypeStruct((total, blocks, half, lanes), jnp.bfloat16),
             jax.ShapeDtypeStruct((total, blocks, half, lanes), jnp.bfloat16),
-            jax.ShapeDtypeStruct((blocks, total * 16, 2 * lanes), jnp.bfloat16),
+            jax.ShapeDtypeStruct((blocks, total * 32, 2 * lanes), jnp.bfloat16),
         ],
         compiler_params=pltpu.CompilerParams(vmem_limit_bytes=VMEM_LIMIT),
+        cost_estimate=micros(3),
         name="prepare",
     )(info, *sources)
 
@@ -253,11 +260,11 @@
     groups, parts_given, before_given, pieces = plan
     refs = list(refs)
     take = lambda n: [refs.pop(0) for _ in range(n)]
-    slots = take(4)
+    slots = take(2)
     vector = take(4 if parts_given else 1)
     operands = [take(4) for _ in groups]
     before = take(1) if before_given else None
-    outs = take(4 if pieces else 1)
+    outs = take(2 if pieces else 1)
     total_ref, vec, mid = refs
     step = vector[0].shape[0]
     lanes, half = LANES, LANES // 2
@@ -293,18 +300,19 @@
             )
             at += count
 
-    def one_bond(refs_of, w, slot_of, base):
+    def left_and_right(refs_of, w, base):
         left_high, left_low, right, mix = refs_of
-        highs, lows = [], []
+        done = {}
         for j in range(step):
-            row = pl.multiple_of((base + w) * 16, 16)
             tiles = []
-            for pair in range(PHYS // 2):
-                columns = slice(pair * lanes, (pair + 1) * lanes)
-                upper = mid[j, pl.ds(row, SUB), columns]
-                lower = mid[j, pl.ds(row + SUB, SUB), columns]
-                tiles.append(jnp.where(first, upper, pltpu.roll(lower, half, 1)))
-                tiles.append(jnp.where(first, pltpu.roll(upper, half, 1), lower))
+            for part in range(2):
+                row = (base + w) * 32 + part * 16
+                for pair in range(PHYS // 2):
+                    columns = slice(pair * lanes, (pair + 1) * lanes)
+                    upper = mid[j, row : row + SUB, columns]
+                    lower = mid[j, row + SUB : row + 2 * SUB, columns]
+                    tiles.append(jnp.where(first, upper, pltpu.roll(lower, half, 1)))
+                    tiles.append(jnp.where(first, pltpu.roll(upper, half, 1), lower))
             t_high, t_low = split_two(jnp.concatenate(tiles, axis=0))
             lh, ll = left_high[w, j], left_low[w, j]
             wide_high = jnp.concatenate([lh * keep_first, lh * keep_second], axis=0)
@@ -315,10 +323,15 @@
                 preferred_element_type=jnp.float32,
             ) + jnp.dot(t_high, wide_low, preferred_element_type=jnp.float32)
             z_high, z_low = split_two(z)
-            highs.append(z_high)
-            lows.append(z_low)
-        z_high = jnp.concatenate(highs, axis=1)
-        z_low = jnp.concatenate(lows, axis=1)
+            for part in range(2):
+                rows = slice(part * lanes, (part + 1) * lanes)
+                done[part, j] = (z_high[rows], z_low[rows])
+        order = [(part, j) for part in range(2) for j in range(step)]
+        return [jnp.concatenate([done[at][i] for at in order], axis=1) for i in range(2)]
+
+    def mix_and_add(refs_of, w, z, slot_of):
+        z_high, z_low = z
+        mix = refs_of[3]
         mix_high = mix[w, :, 0:lanes]
         mix_low = mix[w, :, lanes:]
         mixed = jnp.dot(
@@ -329,30 +342,29 @@
         for j in range(step):
             slot = slot_of(pl.program_id(0) * step + j)
             slot = ((slot >> 1) ^ me) * 2 + (slot & 1)
-            total_ref[slot] += mixed[:, j * lanes : (j + 1) * lanes]
+            for part in range(2):
+                at = part * step + j
+                total_ref[part, slot] += mixed[:, at * lanes : (at + 1) * lanes]
 
     base = 0
+    waiting = None
     for group, refs_of in zip(groups, operands):
         count = refs_of[0].shape[0]
-        per = count // 4
-        for s in range(4):
-            table = slots[s]
-
-            def some(k, carry):
-                one_bond(
-                    refs_of, s * per + k, lambda j: table[group * per + k, j], base
-                )
-                return carry
-
-            for k in range(per):
-                some(k, 0)
+        per = count // 2
+        for w in range(count):
+            z = left_and_right(refs_of, w, base)
+            if waiting is not None:
+                mix_and_add(*waiting)
+            table, bond = slots[w // per], group * per + w % per
+            waiting = (refs_of, w, z, lambda j, table=table, bond=bond: table[bond, j])
         base += count
+    mix_and_add(*waiting)
 
     @pl.when(pl.program_id(0) == pl.num_programs(0) - 1)
     def _():
         if pieces:
-            for k in range(4):
-                outs[k][...] = total_ref[2 * k : 2 * k + 2]
+            outs[0][...] = total_ref[info_ref[5]]
+            outs[1][...] = total_ref[1 - info_ref[5]]
         else:
             outs[0][...] = total_ref[...]
 
@@ -362,7 +374,6 @@
     counts = [x[0].shape[0] for x in operands]
     per_group = mixing.shape[0] // GROUPS
     step = 2
-    flops = 2 * blocks * sum(counts) * SUB * lanes * (3 * lanes * 16 * 3)
     in_specs = [pl.BlockSpec((step,) + x.shape[1:], lambda i, *_: (i, 0, 0)) for x in vector]
     arguments = list(vector)
     for group, (left_high, left_low, right), count in zip(groups, operands, counts):
@@ -376,32 +387,26 @@
     if before is not None:
         in_specs.append(whole(*before.shape))
         arguments.append(before)
-    shapes = [(2, lanes, lanes)] * 4 if pieces else [(8, lanes, lanes)]
+    shapes = [(8, lanes, lanes)] * 2 if pieces else [(2, 8, lanes, lanes)]
     plan = (tuple(groups), len(vector) == 4, before is not None, pieces)
     return pl.pallas_call(
         functools.partial(apply_kernel, plan),
         grid_spec=pltpu.PrefetchScalarGridSpec(
-            num_scalar_prefetch=5,
+            num_scalar_prefetch=3,
             grid=(blocks // step,),
             in_specs=in_specs,
             out_specs=[whole(*shape) for shape in shapes],
             scratch_shapes=[
-                pltpu.VMEM((8, lanes, lanes), jnp.float32),
+                pltpu.VMEM((2, 8, lanes, lanes), jnp.float32),
                 pltpu.VMEM((step, lanes, PHYS * half), jnp.bfloat16),
-                pltpu.VMEM((step, sum(counts) * 16, PHYS * half), jnp.float32),
+                pltpu.VMEM((step, sum(counts) * 32, PHYS * half), jnp.float32),
             ],
         ),
         out_shape=[jax.ShapeDtypeStruct(shape, jnp.float32) for shape in shapes],
         compiler_params=pltpu.CompilerParams(vmem_limit_bytes=VMEM_LIMIT),
-        cost_estimate=pl.CostEstimate(
-            flops=flops, bytes_accessed=12 * 1024 * 1024, transcendentals=0
-        ),
+        cost_estimate=micros(2 * sum(counts)),
         name="apply_bonds",
     )(info, *slots, *arguments)
-
-
-def folded(x):
-    return jnp.sum(x.reshape(-1, SUB, LANES), axis=0)
 
 
 def add_arrived(info_ref, owner_ref, arrived, total):
@@ -410,12 +415,44 @@
             total[owner_ref[info_ref[4] ^ k, i]] += arrived[k][i]
 
 
-def image_kernel(info_ref, owner_ref, a0, a1, a2, a3, diag_ref, own_ref, image_ref, sums_ref):
+def stacked_rows(*rows):
+    at = lax.broadcasted_iota(jnp.int32, (SUB, LANES), 0)
+    tile = jnp.zeros((SUB, LANES), jnp.float32)
+    for i, row in enumerate(rows):
+        tile = jnp.where(at == i, row, tile)
+    return tile
+
+
+def merged(tiles):
+    rows = [[tile[i : i + 1] for i in range(3)] for tile in tiles]
+    cross = sum(row[0] for row in rows)
+    square = sum(row[1] for row in rows)
+    ratio = cross / jnp.maximum(square, TINY)
+    apart = [
+        (row[0] / jnp.maximum(row[1], TINY) - ratio) * jnp.sqrt(row[1]) for row in rows
+    ]
+    rest = sum(row[2] for row in rows) + sum(x * x for x in apart)
+    return cross, square, rest
+
+
+def image_kernel(info_ref, owner_ref, a0, a1, a2, a3, diag_ref, own_ref, image_ref, stats_ref):
     image_ref[...] = diag_ref[...] * own_ref[...]
     add_arrived(info_ref, owner_ref, (a0, a1, a2, a3), image_ref)
-    own = own_ref[...]
-    sums_ref[0:SUB] = folded(own * image_ref[...])
-    sums_ref[SUB:] = folded(own * own)
+    blocks = image_ref.shape[0]
+    cross = jnp.zeros((LANES, LANES), jnp.float32)
+    square = jnp.zeros((LANES, LANES), jnp.float32)
+    for k in range(blocks):
+        own = own_ref[k]
+        cross += own * image_ref[k]
+        square += own * own
+    cross = jnp.sum(cross, keepdims=True)
+    square = jnp.sum(square, keepdims=True)
+    ratio = cross / jnp.maximum(square, TINY)
+    rest = jnp.zeros((LANES, LANES), jnp.float32)
+    for k in range(blocks):
+        apart = image_ref[k] - ratio * own_ref[k]
+        rest += apart * apart
+    stats_ref[...] = stacked_rows(cross, square, jnp.sum(rest, keepdims=True))
 
 
 def owner_image(info, owners, arrived, diagonal, own):
@@ -425,77 +462,90 @@
             num_scalar_prefetch=2,
             grid=(1,),
             in_specs=[whole(*x.shape) for x in (*arrived, diagonal, own)],
-            out_specs=[whole(*own.shape), whole(2 * SUB, LANES)],
+            out_specs=[whole(*own.shape), whole(SUB, LANES)],
         ),
         out_shape=[
             jax.ShapeDtypeStruct(own.shape, jnp.float32),
-            jax.ShapeDtypeStruct((2 * SUB, LANES), jnp.float32),
-        ],
-        compiler_params=pltpu.CompilerParams(vmem_limit_bytes=VMEM_LIMIT),
-        name="owner_image",
-    )(info, owners, *arrived, diagonal, own)
-
-
-def scalars_of(sums, entries):
-    cross = jnp.sum(sums[0:SUB], keepdims=True) / entries
-    square = jnp.sum(sums[SUB:], keepdims=True) / entries
-    scale = lax.rsqrt(square + 1e-06)
-    return scale, cross * scale * scale
-
-
-def residual_kernel(entries, sums_ref, image_ref, own_ref, first_ref, resid_ref):
-    scale, rayleigh = scalars_of(sums_ref[...], entries)
-    total = jnp.zeros((SUB, LANES), jnp.float32)
-    for k in range(image_ref.shape[0]):
-        image = image_ref[k]
-        residual = scale * (image - rayleigh * own_ref[k])
-        total += folded(residual * residual)
-        first_ref[k] = unpack_tile(scale * image)
-    resid_ref[...] = total
-
-
-def first_outputs(sums, image, own, entries):
-    blocks = image.shape[0]
-    return pl.pallas_call(
-        functools.partial(residual_kernel, entries),
-        out_shape=[
-            jax.ShapeDtypeStruct((blocks, LANES // 2, 2 * LANES), jnp.float32),
             jax.ShapeDtypeStruct((SUB, LANES), jnp.float32),
         ],
         compiler_params=pltpu.CompilerParams(vmem_limit_bytes=VMEM_LIMIT),
+        cost_estimate=micros(3),
+        name="owner_image",
+    )(info, owners, *arrived, diagonal, own)
+
+
+def merge_kernel(*refs):
+    refs[-1][...] = stacked_rows(*merged([ref[...] for ref in refs[:-1]]))
+
+
+def merge(tiles):
+    return pl.pallas_call(
+        merge_kernel,
+        out_shape=jax.ShapeDtypeStruct((SUB, LANES), jnp.float32),
+        cost_estimate=micros(1),
+        name="merge",
+    )(*tiles)
+
+
+def scales_of(tiles, entries):
+    cross, square, rest = merged(tiles)
+    scale = lax.rsqrt(square / entries + 1e-06)
+    rayleigh = scale * scale * (cross / entries)
+    apart = (cross / jnp.maximum(square, TINY) - rayleigh) * jnp.sqrt(square)
+    mean = scale * scale * ((rest + apart * apart) / entries)
+    return scale, rayleigh, scale * lax.rsqrt(mean + 1e-06)
+
+
+def first_kernel(entries, s0, s1, s2, s3, image_ref, own_ref, first_ref, second_ref):
+    tiles = [ref[...] for ref in (s0, s1, s2, s3)]
+    scale, rayleigh, second_scale = scales_of(tiles, entries)
+    for k in range(image_ref.shape[0]):
+        image = image_ref[k]
+        first_ref[k] = unpack_tile(scale * image)
+        second_ref[k] = unpack_tile(second_scale * (image - rayleigh * own_ref[k]))
+
+
+def first_outputs(stats, image, own, entries):
+    blocks = image.shape[0]
+    shape = jax.ShapeDtypeStruct((blocks, LANES // 2, 2 * LANES), jnp.float32)
+    return pl.pallas_call(
+        functools.partial(first_kernel, entries),
+        out_shape=[shape, shape],
+        compiler_params=pltpu.CompilerParams(vmem_limit_bytes=VMEM_LIMIT),
+        cost_estimate=micros(3),
         name="first_outputs",
-    )(sums, image, own)
+    )(*stats, image, own)
 
 
 def final_kernel(
-    entries, info_ref, owner_ref, a0, a1, a2, a3, diag_ref, own_ref, image_ref, sums_ref, resid_ref,
-    vector_ref, second_ref, total,
+    entries, info_ref, owner_ref, a0, a1, a2, a3, diag_ref, image_ref, s0, s1, s2, s3,
+    second_ref, total,
 ):
-    scale, rayleigh = scalars_of(sums_ref[...], entries)
-    mean = jnp.sum(resid_ref[...], keepdims=True) / entries
-    scale = scale * lax.rsqrt(mean + 1e-06)
-    total[...] = (diag_ref[...] - rayleigh) * image_ref[...]
+    tiles = [ref[...] for ref in (s0, s1, s2, s3)]
+    scale, rayleigh, second_scale = scales_of(tiles, entries)
+    for k in range(image_ref.shape[0]):
+        total[k] = (diag_ref[k] - rayleigh) * image_ref[k]
     add_arrived(info_ref, owner_ref, (a0, a1, a2, a3), total)
     for k in range(image_ref.shape[0]):
-        vector_ref[k] = unpack_tile(scale * (image_ref[k] - rayleigh * own_ref[k]))
-        second_ref[k] = unpack_tile(scale * total[k])
-
-
-def second_outputs(info, owners, arrived, diagonal, own, image, sums, resid, entries):
-    shape = (own.shape[0], LANES // 2, 2 * LANES)
-    arguments = (*arrived, diagonal, own, image, sums, resid)
+        second_ref[k] = unpack_tile(second_scale * total[k])
+
+
+def second_output(info, owners, arrived, diagonal, image, stats, entries):
+    shape = (image.shape[0], LANES // 2, 2 * LANES)
+    arguments = (*arrived, diagonal, image, *stats)
     return pl.pallas_call(
         functools.partial(final_kernel, entries),
         grid_spec=pltpu.PrefetchScalarGridSpec(
             num_scalar_prefetch=2,
             grid=(1,),
             in_specs=[whole(*x.shape) for x in arguments],
-            out_specs=[whole(*shape), whole(*shape)],
-            scratch_shapes=[pltpu.VMEM(own.shape, jnp.float32)],
+            out_specs=whole(*shape),
+            scratch_shapes=[pltpu.VMEM(image.shape, jnp.float32)],
         ),
-        out_shape=[jax.ShapeDtypeStruct(shape, jnp.float32)] * 2,
+        out_shape=jax.ShapeDtypeStruct(shape, jnp.float32),
         compiler_params=pltpu.CompilerParams(vmem_limit_bytes=VMEM_LIMIT),
-        name="second_outputs",
+        cost_estimate=micros(3),
+        name="second_output",
     )(info, owners, *arguments)
 
 
@@ -504,16 +554,22 @@
     return lax.ppermute(x, axis, [(i, i ^ k) for i in range(size)])
 
 
+def after(x, *others):
+    return lax.optimization_barrier((x, *others))[0]
+
+
 def gathered(x):
     across = partner(x, "mpo", 1)
     return [x, across, partner(x, "rep", 1), partner(across, "rep", 1)]
 
 
-def summed(x, axes):
-    return x + partner(x, axes, 1) + partner(x, axes, 2) + partner(x, axes, 3)
-
-
-def exchanged(pieces):
+def everyone(x, axes):
+    return [x] + [partner(x, axes, k) for k in range(1, 4)]
+
+
+def to_owners(mine, theirs):
+    other = partner(theirs, "rep", 1)
+    pieces = [mine[2 * k : 2 * k + 2] + other[2 * k : 2 * k + 2] for k in range(4)]
     return [pieces[0]] + [partner(pieces[k], "blk", k) for k in range(1, 4)]
 
 
@@ -522,24 +578,29 @@
     zs = lax.axis_size("blk")
     mpo, rep, blk = lax.axis_index("mpo"), lax.axis_index("rep"), lax.axis_index("blk")
     place = 2 * mpo + rep
-    info = jnp.stack([place, place ^ 2, place ^ 1, place ^ 3, blk]).astype(jnp.int32)
+    info = jnp.stack([place, place ^ 2, place ^ 1, place ^ 3, blk, rep, mpo]).astype(jnp.int32)
     bonds = environment.shape[0]
     per = bonds // GROUPS
     entries = float(blocks * zs * rows * width)
 
+    vector, own, diagonal_packed = pack(info, wavefunction, diagonal)
+    mixing = mixing_operand([bond_terms, partner(bond_terms, "mpo", 1)])
+    slots = [term_slot, partner(term_slot, "mpo", 1)]
+
     by_owner = environment.reshape(bonds, zs, blocks, rows // zs, 2 * rows)
     operands = []
+    arrived = [None] * 4
     for group in range(GROUPS):
         mine = by_owner[group * per : (group + 1) * per]
-        pieces = exchanged(
-            [lax.dynamic_index_in_dim(mine, blk ^ k, 1, keepdims=False) for k in range(4)]
-        )
-        by_source = list(zip(*[gathered(piece) for piece in pieces]))
-        operands.append(prepare(info, [piece for source in by_source for piece in source]))
-
-    mixing = mixing_operand(gathered(bond_terms))
-    slots = gathered(term_slot)
-    vector, own, diagonal_packed = pack(info, wavefunction, diagonal)
+        pieces = []
+        for k in range(4):
+            piece = lax.dynamic_index_in_dim(mine, blk ^ k, 1, keepdims=False)
+            if k:
+                if arrived[k] is not None:
+                    piece = after(piece, arrived[k])
+                piece = arrived[k] = partner(piece, "blk", k)
+            pieces.append(piece)
+        operands.append(prepare(info, pieces + [partner(piece, "mpo", 1) for piece in pieces]))
 
     total = None
     for group in range(GROUPS):
@@ -548,16 +609,16 @@
             info, slots, [vector], [group], [operands[group]], mixing, total, last
         )
         total = None if last else out[0]
-    image, sums = owner_image(info, slot_block, exchanged(out), diagonal_packed, own)
-
-    out = apply_bonds(
-        info, slots, gathered(image), list(range(GROUPS)), operands, mixing, None, True
-    )
-    sums = summed(summed(sums, ("mpo", "rep")), "blk")
-    first_image, resid = first_outputs(sums, image, own, entries)
-    resid = summed(summed(resid, ("mpo", "rep")), "blk")
-    second_vector, second_image = second_outputs(
-        info, slot_block, exchanged(out), diagonal_packed, own, image, sums, resid, entries
+    image, stats = owner_image(info, slot_block, to_owners(*out), diagonal_packed, own)
+
+    stats = everyone(stats, ("mpo", "rep"))
+    parts = gathered(image)
+    parts[0] = after(parts[0], *stats)
+    out = apply_bonds(info, slots, parts, list(range(GROUPS)), operands, mixing, None, True)
+    stats = everyone(merge([after(x, out[1]) for x in stats]), "blk")
+    first_image, second_vector = first_outputs(stats, image, own, entries)
+    second_image = second_output(
+        info, slot_block, to_owners(*out), diagonal_packed, image, stats, entries
     )
     return (first_image, second_vector, second_image)
 

time: 227 us -> 182 us (0.80)
  waiting for transfers between devices: 63.8 us -> 41.1 us
  Pallas kernels: 92.8 us -> 75.3 us
  starting transfers between devices: 56.1 us -> 51.2 us
    ppermute x57 -> x40, waiting for transfers between devices: 63.8 us -> 41.1 us  [partner(): return lax.ppermute(x, axis, [(i, i ^ k) for i in range(size)])]
    pallas_call x3 -> x4, Pallas kernels: 59.9 us -> 42.8 us  [apply_bonds(): pl.pallas_call(functools.partial(apply_kernel, plan), grid_spec=pltpu.Pre...]
    ppermute x57 -> x40, starting transfers between devices: 56.1 us -> 51.2 us  [partner(): return lax.ppermute(x, axis, [(i, i ^ k) for i in range(size)])]
    pallas_call x2 -> x3, Pallas kernels: 15.5 us -> 14.3 us  [prepare(): pl.pallas_call(prepare_kernel, grid_spec=pltpu.PrefetchScalarGridSpec(num...]
    pallas_call x2 -> x3, Pallas kernels: 6.11 us -> 7.13 us  [the longest x1 3.24 us: second_output(): pl.pallas_call(functools.partial(final_kernel, entries), grid_spec=pltpu....]
    unnamed x87 -> x91, local copies, waits for them, and re-layouts: 6.6 us -> 6.94 us
  transfers between devices with their start and end apart: 57 -> 40, of which waited for: 17 -> 10; matrix products, arithmetic and copies ran while one was open for 2% -> 1% of each run, Pallas kernels for 28% -> 21%
where the time goes in v3:
time: 182 us; the launch traced here: 180 us
  Pallas kernels  75.3 us (41%)
  starting transfers between devices  51.2 us (28%)
  waiting for transfers between devices  41.1 us (23%)
  local copies, waits for them, and re-layouts  9.18 us (5%)
  other arithmetic  2.56 us (1%)
    ppermute x40, starting transfers between devices, partner(): return lax.ppermute(x, axis, [(i, i ^ k) for i in range(size)])  51.2 us
    pallas_call x4, Pallas kernels, apply_bonds(): pl.pallas_call(functools.partial(apply_kernel, plan), grid_spec=pltpu.Pre...  42.8 us
    ppermute x40, waiting for transfers between devices, partner(): return lax.ppermute(x, axis, [(i, i ^ k) for i in range(size)])  41.1 us
    pallas_call x3, Pallas kernels, prepare(): pl.pallas_call(prepare_kernel, grid_spec=pltpu.PrefetchScalarGridSpec(num...  14.3 us
    unnamed x91, local copies, waits for them, and re-layouts  6.94 us
    pallas_call x1, Pallas kernels, pack(): pl.pallas_call(pack_kernel, grid_spec=pltpu.PrefetchScalarGridSpec(num_sc...  5.7 us
  transfers between devices with their start and end apart: 40, of which 10 were waited for; matrix products, arithmetic and copies ran while one was open for 1% of the time, Pallas kernels for 21%

profile of v3, /device:TPU:0, one launch (start us, length us, event | category | flops | bytes accessed | tf_op | source)
XLA Modules:
  0.0 180.4 jit_solution(6694364905112653319)
XLA Ops:
  2.3 4.1 %collective-permute-start.4 = (f32[2,8,16,128]{3,2,1,0:T(8,128)S(1)}, f32[2,8,16,128]{3,2,1,0:T(8,128)S(1)}, u32[]{:S(2)}, u32[]{:S(2)}) collective-permute-start(f32[2,8,16,128]{3,2,1,0:T(8,128)S(1)} %get-tuple-element.78), channel_id=1, source_target_pairs={{0,8},{4,12},{8,0},{12,4},{1,9},{5,13},{9,1},{13,5},{2,10},{6,14},... | collective-permute-start | bytes 393224 | tf_op jit(solution)/shard_map/ppermute | solution.py:554
  8.0 8.4 %collective-permute-done.4.refs_2_ = f32[2,8,16,128]{3,2,1,0:T(8,128)S(1)} collective-permute-done((f32[2,8,16,128]{3,2,1,0:T(8,128)S(1)}, f32[2,8,16,128]{3,2,1,0:T(8,128)S(1)}, u32[]{:S(2)}, u32[]{:S(2)}) %collective-permute-start.4) | collective-permute-done | bytes 131104 | tf_op jit(solution)/shard_map/ppermute | solution.py:554
  16.4 2.9 %collective-permute-start.8 = (f32[2,8,16,128]{3,2,1,0:T(8,128)S(1)}, f32[2,8,16,128]{3,2,1,0:T(8,128)S(1)}, u32[]{:S(2)}, u32[]{:S(2)}) collective-permute-start(f32[2,8,16,128]{3,2,1,0:T(8,128)S(1)} %get-tuple-element.39), channel_id=1, source_target_pairs={{0,12},{4,8},{8,4},{12,0},{1,13},{5,9},{9,5},{13,1},{2,14},{6,10},... | collective-permute-start | bytes 393224 | tf_op jit(solution)/shard_map/ppermute | solution.py:554
  28.4 5.5 %collective-permute-start.2 = (f32[2,8,16,128]{3,2,1,0:T(8,128)S(1)}, f32[2,8,16,128]{3,2,1,0:T(8,128)S(1)}, u32[]{:S(2)}, u32[]{:S(2)}) collective-permute-start(f32[2,8,16,128]{3,2,1,0:T(8,128)S(1)} %get-tuple-element.35), channel_id=1, source_target_pairs={{0,4},{4,0},{8,12},{12,8},{1,5},{5,1},{9,13},{13,9},{2,6},{6,2},{1... | collective-permute-start | bytes 393224 | tf_op jit(solution)/shard_map/ppermute | solution.py:554
  34.5 5.7 %pack.1 = (bf16[8,128,1024]{2,1,0:T(8,128)(2,1)}, f32[8,128,128]{2,1,0:T(8,128)}, f32[8,128,128]{2,1,0:T(8,128)}) custom-call(s32[7]{0:T(128)} %stack.31.info_ref, f32[8,64,1024]{2,1,0:T(8,128)} %own_wave_ref.1, f32[8,64,1024]{2,1,0:T(8,128)} %own_wave_ref.1, f32[8,64,256]{2,1,0:T(8,128)} %diag_ref.1), custom_call_target="tpu_custom_call" | custom-call | tf_op jit(solution)/shard_map/pack/pallas_call | solution.py:139
  44.6 2.4 %collective-permute-start.9 = (f32[2,8,16,128]{3,2,1,0:T(8,128)S(1)}, f32[2,8,16,128]{3,2,1,0:T(8,128)S(1)}, u32[]{:S(2)}, u32[]{:S(2)}) collective-permute-start(f32[2,8,16,128]{3,2,1,0:T(8,128)S(1)} %get-tuple-element.40), channel_id=1, source_target_pairs={{0,12},{4,8},{8,4},{12,0},{1,13},{5,9},{9,5},{13,1},{2,14},{6,10},... | collective-permute-start | bytes 393224 | tf_op jit(solution)/shard_map/ppermute | solution.py:554
  48.5 4.8 %prepare.5 = (bf16[4,8,64,128]{3,2,1,0:T(8,128)(2,1)}, bf16[4,8,64,128]{3,2,1,0:T(8,128)(2,1)}, bf16[8,128,256]{2,1,0:T(8,128)(2,1)}) custom-call(s32[7]{0:T(128)} %stack.31.info_ref, f32[2,8,16,128]{3,2,1,0:T(8,128)} %copy-done.2, f32[2,8,16,128]{3,2,1,0:T(8,128)} %copy-done.15, f32[2,8,16,128]{3,2,1,0:T(8,128)} %copy-done.13, ...), custom_call_target="tpu_custom_call" | custom-call | flops 3300000000 | bytes 1048576 | tf_op jit(solution)/shard_map/prepare/pallas_call | solution.py:232
  56.7 8.5 %apply_bonds.4.refs_7_ = f32[2,8,128,128]{3,2,1,0:T(8,128)} custom-call(s32[7]{0:T(128)} %stack.31.info_ref, s32[6,8]{1,0:T(8,128)} %refs_0_.9, s32[6,8]{1,0:T(8,128)} %copy-done.38, bf16[8,128,1024]{2,1,0:T(8,128)(2,1)} %get-tuple-element.34.refs_2_, bf16[4,8,64,128]{3,2,1,0:T(8,128)(2,1)} %get-tuple-element.47.refs_3_.refs_6_, ...), custom_call_target="tpu_custom_call" | custom-call | flops 8800000000 | bytes 1048576 | tf_op jit(solution)/shard_map/apply_bonds/pallas_call | solution.py:392
  70.0 4.8 %prepare.4 = (bf16[4,8,64,128]{3,2,1,0:T(8,128)(2,1)}, bf16[4,8,64,128]{3,2,1,0:T(8,128)(2,1)}, bf16[8,128,256]{2,1,0:T(8,128)(2,1)}) custom-call(s32[7]{0:T(128)} %stack.31.info_ref, f32[2,8,16,128]{3,2,1,0:T(8,128)} %copy-done.1, f32[2,8,16,128]{3,2,1,0:T(8,128)} %copy-done.12, f32[2,8,16,128]{3,2,1,0:T(8,128)} %copy-done.10, ...), custom_call_target="tpu_custom_call" | custom-call | flops 3300000000 | bytes 1048576 | tf_op jit(solution)/shard_map/prepare/pallas_call | solution.py:232
  74.8 8.9 %apply_bonds.5.refs_7_ = f32[2,8,128,128]{3,2,1,0:T(8,128)} custom-call(s32[7]{0:T(128)} %stack.31.info_ref, s32[6,8]{1,0:T(8,128)} %refs_0_.9, s32[6,8]{1,0:T(8,128)} %copy-done.38, bf16[8,128,1024]{2,1,0:T(8,128)(2,1)} %get-tuple-element.34.refs_2_, bf16[4,8,64,128]{3,2,1,0:T(8,128)(2,1)} %get-tuple-element.44.refs_3_.refs_10_, ...), custom_call_target="tpu_custom_call" | custom-call | flops 8800000000 | bytes 1048576 | tf_op jit(solution)/shard_map/apply_bonds/pallas_call | solution.py:392
  85.2 4.7 %prepare.3 = (bf16[4,8,64,128]{3,2,1,0:T(8,128)(2,1)}, bf16[4,8,64,128]{3,2,1,0:T(8,128)(2,1)}, bf16[8,128,256]{2,1,0:T(8,128)(2,1)}) custom-call(s32[7]{0:T(128)} %stack.31.info_ref, f32[2,8,16,128]{3,2,1,0:T(8,128)} %copy-done.3, f32[2,8,16,128]{3,2,1,0:T(8,128)} %copy-done.23, f32[2,8,16,128]{3,2,1,0:T(8,128)} %copy-done.17, ...), custom_call_target="tpu_custom_call" | custom-call | flops 3300000000 | bytes 1048576 | tf_op jit(solution)/shard_map/prepare/pallas_call | solution.py:232
  89.9 9.1 %apply_bonds.6 = (f32[8,128,128]{2,1,0:T(8,128)}, f32[8,128,128]{2,1,0:T(8,128)}) custom-call(s32[7]{0:T(128)} %stack.31.info_ref, s32[6,8]{1,0:T(8,128)} %refs_0_.9, s32[6,8]{1,0:T(8,128)} %copy-done.38, bf16[8,128,1024]{2,1,0:T(8,128)(2,1)} %get-tuple-element.34.refs_2_, bf16[4,8,64,128]{3,2,1,0:T(8,128)(2,1)} %get-tuple-element.41.refs_3_.refs_14_, ...), custom_call_target="tpu_custom_call" | custom-call | flops 8800000000 | bytes 1048576 | tf_op jit(solution)/shard_map/apply_bonds/pallas_call | solution.py:392
  104.5 2.8 %collective-permute-start.26 = (f32[2,128,128]{2,1,0:T(8,128)S(1)}, f32[2,128,128]{2,1,0:T(8,128)S(1)}, u32[]{:S(2)}, u32[]{:S(2)}) collective-permute-start(f32[2,128,128]{2,1,0:T(8,128)S(1)} %get-tuple-element.72), channel_id=1, source_target_pairs={{0,12},{4,8},{8,4},{12,0},{1,13},{5,9},{9,5},{13,1},{2,14},{6,10},... | collective-permute-start | bytes 393224 | tf_op jit(solution)/shard_map/ppermute | solution.py:554
  107.9 2.3 %collective-permute-done.24.a1 = f32[2,128,128]{2,1,0:T(8,128)S(1)} collective-permute-done((f32[2,128,128]{2,1,0:T(8,128)S(1)}, f32[2,128,128]{2,1,0:T(8,128)S(1)}, u32[]{:S(2)}, u32[]{:S(2)}) %collective-permute-start.24) | collective-permute-done | bytes 131104 | tf_op jit(solution)/shard_map/ppermute | solution.py:554
  110.2 6.4 %collective-permute-done.25.a2 = f32[2,128,128]{2,1,0:T(8,128)S(1)} collective-permute-done((f32[2,128,128]{2,1,0:T(8,128)S(1)}, f32[2,128,128]{2,1,0:T(8,128)S(1)}, u32[]{:S(2)}, u32[]{:S(2)}) %collective-permute-start.25) | collective-permute-done | bytes 131104 | tf_op jit(solution)/shard_map/ppermute | solution.py:554
  117.3 3.3 %owner_image.1 = (f32[8,128,128]{2,1,0:T(8,128)}, f32[8,128]{1,0:T(8,128)}) custom-call(s32[7]{0:T(128)} %stack.31.info_ref, s32[4,2]{1,0:T(4,128)} %copy.21.owner_ref, f32[2,128,128]{2,1,0:T(8,128)} %get-tuple-element.75.a0, f32[2,128,128]{2,1,0:T(8,128)} %copy-done.34, f32[2,128,128]{2,1,0:T(8,128)} %copy-done.35, f32[2,128,128]{2,1,0:T(8,128)} %copy-done.36, ...), custom_call_target="tpu_custom_call" | custom-call | flops 3300000000 | bytes 1048576 | tf_op jit(solution)/shard_map/owner_image/pallas_call | solution.py:459
  121.1 10.7 %collective-permute-done.30.refs_3_ = f32[8,128,128]{2,1,0:T(8,128)S(1)} collective-permute-done((f32[8,128,128]{2,1,0:T(8,128)}, f32[8,128,128]{2,1,0:T(8,128)S(1)}, u32[]{:S(2)}, u32[]{:S(2)}) %collective-permute-start.30) | collective-permute-done | bytes 524320 | tf_op jit(solution)/shard_map/ppermute | solution.py:554
  133.7 2.5 %collective-permute-done.28.refs_2_ = f32[8,128]{1,0:T(8,128)S(1)} collective-permute-done((f32[8,128]{1,0:T(8,128)}, f32[8,128]{1,0:T(8,128)S(1)}, u32[]{:S(2)}, u32[]{:S(2)}) %collective-permute-start.28) | collective-permute-done | bytes 4128 | tf_op jit(solution)/shard_map/ppermute | solution.py:554
  138.5 16.4 %apply_bonds.7 = (f32[8,128,128]{2,1,0:T(8,128)}, f32[8,128,128]{2,1,0:T(8,128)}) custom-call(s32[7]{0:T(128)} %stack.31.info_ref, s32[6,8]{1,0:T(8,128)} %refs_0_.9, s32[6,8]{1,0:T(8,128)} %copy-done.38, f32[8,128,128]{2,1,0:T(8,128)} %get-tuple-element.56.refs_2_.image_ref, f32[8,128,128]{2,1,0:T(8,128)} %copy-done.7, f32[8,128,128]{2,1,0:T(8,128)} %copy-done.8, ...), custom_call_target="tpu_custom_call" | custom-call | flops 26400000000 | bytes 1048576 | tf_op jit(solution)/shard_map/apply_bonds/pallas_call | solution.py:392
  156.3 3.5 %collective-permute-start.33 = (f32[8,128]{1,0:T(8,128)}, f32[8,128]{1,0:T(8,128)S(1)}, u32[]{:S(2)}, u32[]{:S(2)}) collective-permute-start(f32[8,128]{1,0:T(8,128)} %merge.1.s0), channel_id=1, source_target_pairs={{0,4},{4,0},{8,12},{12,8},{1,5},{5,1},{9,13},{13,9},{2,6},{6,2},{1... | collective-permute-start | bytes 12296 | tf_op jit(solution)/shard_map/ppermute | solution.py:554
  160.0 2.3 %collective-permute-start.35 = (f32[8,128]{1,0:T(8,128)}, f32[8,128]{1,0:T(8,128)S(1)}, u32[]{:S(2)}, u32[]{:S(2)}) collective-permute-start(f32[8,128]{1,0:T(8,128)} %merge.1.s0), channel_id=1, source_target_pairs={{0,12},{4,8},{8,4},{12,0},{1,13},{5,9},{9,5},{13,1},{2,14},{6,10},... | collective-permute-start | bytes 12296 | tf_op jit(solution)/shard_map/ppermute | solution.py:554
  168.5 2.5 %first_outputs.1 = (f32[8,64,256]{2,1,0:T(8,128)}, f32[8,64,256]{2,1,0:T(8,128)}) custom-call(f32[8,128]{1,0:T(8,128)} %merge.1.s0, f32[8,128]{1,0:T(8,128)} %copy-done.39, f32[8,128]{1,0:T(8,128)} %copy-done.40, f32[8,128]{1,0:T(8,128)} %copy-done.41, f32[8,128,128]{2,1,0:T(8,128)} %get-tuple-element.56.refs_2_.image_ref, ...), custom_call_target="tpu_custom_call" | custom-call | flops 3300000000 | bytes 1048576 | tf_op jit(solution)/shard_map/first_outputs/pallas_call | solution.py:511
  171.1 5.4 %collective-permute-done.38.a2 = f32[2,128,128]{2,1,0:T(8,128)S(1)} collective-permute-done((f32[2,128,128]{2,1,0:T(8,128)S(1)}, f32[2,128,128]{2,1,0:T(8,128)S(1)}, u32[]{:S(2)}, u32[]{:S(2)}) %collective-permute-start.38) | collective-permute-done | bytes 131104 | tf_op jit(solution)/shard_map/ppermute | solution.py:554
  177.2 3.2 %second_output.1 = f32[8,64,256]{2,1,0:T(8,128)} custom-call(s32[7]{0:T(128)} %stack.31.info_ref, s32[4,2]{1,0:T(4,128)} %copy.21.owner_ref, f32[2,128,128]{2,1,0:T(8,128)} %get-tuple-element.71.a0, f32[2,128,128]{2,1,0:T(8,128)} %copy-done.30, f32[2,128,128]{2,1,0:T(8,128)} %copy-done.32, f32[2,128,128]{2,1,0:T(8,128)} %copy-done.33, ...), custom_call_target="tpu_custom_call" | custom-call | flops 3300000000 | bytes 1048576 | tf_op jit(solution)/shard_map/second_output/pallas_call | solution.py:536
  (167 shorter events, 48.6 us)
Async XLA Ops:
  2.3 14.1 %collective-permute-start.4 = (f32[2,8,16,128]{3,2,1,0:T(8,128)S(1)}, f32[2,8,16,128]{3,2,1,0:T(8,128)S(1)}, u32[]{:S(2)}, u32[]{:S(2)}) collective-permute-start(f32[2,8,16,128]{3,2,1,0:T(8,128)S(1)} %get-tuple-element.78), channel_id=1, source_target_pairs={{0,8},{4,12},{8,0},{12,4},{1,9},{5,13},{9,1},{13,5},{2,10},{6,14},... | collective-permute-start | bytes 393224 | tf_op jit(solution)/shard_map/ppermute | solution.py:554
  7.7 13.6 %collective-permute-start.1 = (f32[2,8,16,128]{3,2,1,0:T(8,128)S(1)}, f32[2,8,16,128]{3,2,1,0:T(8,128)S(1)}, u32[]{:S(2)}, u32[]{:S(2)}) collective-permute-start(f32[2,8,16,128]{3,2,1,0:T(8,128)S(1)} %get-tuple-element.79), channel_id=1, source_target_pairs={{0,4},{4,0},{8,12},{12,8},{1,5},{5,1},{9,13},{13,9},{2,6},{6,2},{1... | collective-permute-start | bytes 393224 | tf_op jit(solution)/shard_map/ppermute | solution.py:554
  16.4 12.1 %collective-permute-start.8 = (f32[2,8,16,128]{3,2,1,0:T(8,128)S(1)}, f32[2,8,16,128]{3,2,1,0:T(8,128)S(1)}, u32[]{:S(2)}, u32[]{:S(2)}) collective-permute-start(f32[2,8,16,128]{3,2,1,0:T(8,128)S(1)} %get-tuple-element.39), channel_id=1, source_target_pairs={{0,12},{4,8},{8,4},{12,0},{1,13},{5,9},{9,5},{13,1},{2,14},{6,10},... | collective-permute-start | bytes 393224 | tf_op jit(solution)/shard_map/ppermute | solution.py:554
  20.7 21.7 %collective-permute-start.19 = (f32[2,8,16,128]{3,2,1,0:T(8,128)S(1)}, f32[2,8,16,128]{3,2,1,0:T(8,128)S(1)}, u32[]{:S(2)}, u32[]{:S(2)}) collective-permute-start(f32[2,8,16,128]{3,2,1,0:T(8,128)S(1)} %get-tuple-element.76.refs_0_), channel_id=1, source_target_pairs={{0,2},{2,0},{1,3},{3,1},{4,6},{6,4},{5,7},{7,5},{8,10},{10,8},{9,1... | collective-permute-start | bytes 393224 | tf_op jit(solution)/shard_map/ppermute | solution.py:554
  21.3 22.7 %collective-permute-start.20 = (f32[2,8,16,128]{3,2,1,0:T(8,128)S(1)}, f32[2,8,16,128]{3,2,1,0:T(8,128)S(1)}, u32[]{:S(2)}, u32[]{:S(2)}) collective-permute-start(f32[2,8,16,128]{3,2,1,0:T(8,128)S(1)} %collective-permute-done.1.refs_1_), channel_id=1, source_target_pairs={{0,2},{2,0},{1,3},{3,1},{4,6},{6,4},{5,7},{7,5},{8,10},{10,8},{9,1... | collective-permute-start | bytes 393224 | tf_op jit(solution)/shard_map/ppermute | solution.py:554
  23.9 20.7 %collective-permute-start.21 = (f32[2,8,16,128]{3,2,1,0:T(8,128)S(1)}, f32[2,8,16,128]{3,2,1,0:T(8,128)S(1)}, u32[]{:S(2)}, u32[]{:S(2)}) collective-permute-start(f32[2,8,16,128]{3,2,1,0:T(8,128)S(1)} %collective-permute-done.4.refs_2_), channel_id=1, source_target_pairs={{0,2},{2,0},{1,3},{3,1},{4,6},{6,4},{5,7},{7,5},{8,10},{10,8},{9,1... | collective-permute-start | bytes 393224 | tf_op jit(solution)/shard_map/ppermute | solution.py:554
  26.9 17.6 %collective-permute-start.22 = (f32[2,8,16,128]{3,2,1,0:T(8,128)S(1)}, f32[2,8,16,128]{3,2,1,0:T(8,128)S(1)}, u32[]{:S(2)}, u32[]{:S(2)}) collective-permute-start(f32[2,8,16,128]{3,2,1,0:T(8,128)S(1)} %collective-permute-done.7.refs_3_), channel_id=1, source_target_pairs={{0,2},{2,0},{1,3},{3,1},{4,6},{6,4},{5,7},{7,5},{8,10},{10,8},{9,1... | collective-permute-start | bytes 393224 | tf_op jit(solution)/shard_map/ppermute | solution.py:554
  28.4 18.5 %collective-permute-start.2 = (f32[2,8,16,128]{3,2,1,0:T(8,128)S(1)}, f32[2,8,16,128]{3,2,1,0:T(8,128)S(1)}, u32[]{:S(2)}, u32[]{:S(2)}) collective-permute-start(f32[2,8,16,128]{3,2,1,0:T(8,128)S(1)} %get-tuple-element.35), channel_id=1, source_target_pairs={{0,4},{4,0},{8,12},{12,8},{1,5},{5,1},{9,13},{13,9},{2,6},{6,2},{1... | collective-permute-start | bytes 393224 | tf_op jit(solution)/shard_map/ppermute | solution.py:554
  42.4 10.9 %collective-permute-start = (s32[6,8]{1,0:T(8,128)S(1)}, s32[6,8]{1,0:T(8,128)S(1)}, u32[]{:S(2)}, u32[]{:S(2)}) collective-permute-start(s32[6,8]{1,0:T(8,128)S(1)} %copy-done.37), channel_id=1, source_target_pairs={{0,2},{2,0},{1,3},{3,1},{4,6},{6,4},{5,7},{7,5},{8,10},{10,8},{9,1... | collective-permute-start | bytes 584 | tf_op jit(solution)/shard_map/ppermute | solution.py:554
  44.6 21.2 %collective-permute-start.6 = (f32[2,8,16,128]{3,2,1,0:T(8,128)S(1)}, f32[2,8,16,128]{3,2,1,0:T(8,128)S(1)}, u32[]{:S(2)}, u32[]{:S(2)}) collective-permute-start(f32[2,8,16,128]{3,2,1,0:T(8,128)S(1)} %get-tuple-element.38), channel_id=1, source_target_pairs={{0,8},{4,12},{8,0},{12,4},{1,9},{5,13},{9,1},{13,5},{2,10},{6,14},... | collective-permute-start | bytes 393224 | tf_op jit(solution)/shard_map/ppermute | solution.py:554
  44.6 22.8 %collective-permute-start.9 = (f32[2,8,16,128]{3,2,1,0:T(8,128)S(1)}, f32[2,8,16,128]{3,2,1,0:T(8,128)S(1)}, u32[]{:S(2)}, u32[]{:S(2)}) collective-permute-start(f32[2,8,16,128]{3,2,1,0:T(8,128)S(1)} %get-tuple-element.40), channel_id=1, source_target_pairs={{0,12},{4,8},{8,4},{12,0},{1,13},{5,9},{9,5},{13,1},{2,14},{6,10},... | collective-permute-start | bytes 393224 | tf_op jit(solution)/shard_map/ppermute | solution.py:554
  53.3 14.5 %collective-permute-start.3 = (f32[2,8,16,128]{3,2,1,0:T(8,128)S(1)}, f32[2,8,16,128]{3,2,1,0:T(8,128)S(1)}, u32[]{:S(2)}, u32[]{:S(2)}) collective-permute-start(f32[2,8,16,128]{3,2,1,0:T(8,128)S(1)} %get-tuple-element.36), channel_id=1, source_target_pairs={{0,4},{4,0},{8,12},{12,8},{1,5},{5,1},{9,13},{13,9},{2,6},{6,2},{1... | collective-permute-start | bytes 393224 | tf_op jit(solution)/shard_map/ppermute | solution.py:554
  54.5 10.7 %collective-permute-start.17 = (f32[2,8,16,128]{3,2,1,0:T(8,128)S(1)}, f32[2,8,16,128]{3,2,1,0:T(8,128)S(1)}, u32[]{:S(2)}, u32[]{:S(2)}) collective-permute-start(f32[2,8,16,128]{3,2,1,0:T(8,128)S(1)} %collective-permute-done.5.refs_2_), channel_id=1, source_target_pairs={{0,2},{2,0},{1,3},{3,1},{4,6},{6,4},{5,7},{7,5},{8,10},{10,8},{9,1... | collective-permute-start | bytes 393224 | tf_op jit(solution)/shard_map/ppermute | solution.py:554
  55.1 14.3 %collective-permute-start.18 = (f32[2,8,16,128]{3,2,1,0:T(8,128)S(1)}, f32[2,8,16,128]{3,2,1,0:T(8,128)S(1)}, u32[]{:S(2)}, u32[]{:S(2)}) collective-permute-start(f32[2,8,16,128]{3,2,1,0:T(8,128)S(1)} %collective-permute-done.8.refs_3_), channel_id=1, source_target_pairs={{0,2},{2,0},{1,3},{3,1},{4,6},{6,4},{5,7},{7,5},{8,10},{10,8},{9,1... | collective-permute-start | bytes 393224 | tf_op jit(solution)/shard_map/ppermute | solution.py:554
  65.3 18.5 %collective-permute-start.10 = (f32[2,8,16,128]{3,2,1,0:T(8,128)S(1)}, f32[2,8,16,128]{3,2,1,0:T(8,128)S(1)}, u32[]{:S(2)}, u32[]{:S(2)}) collective-permute-start(f32[2,8,16,128]{3,2,1,0:T(8,128)S(1)} %get-tuple-element.87.refs_0_), channel_id=1, source_target_pairs={{0,2},{2,0},{1,3},{3,1},{4,6},{6,4},{5,7},{7,5},{8,10},{10,8},{9,1... | collective-permute-start | bytes 393224 | tf_op jit(solution)/shard_map/ppermute | solution.py:554
  65.8 17.9 %collective-permute-start.12 = (f32[2,8,16,128]{3,2,1,0:T(8,128)S(1)}, f32[2,8,16,128]{3,2,1,0:T(8,128)S(1)}, u32[]{:S(2)}, u32[]{:S(2)}) collective-permute-start(f32[2,8,16,128]{3,2,1,0:T(8,128)S(1)} %collective-permute-done.6.refs_2_), channel_id=1, source_target_pairs={{0,2},{2,0},{1,3},{3,1},{4,6},{6,4},{5,7},{7,5},{8,10},{10,8},{9,1... | collective-permute-start | bytes 393224 | tf_op jit(solution)/shard_map/ppermute | solution.py:554
  67.4 16.4 %collective-permute-start.13 = (f32[2,8,16,128]{3,2,1,0:T(8,128)S(1)}, f32[2,8,16,128]{3,2,1,0:T(8,128)S(1)}, u32[]{:S(2)}, u32[]{:S(2)}) collective-permute-start(f32[2,8,16,128]{3,2,1,0:T(8,128)S(1)} %collective-permute-done.9.refs_3_), channel_id=1, source_target_pairs={{0,2},{2,0},{1,3},{3,1},{4,6},{6,4},{5,7},{7,5},{8,10},{10,8},{9,1... | collective-permute-start | bytes 393224 | tf_op jit(solution)/shard_map/ppermute | solution.py:554
  67.9 15.9 %collective-permute-start.11 = (f32[2,8,16,128]{3,2,1,0:T(8,128)S(1)}, f32[2,8,16,128]{3,2,1,0:T(8,128)S(1)}, u32[]{:S(2)}, u32[]{:S(2)}) collective-permute-start(f32[2,8,16,128]{3,2,1,0:T(8,128)S(1)} %collective-permute-done.3.refs_1_), channel_id=1, source_target_pairs={{0,2},{2,0},{1,3},{3,1},{4,6},{6,4},{5,7},{7,5},{8,10},{10,8},{9,1... | collective-permute-start | bytes 393224 | tf_op jit(solution)/shard_map/ppermute | solution.py:554
  103.8 12.8 %collective-permute-start.25 = (f32[2,128,128]{2,1,0:T(8,128)S(1)}, f32[2,128,128]{2,1,0:T(8,128)S(1)}, u32[]{:S(2)}, u32[]{:S(2)}) collective-permute-start(f32[2,128,128]{2,1,0:T(8,128)S(1)} %get-tuple-element.73), channel_id=1, source_target_pairs={{0,8},{4,12},{8,0},{12,4},{1,9},{5,13},{9,1},{13,5},{2,10},{6,14},... | collective-permute-start | bytes 393224 | tf_op jit(solution)/shard_map/ppermute | solution.py:554
  104.5 12.1 %collective-permute-start.26 = (f32[2,128,128]{2,1,0:T(8,128)S(1)}, f32[2,128,128]{2,1,0:T(8,128)S(1)}, u32[]{:S(2)}, u32[]{:S(2)}) collective-permute-start(f32[2,128,128]{2,1,0:T(8,128)S(1)} %get-tuple-element.72), channel_id=1, source_target_pairs={{0,12},{4,8},{8,4},{12,0},{1,13},{5,9},{9,5},{13,1},{2,14},{6,10},... | collective-permute-start | bytes 393224 | tf_op jit(solution)/shard_map/ppermute | solution.py:554
  120.6 11.2 %collective-permute-start.30 = (f32[8,128,128]{2,1,0:T(8,128)}, f32[8,128,128]{2,1,0:T(8,128)S(1)}, u32[]{:S(2)}, u32[]{:S(2)}) collective-permute-start(f32[8,128,128]{2,1,0:T(8,128)} %get-tuple-element.56.refs_2_.image_ref), channel_id=1, source_target_pairs={{0,2},{2,0},{1,3},{3,1},{4,6},{6,4},{5,7},{7,5},{8,10},{10,8},{9,1... | collective-permute-start | bytes 1572872 | tf_op jit(solution)/shard_map/ppermute | solution.py:554
  121.1 15.8 %collective-permute-start.31 = (f32[8,128,128]{2,1,0:T(8,128)}, f32[8,128,128]{2,1,0:T(8,128)S(1)}, u32[]{:S(2)}, u32[]{:S(2)}) collective-permute-start(f32[8,128,128]{2,1,0:T(8,128)} %get-tuple-element.56.refs_2_.image_ref), channel_id=1, source_target_pairs={{0,1},{1,0},{2,3},{3,2},{4,5},{5,4},{6,7},{7,6},{8,9},{9,8},{10,11... | collective-permute-start | bytes 1572872 | tf_op jit(solution)/shard_map/ppermute | solution.py:554
  164.1 12.4 %collective-permute-start.38 = (f32[2,128,128]{2,1,0:T(8,128)S(1)}, f32[2,128,128]{2,1,0:T(8,128)S(1)}, u32[]{:S(2)}, u32[]{:S(2)}) collective-permute-start(f32[2,128,128]{2,1,0:T(8,128)S(1)} %get-tuple-element.69), channel_id=1, source_target_pairs={{0,8},{4,12},{8,0},{12,4},{1,9},{5,13},{9,1},{13,5},{2,10},{6,14},... | collective-permute-start | bytes 393224 | tf_op jit(solution)/shard_map/ppermute | solution.py:554
  165.1 11.4 %collective-permute-start.39 = (f32[2,128,128]{2,1,0:T(8,128)S(1)}, f32[2,128,128]{2,1,0:T(8,128)S(1)}, u32[]{:S(2)}, u32[]{:S(2)}) collective-permute-start(f32[2,128,128]{2,1,0:T(8,128)S(1)} %get-tuple-element.68), channel_id=1, source_target_pairs={{0,12},{4,8},{8,4},{12,0},{1,13},{5,9},{9,5},{13,1},{2,14},{6,10},... | collective-permute-start | bytes 393224 | tf_op jit(solution)/shard_map/ppermute | solution.py:554
  (61 other events, 556.4 us)

commit v4 on v3

--- a/solution.py
+++ b/solution.py
@@ -11,8 +11,8 @@
 SUB = 8
 PHYS = 16
 TINY = 1e-30
-GROUPS = 3
-VMEM_LIMIT = 56 * 1024 * 1024
+GROUPS = 2
+VMEM_LIMIT = 62 * 1024 * 1024
 
 
 def plain_apply(vector_full, environment, bond_terms, term_slot, slot_block, diagonal):
@@ -104,12 +104,12 @@
     return jnp.concatenate([upright[: LANES // 2], upright[LANES // 2 :]], axis=1)
 
 
-def store_vector(parts, j, rows_of, put):
+def store_vector(parts, rows_of, put):
     first = lane_is_first(SUB)
     for pair in range(PHYS // 2):
         for part, row in zip(parts, rows_of):
-            even = part[j, pl.ds(2 * pair, SUB, stride=PHYS), :]
-            odd = part[j, pl.ds(2 * pair + 1, SUB, stride=PHYS), :]
+            even = part[pl.ds(2 * pair, SUB, stride=PHYS), :]
+            odd = part[pl.ds(2 * pair + 1, SUB, stride=PHYS), :]
             upper = jnp.where(first, even, pltpu.roll(odd, LANES // 2, 1))
             lower = jnp.where(first, pltpu.roll(even, LANES // 2, 1), odd)
             high, low = split_two(jnp.concatenate([upper, lower], axis=0))
@@ -129,7 +129,7 @@
             vec_ref[j, row : row + 16, columns] = high
             vec_ref[j, row + half : row + half + 16, columns] = low
 
-        store_vector([tiles.at[q] for q in range(4)], j, [16 * q for q in range(4)], put)
+        store_vector([tiles.at[q, j] for q in range(4)], [16 * q for q in range(4)], put)
 
 
 def pack(info, wavefunction, diagonal):
@@ -155,6 +155,7 @@
             jax.ShapeDtypeStruct((blocks, LANES, LANES), jnp.float32),
         ],
         compiler_params=pltpu.CompilerParams(vmem_limit_bytes=VMEM_LIMIT),
+        cost_estimate=micros(5),
         name="pack",
     )(info, wavefunction, wavefunction, diagonal)
 
@@ -168,18 +169,16 @@
     row = lax.broadcasted_iota(jnp.int32, (LANES, LANES), 0) // PHYS
     column = lax.broadcasted_iota(jnp.int32, (LANES, LANES), 1) % SUB
     same = row == column
-    per = sources[0].shape[0] // GROUPS
     at = 0
-    for group in range(GROUPS):
-        for source in sources:
-            for k in range(per):
-                for place, term in enumerate(split_two(source[group * per + k].T)):
-                    wide = jnp.dot(term, spread, preferred_element_type=jnp.float32)
-                    tall = jnp.concatenate([wide] * SUB, axis=0)
-                    out_ref[at, :, place * LANES : (place + 1) * LANES] = jnp.where(
-                        same, tall, 0.0
-                    ).astype(jnp.bfloat16)
-                at += 1
+    for source in sources:
+        for k in range(source.shape[0]):
+            for place, term in enumerate(split_two(source[k].T)):
+                wide = jnp.dot(term, spread, preferred_element_type=jnp.float32)
+                tall = jnp.concatenate([wide] * SUB, axis=0)
+                out_ref[at, :, place * LANES : (place + 1) * LANES] = jnp.where(
+                    same, tall, 0.0
+                ).astype(jnp.bfloat16)
+            at += 1
 
 
 def mixing_operand(sources):
@@ -188,97 +187,161 @@
         mixing_kernel,
         out_shape=jax.ShapeDtypeStruct((count, LANES, 2 * LANES), jnp.bfloat16),
         compiler_params=pltpu.CompilerParams(vmem_limit_bytes=VMEM_LIMIT),
+        cost_estimate=micros(2),
         name="mixing",
     )(*sources)
 
 
-def prepare_kernel(info_ref, *refs):
-    sources, (left_high, left_low, right_out, blocks_ref) = refs[:-4], refs[-4:]
-    zs = 4
-    per, blocks, rows, lanes = sources[0].shape
-    half = lanes // 2
+def store_right(columns, count, right_out, j):
+    used = 32 * count
+    high, low = split_two(columns.T[:used])
+    right_out[j, 0:used, 0:LANES] = jnp.concatenate([high, high], axis=1)
+    right_out[j, 0:used, LANES:] = jnp.concatenate([low, low], axis=1)
+
+
+def own_operands_kernel(info_ref, *refs):
+    pieces, (left_high, left_low, right_out, send, blocks_ref) = refs[:4], refs[4:]
+    per, blocks, half, lanes = left_high.shape
+    rows = half // 4
     wide = half // 2
     first = lane_is_first(half)
-    lane = lax.broadcasted_iota(jnp.int32, (half, lanes), 1)
+    first_wide = lane_is_first(wide)
+    lane = lax.broadcasted_iota(jnp.int32, (half, lanes), 1) // wide
+    lane_rows = lax.broadcasted_iota(jnp.int32, (rows, lanes), 1) // wide
     start = info_ref[6] * wide
-    count = lanes // wide
-    pairs = [(s, k) for s in range(len(sources) // zs) for k in range(per)]
+    other = wide - start
     for j in range(blocks):
-        for base in range(0, len(pairs), count):
-            group = pairs[base : base + count]
-            columns = jnp.zeros((half, lanes), jnp.float32)
-            for at, (s, k) in enumerate(group):
-                for z in range(zs):
-                    row = pl.multiple_of((info_ref[4] ^ z) * rows, rows)
-                    blocks_ref[base + at, j, pl.ds(row, rows), :] = sources[s * zs + z][k, j]
-                block = blocks_ref[base + at, j]
-                high, low = split_two(jnp.where(first, block, pltpu.roll(block, half, 1)))
-                left_high[base + at, j] = high
-                left_low[base + at, j] = low
-                shift = lax.rem(wide * at + lanes + half - start, lanes)
-                columns = jnp.where(lane // wide == at, pltpu.roll(block, shift, 1), columns)
-            upright = columns.T[: wide * len(group)]
-            high, low = split_two(upright)
-            where = pl.ds(wide * base, wide * len(group))
-            right_out[j, where, 0:lanes] = jnp.concatenate([high, high], axis=1)
-            right_out[j, where, lanes : 2 * lanes] = jnp.concatenate([low, low], axis=1)
-
-
-def prepare(info, sources):
-    per, blocks, rows, lanes = sources[0].shape
-    total = per * len(sources) // 4
+        columns = jnp.zeros((half, lanes), jnp.float32)
+        for w in range(per):
+            for z in range(4):
+                row = pl.multiple_of((info_ref[4] ^ z) * rows, rows)
+                piece = pieces[z][w, 0, j] if z == 0 else pieces[z][w, j]
+                blocks_ref[w, j, pl.ds(row, rows), :] = piece
+            block = blocks_ref[w, j]
+            turned = pltpu.roll(block, half, 1)
+            high, low = split_two(jnp.where(first, block, turned))
+            left_high[w, j] = high
+            left_low[w, j] = low
+            send[w, j, 0:wide] = jnp.where(first_wide, block[:wide], turned[wide:])
+            mine = pltpu.roll(block, lax.rem(wide * w + lanes + half - start, lanes), 1)
+            columns = jnp.where(lane == w, mine, columns)
+            packed = jnp.zeros((rows, lanes), jnp.float32)
+            for g in range(4):
+                shift = lax.rem(wide * g + lanes + half - other, lanes)
+                theirs = pltpu.roll(block[rows * g : rows * (g + 1)], shift, 1)
+                packed = jnp.where(lane_rows == g, theirs, packed)
+            send[w, j, wide : wide + rows] = packed
+        store_right(columns, per, right_out, j)
+
+
+def other_operands_kernel(sent, left_high, left_low, right_out):
+    per, blocks, half, lanes = left_high.shape
+    rows = half // 4
+    wide = half // 2
+    first = lane_is_first(wide)
+    lane_rows = lax.broadcasted_iota(jnp.int32, (rows, lanes), 1) // wide
+    for j in range(blocks):
+        columns = [jnp.zeros((rows, lanes), jnp.float32) for _ in range(4)]
+        for w in range(per):
+            both = sent[w, j, 0:wide]
+            turned = pltpu.roll(both, half, 1)
+            full = jnp.concatenate(
+                [jnp.where(first, both, turned), jnp.where(first, turned, both)], axis=0
+            )
+            high, low = split_two(full)
+            left_high[w, j] = high
+            left_low[w, j] = low
+            packed = sent[w, j, wide : wide + rows]
+            for g in range(4):
+                shift = (wide * (w - g)) % lanes
+                moved = pltpu.roll(packed, shift, 1) if shift else packed
+                columns[g] = jnp.where(lane_rows == w, moved, columns[g])
+        store_right(jnp.concatenate(columns, axis=0), per, right_out, j)
+
+
+def operand_specs(per, step, half, lanes):
+    return [
+        pl.BlockSpec((per, step, half, lanes), lambda i, *_: (0, i, 0, 0)),
+        pl.BlockSpec((per, step, half, lanes), lambda i, *_: (0, i, 0, 0)),
+        pl.BlockSpec((step, per * 32, 2 * lanes), lambda i, *_: (i, 0, 0)),
+    ]
+
+
+def operand_shapes(per, blocks, half, lanes):
+    return [
+        jax.ShapeDtypeStruct((per, blocks, half, lanes), jnp.bfloat16),
+        jax.ShapeDtypeStruct((per, blocks, half, lanes), jnp.bfloat16),
+        jax.ShapeDtypeStruct((blocks, per * 32, 2 * lanes), jnp.bfloat16),
+    ]
+
+
+def own_operands(info, by_owner, group, pieces):
+    per, blocks, rows, lanes = pieces[0].shape
     half = lanes // 2
-    step = 2
-    return pl.pallas_call(
-        prepare_kernel,
+    step = 4
+    return pl.pallas_call(
+        own_operands_kernel,
         grid_spec=pltpu.PrefetchScalarGridSpec(
             num_scalar_prefetch=1,
             grid=(blocks // step,),
             in_specs=[
-                pl.BlockSpec((per, step, rows, lanes), lambda i, *_: (0, i, 0, 0))
-                for _ in sources
-            ],
-            out_specs=[
-                pl.BlockSpec((total, step, half, lanes), lambda i, *_: (0, i, 0, 0)),
-                pl.BlockSpec((total, step, half, lanes), lambda i, *_: (0, i, 0, 0)),
-                pl.BlockSpec((step, total * 32, 2 * lanes), lambda i, *_: (i, 0, 0)),
-            ],
-            scratch_shapes=[pltpu.VMEM((total, step, half, lanes), jnp.float32)],
+                pl.BlockSpec(
+                    (per, 1, step, rows, lanes), lambda i, info: (group, info[4], i, 0, 0)
+                )
+            ]
+            + [pl.BlockSpec((per, step, rows, lanes), lambda i, *_: (0, i, 0, 0))] * 3,
+            out_specs=operand_specs(per, step, half, lanes)
+            + [pl.BlockSpec((per, step, 3 * rows, lanes), lambda i, *_: (0, i, 0, 0))],
+            scratch_shapes=[pltpu.VMEM((per, step, half, lanes), jnp.float32)],
         ),
-        out_shape=[
-            jax.ShapeDtypeStruct((total, blocks, half, lanes), jnp.bfloat16),
-            jax.ShapeDtypeStruct((total, blocks, half, lanes), jnp.bfloat16),
-            jax.ShapeDtypeStruct((blocks, total * 32, 2 * lanes), jnp.bfloat16),
-        ],
+        out_shape=operand_shapes(per, blocks, half, lanes)
+        + [jax.ShapeDtypeStruct((per, blocks, 3 * rows, lanes), jnp.float32)],
         compiler_params=pltpu.CompilerParams(vmem_limit_bytes=VMEM_LIMIT),
         cost_estimate=micros(3),
-        name="prepare",
-    )(info, *sources)
+        name="own_operands",
+    )(info, by_owner, *pieces)
+
+
+def other_operands(sent):
+    per, blocks, rows, lanes = sent.shape
+    half = lanes // 2
+    step = 4
+    return pl.pallas_call(
+        other_operands_kernel,
+        grid=(blocks // step,),
+        in_specs=[pl.BlockSpec((per, step, rows, lanes), lambda i: (0, i, 0, 0))],
+        out_specs=operand_specs(per, step, half, lanes),
+        out_shape=operand_shapes(per, blocks, half, lanes),
+        compiler_params=pltpu.CompilerParams(vmem_limit_bytes=VMEM_LIMIT),
+        cost_estimate=micros(3),
+        name="other_operands",
+    )(sent)
 
 
 def apply_kernel(plan, info_ref, *refs):
-    groups, parts_given, before_given, pieces = plan
+    chunks, parts_given, before_given, pieces = plan
     refs = list(refs)
     take = lambda n: [refs.pop(0) for _ in range(n)]
     slots = take(2)
     vector = take(4 if parts_given else 1)
-    operands = [take(4) for _ in groups]
+    operands = [take(4) for _ in chunks]
     before = take(1) if before_given else None
     outs = take(2 if pieces else 1)
     total_ref, vec, mid = refs
-    step = vector[0].shape[0]
+    step = mid.shape[0]
     lanes, half = LANES, LANES // 2
     first = lane_is_first(SUB)
     first_half = lane_is_first(half)
     keep_first = jnp.where(first_half, 1.0, 0.0).astype(jnp.bfloat16)
     keep_second = jnp.where(first_half, 0.0, 1.0).astype(jnp.bfloat16)
+    nothing = jnp.zeros((lanes, lanes), jnp.bfloat16)
     me = info_ref[4]
 
     @pl.when(pl.program_id(0) == 0)
     def _():
         total_ref[...] = before[0][...] if before_given else jnp.zeros_like(total_ref)
 
-    for j in range(step):
+    def right_side(j):
         if parts_given:
 
             def put(row, pair, high, low):
@@ -287,7 +350,7 @@
                 vec[j, pl.ds(row + half, 16), columns] = low
 
             rows_of = [pl.multiple_of(info_ref[g] * 16, 16) for g in range(4)]
-            store_vector(vector, j, rows_of, put)
+            store_vector([x.at[pl.ds(j * lanes, lanes)] for x in vector], rows_of, put)
             source = vec[j]
         else:
             source = vector[0][j]
@@ -300,13 +363,13 @@
             )
             at += count
 
-    def left_and_right(refs_of, w, base):
+    def left_side(js, refs_of, w, row_of):
         left_high, left_low, right, mix = refs_of
         done = {}
-        for j in range(step):
+        for j in js:
             tiles = []
             for part in range(2):
-                row = (base + w) * 32 + part * 16
+                row = row_of + part * 16
                 for pair in range(PHYS // 2):
                     columns = slice(pair * lanes, (pair + 1) * lanes)
                     upper = mid[j, row : row + SUB, columns]
@@ -317,19 +380,26 @@
             lh, ll = left_high[w, j], left_low[w, j]
             wide_high = jnp.concatenate([lh * keep_first, lh * keep_second], axis=0)
             wide_low = jnp.concatenate([ll * keep_first, ll * keep_second], axis=0)
+            weights = jnp.concatenate(
+                [
+                    jnp.concatenate([wide_high, wide_low], axis=1),
+                    jnp.concatenate([wide_high, nothing], axis=1),
+                ],
+                axis=0,
+            )
             z = jnp.dot(
                 jnp.concatenate([t_high, t_low], axis=1),
-                jnp.concatenate([wide_high, wide_high], axis=0),
+                weights,
                 preferred_element_type=jnp.float32,
-            ) + jnp.dot(t_high, wide_low, preferred_element_type=jnp.float32)
-            z_high, z_low = split_two(z)
+            )
+            z_high, z_low = split_two(z[:, :lanes] + z[:, lanes:])
             for part in range(2):
                 rows = slice(part * lanes, (part + 1) * lanes)
                 done[part, j] = (z_high[rows], z_low[rows])
-        order = [(part, j) for part in range(2) for j in range(step)]
+        order = [(part, j) for part in range(2) for j in js]
         return [jnp.concatenate([done[at][i] for at in order], axis=1) for i in range(2)]
 
-    def mix_and_add(refs_of, w, z, slot_of):
+    def mix_and_add(js, refs_of, w, z, table, bond):
         z_high, z_low = z
         mix = refs_of[3]
         mix_high = mix[w, :, 0:lanes]
@@ -339,25 +409,31 @@
             jnp.concatenate([z_high, z_low], axis=0),
             preferred_element_type=jnp.float32,
         ) + jnp.dot(mix_low, z_high, preferred_element_type=jnp.float32)
-        for j in range(step):
-            slot = slot_of(pl.program_id(0) * step + j)
+        for i, j in enumerate(js):
+            slot = table[bond, pl.program_id(0) * step + j]
             slot = ((slot >> 1) ^ me) * 2 + (slot & 1)
             for part in range(2):
-                at = part * step + j
+                at = part * len(js) + i
                 total_ref[part, slot] += mixed[:, at * lanes : (at + 1) * lanes]
 
-    base = 0
+    bonds = []
+    for chunk, refs_of in zip(chunks, operands):
+        count = refs_of[0].shape[0]
+        source, group = chunk // GROUPS, chunk % GROUPS
+        for w in range(count):
+            bonds.append((refs_of, w, slots[source], group * count + w))
+    right_side(0)
+    right_side(1)
     waiting = None
-    for group, refs_of in zip(groups, operands):
-        count = refs_of[0].shape[0]
-        per = count // 2
-        for w in range(count):
-            z = left_and_right(refs_of, w, base)
+    for start in range(0, step, 2):
+        js = (start, start + 1)
+        for at, (refs_of, w, table, bond) in enumerate(bonds):
+            z = left_side(js, refs_of, w, at * 32)
             if waiting is not None:
                 mix_and_add(*waiting)
-            table, bond = slots[w // per], group * per + w % per
-            waiting = (refs_of, w, z, lambda j, table=table, bond=bond: table[bond, j])
-        base += count
+            waiting = (js, refs_of, w, z, table, bond)
+            if start + 2 < step and at in (1, 3):
+                right_side(start + 2 + at // 2)
     mix_and_add(*waiting)
 
     @pl.when(pl.program_id(0) == pl.num_programs(0) - 1)
@@ -369,26 +445,27 @@
             outs[0][...] = total_ref[...]
 
 
-def apply_bonds(info, slots, vector, groups, operands, mixing, before, pieces):
-    blocks, half, lanes = operands[0][0].shape[1:]
-    counts = [x[0].shape[0] for x in operands]
-    per_group = mixing.shape[0] // GROUPS
-    step = 2
-    in_specs = [pl.BlockSpec((step,) + x.shape[1:], lambda i, *_: (i, 0, 0)) for x in vector]
+def apply_bonds(info, slots, vector, chunks, operands, mixing, before, pieces):
+    count, blocks, half, lanes = operands[0][0].shape
+    step = 4
+    parts_given = len(vector) == 4
+    if parts_given:
+        in_specs = [pl.BlockSpec((step * lanes, lanes), lambda i, *_: (i, 0))] * 4
+    else:
+        in_specs = [pl.BlockSpec((step,) + vector[0].shape[1:], lambda i, *_: (i, 0, 0))]
     arguments = list(vector)
-    for group, (left_high, left_low, right), count in zip(groups, operands, counts):
-        in_specs += [
-            pl.BlockSpec((count, step, half, lanes), lambda i, *_: (0, i, 0, 0)),
-            pl.BlockSpec((count, step, half, lanes), lambda i, *_: (0, i, 0, 0)),
-            pl.BlockSpec((step,) + right.shape[1:], lambda i, *_: (i, 0, 0)),
-            pl.BlockSpec((per_group,) + mixing.shape[1:], lambda i, *_, g=group: (g, 0, 0)),
-        ]
+    for chunk, (left_high, left_low, right) in zip(chunks, operands):
+        in_specs += operand_specs(count, step, half, lanes)
+        in_specs.append(
+            pl.BlockSpec((count,) + mixing.shape[1:], lambda i, *_, at=chunk: (at, 0, 0))
+        )
         arguments += [left_high, left_low, right, mixing]
     if before is not None:
         in_specs.append(whole(*before.shape))
         arguments.append(before)
     shapes = [(8, lanes, lanes)] * 2 if pieces else [(2, 8, lanes, lanes)]
-    plan = (tuple(groups), len(vector) == 4, before is not None, pieces)
+    plan = (tuple(chunks), parts_given, before is not None, pieces)
+    total = count * len(chunks)
     return pl.pallas_call(
         functools.partial(apply_kernel, plan),
         grid_spec=pltpu.PrefetchScalarGridSpec(
@@ -399,12 +476,12 @@
             scratch_shapes=[
                 pltpu.VMEM((2, 8, lanes, lanes), jnp.float32),
                 pltpu.VMEM((step, lanes, PHYS * half), jnp.bfloat16),
-                pltpu.VMEM((step, sum(counts) * 32, PHYS * half), jnp.float32),
+                pltpu.VMEM((step, total * 32, PHYS * half), jnp.float32),
             ],
         ),
         out_shape=[jax.ShapeDtypeStruct(shape, jnp.float32) for shape in shapes],
         compiler_params=pltpu.CompilerParams(vmem_limit_bytes=VMEM_LIMIT),
-        cost_estimate=micros(2 * sum(counts)),
+        cost_estimate=micros(2 + total),
         name="apply_bonds",
     )(info, *slots, *arguments)
 
@@ -435,56 +512,71 @@
     return cross, square, rest
 
 
-def image_kernel(info_ref, owner_ref, a0, a1, a2, a3, diag_ref, own_ref, image_ref, stats_ref):
-    image_ref[...] = diag_ref[...] * own_ref[...]
-    add_arrived(info_ref, owner_ref, (a0, a1, a2, a3), image_ref)
-    blocks = image_ref.shape[0]
+def image_kernel(info_ref, owner_ref, a0, a1, a2, a3, diag_ref, own_ref, image_ref, total):
+    total[...] = diag_ref[...] * own_ref[...]
+    add_arrived(info_ref, owner_ref, (a0, a1, a2, a3), total)
+    blocks = total.shape[0]
     cross = jnp.zeros((LANES, LANES), jnp.float32)
     square = jnp.zeros((LANES, LANES), jnp.float32)
     for k in range(blocks):
-        own = own_ref[k]
-        cross += own * image_ref[k]
+        own, image = own_ref[k], total[k]
+        image_ref[k * LANES : (k + 1) * LANES] = image
+        cross += own * image
         square += own * own
     cross = jnp.sum(cross, keepdims=True)
     square = jnp.sum(square, keepdims=True)
     ratio = cross / jnp.maximum(square, TINY)
     rest = jnp.zeros((LANES, LANES), jnp.float32)
     for k in range(blocks):
-        apart = image_ref[k] - ratio * own_ref[k]
+        apart = total[k] - ratio * own_ref[k]
         rest += apart * apart
-    stats_ref[...] = stacked_rows(cross, square, jnp.sum(rest, keepdims=True))
+    image_ref[blocks * LANES :] = stacked_rows(cross, square, jnp.sum(rest, keepdims=True))
 
 
 def owner_image(info, owners, arrived, diagonal, own):
+    rows = own.shape[0] * LANES + SUB
     return pl.pallas_call(
         image_kernel,
         grid_spec=pltpu.PrefetchScalarGridSpec(
             num_scalar_prefetch=2,
             grid=(1,),
             in_specs=[whole(*x.shape) for x in (*arrived, diagonal, own)],
-            out_specs=[whole(*own.shape), whole(SUB, LANES)],
+            out_specs=whole(rows, LANES),
+            scratch_shapes=[pltpu.VMEM(own.shape, jnp.float32)],
         ),
-        out_shape=[
-            jax.ShapeDtypeStruct(own.shape, jnp.float32),
-            jax.ShapeDtypeStruct((SUB, LANES), jnp.float32),
-        ],
+        out_shape=jax.ShapeDtypeStruct((rows, LANES), jnp.float32),
         compiler_params=pltpu.CompilerParams(vmem_limit_bytes=VMEM_LIMIT),
         cost_estimate=micros(3),
         name="owner_image",
     )(info, owners, *arrived, diagonal, own)
 
 
-def merge_kernel(*refs):
-    refs[-1][...] = stacked_rows(*merged([ref[...] for ref in refs[:-1]]))
-
-
-def merge(tiles):
-    return pl.pallas_call(
-        merge_kernel,
-        out_shape=jax.ShapeDtypeStruct((SUB, LANES), jnp.float32),
+def join_kernel(mine, other, *refs):
+    tiles = refs[:-4] if len(refs) == 4 else refs[:-5]
+    pieces = refs[len(tiles) : len(tiles) + 4]
+    for k in range(4):
+        for i in range(2):
+            pieces[k][i] = mine[2 * k + i] + other[2 * k + i]
+    if tiles:
+        refs[-1][...] = stacked_rows(*merged([ref[...] for ref in tiles]))
+
+
+def join(mine, other, images):
+    shapes = [jax.ShapeDtypeStruct((2, LANES, LANES), jnp.float32)] * 4
+    if images:
+        shapes.append(jax.ShapeDtypeStruct((SUB, LANES), jnp.float32))
+    last = images[0].shape[0] // SUB - 1 if images else 0
+    return pl.pallas_call(
+        join_kernel,
+        grid=(1,),
+        in_specs=[whole(*mine.shape), whole(*other.shape)]
+        + [pl.BlockSpec((SUB, LANES), lambda i: (last, 0)) for _ in images],
+        out_specs=[whole(*x.shape) for x in shapes],
+        out_shape=shapes,
+        compiler_params=pltpu.CompilerParams(vmem_limit_bytes=VMEM_LIMIT),
         cost_estimate=micros(1),
-        name="merge",
-    )(*tiles)
+        name="join",
+    )(mine, other, *images)
 
 
 def scales_of(tiles, entries):
@@ -499,18 +591,26 @@
 def first_kernel(entries, s0, s1, s2, s3, image_ref, own_ref, first_ref, second_ref):
     tiles = [ref[...] for ref in (s0, s1, s2, s3)]
     scale, rayleigh, second_scale = scales_of(tiles, entries)
-    for k in range(image_ref.shape[0]):
-        image = image_ref[k]
+    for k in range(own_ref.shape[0]):
+        image = image_ref[k * LANES : (k + 1) * LANES]
         first_ref[k] = unpack_tile(scale * image)
         second_ref[k] = unpack_tile(second_scale * (image - rayleigh * own_ref[k]))
 
 
 def first_outputs(stats, image, own, entries):
-    blocks = image.shape[0]
-    shape = jax.ShapeDtypeStruct((blocks, LANES // 2, 2 * LANES), jnp.float32)
+    step = 4
+    blocks = own.shape[0]
+    shape = (step, LANES // 2, 2 * LANES)
     return pl.pallas_call(
         functools.partial(first_kernel, entries),
-        out_shape=[shape, shape],
+        grid=(blocks // step,),
+        in_specs=[whole(SUB, LANES)] * 4
+        + [
+            pl.BlockSpec((step * LANES, LANES), lambda i: (i, 0)),
+            pl.BlockSpec((step, LANES, LANES), lambda i: (i, 0, 0)),
+        ],
+        out_specs=[pl.BlockSpec(shape, lambda i: (i, 0, 0))] * 2,
+        out_shape=[jax.ShapeDtypeStruct((blocks,) + shape[1:], jnp.float32)] * 2,
         compiler_params=pltpu.CompilerParams(vmem_limit_bytes=VMEM_LIMIT),
         cost_estimate=micros(3),
         name="first_outputs",
@@ -523,30 +623,32 @@
 ):
     tiles = [ref[...] for ref in (s0, s1, s2, s3)]
     scale, rayleigh, second_scale = scales_of(tiles, entries)
-    for k in range(image_ref.shape[0]):
-        total[k] = (diag_ref[k] - rayleigh) * image_ref[k]
+    for k in range(total.shape[0]):
+        total[k] = (diag_ref[k] - rayleigh) * image_ref[k * LANES : (k + 1) * LANES]
     add_arrived(info_ref, owner_ref, (a0, a1, a2, a3), total)
-    for k in range(image_ref.shape[0]):
+    for k in range(total.shape[0]):
         second_ref[k] = unpack_tile(second_scale * total[k])
 
 
 def second_output(info, owners, arrived, diagonal, image, stats, entries):
-    shape = (image.shape[0], LANES // 2, 2 * LANES)
-    arguments = (*arrived, diagonal, image, *stats)
+    blocks = diagonal.shape[0]
+    shape = (blocks, LANES // 2, 2 * LANES)
     return pl.pallas_call(
         functools.partial(final_kernel, entries),
         grid_spec=pltpu.PrefetchScalarGridSpec(
             num_scalar_prefetch=2,
             grid=(1,),
-            in_specs=[whole(*x.shape) for x in arguments],
+            in_specs=[whole(*x.shape) for x in (*arrived, diagonal)]
+            + [whole(blocks * LANES, LANES)]
+            + [whole(SUB, LANES)] * 4,
             out_specs=whole(*shape),
-            scratch_shapes=[pltpu.VMEM(image.shape, jnp.float32)],
+            scratch_shapes=[pltpu.VMEM(diagonal.shape, jnp.float32)],
         ),
         out_shape=jax.ShapeDtypeStruct(shape, jnp.float32),
         compiler_params=pltpu.CompilerParams(vmem_limit_bytes=VMEM_LIMIT),
         cost_estimate=micros(3),
         name="second_output",
-    )(info, owners, *arguments)
+    )(info, owners, *arrived, diagonal, image, *stats)
 
 
 def partner(x, axis, k):
@@ -567,10 +669,10 @@
     return [x] + [partner(x, axes, k) for k in range(1, 4)]
 
 
-def to_owners(mine, theirs):
-    other = partner(theirs, "rep", 1)
-    pieces = [mine[2 * k : 2 * k + 2] + other[2 * k : 2 * k + 2] for k in range(4)]
-    return [pieces[0]] + [partner(pieces[k], "blk", k) for k in range(1, 4)]
+def to_owners(mine, theirs, images):
+    out = join(mine, partner(theirs, "rep", 1), images)
+    arrived = [out[0]] + [partner(out[k], "blk", k) for k in range(1, 4)]
+    return arrived, everyone(out[4], "blk") if images else None
 
 
 def per_device(wavefunction, environment, bond_terms, diagonal, term_slot, slot_block):
@@ -588,37 +690,42 @@
     slots = [term_slot, partner(term_slot, "mpo", 1)]
 
     by_owner = environment.reshape(bonds, zs, blocks, rows // zs, 2 * rows)
-    operands = []
-    arrived = [None] * 4
+    pieces = [[None] * 4 for _ in range(GROUPS)]
     for group in range(GROUPS):
         mine = by_owner[group * per : (group + 1) * per]
-        pieces = []
-        for k in range(4):
+        for k in range(1, 4):
             piece = lax.dynamic_index_in_dim(mine, blk ^ k, 1, keepdims=False)
-            if k:
-                if arrived[k] is not None:
-                    piece = after(piece, arrived[k])
-                piece = arrived[k] = partner(piece, "blk", k)
-            pieces.append(piece)
-        operands.append(prepare(info, pieces + [partner(piece, "mpo", 1) for piece in pieces]))
+            if group:
+                piece = after(piece, pieces[group - 1][k])
+            pieces[group][k] = partner(piece, "blk", k)
+    pieces[0][1] = after(pieces[0][1], vector, mixing)
+    made, sent = [], []
+    for group in range(GROUPS):
+        *own_set, send = own_operands(info, by_owner, group, pieces[group][1:])
+        made.append(own_set)
+        sent.append(send)
+    received = [partner(send, "mpo", 1) for send in sent]
+    operands = [[made[g], other_operands(received[g])] for g in range(GROUPS)]
 
     total = None
     for group in range(GROUPS):
         last = group == GROUPS - 1
+        given = vector if last else after(vector, *sent)
         out = apply_bonds(
-            info, slots, [vector], [group], [operands[group]], mixing, total, last
+            info, slots, [given], [group, GROUPS + group], operands[group], mixing, total, last
         )
         total = None if last else out[0]
-    image, stats = owner_image(info, slot_block, to_owners(*out), diagonal_packed, own)
-
-    stats = everyone(stats, ("mpo", "rep"))
+    arrived, _ = to_owners(*out, [])
+    image = owner_image(info, slot_block, arrived, diagonal_packed, own)
+
     parts = gathered(image)
-    parts[0] = after(parts[0], *stats)
-    out = apply_bonds(info, slots, parts, list(range(GROUPS)), operands, mixing, None, True)
-    stats = everyone(merge([after(x, out[1]) for x in stats]), "blk")
+    chunks = [group + GROUPS * source for group in range(GROUPS) for source in range(2)]
+    flat = [operands[group][source] for group in range(GROUPS) for source in range(2)]
+    out = apply_bonds(info, slots, parts, chunks, flat, mixing, None, True)
+    arrived, stats = to_owners(*out, parts)
     first_image, second_vector = first_outputs(stats, image, own, entries)
     second_image = second_output(
-        info, slot_block, to_owners(*out), diagonal_packed, image, stats, entries
+        info, slot_block, arrived, diagonal_packed, image, stats, entries
     )
     return (first_image, second_vector, second_image)
 

time: 182 us -> 168 us (0.923)
  starting transfers between devices: 51.2 us -> 32.4 us
  waiting for transfers between devices: 41.1 us -> 51.5 us
  Pallas kernels: 75.3 us -> 70.8 us
  local copies, waits for them, and re-layouts: 9.18 us -> 12.1 us
  other arithmetic: 2.56 us -> 0 us
    ppermute x40 -> x24, starting transfers between devices: 51.2 us -> 32.4 us  [partner(): return lax.ppermute(x, axis, [(i, i ^ k) for i in range(size)])]
    ppermute x40 -> x24, waiting for transfers between devices: 41.1 us -> 51.5 us  [partner(): return lax.ppermute(x, axis, [(i, i ^ k) for i in range(size)])]
    pallas_call x4 -> x3, Pallas kernels: 42.8 us -> 34.5 us  [apply_bonds(): pl.pallas_call(functools.partial(apply_kernel, plan), grid_spec=pltpu.Pre...]
    pallas_call x5 -> x7, Pallas kernels: 18.2 us -> 21.9 us  [the longest x2 9.37 us: own_operands(): pl.pallas_call(own_operands_kernel, grid_spec=pltpu.PrefetchScalarGridSpe...]
    unnamed x91 -> x53, local copies, waits for them, and re-layouts: 6.94 us -> 9.89 us
    add x2 -> x0, other arithmetic: 2.56 us -> none  [to_owners(): pieces = [mine[2 * k:2 * k + 2] + other[2 * k:2 * k + 2] for k in range(4)]]
  transfers between devices with their start and end apart: 40 -> 24, of which waited for: 10 -> 10; matrix products, arithmetic and copies ran while one was open for 1% -> 1% of each run, Pallas kernels for 21% -> 16%
where the time goes in v4:
time: 168 us
  Pallas kernels  70.8 us (42%)
  waiting for transfers between devices  51.5 us (31%)
  starting transfers between devices  32.4 us (19%)
  local copies, waits for them, and re-layouts  12.1 us (7%)
    ppermute x24, waiting for transfers between devices, partner(): return lax.ppermute(x, axis, [(i, i ^ k) for i in range(size)])  51.5 us
    pallas_call x3, Pallas kernels, apply_bonds(): pl.pallas_call(functools.partial(apply_kernel, plan), grid_spec=pltpu.Pre...  34.5 us
    ppermute x24, starting transfers between devices, partner(): return lax.ppermute(x, axis, [(i, i ^ k) for i in range(size)])  32.4 us
    unnamed x53, local copies, waits for them, and re-layouts  9.89 us
    pallas_call x2, Pallas kernels, own_operands(): pl.pallas_call(own_operands_kernel, grid_spec=pltpu.PrefetchScalarGridSpe...  9.37 us
    pallas_call x2, Pallas kernels, other_operands(): pl.pallas_call(other_operands_kernel, grid=(blocks // step,), in_specs=[p...  6.18 us
    pallas_call x1, Pallas kernels, pack(): pl.pallas_call(pack_kernel, grid_spec=pltpu.PrefetchScalarGridSpec(num_sc...  5.59 us
    pallas_call x2, Pallas kernels, join(): pl.pallas_call(join_kernel, grid=(1,), in_specs=[whole(*mine.shape), whol...  4.05 us
  transfers between devices with their start and end apart: 24, of which 10 were waited for; matrix products, arithmetic and copies ran while one was open for 1% of the time, Pallas kernels for 16%

profile of v4, /device:TPU:0, one launch (start us, length us, event | category | flops | bytes accessed | tf_op | source)
XLA Modules:
  0.0 167.6 jit_solution(9579119011848200286)
XLA Ops:
  2.3 3.1 %collective-permute-start.1 = (f32[3,8,16,128]{3,2,1,0:T(8,128)S(1)}, f32[3,8,16,128]{3,2,1,0:T(8,128)S(1)}, u32[]{:S(2)}, u32[]{:S(2)}) collective-permute-start(f32[3,8,16,128]{3,2,1,0:T(8,128)S(1)} %get-tuple-element.81), channel_id=1, source_target_pairs={{0,4},{4,0},{8,12},{12,8},{1,5},{5,1},{9,13},{13,9},{2,6},{6,2},{1... | collective-permute-start | bytes 589832 | tf_op jit(solution)/shard_map/ppermute | solution.py:656
  6.9 2.6 %collective-permute-start.3 = (f32[3,8,16,128]{3,2,1,0:T(8,128)S(1)}, f32[3,8,16,128]{3,2,1,0:T(8,128)S(1)}, u32[]{:S(2)}, u32[]{:S(2)}) collective-permute-start(f32[3,8,16,128]{3,2,1,0:T(8,128)S(1)} %get-tuple-element.80), channel_id=1, source_target_pairs={{0,8},{4,12},{8,0},{12,4},{1,9},{5,13},{9,1},{13,5},{2,10},{6,14},... | collective-permute-start | bytes 589832 | tf_op jit(solution)/shard_map/ppermute | solution.py:656
  10.3 5.6 %pack.1 = (bf16[8,128,1024]{2,1,0:T(8,128)(2,1)}, f32[8,128,128]{2,1,0:T(8,128)}, f32[8,128,128]{2,1,0:T(8,128)}) custom-call(s32[7]{0:T(128)} %stack.31.info_ref, f32[8,64,1024]{2,1,0:T(8,128)} %own_wave_ref.1, f32[8,64,1024]{2,1,0:T(8,128)} %own_wave_ref.1, f32[8,64,256]{2,1,0:T(8,128)} %diag_ref.1), custom_call_target="tpu_custom_call" | custom-call | flops 5500000256 | bytes 1048576 | tf_op jit(solution)/shard_map/pack/pallas_call | solution.py:139
  17.9 6.1 %collective-permute-done.3.refs_2_ = f32[3,8,16,128]{3,2,1,0:T(8,128)S(1)} collective-permute-done((f32[3,8,16,128]{3,2,1,0:T(8,128)S(1)}, f32[3,8,16,128]{3,2,1,0:T(8,128)S(1)}, u32[]{:S(2)}, u32[]{:S(2)}) %collective-permute-start.3) | collective-permute-done | bytes 196640 | tf_op jit(solution)/shard_map/ppermute | solution.py:656
  24.8 4.8 %own_operands.3 = (bf16[3,8,64,128]{3,2,1,0:T(8,128)(2,1)}, bf16[3,8,64,128]{3,2,1,0:T(8,128)(2,1)}, bf16[8,96,256]{2,1,0:T(8,128)(2,1)}, f32[3,8,48,128]{3,2,1,0:T(8,128)}) custom-call(s32[7]{0:T(128)} %stack.31.info_ref, f32[6,4,8,16,128]{4,3,2,1,0:T(8,128)} %bitcast.36, f32[3,8,16,128]{3,2,1,0:T(8,128)} %copy-done.8, f32[3,8,16,128]{3,2,1,0:T(8,128)} %copy-done.9, ...), custom_call_target="tpu_custom_call" | custom-call | flops 3300000000 | bytes 1048576 | tf_op jit(solution)/shard_map/own_operands/pallas_call | solution.py:282
  30.1 3.1 %collective-permute-start.2 = (f32[3,8,16,128]{3,2,1,0:T(8,128)S(1)}, f32[3,8,16,128]{3,2,1,0:T(8,128)S(1)}, u32[]{:S(2)}, u32[]{:S(2)}) collective-permute-start(f32[3,8,16,128]{3,2,1,0:T(8,128)S(1)} %get-tuple-element.41), channel_id=1, source_target_pairs={{0,4},{4,0},{8,12},{12,8},{1,5},{5,1},{9,13},{13,9},{2,6},{6,2},{1... | collective-permute-start | bytes 589832 | tf_op jit(solution)/shard_map/ppermute | solution.py:656
  39.0 10.2 %collective-permute-done.4.refs_2_ = f32[3,8,16,128]{3,2,1,0:T(8,128)S(1)} collective-permute-done((f32[3,8,16,128]{3,2,1,0:T(8,128)S(1)}, f32[3,8,16,128]{3,2,1,0:T(8,128)S(1)}, u32[]{:S(2)}, u32[]{:S(2)}) %collective-permute-start.4) | collective-permute-done | bytes 196640 | tf_op jit(solution)/shard_map/ppermute | solution.py:656
  50.6 4.6 %own_operands.2 = (bf16[3,8,64,128]{3,2,1,0:T(8,128)(2,1)}, bf16[3,8,64,128]{3,2,1,0:T(8,128)(2,1)}, bf16[8,96,256]{2,1,0:T(8,128)(2,1)}, f32[3,8,48,128]{3,2,1,0:T(8,128)}) custom-call(s32[7]{0:T(128)} %stack.31.info_ref, f32[6,4,8,16,128]{4,3,2,1,0:T(8,128)} %bitcast.37, f32[3,8,16,128]{3,2,1,0:T(8,128)} %copy-done.11, f32[3,8,16,128]{3,2,1,0:T(8,128)} %copy-done.12, ...), custom_call_target="tpu_custom_call" | custom-call | flops 3300000000 | bytes 1048576 | tf_op jit(solution)/shard_map/own_operands/pallas_call | solution.py:282
  57.6 3.1 %other_operands.3 = (bf16[3,8,64,128]{3,2,1,0:T(8,128)(2,1)}, bf16[3,8,64,128]{3,2,1,0:T(8,128)(2,1)}, bf16[8,96,256]{2,1,0:T(8,128)(2,1)}) custom-call(f32[3,8,48,128]{3,2,1,0:T(8,128)} %copy-done.1), custom_call_target="tpu_custom_call" | custom-call | flops 3300000000 | bytes 1048576 | tf_op jit(solution)/shard_map/other_operands/pallas_call | solution.py:309
  61.3 9.3 %apply_bonds.3.refs_11_ = f32[2,8,128,128]{3,2,1,0:T(8,128)} custom-call(s32[7]{0:T(128)} %stack.31.info_ref, s32[6,8]{1,0:T(8,128)} %refs_0_.7, s32[6,8]{1,0:T(8,128)} %copy-done.22, bf16[8,128,1024]{2,1,0:T(8,128)(2,1)} %get-tuple-element.53.refs_2_, bf16[3,8,64,128]{3,2,1,0:T(8,128)(2,1)} %get-tuple-element.54.refs_3_.refs_6_, ...), custom_call_target="tpu_custom_call" | custom-call | flops 8800000000 | bytes 1048576 | tf_op jit(solution)/shard_map/apply_bonds/pallas_call | solution.py:469
  71.4 3.1 %other_operands.2 = (bf16[3,8,64,128]{3,2,1,0:T(8,128)(2,1)}, bf16[3,8,64,128]{3,2,1,0:T(8,128)(2,1)}, bf16[8,96,256]{2,1,0:T(8,128)(2,1)}) custom-call(f32[3,8,48,128]{3,2,1,0:T(8,128)} %copy-done.2), custom_call_target="tpu_custom_call" | custom-call | flops 3300000000 | bytes 1048576 | tf_op jit(solution)/shard_map/other_operands/pallas_call | solution.py:309
  74.5 9.6 %apply_bonds.4 = (f32[8,128,128]{2,1,0:T(8,128)}, f32[8,128,128]{2,1,0:T(8,128)}) custom-call(s32[7]{0:T(128)} %stack.31.info_ref, s32[6,8]{1,0:T(8,128)} %refs_0_.7, s32[6,8]{1,0:T(8,128)} %copy-done.22, bf16[8,128,1024]{2,1,0:T(8,128)(2,1)} %get-tuple-element.53.refs_2_, bf16[3,8,64,128]{3,2,1,0:T(8,128)(2,1)} %get-tuple-element.44.refs_3_.refs_14_, ...), custom_call_target="tpu_custom_call" | custom-call | flops 8800000000 | bytes 1048576 | tf_op jit(solution)/shard_map/apply_bonds/pallas_call | solution.py:469
  84.2 2.1 %collective-permute-done.10.other = f32[8,128,128]{2,1,0:T(8,128)S(1)} collective-permute-done((f32[8,128,128]{2,1,0:T(8,128)}, f32[8,128,128]{2,1,0:T(8,128)S(1)}, u32[]{:S(2)}, u32[]{:S(2)}) %collective-permute-start.10) | collective-permute-done | bytes 524320 | tf_op jit(solution)/shard_map/ppermute | solution.py:656
  87.1 2.0 %join.2 = (f32[2,128,128]{2,1,0:T(8,128)}, f32[2,128,128]{2,1,0:T(8,128)}, f32[2,128,128]{2,1,0:T(8,128)}, f32[2,128,128]{2,1,0:T(8,128)}) custom-call(f32[8,128,128]{2,1,0:T(8,128)} %get-tuple-element.60.mine, f32[8,128,128]{2,1,0:T(8,128)} %copy-done.7), custom_call_target="tpu_custom_call" | custom-call | flops 1100000000 | bytes 1048576 | tf_op jit(solution)/shard_map/join/pallas_call | solution.py:569
  94.5 2.6 %collective-permute-done.11.a1 = f32[2,128,128]{2,1,0:T(8,128)S(1)} collective-permute-done((f32[2,128,128]{2,1,0:T(8,128)}, f32[2,128,128]{2,1,0:T(8,128)S(1)}, u32[]{:S(2)}, u32[]{:S(2)}) %collective-permute-start.11) | collective-permute-done | bytes 131104 | tf_op jit(solution)/shard_map/ppermute | solution.py:656
  97.1 7.1 %collective-permute-done.12.a2 = f32[2,128,128]{2,1,0:T(8,128)S(1)} collective-permute-done((f32[2,128,128]{2,1,0:T(8,128)}, f32[2,128,128]{2,1,0:T(8,128)S(1)}, u32[]{:S(2)}, u32[]{:S(2)}) %collective-permute-start.12) | collective-permute-done | bytes 131104 | tf_op jit(solution)/shard_map/ppermute | solution.py:656
  104.9 3.5 %owner_image.1.refs_2_.refs_0_.image_ref = f32[1032,128]{1,0:T(8,128)} custom-call(s32[7]{0:T(128)} %stack.31.info_ref, s32[4,2]{1,0:T(4,128)} %copy.15.owner_ref, f32[2,128,128]{2,1,0:T(8,128)} %get-tuple-element.62.a0, f32[2,128,128]{2,1,0:T(8,128)} %copy-done.17, f32[2,128,128]{2,1,0:T(8,128)} %copy-done.18, f32[2,128,128]{2,1,0:T(8,128)} %copy-done.19, ...), custom_call_target="tpu_custom_call" | custom-call | flops 3300000000 | bytes 1048576 | tf_op jit(solution)/shard_map/owner_image/pallas_call | solution.py:538
  108.9 11.9 %collective-permute-done.14.refs_3_.refs_1_ = f32[1032,128]{1,0:T(8,128)S(1)} collective-permute-done((f32[1032,128]{1,0:T(8,128)}, f32[1032,128]{1,0:T(8,128)S(1)}, u32[]{:S(2)}, u32[]{:S(2)}) %collective-permute-start.14) | collective-permute-done | bytes 528416 | tf_op jit(solution)/shard_map/ppermute | solution.py:656
  123.6 15.6 %apply_bonds.5 = (f32[8,128,128]{2,1,0:T(8,128)}, f32[8,128,128]{2,1,0:T(8,128)}) custom-call(s32[7]{0:T(128)} %stack.31.info_ref, s32[6,8]{1,0:T(8,128)} %refs_0_.7, s32[6,8]{1,0:T(8,128)} %copy-done.22, f32[1032,128]{1,0:T(8,128)} %owner_image.1.refs_2_.refs_0_.image_ref, f32[1032,128]{1,0:T(8,128)} %copy-done.3, f32[1032,128]{1,0:T(8,128)} %copy-done.4, ...), custom_call_target="tpu_custom_call" | custom-call | flops 15399999488 | bytes 1048576 | tf_op jit(solution)/shard_map/apply_bonds/pallas_call | solution.py:469
  144.2 3.0 %collective-permute-start.18 = (f32[8,128]{1,0:T(8,128)}, f32[8,128]{1,0:T(8,128)S(1)}, u32[]{:S(2)}, u32[]{:S(2)}) collective-permute-start(f32[8,128]{1,0:T(8,128)} %get-tuple-element.70.s0), channel_id=1, source_target_pairs={{0,4},{4,0},{8,12},{12,8},{1,5},{5,1},{9,13},{13,9},{2,6},{6,2},{1... | collective-permute-start | bytes 12296 | tf_op jit(solution)/shard_map/ppermute | solution.py:656
  150.8 2.4 %collective-permute-start.22 = (f32[2,128,128]{2,1,0:T(8,128)}, f32[2,128,128]{2,1,0:T(8,128)S(1)}, u32[]{:S(2)}, u32[]{:S(2)}) collective-permute-start(f32[2,128,128]{2,1,0:T(8,128)} %get-tuple-element.75), channel_id=1, source_target_pairs={{0,8},{4,12},{8,0},{12,4},{1,9},{5,13},{9,1},{13,5},{2,10},{6,14},... | collective-permute-start | bytes 393224 | tf_op jit(solution)/shard_map/ppermute | solution.py:656
  155.8 2.3 %first_outputs.1 = (f32[8,64,256]{2,1,0:T(8,128)}, f32[8,64,256]{2,1,0:T(8,128)}) custom-call(f32[8,128]{1,0:T(8,128)} %get-tuple-element.70.s0, f32[8,128]{1,0:T(8,128)} %copy-done.23, f32[8,128]{1,0:T(8,128)} %copy-done.24, f32[8,128]{1,0:T(8,128)} %copy-done.25, f32[1032,128]{1,0:T(8,128)} %owner_image.1.refs_2_.refs_0_.image_ref, ...), custom_call_target="tpu_custom_call" | custom-call | flops 3300000000 | bytes 1048576 | tf_op jit(solution)/shard_map/first_outputs/pallas_call | solution.py:604
  158.1 5.6 %collective-permute-done.22.a2 = f32[2,128,128]{2,1,0:T(8,128)S(1)} collective-permute-done((f32[2,128,128]{2,1,0:T(8,128)}, f32[2,128,128]{2,1,0:T(8,128)S(1)}, u32[]{:S(2)}, u32[]{:S(2)}) %collective-permute-start.22) | collective-permute-done | bytes 131104 | tf_op jit(solution)/shard_map/ppermute | solution.py:656
  164.4 3.2 %second_output.1 = f32[8,64,256]{2,1,0:T(8,128)} custom-call(s32[7]{0:T(128)} %stack.31.info_ref, s32[4,2]{1,0:T(4,128)} %copy.15.owner_ref, f32[2,128,128]{2,1,0:T(8,128)} %get-tuple-element.73.a0, f32[2,128,128]{2,1,0:T(8,128)} %copy-done.14, f32[2,128,128]{2,1,0:T(8,128)} %copy-done.15, f32[2,128,128]{2,1,0:T(8,128)} %copy-done.16, ...), custom_call_target="tpu_custom_call" | custom-call | flops 3300000000 | bytes 1048576 | tf_op jit(solution)/shard_map/second_output/pallas_call | solution.py:636
  (95 shorter events, 40.2 us)
Async XLA Ops:
  2.3 15.6 %collective-permute-start.1 = (f32[3,8,16,128]{3,2,1,0:T(8,128)S(1)}, f32[3,8,16,128]{3,2,1,0:T(8,128)S(1)}, u32[]{:S(2)}, u32[]{:S(2)}) collective-permute-start(f32[3,8,16,128]{3,2,1,0:T(8,128)S(1)} %get-tuple-element.81), channel_id=1, source_target_pairs={{0,4},{4,0},{8,12},{12,8},{1,5},{5,1},{9,13},{13,9},{2,6},{6,2},{1... | collective-permute-start | bytes 589832 | tf_op jit(solution)/shard_map/ppermute | solution.py:656
  5.4 10.5 %collective-permute-start.7 = (f32[6,16,16]{2,1,0:T(8,128)S(1)}, f32[6,16,16]{2,1,0:T(8,128)}, u32[]{:S(2)}, u32[]{:S(2)}) collective-permute-start(f32[6,16,16]{2,1,0:T(8,128)S(1)} %copy-done.20), channel_id=1, source_target_pairs={{0,2},{2,0},{1,3},{3,1},{4,6},{6,4},{5,7},{7,5},{8,10},{10,8},{9,1... | collective-permute-start | bytes 18440 | tf_op jit(solution)/shard_map/ppermute | solution.py:656
  6.9 17.2 %collective-permute-start.3 = (f32[3,8,16,128]{3,2,1,0:T(8,128)S(1)}, f32[3,8,16,128]{3,2,1,0:T(8,128)S(1)}, u32[]{:S(2)}, u32[]{:S(2)}) collective-permute-start(f32[3,8,16,128]{3,2,1,0:T(8,128)S(1)} %get-tuple-element.80), channel_id=1, source_target_pairs={{0,8},{4,12},{8,0},{12,4},{1,9},{5,13},{9,1},{13,5},{2,10},{6,14},... | collective-permute-start | bytes 589832 | tf_op jit(solution)/shard_map/ppermute | solution.py:656
  9.4 14.6 %collective-permute-start.5 = (f32[3,8,16,128]{3,2,1,0:T(8,128)S(1)}, f32[3,8,16,128]{3,2,1,0:T(8,128)S(1)}, u32[]{:S(2)}, u32[]{:S(2)}) collective-permute-start(f32[3,8,16,128]{3,2,1,0:T(8,128)S(1)} %get-tuple-element.79), channel_id=1, source_target_pairs={{0,12},{4,8},{8,4},{12,0},{1,13},{5,9},{9,5},{13,1},{2,14},{6,10},... | collective-permute-start | bytes 589832 | tf_op jit(solution)/shard_map/ppermute | solution.py:656
  29.5 27.2 %collective-permute-start.9 = (f32[3,8,48,128]{3,2,1,0:T(8,128)}, f32[3,8,48,128]{3,2,1,0:T(8,128)S(1)}, u32[]{:S(2)}, u32[]{:S(2)}) collective-permute-start(f32[3,8,48,128]{3,2,1,0:T(8,128)} %get-tuple-element.52), channel_id=1, source_target_pairs={{0,2},{2,0},{1,3},{3,1},{4,6},{6,4},{5,7},{7,5},{8,10},{10,8},{9,1... | collective-permute-start | bytes 1769480 | tf_op jit(solution)/shard_map/ppermute | solution.py:656
  30.1 8.9 %collective-permute-start.2 = (f32[3,8,16,128]{3,2,1,0:T(8,128)S(1)}, f32[3,8,16,128]{3,2,1,0:T(8,128)S(1)}, u32[]{:S(2)}, u32[]{:S(2)}) collective-permute-start(f32[3,8,16,128]{3,2,1,0:T(8,128)S(1)} %get-tuple-element.41), channel_id=1, source_target_pairs={{0,4},{4,0},{8,12},{12,8},{1,5},{5,1},{9,13},{13,9},{2,6},{6,2},{1... | collective-permute-start | bytes 589832 | tf_op jit(solution)/shard_map/ppermute | solution.py:656
  33.2 16.1 %collective-permute-start.4 = (f32[3,8,16,128]{3,2,1,0:T(8,128)S(1)}, f32[3,8,16,128]{3,2,1,0:T(8,128)S(1)}, u32[]{:S(2)}, u32[]{:S(2)}) collective-permute-start(f32[3,8,16,128]{3,2,1,0:T(8,128)S(1)} %get-tuple-element.42), channel_id=1, source_target_pairs={{0,8},{4,12},{8,0},{12,4},{1,9},{5,13},{9,1},{13,5},{2,10},{6,14},... | collective-permute-start | bytes 589832 | tf_op jit(solution)/shard_map/ppermute | solution.py:656
  34.3 15.0 %collective-permute-start.6 = (f32[3,8,16,128]{3,2,1,0:T(8,128)S(1)}, f32[3,8,16,128]{3,2,1,0:T(8,128)S(1)}, u32[]{:S(2)}, u32[]{:S(2)}) collective-permute-start(f32[3,8,16,128]{3,2,1,0:T(8,128)S(1)} %get-tuple-element.43), channel_id=1, source_target_pairs={{0,12},{4,8},{8,4},{12,0},{1,13},{5,9},{9,5},{13,1},{2,14},{6,10},... | collective-permute-start | bytes 589832 | tf_op jit(solution)/shard_map/ppermute | solution.py:656
  35.7 25.0 %collective-permute-start = (s32[6,8]{1,0:T(8,128)S(1)}, s32[6,8]{1,0:T(8,128)S(1)}, u32[]{:S(2)}, u32[]{:S(2)}) collective-permute-start(s32[6,8]{1,0:T(8,128)S(1)} %copy-done.21), channel_id=1, source_target_pairs={{0,2},{2,0},{1,3},{3,1},{4,6},{6,4},{5,7},{7,5},{8,10},{10,8},{9,1... | collective-permute-start | bytes 584 | tf_op jit(solution)/shard_map/ppermute | solution.py:656
  55.2 15.3 %collective-permute-start.8 = (f32[3,8,48,128]{3,2,1,0:T(8,128)}, f32[3,8,48,128]{3,2,1,0:T(8,128)S(1)}, u32[]{:S(2)}, u32[]{:S(2)}) collective-permute-start(f32[3,8,48,128]{3,2,1,0:T(8,128)} %get-tuple-element.47), channel_id=1, source_target_pairs={{0,2},{2,0},{1,3},{3,1},{4,6},{6,4},{5,7},{7,5},{8,10},{10,8},{9,1... | collective-permute-start | bytes 1769480 | tf_op jit(solution)/shard_map/ppermute | solution.py:656
  84.1 2.2 %collective-permute-start.10 = (f32[8,128,128]{2,1,0:T(8,128)}, f32[8,128,128]{2,1,0:T(8,128)S(1)}, u32[]{:S(2)}, u32[]{:S(2)}) collective-permute-start(f32[8,128,128]{2,1,0:T(8,128)} %get-tuple-element.61), channel_id=1, source_target_pairs={{0,1},{1,0},{2,3},{3,2},{4,5},{5,4},{6,7},{7,6},{8,9},{9,8},{10,11... | collective-permute-start | bytes 1572872 | tf_op jit(solution)/shard_map/ppermute | solution.py:656
  89.1 8.0 %collective-permute-start.11 = (f32[2,128,128]{2,1,0:T(8,128)}, f32[2,128,128]{2,1,0:T(8,128)S(1)}, u32[]{:S(2)}, u32[]{:S(2)}) collective-permute-start(f32[2,128,128]{2,1,0:T(8,128)} %get-tuple-element.63), channel_id=1, source_target_pairs={{0,4},{4,0},{8,12},{12,8},{1,5},{5,1},{9,13},{13,9},{2,6},{6,2},{1... | collective-permute-start | bytes 393224 | tf_op jit(solution)/shard_map/ppermute | solution.py:656
  91.1 13.1 %collective-permute-start.12 = (f32[2,128,128]{2,1,0:T(8,128)}, f32[2,128,128]{2,1,0:T(8,128)S(1)}, u32[]{:S(2)}, u32[]{:S(2)}) collective-permute-start(f32[2,128,128]{2,1,0:T(8,128)} %get-tuple-element.64), channel_id=1, source_target_pairs={{0,8},{4,12},{8,0},{12,4},{1,9},{5,13},{9,1},{13,5},{2,10},{6,14},... | collective-permute-start | bytes 393224 | tf_op jit(solution)/shard_map/ppermute | solution.py:656
  92.4 11.8 %collective-permute-start.13 = (f32[2,128,128]{2,1,0:T(8,128)}, f32[2,128,128]{2,1,0:T(8,128)S(1)}, u32[]{:S(2)}, u32[]{:S(2)}) collective-permute-start(f32[2,128,128]{2,1,0:T(8,128)} %get-tuple-element.65), channel_id=1, source_target_pairs={{0,12},{4,8},{8,4},{12,0},{1,13},{5,9},{9,5},{13,1},{2,14},{6,10},... | collective-permute-start | bytes 393224 | tf_op jit(solution)/shard_map/ppermute | solution.py:656
  108.4 12.4 %collective-permute-start.14 = (f32[1032,128]{1,0:T(8,128)}, f32[1032,128]{1,0:T(8,128)S(1)}, u32[]{:S(2)}, u32[]{:S(2)}) collective-permute-start(f32[1032,128]{1,0:T(8,128)} %owner_image.1.refs_2_.refs_0_.image_ref), channel_id=1, source_target_pairs={{0,2},{2,0},{1,3},{3,1},{4,6},{6,4},{5,7},{7,5},{8,10},{10,8},{9,1... | collective-permute-start | bytes 1585160 | tf_op jit(solution)/shard_map/ppermute | solution.py:656
  108.9 11.9 %collective-permute-start.15 = (f32[1032,128]{1,0:T(8,128)}, f32[1032,128]{1,0:T(8,128)S(1)}, u32[]{:S(2)}, u32[]{:S(2)}) collective-permute-start(f32[1032,128]{1,0:T(8,128)} %owner_image.1.refs_2_.refs_0_.image_ref), channel_id=1, source_target_pairs={{0,1},{1,0},{2,3},{3,2},{4,5},{5,4},{6,7},{7,6},{8,9},{9,8},{10,11... | collective-permute-start | bytes 1585160 | tf_op jit(solution)/shard_map/ppermute | solution.py:656
  120.8 1.9 %collective-permute-start.16 = (f32[1032,128]{1,0:T(8,128)S(1)}, f32[1032,128]{1,0:T(8,128)S(1)}, u32[]{:S(2)}, u32[]{:S(2)}) collective-permute-start(f32[1032,128]{1,0:T(8,128)S(1)} %collective-permute-done.14.refs_3_.refs_1_), channel_id=1, source_target_pairs={{0,1},{1,0},{2,3},{3,2},{4,5},{5,4},{6,7},{7,6},{8,9},{9,8},{10,11... | collective-permute-start | bytes 1585160 | tf_op jit(solution)/shard_map/ppermute | solution.py:656
  139.2 2.2 %collective-permute-start.17 = (f32[8,128,128]{2,1,0:T(8,128)}, f32[8,128,128]{2,1,0:T(8,128)S(1)}, u32[]{:S(2)}, u32[]{:S(2)}) collective-permute-start(f32[8,128,128]{2,1,0:T(8,128)} %get-tuple-element.69), channel_id=1, source_target_pairs={{0,1},{1,0},{2,3},{3,2},{4,5},{5,4},{6,7},{7,6},{8,9},{9,8},{10,11... | collective-permute-start | bytes 1572872 | tf_op jit(solution)/shard_map/ppermute | solution.py:656
  144.2 9.0 %collective-permute-start.18 = (f32[8,128]{1,0:T(8,128)}, f32[8,128]{1,0:T(8,128)S(1)}, u32[]{:S(2)}, u32[]{:S(2)}) collective-permute-start(f32[8,128]{1,0:T(8,128)} %get-tuple-element.70.s0), channel_id=1, source_target_pairs={{0,4},{4,0},{8,12},{12,8},{1,5},{5,1},{9,13},{13,9},{2,6},{6,2},{1... | collective-permute-start | bytes 12296 | tf_op jit(solution)/shard_map/ppermute | solution.py:656
  147.2 7.4 %collective-permute-start.19 = (f32[8,128]{1,0:T(8,128)}, f32[8,128]{1,0:T(8,128)S(1)}, u32[]{:S(2)}, u32[]{:S(2)}) collective-permute-start(f32[8,128]{1,0:T(8,128)} %get-tuple-element.70.s0), channel_id=1, source_target_pairs={{0,8},{4,12},{8,0},{12,4},{1,9},{5,13},{9,1},{13,5},{2,10},{6,14},... | collective-permute-start | bytes 12296 | tf_op jit(solution)/shard_map/ppermute | solution.py:656
  148.8 5.8 %collective-permute-start.20 = (f32[8,128]{1,0:T(8,128)}, f32[8,128]{1,0:T(8,128)S(1)}, u32[]{:S(2)}, u32[]{:S(2)}) collective-permute-start(f32[8,128]{1,0:T(8,128)} %get-tuple-element.70.s0), channel_id=1, source_target_pairs={{0,12},{4,8},{8,4},{12,0},{1,13},{5,9},{9,5},{13,1},{2,14},{6,10},... | collective-permute-start | bytes 12296 | tf_op jit(solution)/shard_map/ppermute | solution.py:656
  150.2 7.9 %collective-permute-start.21 = (f32[2,128,128]{2,1,0:T(8,128)}, f32[2,128,128]{2,1,0:T(8,128)S(1)}, u32[]{:S(2)}, u32[]{:S(2)}) collective-permute-start(f32[2,128,128]{2,1,0:T(8,128)} %get-tuple-element.74), channel_id=1, source_target_pairs={{0,4},{4,0},{8,12},{12,8},{1,5},{5,1},{9,13},{13,9},{2,6},{6,2},{1... | collective-permute-start | bytes 393224 | tf_op jit(solution)/shard_map/ppermute | solution.py:656
  150.8 12.9 %collective-permute-start.22 = (f32[2,128,128]{2,1,0:T(8,128)}, f32[2,128,128]{2,1,0:T(8,128)S(1)}, u32[]{:S(2)}, u32[]{:S(2)}) collective-permute-start(f32[2,128,128]{2,1,0:T(8,128)} %get-tuple-element.75), channel_id=1, source_target_pairs={{0,8},{4,12},{8,0},{12,4},{1,9},{5,13},{9,1},{13,5},{2,10},{6,14},... | collective-permute-start | bytes 393224 | tf_op jit(solution)/shard_map/ppermute | solution.py:656
  153.2 10.5 %collective-permute-start.23 = (f32[2,128,128]{2,1,0:T(8,128)}, f32[2,128,128]{2,1,0:T(8,128)S(1)}, u32[]{:S(2)}, u32[]{:S(2)}) collective-permute-start(f32[2,128,128]{2,1,0:T(8,128)} %get-tuple-element.76), channel_id=1, source_target_pairs={{0,12},{4,8},{8,4},{12,0},{1,13},{5,9},{9,5},{13,1},{2,14},{6,10},... | collective-permute-start | bytes 393224 | tf_op jit(solution)/shard_map/ppermute | solution.py:656
  (26 other events, 71.0 us)

commit v5 on v4

--- a/solution.py
+++ b/solution.py
@@ -12,7 +12,7 @@
 PHYS = 16
 TINY = 1e-30
 GROUPS = 2
-VMEM_LIMIT = 62 * 1024 * 1024
+VMEM_LIMIT = 63 * 1024 * 1024 + 512 * 1024
 
 
 def plain_apply(vector_full, environment, bond_terms, term_slot, slot_block, diagonal):
@@ -172,12 +172,13 @@
     at = 0
     for source in sources:
         for k in range(source.shape[0]):
-            for place, term in enumerate(split_two(source[k].T)):
+            high, low = split_two(source[k].T)
+            for term, places in ((high, (0, 1)), (low, (2,))):
                 wide = jnp.dot(term, spread, preferred_element_type=jnp.float32)
                 tall = jnp.concatenate([wide] * SUB, axis=0)
-                out_ref[at, :, place * LANES : (place + 1) * LANES] = jnp.where(
-                    same, tall, 0.0
-                ).astype(jnp.bfloat16)
+                tall = jnp.where(same, tall, 0.0).astype(jnp.bfloat16)
+                for place in places:
+                    out_ref[at, :, place * LANES : (place + 1) * LANES] = tall
             at += 1
 
 
@@ -185,78 +186,69 @@
     count = sources[0].shape[0] * len(sources)
     return pl.pallas_call(
         mixing_kernel,
-        out_shape=jax.ShapeDtypeStruct((count, LANES, 2 * LANES), jnp.bfloat16),
+        out_shape=jax.ShapeDtypeStruct((count, LANES, 3 * LANES), jnp.bfloat16),
         compiler_params=pltpu.CompilerParams(vmem_limit_bytes=VMEM_LIMIT),
         cost_estimate=micros(2),
         name="mixing",
     )(*sources)
 
 
-def store_right(columns, count, right_out, j):
-    used = 32 * count
-    high, low = split_two(columns.T[:used])
-    right_out[j, 0:used, 0:LANES] = jnp.concatenate([high, high], axis=1)
-    right_out[j, 0:used, LANES:] = jnp.concatenate([low, low], axis=1)
-
-
 def own_operands_kernel(info_ref, *refs):
-    pieces, (left_high, left_low, right_out, send, blocks_ref) = refs[:4], refs[4:]
+    pieces, (left_high, left_low, right_out, send, blocks_ref, upright_ref) = refs[:4], refs[4:]
     per, blocks, half, lanes = left_high.shape
     rows = half // 4
     wide = half // 2
     first = lane_is_first(half)
     first_wide = lane_is_first(wide)
-    lane = lax.broadcasted_iota(jnp.int32, (half, lanes), 1) // wide
-    lane_rows = lax.broadcasted_iota(jnp.int32, (rows, lanes), 1) // wide
-    start = info_ref[6] * wide
-    other = wide - start
+    first_rows = lane_is_first(rows)
+    mine_at = pl.multiple_of(half + info_ref[6] * wide, wide)
+    theirs_at = pl.multiple_of(lanes - wide - info_ref[6] * wide, wide)
     for j in range(blocks):
-        columns = jnp.zeros((half, lanes), jnp.float32)
         for w in range(per):
             for z in range(4):
                 row = pl.multiple_of((info_ref[4] ^ z) * rows, rows)
                 piece = pieces[z][w, 0, j] if z == 0 else pieces[z][w, j]
                 blocks_ref[w, j, pl.ds(row, rows), :] = piece
+        for w in range(per):
             block = blocks_ref[w, j]
+            upright_ref[w, j] = jnp.concatenate([block, block], axis=0).T
             turned = pltpu.roll(block, half, 1)
             high, low = split_two(jnp.where(first, block, turned))
             left_high[w, j] = high
             left_low[w, j] = low
             send[w, j, 0:wide] = jnp.where(first_wide, block[:wide], turned[wide:])
-            mine = pltpu.roll(block, lax.rem(wide * w + lanes + half - start, lanes), 1)
-            columns = jnp.where(lane == w, mine, columns)
-            packed = jnp.zeros((rows, lanes), jnp.float32)
-            for g in range(4):
-                shift = lax.rem(wide * g + lanes + half - other, lanes)
-                theirs = pltpu.roll(block[rows * g : rows * (g + 1)], shift, 1)
-                packed = jnp.where(lane_rows == g, theirs, packed)
-            send[w, j, wide : wide + rows] = packed
-        store_right(columns, per, right_out, j)
-
-
-def other_operands_kernel(sent, left_high, left_low, right_out):
+        for w in range(per):
+            high, low = split_two(upright_ref[w, j, pl.ds(mine_at, wide), :])
+            right_out[j, wide * w : wide * (w + 1), 0:lanes] = high
+            right_out[j, wide * w : wide * (w + 1), lanes:] = low
+            upper = upright_ref[w, j, pl.ds(theirs_at, rows), :]
+            lower = upright_ref[w, j, pl.ds(theirs_at + rows, rows), :]
+            send[w, j, wide : wide + rows] = jnp.where(first_rows, upper, lower)
+
+
+def other_operands(sent, left_high, left_low, right_out, j):
     per, blocks, half, lanes = left_high.shape
     rows = half // 4
     wide = half // 2
     first = lane_is_first(wide)
-    lane_rows = lax.broadcasted_iota(jnp.int32, (rows, lanes), 1) // wide
-    for j in range(blocks):
-        columns = [jnp.zeros((rows, lanes), jnp.float32) for _ in range(4)]
-        for w in range(per):
-            both = sent[w, j, 0:wide]
-            turned = pltpu.roll(both, half, 1)
-            full = jnp.concatenate(
-                [jnp.where(first, both, turned), jnp.where(first, turned, both)], axis=0
-            )
-            high, low = split_two(full)
-            left_high[w, j] = high
-            left_low[w, j] = low
-            packed = sent[w, j, wide : wide + rows]
-            for g in range(4):
-                shift = (wide * (w - g)) % lanes
-                moved = pltpu.roll(packed, shift, 1) if shift else packed
-                columns[g] = jnp.where(lane_rows == w, moved, columns[g])
-        store_right(jnp.concatenate(columns, axis=0), per, right_out, j)
+    first_rows = lane_is_first(rows)
+    for w in range(per):
+        both = sent[w, j, 0:wide]
+        turned = pltpu.roll(both, half, 1)
+        full = jnp.concatenate(
+            [jnp.where(first, both, turned), jnp.where(first, turned, both)], axis=0
+        )
+        high, low = split_two(full)
+        left_high[w, j] = high
+        left_low[w, j] = low
+        both = sent[w, j, wide : wide + rows]
+        turned = pltpu.roll(both, half, 1)
+        full = jnp.concatenate(
+            [jnp.where(first_rows, both, turned), jnp.where(first_rows, turned, both)], axis=0
+        )
+        high, low = split_two(full)
+        right_out[j, wide * w : wide * (w + 1), 0:lanes] = high
+        right_out[j, wide * w : wide * (w + 1), lanes:] = low
 
 
 def operand_specs(per, step, half, lanes):
@@ -292,42 +284,36 @@
             + [pl.BlockSpec((per, step, rows, lanes), lambda i, *_: (0, i, 0, 0))] * 3,
             out_specs=operand_specs(per, step, half, lanes)
             + [pl.BlockSpec((per, step, 3 * rows, lanes), lambda i, *_: (0, i, 0, 0))],
-            scratch_shapes=[pltpu.VMEM((per, step, half, lanes), jnp.float32)],
+            scratch_shapes=[
+                pltpu.VMEM((per, step, half, lanes), jnp.float32),
+                pltpu.VMEM((per, step, lanes, lanes), jnp.float32),
+            ],
         ),
         out_shape=operand_shapes(per, blocks, half, lanes)
         + [jax.ShapeDtypeStruct((per, blocks, 3 * rows, lanes), jnp.float32)],
         compiler_params=pltpu.CompilerParams(vmem_limit_bytes=VMEM_LIMIT),
-        cost_estimate=micros(3),
+        cost_estimate=micros(12),
         name="own_operands",
     )(info, by_owner, *pieces)
 
 
-def other_operands(sent):
-    per, blocks, rows, lanes = sent.shape
-    half = lanes // 2
-    step = 4
-    return pl.pallas_call(
-        other_operands_kernel,
-        grid=(blocks // step,),
-        in_specs=[pl.BlockSpec((per, step, rows, lanes), lambda i: (0, i, 0, 0))],
-        out_specs=operand_specs(per, step, half, lanes),
-        out_shape=operand_shapes(per, blocks, half, lanes),
-        compiler_params=pltpu.CompilerParams(vmem_limit_bytes=VMEM_LIMIT),
-        cost_estimate=micros(3),
-        name="other_operands",
-    )(sent)
-
-
 def apply_kernel(plan, info_ref, *refs):
-    chunks, parts_given, before_given, pieces = plan
+    chunks, parts_given, sent_given, before_given, pieces = plan
     refs = list(refs)
     take = lambda n: [refs.pop(0) for _ in range(n)]
     slots = take(2)
     vector = take(4 if parts_given else 1)
-    operands = [take(4) for _ in chunks]
-    before = take(1) if before_given else None
+    tiles = take(4) if parts_given else []
+    operands = [take(3) for _ in chunks[: -1 if sent_given else None]]
+    sent = take(1)[0] if sent_given else None
+    mixes = take(len(chunks))
+    before = take(1)[0] if before_given else None
     outs = take(2 if pieces else 1)
-    total_ref, vec, mid = refs
+    if sent_given:
+        operands.append(take(3))
+    total_ref, vec, mid = take(3)
+    if before_given:
+        prior, arrival = take(2)
     step = mid.shape[0]
     lanes, half = LANES, LANES // 2
     first = lane_is_first(SUB)
@@ -339,9 +325,13 @@
 
     @pl.when(pl.program_id(0) == 0)
     def _():
-        total_ref[...] = before[0][...] if before_given else jnp.zeros_like(total_ref)
+        if before_given:
+            pltpu.make_async_copy(before, prior, arrival).start()
+        total_ref[...] = jnp.zeros_like(total_ref)
 
     def right_side(j):
+        if sent_given:
+            other_operands(sent, *operands[-1], j)
         if parts_given:
 
             def put(row, pair, high, low):
@@ -356,140 +346,152 @@
             source = vector[0][j]
         source = jnp.concatenate([source, source], axis=0)
         at = 0
-        for left_high, left_low, right, mix in operands:
+        for left_high, left_low, right in operands:
             count = right.shape[1]
             mid[j, at : at + count, :] = jnp.dot(
                 right[j], source, preferred_element_type=jnp.float32
             )
             at += count
 
-    def left_side(js, refs_of, w, row_of):
-        left_high, left_low, right, mix = refs_of
-        done = {}
-        for j in js:
-            tiles = []
-            for part in range(2):
-                row = row_of + part * 16
-                for pair in range(PHYS // 2):
-                    columns = slice(pair * lanes, (pair + 1) * lanes)
-                    upper = mid[j, row : row + SUB, columns]
-                    lower = mid[j, row + SUB : row + 2 * SUB, columns]
-                    tiles.append(jnp.where(first, upper, pltpu.roll(lower, half, 1)))
-                    tiles.append(jnp.where(first, pltpu.roll(upper, half, 1), lower))
-            t_high, t_low = split_two(jnp.concatenate(tiles, axis=0))
-            lh, ll = left_high[w, j], left_low[w, j]
-            wide_high = jnp.concatenate([lh * keep_first, lh * keep_second], axis=0)
-            wide_low = jnp.concatenate([ll * keep_first, ll * keep_second], axis=0)
-            weights = jnp.concatenate(
-                [
-                    jnp.concatenate([wide_high, wide_low], axis=1),
-                    jnp.concatenate([wide_high, nothing], axis=1),
-                ],
-                axis=0,
-            )
-            z = jnp.dot(
-                jnp.concatenate([t_high, t_low], axis=1),
-                weights,
-                preferred_element_type=jnp.float32,
-            )
-            z_high, z_low = split_two(z[:, :lanes] + z[:, lanes:])
-            for part in range(2):
-                rows = slice(part * lanes, (part + 1) * lanes)
-                done[part, j] = (z_high[rows], z_low[rows])
-        order = [(part, j) for part in range(2) for j in js]
-        return [jnp.concatenate([done[at][i] for at in order], axis=1) for i in range(2)]
-
-    def mix_and_add(js, refs_of, w, z, table, bond):
-        z_high, z_low = z
-        mix = refs_of[3]
-        mix_high = mix[w, :, 0:lanes]
-        mix_low = mix[w, :, lanes:]
+    def left_side(j, refs_of, w, row_of):
+        left_high, left_low, right = refs_of
+        tiles = []
+        for part in range(2):
+            row = row_of + part * 16
+            for pair in range(PHYS // 2):
+                columns = slice(pair * lanes, (pair + 1) * lanes)
+                upper = mid[j, row : row + SUB, columns]
+                lower = mid[j, row + SUB : row + 2 * SUB, columns]
+                tiles.append(jnp.where(first, upper, pltpu.roll(lower, half, 1)))
+                tiles.append(jnp.where(first, pltpu.roll(upper, half, 1), lower))
+        t_high, t_low = split_two(jnp.concatenate(tiles, axis=0))
+        lh, ll = left_high[w, j], left_low[w, j]
+        wide_high = jnp.concatenate([lh * keep_first, lh * keep_second], axis=0)
+        wide_low = jnp.concatenate([ll * keep_first, ll * keep_second], axis=0)
+        weights = jnp.concatenate(
+            [
+                jnp.concatenate([wide_high, wide_low], axis=1),
+                jnp.concatenate([wide_high, nothing], axis=1),
+            ],
+            axis=0,
+        )
+        z = jnp.dot(
+            jnp.concatenate([t_high, t_low], axis=1), weights, preferred_element_type=jnp.float32
+        )
+        return split_two(z[:, :lanes] + z[:, lanes:])
+
+    def mix_and_add(j, mix, w, z, table, bond):
+        z_high, z_low = [jnp.concatenate([x[:lanes], x[lanes:]], axis=1) for x in z]
         mixed = jnp.dot(
-            jnp.concatenate([mix_high, mix_high], axis=1),
-            jnp.concatenate([z_high, z_low], axis=0),
+            mix[w],
+            jnp.concatenate([z_high, z_low, z_high], axis=0),
             preferred_element_type=jnp.float32,
-        ) + jnp.dot(mix_low, z_high, preferred_element_type=jnp.float32)
-        for i, j in enumerate(js):
-            slot = table[bond, pl.program_id(0) * step + j]
-            slot = ((slot >> 1) ^ me) * 2 + (slot & 1)
-            for part in range(2):
-                at = part * len(js) + i
-                total_ref[part, slot] += mixed[:, at * lanes : (at + 1) * lanes]
+        )
+        slot = table[bond, pl.program_id(0) * step + j]
+        slot = ((slot >> 1) ^ me) * 2 + (slot & 1)
+        for part in range(2):
+            total_ref[part, slot] += mixed[:, part * lanes : (part + 1) * lanes]
 
     bonds = []
-    for chunk, refs_of in zip(chunks, operands):
-        count = refs_of[0].shape[0]
+    for chunk, refs_of, mix in zip(chunks, operands, mixes):
+        count = mix.shape[0]
         source, group = chunk // GROUPS, chunk % GROUPS
         for w in range(count):
-            bonds.append((refs_of, w, slots[source], group * count + w))
+            bonds.append((refs_of, mix, w, slots[source], group * count + w))
     right_side(0)
-    right_side(1)
     waiting = None
-    for start in range(0, step, 2):
-        js = (start, start + 1)
-        for at, (refs_of, w, table, bond) in enumerate(bonds):
-            z = left_side(js, refs_of, w, at * 32)
+    for j in range(step):
+        for at, (refs_of, mix, w, table, bond) in enumerate(bonds):
+            z = left_side(j, refs_of, w, at * 32)
             if waiting is not None:
                 mix_and_add(*waiting)
-            waiting = (js, refs_of, w, z, table, bond)
-            if start + 2 < step and at in (1, 3):
-                right_side(start + 2 + at // 2)
+            waiting = (j, mix, w, z, table, bond)
+            if j + 1 < step and at == len(bonds) // 3:
+                right_side(j + 1)
     mix_and_add(*waiting)
 
     @pl.when(pl.program_id(0) == pl.num_programs(0) - 1)
     def _():
+        if before_given:
+            pltpu.make_async_copy(before, prior, arrival).wait()
+            total_ref[...] += prior[...]
         if pieces:
-            outs[0][...] = total_ref[info_ref[5]]
-            outs[1][...] = total_ref[1 - info_ref[5]]
+            stats = jnp.zeros((SUB, lanes), jnp.float32)
+            if parts_given:
+                stats = stacked_rows(*merged([tile[...] for tile in tiles]))
+            for out, part in ((outs[0], info_ref[5]), (outs[1], 1 - info_ref[5])):
+                for k in range(4):
+                    for i in range(2):
+                        out[k, i * lanes : (i + 1) * lanes] = total_ref[part, 2 * k + i]
+                    out[k, 2 * lanes :] = stats
+                stats = jnp.zeros((SUB, lanes), jnp.float32)
         else:
             outs[0][...] = total_ref[...]
 
 
-def apply_bonds(info, slots, vector, chunks, operands, mixing, before, pieces):
+def apply_bonds(info, slots, vector, chunks, operands, sent, mixing, before, pieces):
     count, blocks, half, lanes = operands[0][0].shape
     step = 4
     parts_given = len(vector) == 4
     if parts_given:
+        last = vector[0].shape[0] // SUB - 1
         in_specs = [pl.BlockSpec((step * lanes, lanes), lambda i, *_: (i, 0))] * 4
+        in_specs += [pl.BlockSpec((SUB, lanes), lambda i, *_: (last, 0))] * 4
     else:
         in_specs = [pl.BlockSpec((step,) + vector[0].shape[1:], lambda i, *_: (i, 0, 0))]
-    arguments = list(vector)
-    for chunk, (left_high, left_low, right) in zip(chunks, operands):
+    arguments = list(vector) * (2 if parts_given else 1)
+    for made in operands:
         in_specs += operand_specs(count, step, half, lanes)
+        arguments += made
+    if sent is not None:
+        in_specs.append(
+            pl.BlockSpec((count, step) + sent.shape[2:], lambda i, *_: (0, i, 0, 0))
+        )
+        arguments.append(sent)
+    for chunk in chunks:
         in_specs.append(
             pl.BlockSpec((count,) + mixing.shape[1:], lambda i, *_, at=chunk: (at, 0, 0))
         )
-        arguments += [left_high, left_low, right, mixing]
+        arguments.append(mixing)
+    total = count * len(chunks)
+    scratch = [
+        pltpu.VMEM((2, 8, lanes, lanes), jnp.float32),
+        pltpu.VMEM((step, lanes, PHYS * half), jnp.bfloat16),
+        pltpu.VMEM((step, total * 32, PHYS * half), jnp.float32),
+    ]
     if before is not None:
-        in_specs.append(whole(*before.shape))
+        in_specs.append(pl.BlockSpec(memory_space=pl.ANY))
         arguments.append(before)
-    shapes = [(8, lanes, lanes)] * 2 if pieces else [(2, 8, lanes, lanes)]
-    plan = (tuple(chunks), parts_given, before is not None, pieces)
-    total = count * len(chunks)
-    return pl.pallas_call(
+        scratch += [pltpu.VMEM(before.shape, jnp.float32), pltpu.SemaphoreType.DMA]
+    shapes = [(4, 2 * lanes + SUB, lanes)] * 2 if pieces else [(2, 8, lanes, lanes)]
+    out_specs = [whole(*shape) for shape in shapes]
+    out_shape = [jax.ShapeDtypeStruct(shape, jnp.float32) for shape in shapes]
+    if sent is not None:
+        out_specs += operand_specs(count, step, half, lanes)
+        out_shape += operand_shapes(count, blocks, half, lanes)
+    plan = (tuple(chunks), parts_given, sent is not None, before is not None, pieces)
+    out = pl.pallas_call(
         functools.partial(apply_kernel, plan),
         grid_spec=pltpu.PrefetchScalarGridSpec(
             num_scalar_prefetch=3,
             grid=(blocks // step,),
             in_specs=in_specs,
-            out_specs=[whole(*shape) for shape in shapes],
-            scratch_shapes=[
-                pltpu.VMEM((2, 8, lanes, lanes), jnp.float32),
-                pltpu.VMEM((step, lanes, PHYS * half), jnp.bfloat16),
-                pltpu.VMEM((step, total * 32, PHYS * half), jnp.float32),
-            ],
+            out_specs=out_specs,
+            scratch_shapes=scratch,
         ),
-        out_shape=[jax.ShapeDtypeStruct(shape, jnp.float32) for shape in shapes],
+        out_shape=out_shape,
         compiler_params=pltpu.CompilerParams(vmem_limit_bytes=VMEM_LIMIT),
         cost_estimate=micros(2 + total),
         name="apply_bonds",
     )(info, *slots, *arguments)
+    return out[: len(shapes)], out[len(shapes) :]
 
 
 def add_arrived(info_ref, owner_ref, arrived, total):
     for k in range(4):
         for i in range(2):
-            total[owner_ref[info_ref[4] ^ k, i]] += arrived[k][i]
+            rows = slice(i * LANES, (i + 1) * LANES)
+            total[owner_ref[info_ref[4] ^ k, i]] += arrived[k][rows]
 
 
 def stacked_rows(*rows):
@@ -551,86 +553,28 @@
     )(info, owners, *arrived, diagonal, own)
 
 
-def join_kernel(mine, other, *refs):
-    tiles = refs[:-4] if len(refs) == 4 else refs[:-5]
-    pieces = refs[len(tiles) : len(tiles) + 4]
-    for k in range(4):
-        for i in range(2):
-            pieces[k][i] = mine[2 * k + i] + other[2 * k + i]
-    if tiles:
-        refs[-1][...] = stacked_rows(*merged([ref[...] for ref in tiles]))
-
-
-def join(mine, other, images):
-    shapes = [jax.ShapeDtypeStruct((2, LANES, LANES), jnp.float32)] * 4
-    if images:
-        shapes.append(jax.ShapeDtypeStruct((SUB, LANES), jnp.float32))
-    last = images[0].shape[0] // SUB - 1 if images else 0
-    return pl.pallas_call(
-        join_kernel,
-        grid=(1,),
-        in_specs=[whole(*mine.shape), whole(*other.shape)]
-        + [pl.BlockSpec((SUB, LANES), lambda i: (last, 0)) for _ in images],
-        out_specs=[whole(*x.shape) for x in shapes],
-        out_shape=shapes,
-        compiler_params=pltpu.CompilerParams(vmem_limit_bytes=VMEM_LIMIT),
-        cost_estimate=micros(1),
-        name="join",
-    )(mine, other, *images)
-
-
-def scales_of(tiles, entries):
-    cross, square, rest = merged(tiles)
+def final_kernel(
+    entries, info_ref, owner_ref, a0, a1, a2, a3, diag_ref, own_ref, image_ref, first_ref,
+    vector_ref, second_ref, total,
+):
+    arrived = (a0, a1, a2, a3)
+    cross, square, rest = merged([ref[2 * LANES :] for ref in arrived])
     scale = lax.rsqrt(square / entries + 1e-06)
     rayleigh = scale * scale * (cross / entries)
     apart = (cross / jnp.maximum(square, TINY) - rayleigh) * jnp.sqrt(square)
     mean = scale * scale * ((rest + apart * apart) / entries)
-    return scale, rayleigh, scale * lax.rsqrt(mean + 1e-06)
-
-
-def first_kernel(entries, s0, s1, s2, s3, image_ref, own_ref, first_ref, second_ref):
-    tiles = [ref[...] for ref in (s0, s1, s2, s3)]
-    scale, rayleigh, second_scale = scales_of(tiles, entries)
-    for k in range(own_ref.shape[0]):
+    second_scale = scale * lax.rsqrt(mean + 1e-06)
+    for k in range(total.shape[0]):
         image = image_ref[k * LANES : (k + 1) * LANES]
+        total[k] = (diag_ref[k] - rayleigh) * image
         first_ref[k] = unpack_tile(scale * image)
-        second_ref[k] = unpack_tile(second_scale * (image - rayleigh * own_ref[k]))
-
-
-def first_outputs(stats, image, own, entries):
-    step = 4
-    blocks = own.shape[0]
-    shape = (step, LANES // 2, 2 * LANES)
-    return pl.pallas_call(
-        functools.partial(first_kernel, entries),
-        grid=(blocks // step,),
-        in_specs=[whole(SUB, LANES)] * 4
-        + [
-            pl.BlockSpec((step * LANES, LANES), lambda i: (i, 0)),
-            pl.BlockSpec((step, LANES, LANES), lambda i: (i, 0, 0)),
-        ],
-        out_specs=[pl.BlockSpec(shape, lambda i: (i, 0, 0))] * 2,
-        out_shape=[jax.ShapeDtypeStruct((blocks,) + shape[1:], jnp.float32)] * 2,
-        compiler_params=pltpu.CompilerParams(vmem_limit_bytes=VMEM_LIMIT),
-        cost_estimate=micros(3),
-        name="first_outputs",
-    )(*stats, image, own)
-
-
-def final_kernel(
-    entries, info_ref, owner_ref, a0, a1, a2, a3, diag_ref, image_ref, s0, s1, s2, s3,
-    second_ref, total,
-):
-    tiles = [ref[...] for ref in (s0, s1, s2, s3)]
-    scale, rayleigh, second_scale = scales_of(tiles, entries)
-    for k in range(total.shape[0]):
-        total[k] = (diag_ref[k] - rayleigh) * image_ref[k * LANES : (k + 1) * LANES]
-    add_arrived(info_ref, owner_ref, (a0, a1, a2, a3), total)
+        vector_ref[k] = unpack_tile(second_scale * (image - rayleigh * own_ref[k]))
+    add_arrived(info_ref, owner_ref, arrived, total)
     for k in range(total.shape[0]):
         second_ref[k] = unpack_tile(second_scale * total[k])
 
 
-def second_output(info, owners, arrived, diagonal, image, stats, entries):
+def outputs(info, owners, arrived, diagonal, own, image, entries):
     blocks = diagonal.shape[0]
     shape = (blocks, LANES // 2, 2 * LANES)
     return pl.pallas_call(
@@ -638,17 +582,16 @@
         grid_spec=pltpu.PrefetchScalarGridSpec(
             num_scalar_prefetch=2,
             grid=(1,),
-            in_specs=[whole(*x.shape) for x in (*arrived, diagonal)]
-            + [whole(blocks * LANES, LANES)]
-            + [whole(SUB, LANES)] * 4,
-            out_specs=whole(*shape),
+            in_specs=[whole(*x.shape) for x in (*arrived, diagonal, own)]
+            + [whole(blocks * LANES, LANES)],
+            out_specs=[whole(*shape)] * 3,
             scratch_shapes=[pltpu.VMEM(diagonal.shape, jnp.float32)],
         ),
-        out_shape=jax.ShapeDtypeStruct(shape, jnp.float32),
+        out_shape=[jax.ShapeDtypeStruct(shape, jnp.float32)] * 3,
         compiler_params=pltpu.CompilerParams(vmem_limit_bytes=VMEM_LIMIT),
-        cost_estimate=micros(3),
-        name="second_output",
-    )(info, owners, *arrived, diagonal, image, *stats)
+        cost_estimate=micros(4),
+        name="outputs",
+    )(info, owners, *arrived, diagonal, own, image)
 
 
 def partner(x, axis, k):
@@ -665,14 +608,14 @@
     return [x, across, partner(x, "rep", 1), partner(across, "rep", 1)]
 
 
-def everyone(x, axes):
-    return [x] + [partner(x, axes, k) for k in range(1, 4)]
-
-
-def to_owners(mine, theirs, images):
-    out = join(mine, partner(theirs, "rep", 1), images)
-    arrived = [out[0]] + [partner(out[k], "blk", k) for k in range(1, 4)]
-    return arrived, everyone(out[4], "blk") if images else None
+def everyone_of(pieces, axis):
+    return [pieces[0]] + [partner(pieces[k], axis, k) for k in range(1, 4)]
+
+
+def to_owners(mine, theirs):
+    other = partner(theirs, "rep", 1)
+    pieces = [mine[k] + other[k] for k in range(4)]
+    return everyone_of(pieces, "blk")
 
 
 def per_device(wavefunction, environment, bond_terms, diagonal, term_slot, slot_block):
@@ -696,7 +639,7 @@
         for k in range(1, 4):
             piece = lax.dynamic_index_in_dim(mine, blk ^ k, 1, keepdims=False)
             if group:
-                piece = after(piece, pieces[group - 1][k])
+                piece = after(piece, pieces[group - 1][1])
             pieces[group][k] = partner(piece, "blk", k)
     pieces[0][1] = after(pieces[0][1], vector, mixing)
     made, sent = [], []
@@ -705,29 +648,26 @@
         made.append(own_set)
         sent.append(send)
     received = [partner(send, "mpo", 1) for send in sent]
-    operands = [[made[g], other_operands(received[g])] for g in range(GROUPS)]
 
     total = None
+    operands = []
     for group in range(GROUPS):
         last = group == GROUPS - 1
         given = vector if last else after(vector, *sent)
-        out = apply_bonds(
-            info, slots, [given], [group, GROUPS + group], operands[group], mixing, total, last
-        )
+        out, other = apply_bonds(
+            info, slots, [given], [group, GROUPS + group], [made[group]], received[group], mixing,
+            total, last,
+        )
+        operands += [made[group], other]
         total = None if last else out[0]
-    arrived, _ = to_owners(*out, [])
-    image = owner_image(info, slot_block, arrived, diagonal_packed, own)
+    image = owner_image(info, slot_block, to_owners(*out), diagonal_packed, own)
 
     parts = gathered(image)
     chunks = [group + GROUPS * source for group in range(GROUPS) for source in range(2)]
-    flat = [operands[group][source] for group in range(GROUPS) for source in range(2)]
-    out = apply_bonds(info, slots, parts, chunks, flat, mixing, None, True)
-    arrived, stats = to_owners(*out, parts)
-    first_image, second_vector = first_outputs(stats, image, own, entries)
-    second_image = second_output(
-        info, slot_block, arrived, diagonal_packed, image, stats, entries
-    )
-    return (first_image, second_vector, second_image)
+    out, _ = apply_bonds(info, slots, parts, chunks, operands, None, mixing, None, True)
+    return tuple(
+        outputs(info, slot_block, to_owners(*out), diagonal_packed, own, image, entries)
+    )
 
 
 def solution(mesh):

time: 168 us -> 153 us (0.911)
  Pallas kernels: 70.8 us -> 57.1 us
  other arithmetic: 0 us -> 3.61 us
  starting transfers between devices: 32.4 us -> 29.8 us
    pallas_call x6 -> x1, Pallas kernels: 15.8 us -> 3.77 us  [outputs(): pl.pallas_call(functools.partial(final_kernel, entries), grid_spec=pltpu....]
    unnamed x53 -> x29, local copies, waits for them, and re-layouts: 9.89 us -> 5.04 us
    add x0 -> x2, other arithmetic: none -> 3.61 us  [to_owners(): pieces = [mine[k] + other[k] for k in range(4)]]
    ppermute x24 -> x21, starting transfers between devices: 32.4 us -> 29.8 us  [partner(): return lax.ppermute(x, axis, [(i, i ^ k) for i in range(size)])]
    squeeze x2, local copies, waits for them, and re-layouts: 0.09 us -> 2.69 us  [per_device(): piece = lax.dynamic_index_in_dim(mine, blk ^ k, 1, keepdims=False)]
    pallas_call x2, Pallas kernels: 9.37 us -> 7.2 us  [own_operands(): pl.pallas_call(own_operands_kernel, grid_spec=pltpu.PrefetchScalarGridSpe...]
    ppermute x24 -> x21, waiting for transfers between devices: 51.5 us -> 50.7 us  [partner(): return lax.ppermute(x, axis, [(i, i ^ k) for i in range(size)])]
  transfers between devices with their start and end apart: 24 -> 21, of which waited for: 10 -> 10; matrix products, arithmetic and copies ran while one was open for 1% -> 2% of each run, Pallas kernels for 16% -> 16%
where the time goes in v5:
time: 153 us
  Pallas kernels  57.1 us (37%)
  waiting for transfers between devices  50.7 us (33%)
  starting transfers between devices  29.8 us (19%)
  local copies, waits for them, and re-layouts  10.8 us (7%)
  other arithmetic  3.61 us (2%)
    ppermute x21, waiting for transfers between devices, partner(): return lax.ppermute(x, axis, [(i, i ^ k) for i in range(size)])  50.7 us
    pallas_call x3, Pallas kernels, apply_bonds(): pl.pallas_call(functools.partial(apply_kernel, plan), grid_spec=pltpu.Pre...  34.8 us
    ppermute x21, starting transfers between devices, partner(): return lax.ppermute(x, axis, [(i, i ^ k) for i in range(size)])  29.8 us
    pallas_call x2, Pallas kernels, own_operands(): pl.pallas_call(own_operands_kernel, grid_spec=pltpu.PrefetchScalarGridSpe...  7.2 us
    pallas_call x1, Pallas kernels, pack(): pl.pallas_call(pack_kernel, grid_spec=pltpu.PrefetchScalarGridSpec(num_sc...  5.58 us
    unnamed x29, local copies, waits for them, and re-layouts  5.04 us
    pallas_call x1, Pallas kernels, outputs(): pl.pallas_call(functools.partial(final_kernel, entries), grid_spec=pltpu....  3.77 us
    add x2, other arithmetic, to_owners(): pieces = [mine[k] + other[k] for k in range(4)]  3.61 us
  transfers between devices with their start and end apart: 21, of which 10 were waited for; matrix products, arithmetic and copies ran while one was open for 2% of the time, Pallas kernels for 16%

profile of v5, /device:TPU:0, one launch (start us, length us, event | category | flops | bytes accessed | tf_op | source)
XLA Modules:
  0.0 152.8 jit_solution(15144178792235907515)
XLA Ops:
  0.7 2.4 %fusion.8 = (f32[3,32,16,128]{3,2,1,0:T(8,128)S(1)}, f32[3,32,16,128]{3,2,1,0:T(8,128)}) fusion(f32[6,32,16,128]{3,2,1,0:T(8,128)} %param.7), kind=kLoop, calls=%fused_computation.22 | loop fusion | bytes 3145728 | tf_op jit(solution)/shard_map/slice | solution.py:638
  3.8 3.0 %collective-permute-start.1 = (f32[3,8,16,128]{3,2,1,0:T(8,128)}, f32[3,8,16,128]{3,2,1,0:T(8,128)}, u32[]{:S(2)}, u32[]{:S(2)}) collective-permute-start(f32[3,8,16,128]{3,2,1,0:T(8,128)} %get-tuple-element.69), channel_id=1, source_target_pairs={{0,4},{4,0},{8,12},{12,8},{1,5},{5,1},{9,13},{13,9},{2,6},{6,2},{1... | collective-permute-start | bytes 589832 | tf_op jit(solution)/shard_map/ppermute | solution.py:599
  8.4 2.6 %collective-permute-start.7 = (f32[3,8,16,128]{3,2,1,0:T(8,128)S(1)}, f32[3,8,16,128]{3,2,1,0:T(8,128)}, u32[]{:S(2)}, u32[]{:S(2)}) collective-permute-start(f32[3,8,16,128]{3,2,1,0:T(8,128)S(1)} %get-tuple-element.68), channel_id=1, source_target_pairs={{0,8},{4,12},{8,0},{12,4},{1,9},{5,13},{9,1},{13,5},{2,10},{6,14},... | collective-permute-start | bytes 589832 | tf_op jit(solution)/shard_map/ppermute | solution.py:599
  12.2 5.6 %pack.1 = (bf16[8,128,1024]{2,1,0:T(8,128)(2,1)}, f32[8,128,128]{2,1,0:T(8,128)}, f32[8,128,128]{2,1,0:T(8,128)}) custom-call(s32[7]{0:T(128)} %stack.31.info_ref, f32[8,64,1024]{2,1,0:T(8,128)} %own_wave_ref.1, f32[8,64,1024]{2,1,0:T(8,128)} %own_wave_ref.1, f32[8,64,256]{2,1,0:T(8,128)} %diag_ref.1), custom_call_target="tpu_custom_call" | custom-call | flops 5500000256 | bytes 1048576 | tf_op jit(solution)/shard_map/pack/pallas_call | solution.py:139
  17.7 1.9 %dynamic-slice_bitcast_fusion.2 = (f32[3,8,16,128]{3,2,1,0:T(8,128)}, f32[3,8,16,128]{3,2,1,0:T(8,128)}, f32[3,8,16,128]{3,2,1,0:T(8,128)}) fusion(f32[3,4,8,16,128]{4,3,2,1,0:T(8,128)} %bitcast.50, s32[]{:T(128)S(6)} %select_n.15, s32[]{:T(128)S(6)} %select_n.14, s32[]{:T(128)S(6)} %select_n.13), kind=kLoop, calls=%fused_computation.2 | loop fusion | bytes 1179660 | tf_op jit(solution)/shard_map/jit(dynamic_index_in_dim)/squeeze | solution.py:640
  19.7 2.2 %mixing.1.refs_7_.refs_8_.refs_22_.refs_23_.refs_24_.refs_25_ = bf16[12,128,384]{2,1,0:T(8,128)(2,1)} custom-call(f32[6,16,16]{2,1,0:T(8,128)} %refs_0_.4, f32[6,16,16]{2,1,0:T(8,128)} %collective-permute-done.6.refs_1_), custom_call_target="tpu_custom_call" | custom-call | flops 2200000000 | bytes 1048576 | tf_op jit(solution)/shard_map/mixing/pallas_call | solution.py:187
  22.8 3.5 %collective-permute-start.3 = (f32[3,8,16,128]{3,2,1,0:T(8,128)}, f32[3,8,16,128]{3,2,1,0:T(8,128)}, u32[]{:S(2)}, u32[]{:S(2)}) collective-permute-start(f32[3,8,16,128]{3,2,1,0:T(8,128)} %get-tuple-element.32), channel_id=1, source_target_pairs={{0,8},{4,12},{8,0},{12,4},{1,9},{5,13},{9,1},{13,5},{2,10},{6,14},... | collective-permute-start | bytes 589832 | tf_op jit(solution)/shard_map/ppermute | solution.py:599
  27.8 3.6 %own_operands.3 = (bf16[3,8,64,128]{3,2,1,0:T(8,128)(2,1)}, bf16[3,8,64,128]{3,2,1,0:T(8,128)(2,1)}, bf16[8,96,256]{2,1,0:T(8,128)(2,1)}, f32[3,8,48,128]{3,2,1,0:T(8,128)}) custom-call(s32[7]{0:T(128)} %stack.31.info_ref, f32[6,4,8,16,128]{4,3,2,1,0:T(8,128)} %bitcast.52, f32[3,8,16,128]{3,2,1,0:T(8,128)} %collective-permute-done.1.refs_1_, ...), custom_call_target="tpu_custom_call" | custom-call | flops 13200000000 | bytes 1048576 | tf_op jit(solution)/shard_map/own_operands/pallas_call | solution.py:274
  32.3 10.2 %collective-permute-done.3.refs_2_ = f32[3,8,16,128]{3,2,1,0:T(8,128)} collective-permute-done((f32[3,8,16,128]{3,2,1,0:T(8,128)}, f32[3,8,16,128]{3,2,1,0:T(8,128)}, u32[]{:S(2)}, u32[]{:S(2)}) %collective-permute-start.3) | collective-permute-done | bytes 196640 | tf_op jit(solution)/shard_map/ppermute | solution.py:599
  43.2 3.6 %own_operands.2 = (bf16[3,8,64,128]{3,2,1,0:T(8,128)(2,1)}, bf16[3,8,64,128]{3,2,1,0:T(8,128)(2,1)}, bf16[8,96,256]{2,1,0:T(8,128)(2,1)}, f32[3,8,48,128]{3,2,1,0:T(8,128)}) custom-call(s32[7]{0:T(128)} %stack.31.info_ref, f32[6,4,8,16,128]{4,3,2,1,0:T(8,128)} %bitcast.53, f32[3,8,16,128]{3,2,1,0:T(8,128)} %collective-permute-done.2.refs_1_, ...), custom_call_target="tpu_custom_call" | custom-call | flops 13200000000 | bytes 1048576 | tf_op jit(solution)/shard_map/own_operands/pallas_call | solution.py:274
  47.7 9.6 %apply_bonds.3 = (f32[2,8,128,128]{3,2,1,0:T(8,128)}, bf16[3,8,64,128]{3,2,1,0:T(8,128)(2,1)}, bf16[3,8,64,128]{3,2,1,0:T(8,128)(2,1)}, bf16[8,96,256]{2,1,0:T(8,128)(2,1)}) custom-call(s32[7]{0:T(128)} %stack.31.info_ref, s32[6,8]{1,0:T(8,128)} %refs_0_.7, s32[6,8]{1,0:T(8,128)} %copy-done.13, bf16[8,128,1024]{2,1,0:T(8,128)(2,1)} %get-tuple-element.40.refs_2_, ...), custom_call_target="tpu_custom_call" | custom-call | flops 8800000000 | bytes 1048576 | tf_op jit(solution)/shard_map/apply_bonds/pallas_call | solution.py:473
  59.0 9.6 %apply_bonds.4 = (f32[4,264,128]{2,1,0:T(8,128)}, f32[4,264,128]{2,1,0:T(8,128)}, bf16[3,8,64,128]{3,2,1,0:T(8,128)(2,1)}, bf16[3,8,64,128]{3,2,1,0:T(8,128)(2,1)}, bf16[8,96,256]{2,1,0:T(8,128)(2,1)}) custom-call(s32[7]{0:T(128)} %stack.31.info_ref, s32[6,8]{1,0:T(8,128)} %refs_0_.7, s32[6,8]{1,0:T(8,128)} %copy-done.13, ...), custom_call_target="tpu_custom_call" | custom-call | flops 8800000000 | bytes 1048576 | tf_op jit(solution)/shard_map/apply_bonds/pallas_call | solution.py:473
  68.7 2.1 %collective-permute-done.10 = f32[4,264,128]{2,1,0:T(8,128)S(1)} collective-permute-done((f32[4,264,128]{2,1,0:T(8,128)}, f32[4,264,128]{2,1,0:T(8,128)S(1)}, u32[]{:S(2)}, u32[]{:S(2)}) %collective-permute-start.10) | collective-permute-done | bytes 540704 | tf_op jit(solution)/shard_map/ppermute | solution.py:599
  72.6 6.3 %collective-permute-start.11 = (f32[264,128]{1,0:T(8,128)S(1)}, f32[264,128]{1,0:T(8,128)S(1)}, u32[]{:S(2)}, u32[]{:S(2)}) collective-permute-start(f32[264,128]{1,0:T(8,128)S(1)} %get-tuple-element.65), channel_id=1, source_target_pairs={{0,4},{4,0},{8,12},{12,8},{1,5},{5,1},{9,13},{13,9},{2,6},{6,2},{1... | collective-permute-start | bytes 405512 | tf_op jit(solution)/shard_map/ppermute | solution.py:599
  82.0 2.7 %collective-permute-done.11.a1 = f32[264,128]{1,0:T(8,128)S(1)} collective-permute-done((f32[264,128]{1,0:T(8,128)S(1)}, f32[264,128]{1,0:T(8,128)S(1)}, u32[]{:S(2)}, u32[]{:S(2)}) %collective-permute-start.11) | collective-permute-done | bytes 135200 | tf_op jit(solution)/shard_map/ppermute | solution.py:599
  84.8 7.4 %collective-permute-done.12.a2 = f32[264,128]{1,0:T(8,128)S(1)} collective-permute-done((f32[264,128]{1,0:T(8,128)S(1)}, f32[264,128]{1,0:T(8,128)S(1)}, u32[]{:S(2)}, u32[]{:S(2)}) %collective-permute-start.12) | collective-permute-done | bytes 135200 | tf_op jit(solution)/shard_map/ppermute | solution.py:599
  92.9 3.5 %owner_image.1.refs_2_.refs_6_.image_ref = f32[1032,128]{1,0:T(8,128)} custom-call(s32[7]{0:T(128)} %stack.31.info_ref, s32[4,2]{1,0:T(4,128)} %copy.16.owner_ref, f32[264,128]{1,0:T(8,128)} %get-tuple-element.66.a0, f32[264,128]{1,0:T(8,128)} %copy-done.7, f32[264,128]{1,0:T(8,128)} %copy-done.9, f32[264,128]{1,0:T(8,128)} %copy-done.10, ...), custom_call_target="tpu_custom_call" | custom-call | flops 3300000000 | bytes 1048576 | tf_op jit(solution)/shard_map/owner_image/pallas_call | solution.py:540
  96.4 11.8 %collective-permute-done.14.refs_3_.refs_7_ = f32[1032,128]{1,0:T(8,128)S(1)} collective-permute-done((f32[1032,128]{1,0:T(8,128)}, f32[1032,128]{1,0:T(8,128)S(1)}, u32[]{:S(2)}, u32[]{:S(2)}) %collective-permute-start.14) | collective-permute-done | bytes 528416 | tf_op jit(solution)/shard_map/ppermute | solution.py:599
  111.7 15.7 %apply_bonds.5 = (f32[4,264,128]{2,1,0:T(8,128)}, f32[4,264,128]{2,1,0:T(8,128)}) custom-call(s32[7]{0:T(128)} %stack.31.info_ref, s32[6,8]{1,0:T(8,128)} %refs_0_.7, s32[6,8]{1,0:T(8,128)} %copy-done.13, f32[1032,128]{1,0:T(8,128)} %owner_image.1.refs_2_.refs_6_.image_ref, f32[1032,128]{1,0:T(8,128)} %copy-done.1, f32[1032,128]{1,0:T(8,128)} %copy-done.2, ...), custom_call_target="tpu_custom_call" | custom-call | flops 15399999488 | bytes 1048576 | tf_op jit(solution)/shard_map/apply_bonds/pallas_call | solution.py:473
  127.6 2.0 %collective-permute-done.17 = f32[4,264,128]{2,1,0:T(8,128)S(1)} collective-permute-done((f32[4,264,128]{2,1,0:T(8,128)}, f32[4,264,128]{2,1,0:T(8,128)S(1)}, u32[]{:S(2)}, u32[]{:S(2)}) %collective-permute-start.17) | collective-permute-done | bytes 540704 | tf_op jit(solution)/shard_map/ppermute | solution.py:599
  131.4 3.7 %collective-permute-start.18 = (f32[264,128]{1,0:T(8,128)S(1)}, f32[264,128]{1,0:T(8,128)S(1)}, u32[]{:S(2)}, u32[]{:S(2)}) collective-permute-start(f32[264,128]{1,0:T(8,128)S(1)} %get-tuple-element.61), channel_id=1, source_target_pairs={{0,4},{4,0},{8,12},{12,8},{1,5},{5,1},{9,13},{13,9},{2,6},{6,2},{1... | collective-permute-start | bytes 405512 | tf_op jit(solution)/shard_map/ppermute | solution.py:599
  137.4 3.4 %collective-permute-done.18.a1 = f32[264,128]{1,0:T(8,128)S(1)} collective-permute-done((f32[264,128]{1,0:T(8,128)S(1)}, f32[264,128]{1,0:T(8,128)S(1)}, u32[]{:S(2)}, u32[]{:S(2)}) %collective-permute-start.18) | collective-permute-done | bytes 135200 | tf_op jit(solution)/shard_map/ppermute | solution.py:599
  140.9 7.4 %collective-permute-done.19.a2 = f32[264,128]{1,0:T(8,128)S(1)} collective-permute-done((f32[264,128]{1,0:T(8,128)S(1)}, f32[264,128]{1,0:T(8,128)S(1)}, u32[]{:S(2)}, u32[]{:S(2)}) %collective-permute-start.19) | collective-permute-done | bytes 135200 | tf_op jit(solution)/shard_map/ppermute | solution.py:599
  149.0 3.8 %outputs.1 = (f32[8,64,256]{2,1,0:T(8,128)}, f32[8,64,256]{2,1,0:T(8,128)}, f32[8,64,256]{2,1,0:T(8,128)}) custom-call(s32[7]{0:T(128)} %stack.31.info_ref, s32[4,2]{1,0:T(4,128)} %copy.16.owner_ref, f32[264,128]{1,0:T(8,128)} %get-tuple-element.62.a0, f32[264,128]{1,0:T(8,128)} %copy-done.5, f32[264,128]{1,0:T(8,128)} %copy-done.6, f32[264,128]{1,0:T(8,128)} %copy-done.8, ...), custom_call_target="tpu_custom_call" | custom-call | flops 4400000000 | bytes 1048576 | tf_op jit(solution)/shard_map/outputs/pallas_call | solution.py:580
  (62 shorter events, 24.4 us)
Async XLA Ops:
  0.7 10.5 %copy-start.12 = (s32[6,8]{1,0:T(8,128)S(1)}, s32[6,8]{1,0:T(8,128)}, u32[]{:S(2)}) copy-start(s32[6,8]{1,0:T(8,128)} %refs_0_.7) | copy-start | bytes 580
  3.8 18.0 %collective-permute-start.1 = (f32[3,8,16,128]{3,2,1,0:T(8,128)}, f32[3,8,16,128]{3,2,1,0:T(8,128)}, u32[]{:S(2)}, u32[]{:S(2)}) collective-permute-start(f32[3,8,16,128]{3,2,1,0:T(8,128)} %get-tuple-element.69), channel_id=1, source_target_pairs={{0,4},{4,0},{8,12},{12,8},{1,5},{5,1},{9,13},{13,9},{2,6},{6,2},{1... | collective-permute-start | bytes 589832 | tf_op jit(solution)/shard_map/ppermute | solution.py:599
  6.9 12.8 %collective-permute-start.6 = (f32[6,16,16]{2,1,0:T(8,128)S(1)}, f32[6,16,16]{2,1,0:T(8,128)}, u32[]{:S(2)}, u32[]{:S(2)}) collective-permute-start(f32[6,16,16]{2,1,0:T(8,128)S(1)} %copy-done.11), channel_id=1, source_target_pairs={{0,2},{2,0},{1,3},{3,1},{4,6},{6,4},{5,7},{7,5},{8,10},{10,8},{9,1... | collective-permute-start | bytes 18440 | tf_op jit(solution)/shard_map/ppermute | solution.py:599
  8.4 17.9 %collective-permute-start.7 = (f32[3,8,16,128]{3,2,1,0:T(8,128)S(1)}, f32[3,8,16,128]{3,2,1,0:T(8,128)}, u32[]{:S(2)}, u32[]{:S(2)}) collective-permute-start(f32[3,8,16,128]{3,2,1,0:T(8,128)S(1)} %get-tuple-element.68), channel_id=1, source_target_pairs={{0,8},{4,12},{8,0},{12,4},{1,9},{5,13},{9,1},{13,5},{2,10},{6,14},... | collective-permute-start | bytes 589832 | tf_op jit(solution)/shard_map/ppermute | solution.py:599
  10.9 16.9 %collective-permute-start.8 = (f32[3,8,16,128]{3,2,1,0:T(8,128)S(1)}, f32[3,8,16,128]{3,2,1,0:T(8,128)}, u32[]{:S(2)}, u32[]{:S(2)}) collective-permute-start(f32[3,8,16,128]{3,2,1,0:T(8,128)S(1)} %get-tuple-element.67), channel_id=1, source_target_pairs={{0,12},{4,8},{8,4},{12,0},{1,13},{5,9},{9,5},{13,1},{2,14},{6,10},... | collective-permute-start | bytes 589832 | tf_op jit(solution)/shard_map/ppermute | solution.py:599
  11.2 35.9 %collective-permute-start = (s32[6,8]{1,0:T(8,128)S(1)}, s32[6,8]{1,0:T(8,128)S(1)}, u32[]{:S(2)}, u32[]{:S(2)}) collective-permute-start(s32[6,8]{1,0:T(8,128)S(1)} %copy-done.12), channel_id=1, source_target_pairs={{0,2},{2,0},{1,3},{3,1},{4,6},{6,4},{5,7},{7,5},{8,10},{10,8},{9,1... | collective-permute-start | bytes 584 | tf_op jit(solution)/shard_map/ppermute | solution.py:599
  21.9 10.4 %collective-permute-start.2 = (f32[3,8,16,128]{3,2,1,0:T(8,128)}, f32[3,8,16,128]{3,2,1,0:T(8,128)}, u32[]{:S(2)}, u32[]{:S(2)}) collective-permute-start(f32[3,8,16,128]{3,2,1,0:T(8,128)} %get-tuple-element.31), channel_id=1, source_target_pairs={{0,4},{4,0},{8,12},{12,8},{1,5},{5,1},{9,13},{13,9},{2,6},{6,2},{1... | collective-permute-start | bytes 589832 | tf_op jit(solution)/shard_map/ppermute | solution.py:599
  22.8 19.7 %collective-permute-start.3 = (f32[3,8,16,128]{3,2,1,0:T(8,128)}, f32[3,8,16,128]{3,2,1,0:T(8,128)}, u32[]{:S(2)}, u32[]{:S(2)}) collective-permute-start(f32[3,8,16,128]{3,2,1,0:T(8,128)} %get-tuple-element.32), channel_id=1, source_target_pairs={{0,8},{4,12},{8,0},{12,4},{1,9},{5,13},{9,1},{13,5},{2,10},{6,14},... | collective-permute-start | bytes 589832 | tf_op jit(solution)/shard_map/ppermute | solution.py:599
  26.2 16.2 %collective-permute-start.4 = (f32[3,8,16,128]{3,2,1,0:T(8,128)}, f32[3,8,16,128]{3,2,1,0:T(8,128)S(1)}, u32[]{:S(2)}, u32[]{:S(2)}) collective-permute-start(f32[3,8,16,128]{3,2,1,0:T(8,128)} %get-tuple-element.33), channel_id=1, source_target_pairs={{0,12},{4,8},{8,4},{12,0},{1,13},{5,9},{9,5},{13,1},{2,14},{6,10},... | collective-permute-start | bytes 589832 | tf_op jit(solution)/shard_map/ppermute | solution.py:599
  31.4 15.7 %collective-permute-start.9 = (f32[3,8,48,128]{3,2,1,0:T(8,128)}, f32[3,8,48,128]{3,2,1,0:T(8,128)}, u32[]{:S(2)}, u32[]{:S(2)}) collective-permute-start(f32[3,8,48,128]{3,2,1,0:T(8,128)} %get-tuple-element.39), channel_id=1, source_target_pairs={{0,2},{2,0},{1,3},{3,1},{4,6},{6,4},{5,7},{7,5},{8,10},{10,8},{9,1... | collective-permute-start | bytes 1769480 | tf_op jit(solution)/shard_map/ppermute | solution.py:599
  46.7 12.2 %collective-permute-start.5 = (f32[3,8,48,128]{3,2,1,0:T(8,128)}, f32[3,8,48,128]{3,2,1,0:T(8,128)}, u32[]{:S(2)}, u32[]{:S(2)}) collective-permute-start(f32[3,8,48,128]{3,2,1,0:T(8,128)} %get-tuple-element.37), channel_id=1, source_target_pairs={{0,2},{2,0},{1,3},{3,1},{4,6},{6,4},{5,7},{7,5},{8,10},{10,8},{9,1... | collective-permute-start | bytes 1769480 | tf_op jit(solution)/shard_map/ppermute | solution.py:599
  68.6 12.7 %copy-start = (s32[4,2]{0,1:T(2,128)S(1)}, s32[4,2]{0,1:T(2,128)}, u32[]{:S(2)}) copy-start(s32[4,2]{0,1:T(2,128)} %param.11) | copy-start | bytes 100
  68.6 2.2 %collective-permute-start.10 = (f32[4,264,128]{2,1,0:T(8,128)}, f32[4,264,128]{2,1,0:T(8,128)S(1)}, u32[]{:S(2)}, u32[]{:S(2)}) collective-permute-start(f32[4,264,128]{2,1,0:T(8,128)} %get-tuple-element.46), channel_id=1, source_target_pairs={{0,1},{1,0},{2,3},{3,2},{4,5},{5,4},{6,7},{7,6},{8,9},{9,8},{10,11... | collective-permute-start | bytes 1622024 | tf_op jit(solution)/shard_map/ppermute | solution.py:599
  72.6 12.1 %collective-permute-start.11 = (f32[264,128]{1,0:T(8,128)S(1)}, f32[264,128]{1,0:T(8,128)S(1)}, u32[]{:S(2)}, u32[]{:S(2)}) collective-permute-start(f32[264,128]{1,0:T(8,128)S(1)} %get-tuple-element.65), channel_id=1, source_target_pairs={{0,4},{4,0},{8,12},{12,8},{1,5},{5,1},{9,13},{13,9},{2,6},{6,2},{1... | collective-permute-start | bytes 405512 | tf_op jit(solution)/shard_map/ppermute | solution.py:599
  79.0 13.2 %collective-permute-start.12 = (f32[264,128]{1,0:T(8,128)S(1)}, f32[264,128]{1,0:T(8,128)S(1)}, u32[]{:S(2)}, u32[]{:S(2)}) collective-permute-start(f32[264,128]{1,0:T(8,128)S(1)} %get-tuple-element.64), channel_id=1, source_target_pairs={{0,8},{4,12},{8,0},{12,4},{1,9},{5,13},{9,1},{13,5},{2,10},{6,14},... | collective-permute-start | bytes 405512 | tf_op jit(solution)/shard_map/ppermute | solution.py:599
  79.7 12.5 %collective-permute-start.13 = (f32[264,128]{1,0:T(8,128)S(1)}, f32[264,128]{1,0:T(8,128)S(1)}, u32[]{:S(2)}, u32[]{:S(2)}) collective-permute-start(f32[264,128]{1,0:T(8,128)S(1)} %get-tuple-element.63), channel_id=1, source_target_pairs={{0,12},{4,8},{8,4},{12,0},{1,13},{5,9},{9,5},{13,1},{2,14},{6,10},... | collective-permute-start | bytes 405512 | tf_op jit(solution)/shard_map/ppermute | solution.py:599
  84.7 7.4 %copy-start.7 = (f32[264,128]{1,0:T(8,128)}, f32[264,128]{1,0:T(8,128)S(1)}, u32[]{:S(2)}) copy-start(f32[264,128]{1,0:T(8,128)S(1)} %collective-permute-done.11.a1) | copy-start | bytes 405508
  96.4 11.8 %collective-permute-start.14 = (f32[1032,128]{1,0:T(8,128)}, f32[1032,128]{1,0:T(8,128)S(1)}, u32[]{:S(2)}, u32[]{:S(2)}) collective-permute-start(f32[1032,128]{1,0:T(8,128)} %owner_image.1.refs_2_.refs_6_.image_ref), channel_id=1, source_target_pairs={{0,2},{2,0},{1,3},{3,1},{4,6},{6,4},{5,7},{7,5},{8,10},{10,8},{9,1... | collective-permute-start | bytes 1585160 | tf_op jit(solution)/shard_map/ppermute | solution.py:599
  96.4 12.7 %collective-permute-start.15 = (f32[1032,128]{1,0:T(8,128)}, f32[1032,128]{1,0:T(8,128)S(1)}, u32[]{:S(2)}, u32[]{:S(2)}) collective-permute-start(f32[1032,128]{1,0:T(8,128)} %owner_image.1.refs_2_.refs_6_.image_ref), channel_id=1, source_target_pairs={{0,1},{1,0},{2,3},{3,2},{4,5},{5,4},{6,7},{7,6},{8,9},{9,8},{10,11... | collective-permute-start | bytes 1585160 | tf_op jit(solution)/shard_map/ppermute | solution.py:599
  109.0 1.9 %collective-permute-start.16 = (f32[1032,128]{1,0:T(8,128)S(1)}, f32[1032,128]{1,0:T(8,128)S(1)}, u32[]{:S(2)}, u32[]{:S(2)}) collective-permute-start(f32[1032,128]{1,0:T(8,128)S(1)} %collective-permute-done.14.refs_3_.refs_7_), channel_id=1, source_target_pairs={{0,1},{1,0},{2,3},{3,2},{4,5},{5,4},{6,7},{7,6},{8,9},{9,8},{10,11... | collective-permute-start | bytes 1585160 | tf_op jit(solution)/shard_map/ppermute | solution.py:599
  127.4 2.2 %collective-permute-start.17 = (f32[4,264,128]{2,1,0:T(8,128)}, f32[4,264,128]{2,1,0:T(8,128)S(1)}, u32[]{:S(2)}, u32[]{:S(2)}) collective-permute-start(f32[4,264,128]{2,1,0:T(8,128)} %get-tuple-element.56), channel_id=1, source_target_pairs={{0,1},{1,0},{2,3},{3,2},{4,5},{5,4},{6,7},{7,6},{8,9},{9,8},{10,11... | collective-permute-start | bytes 1622024 | tf_op jit(solution)/shard_map/ppermute | solution.py:599
  131.4 9.5 %collective-permute-start.18 = (f32[264,128]{1,0:T(8,128)S(1)}, f32[264,128]{1,0:T(8,128)S(1)}, u32[]{:S(2)}, u32[]{:S(2)}) collective-permute-start(f32[264,128]{1,0:T(8,128)S(1)} %get-tuple-element.61), channel_id=1, source_target_pairs={{0,4},{4,0},{8,12},{12,8},{1,5},{5,1},{9,13},{13,9},{2,6},{6,2},{1... | collective-permute-start | bytes 405512 | tf_op jit(solution)/shard_map/ppermute | solution.py:599
  135.1 13.2 %collective-permute-start.19 = (f32[264,128]{1,0:T(8,128)S(1)}, f32[264,128]{1,0:T(8,128)S(1)}, u32[]{:S(2)}, u32[]{:S(2)}) collective-permute-start(f32[264,128]{1,0:T(8,128)S(1)} %get-tuple-element.60), channel_id=1, source_target_pairs={{0,8},{4,12},{8,0},{12,4},{1,9},{5,13},{9,1},{13,5},{2,10},{6,14},... | collective-permute-start | bytes 405512 | tf_op jit(solution)/shard_map/ppermute | solution.py:599
  135.8 12.5 %collective-permute-start.20 = (f32[264,128]{1,0:T(8,128)S(1)}, f32[264,128]{1,0:T(8,128)S(1)}, u32[]{:S(2)}, u32[]{:S(2)}) collective-permute-start(f32[264,128]{1,0:T(8,128)S(1)} %get-tuple-element.59), channel_id=1, source_target_pairs={{0,12},{4,8},{8,4},{12,0},{1,13},{5,9},{9,5},{13,1},{2,14},{6,10},... | collective-permute-start | bytes 405512 | tf_op jit(solution)/shard_map/ppermute | solution.py:599
  (11 other events, 21.2 us)

commit v6 on v5

--- a/solution.py
+++ b/solution.py
@@ -11,8 +11,9 @@
 SUB = 8
 PHYS = 16
 TINY = 1e-30
-GROUPS = 2
-VMEM_LIMIT = 63 * 1024 * 1024 + 512 * 1024
+GROUPS = 3
+SMALL_VMEM = 16 * 1024 * 1024
+APPLY_VMEM = 36 * 1024 * 1024
 
 
 def plain_apply(vector_full, environment, bond_terms, term_slot, slot_block, diagonal):
@@ -154,7 +155,7 @@
             jax.ShapeDtypeStruct((blocks, LANES, LANES), jnp.float32),
             jax.ShapeDtypeStruct((blocks, LANES, LANES), jnp.float32),
         ],
-        compiler_params=pltpu.CompilerParams(vmem_limit_bytes=VMEM_LIMIT),
+        compiler_params=pltpu.CompilerParams(vmem_limit_bytes=SMALL_VMEM),
         cost_estimate=micros(5),
         name="pack",
     )(info, wavefunction, wavefunction, diagonal)
@@ -187,7 +188,7 @@
     return pl.pallas_call(
         mixing_kernel,
         out_shape=jax.ShapeDtypeStruct((count, LANES, 3 * LANES), jnp.bfloat16),
-        compiler_params=pltpu.CompilerParams(vmem_limit_bytes=VMEM_LIMIT),
+        compiler_params=pltpu.CompilerParams(vmem_limit_bytes=SMALL_VMEM),
         cost_estimate=micros(2),
         name="mixing",
     )(*sources)
@@ -291,8 +292,8 @@
         ),
         out_shape=operand_shapes(per, blocks, half, lanes)
         + [jax.ShapeDtypeStruct((per, blocks, 3 * rows, lanes), jnp.float32)],
-        compiler_params=pltpu.CompilerParams(vmem_limit_bytes=VMEM_LIMIT),
-        cost_estimate=micros(12),
+        compiler_params=pltpu.CompilerParams(vmem_limit_bytes=SMALL_VMEM),
+        cost_estimate=micros(6),
         name="own_operands",
     )(info, by_owner, *pieces)
 
@@ -353,7 +354,7 @@
             )
             at += count
 
-    def left_side(j, refs_of, w, row_of):
+    def prepared(j, refs_of, w, row_of):
         left_high, left_low, right = refs_of
         tiles = []
         for part in range(2):
@@ -375,18 +376,17 @@
             ],
             axis=0,
         )
-        z = jnp.dot(
-            jnp.concatenate([t_high, t_low], axis=1), weights, preferred_element_type=jnp.float32
-        )
-        return split_two(z[:, :lanes] + z[:, lanes:])
-
-    def mix_and_add(j, mix, w, z, table, bond):
+        return jnp.concatenate([t_high, t_low], axis=1), weights
+
+    def mix_unit(mixing, w, z):
         z_high, z_low = [jnp.concatenate([x[:lanes], x[lanes:]], axis=1) for x in z]
-        mixed = jnp.dot(
-            mix[w],
+        return jnp.dot(
+            mixing[w],
             jnp.concatenate([z_high, z_low, z_high], axis=0),
             preferred_element_type=jnp.float32,
         )
+
+    def add_up(j, table, bond, mixed):
         slot = table[bond, pl.program_id(0) * step + j]
         slot = ((slot >> 1) ^ me) * 2 + (slot & 1)
         for part in range(2):
@@ -399,16 +399,31 @@
         for w in range(count):
             bonds.append((refs_of, mix, w, slots[source], group * count + w))
     right_side(0)
+    units = [(j, at) for j in range(step) for at in range(len(bonds))]
+
+    def prepare_unit(n):
+        j, at = units[n]
+        refs_of, mixing, w, table, bond = bonds[at]
+        return prepared(j, refs_of, w, at * 32)
+
+    ready = prepare_unit(0)
     waiting = None
-    for j in range(step):
-        for at, (refs_of, mix, w, table, bond) in enumerate(bonds):
-            z = left_side(j, refs_of, w, at * 32)
-            if waiting is not None:
-                mix_and_add(*waiting)
-            waiting = (j, mix, w, z, table, bond)
-            if j + 1 < step and at == len(bonds) // 3:
-                right_side(j + 1)
-    mix_and_add(*waiting)
+    for n, (j, at) in enumerate(units):
+        refs_of, mixing, w, table, bond = bonds[at]
+        z = jnp.dot(*ready, preferred_element_type=jnp.float32)
+        if j + 1 < step and at == len(bonds) // 3:
+            right_side(j + 1)
+        if n + 1 < len(units):
+            ready = prepare_unit(n + 1)
+        if waiting is not None:
+            before_j, before_mixing, before_w, before_table, before_bond, before_z = waiting
+            mixed = mix_unit(before_mixing, before_w, before_z)
+        z = split_two(z[:, :lanes] + z[:, lanes:])
+        if waiting is not None:
+            add_up(before_j, before_table, before_bond, mixed)
+        waiting = (j, mixing, w, table, bond, z)
+    j, mixing, w, table, bond, z = waiting
+    add_up(j, table, bond, mix_unit(mixing, w, z))
 
     @pl.when(pl.program_id(0) == pl.num_programs(0) - 1)
     def _():
@@ -480,8 +495,8 @@
             scratch_shapes=scratch,
         ),
         out_shape=out_shape,
-        compiler_params=pltpu.CompilerParams(vmem_limit_bytes=VMEM_LIMIT),
-        cost_estimate=micros(2 + total),
+        compiler_params=pltpu.CompilerParams(vmem_limit_bytes=APPLY_VMEM),
+        cost_estimate=micros(1),
         name="apply_bonds",
     )(info, *slots, *arguments)
     return out[: len(shapes)], out[len(shapes) :]
@@ -547,7 +562,7 @@
             scratch_shapes=[pltpu.VMEM(own.shape, jnp.float32)],
         ),
         out_shape=jax.ShapeDtypeStruct((rows, LANES), jnp.float32),
-        compiler_params=pltpu.CompilerParams(vmem_limit_bytes=VMEM_LIMIT),
+        compiler_params=pltpu.CompilerParams(vmem_limit_bytes=SMALL_VMEM),
         cost_estimate=micros(3),
         name="owner_image",
     )(info, owners, *arrived, diagonal, own)
@@ -588,7 +603,7 @@
             scratch_shapes=[pltpu.VMEM(diagonal.shape, jnp.float32)],
         ),
         out_shape=[jax.ShapeDtypeStruct(shape, jnp.float32)] * 3,
-        compiler_params=pltpu.CompilerParams(vmem_limit_bytes=VMEM_LIMIT),
+        compiler_params=pltpu.CompilerParams(vmem_limit_bytes=SMALL_VMEM),
         cost_estimate=micros(4),
         name="outputs",
     )(info, owners, *arrived, diagonal, own, image)
@@ -643,23 +658,28 @@
             pieces[group][k] = partner(piece, "blk", k)
     pieces[0][1] = after(pieces[0][1], vector, mixing)
     made, sent = [], []
+    total = None
+    operands = []
+    done = 0
+
+    def apply_group(group, vector):
+        last = group == GROUPS - 1
+        out, other = apply_bonds(
+            info, slots, [vector], [group, GROUPS + group], [made[group]],
+            partner(sent[group], "mpo", 1), mixing, total, last,
+        )
+        operands.extend([made[group], other])
+        return out
+
     for group in range(GROUPS):
+        if group >= 2:
+            total = apply_group(group - 2, after(vector, sent[group - 1]))[0]
+            pieces[group][3] = after(pieces[group][3], total)
         *own_set, send = own_operands(info, by_owner, group, pieces[group][1:])
         made.append(own_set)
         sent.append(send)
-    received = [partner(send, "mpo", 1) for send in sent]
-
-    total = None
-    operands = []
-    for group in range(GROUPS):
-        last = group == GROUPS - 1
-        given = vector if last else after(vector, *sent)
-        out, other = apply_bonds(
-            info, slots, [given], [group, GROUPS + group], [made[group]], received[group], mixing,
-            total, last,
-        )
-        operands += [made[group], other]
-        total = None if last else out[0]
+    total = apply_group(GROUPS - 2, after(vector, sent[-1]))[0]
+    out = apply_group(GROUPS - 1, vector)
     image = owner_image(info, slot_block, to_owners(*out), diagonal_packed, own)
 
     parts = gathered(image)

time: 153 us -> 137 us (0.90)
  Pallas kernels: 57.1 us -> 42.5 us
  starting transfers between devices: 29.8 us -> 34.1 us
  waiting for transfers between devices: 50.7 us -> 47 us
  other arithmetic: 3.61 us -> 0.93 us
    ppermute x21 -> x25, starting transfers between devices: 29.8 us -> 34.1 us  [partner(): return lax.ppermute(x, axis, [(i, i ^ k) for i in range(size)])]
    ppermute x21 -> x25, waiting for transfers between devices: 50.7 us -> 47 us  [partner(): return lax.ppermute(x, axis, [(i, i ^ k) for i in range(size)])]
    pallas_call x3 -> x4, Pallas kernels: 34.8 us -> 31.2 us  [apply_bonds(): pl.pallas_call(functools.partial(apply_kernel, plan), grid_spec=pltpu.Pre...]
    pallas_call x2 -> x3, Pallas kernels: 7.2 us -> 4.09 us  [own_operands(): pl.pallas_call(own_operands_kernel, grid_spec=pltpu.PrefetchScalarGridSpe...]
    pallas_call x1, Pallas kernels: 5.58 us -> 2.53 us  [pack(): pl.pallas_call(pack_kernel, grid_spec=pltpu.PrefetchScalarGridSpec(num_sc...]
    add x2, other arithmetic: 3.61 us -> 0.93 us  [to_owners(): pieces = [mine[k] + other[k] for k in range(4)]]
    pallas_call x1, Pallas kernels: 2.18 us -> 0.34 us  [mixing_operand(): pl.pallas_call(mixing_kernel, out_shape=jax.ShapeDtypeStruct((count, LANE...]
    pallas_call x1, Pallas kernels: 3.77 us -> 2.08 us  [outputs(): pl.pallas_call(functools.partial(final_kernel, entries), grid_spec=pltpu....]
  transfers between devices with their start and end apart: 21 -> 25, of which waited for: 10 -> 11; matrix products, arithmetic and copies ran while one was open for 2% -> 2% of each run, Pallas kernels for 16% -> 13%
where the time goes in v6:
time: 137 us
  waiting for transfers between devices  47 us (34%)
  Pallas kernels  42.5 us (31%)
  starting transfers between devices  34.1 us (25%)
  local copies, waits for them, and re-layouts  11 us (8%)
    ppermute x25, waiting for transfers between devices, partner(): return lax.ppermute(x, axis, [(i, i ^ k) for i in range(size)])  47 us
    ppermute x25, starting transfers between devices, partner(): return lax.ppermute(x, axis, [(i, i ^ k) for i in range(size)])  34.1 us
    pallas_call x4, Pallas kernels, apply_bonds(): pl.pallas_call(functools.partial(apply_kernel, plan), grid_spec=pltpu.Pre...  31.2 us
    unnamed x69, local copies, waits for them, and re-layouts  4.54 us
    pallas_call x3, Pallas kernels, own_operands(): pl.pallas_call(own_operands_kernel, grid_spec=pltpu.PrefetchScalarGridSpe...  4.09 us
    squeeze x3, local copies, waits for them, and re-layouts, per_device(): piece = lax.dynamic_index_in_dim(mine, blk ^ k, 1, keepdims=False)  3.68 us
  transfers between devices with their start and end apart: 25, of which 11 were waited for; matrix products, arithmetic and copies ran while one was open for 2% of the time, Pallas kernels for 13%

profile of v6, /device:TPU:0, one launch (start us, length us, event | category | flops | bytes accessed | tf_op | source)
XLA Modules:
  0.0 136.7 jit_solution(16352570886444338860)
XLA Ops:
  0.7 2.7 %fusion.8 = (f32[2,32,16,128]{3,2,1,0:T(8,128)}, f32[2,32,16,128]{3,2,1,0:T(8,128)}, f32[2,32,16,128]{3,2,1,0:T(8,128)}) fusion(f32[6,32,16,128]{3,2,1,0:T(8,128)} %param.7), kind=kLoop, calls=%fused_computation.25 | loop fusion | bytes 3145728 | tf_op jit(solution)/shard_map/slice | solution.py:653
  5.2 3.0 %collective-permute-start.1 = (f32[2,8,16,128]{3,2,1,0:T(8,128)}, f32[2,8,16,128]{3,2,1,0:T(8,128)S(1)}, u32[]{:S(2)}, u32[]{:S(2)}) collective-permute-start(f32[2,8,16,128]{3,2,1,0:T(8,128)} %get-tuple-element.96), channel_id=1, source_target_pairs={{0,4},{4,0},{8,12},{12,8},{1,5},{5,1},{9,13},{13,9},{2,6},{6,2},{1... | collective-permute-start | bytes 393224 | tf_op jit(solution)/shard_map/ppermute | solution.py:614
  9.8 2.5 %collective-permute-start.10 = (f32[2,8,16,128]{3,2,1,0:T(8,128)}, f32[2,8,16,128]{3,2,1,0:T(8,128)S(1)}, u32[]{:S(2)}, u32[]{:S(2)}) collective-permute-start(f32[2,8,16,128]{3,2,1,0:T(8,128)} %get-tuple-element.94), channel_id=1, source_target_pairs={{0,12},{4,8},{8,4},{12,0},{1,13},{5,9},{9,5},{13,1},{2,14},{6,10},... | collective-permute-start | bytes 393224 | tf_op jit(solution)/shard_map/ppermute | solution.py:614
  14.8 2.5 %pack.1 = (bf16[8,128,1024]{2,1,0:T(8,128)(2,1)S(1)}, f32[8,128,128]{2,1,0:T(8,128)S(1)}, f32[8,128,128]{2,1,0:T(8,128)S(1)}) custom-call(s32[7]{0:T(128)S(1)} %stack.31.info_ref, f32[8,64,1024]{2,1,0:T(8,128)S(1)} %copy-done.21, f32[8,64,1024]{2,1,0:T(8,128)S(1)} %copy-done.21, f32[8,64,256]{2,1,0:T(8,128)S(1)} %copy-done.22), custom_call_target="tpu_custom_call" | custom-call | flops 5500000256 | bytes 1048576 | tf_op jit(solution)/shard_map/pack/pallas_call | solution.py:140
  22.8 9.3 %collective-permute-done.9.refs_2_ = f32[2,8,16,128]{3,2,1,0:T(8,128)S(1)} collective-permute-done((f32[2,8,16,128]{3,2,1,0:T(8,128)}, f32[2,8,16,128]{3,2,1,0:T(8,128)S(1)}, u32[]{:S(2)}, u32[]{:S(2)}) %collective-permute-start.9) | collective-permute-done | bytes 131104 | tf_op jit(solution)/shard_map/ppermute | solution.py:614
  35.4 6.4 %collective-permute-start.3 = (f32[2,8,16,128]{3,2,1,0:T(8,128)S(1)}, f32[2,8,16,128]{3,2,1,0:T(8,128)S(1)}, u32[]{:S(2)}, u32[]{:S(2)}) collective-permute-start(f32[2,8,16,128]{3,2,1,0:T(8,128)S(1)} %get-tuple-element.45), channel_id=1, source_target_pairs={{0,4},{4,0},{8,12},{12,8},{1,5},{5,1},{9,13},{13,9},{2,6},{6,2},{1... | collective-permute-start | bytes 393224 | tf_op jit(solution)/shard_map/ppermute | solution.py:614
  43.2 5.5 %apply_bonds.4 = (f32[2,8,128,128]{3,2,1,0:T(8,128)S(1)}, bf16[2,8,64,128]{3,2,1,0:T(8,128)(2,1)S(1)}, bf16[2,8,64,128]{3,2,1,0:T(8,128)(2,1)S(1)}, bf16[8,64,256]{2,1,0:T(8,128)(2,1)S(1)}) custom-call(s32[7]{0:T(128)S(1)} %stack.31.info_ref, s32[6,8]{1,0:T(8,128)S(1)} %copy-done.20, s32[6,8]{1,0:T(8,128)S(1)} %collective-permute-done.refs_1_, ...), custom_call_target="tpu_custom_call" | custom-call | flops 1100000000 | bytes 1048576 | tf_op jit(solution)/shard_map/apply_bonds/pallas_call | solution.py:488
  50.1 2.1 %collective-permute-start.12 = (f32[2,8,48,128]{3,2,1,0:T(8,128)S(1)}, f32[2,8,48,128]{3,2,1,0:T(8,128)S(1)}, u32[]{:S(2)}, u32[]{:S(2)}) collective-permute-start(f32[2,8,48,128]{3,2,1,0:T(8,128)S(1)} %get-tuple-element.62), channel_id=1, source_target_pairs={{0,2},{2,0},{1,3},{3,1},{4,6},{6,4},{5,7},{7,5},{8,10},{10,8},{9,1... | collective-permute-start | bytes 1179656 | tf_op jit(solution)/shard_map/ppermute | solution.py:614
  52.5 5.6 %apply_bonds.5 = (f32[2,8,128,128]{3,2,1,0:T(8,128)S(1)}, bf16[2,8,64,128]{3,2,1,0:T(8,128)(2,1)S(1)}, bf16[2,8,64,128]{3,2,1,0:T(8,128)(2,1)S(1)}, bf16[8,64,256]{2,1,0:T(8,128)(2,1)S(1)}) custom-call(s32[7]{0:T(128)S(1)} %stack.31.info_ref, s32[6,8]{1,0:T(8,128)S(1)} %copy-done.20, s32[6,8]{1,0:T(8,128)S(1)} %collective-permute-done.refs_1_, ...), custom_call_target="tpu_custom_call" | custom-call | flops 1100000000 | bytes 1048576 | tf_op jit(solution)/shard_map/apply_bonds/pallas_call | solution.py:488
  59.4 5.7 %apply_bonds.6 = (f32[4,264,128]{2,1,0:T(8,128)S(1)}, f32[4,264,128]{2,1,0:T(8,128)S(1)}, bf16[2,8,64,128]{3,2,1,0:T(8,128)(2,1)S(1)}, bf16[2,8,64,128]{3,2,1,0:T(8,128)(2,1)S(1)}, bf16[8,64,256]{2,1,0:T(8,128)(2,1)S(1)}) custom-call(s32[7]{0:T(128)S(1)} %stack.31.info_ref, s32[6,8]{1,0:T(8,128)S(1)} %copy-done.20, s32[6,8]{1,0:T(8,128)S(1)} %collective-permute-done.refs_1_, ...), custom_call_target="tpu_custom_call" | custom-call | flops 1100000000 | bytes 1048576 | tf_op jit(solution)/shard_map/apply_bonds/pallas_call | solution.py:488
  65.2 1.9 %collective-permute-done.14 = f32[4,264,128]{2,1,0:T(8,128)S(1)} collective-permute-done((f32[4,264,128]{2,1,0:T(8,128)S(1)}, f32[4,264,128]{2,1,0:T(8,128)S(1)}, u32[]{:S(2)}, u32[]{:S(2)}) %collective-permute-start.14) | collective-permute-done | bytes 540704 | tf_op jit(solution)/shard_map/ppermute | solution.py:614
  68.0 2.4 %collective-permute-start.16 = (f32[264,128]{1,0:T(8,128)}, f32[264,128]{1,0:T(8,128)}, u32[]{:S(2)}, u32[]{:S(2)}) collective-permute-start(f32[264,128]{1,0:T(8,128)} %get-tuple-element.91), channel_id=1, source_target_pairs={{0,8},{4,12},{8,0},{12,4},{1,9},{5,13},{9,1},{13,5},{2,10},{6,14},... | collective-permute-start | bytes 405512 | tf_op jit(solution)/shard_map/ppermute | solution.py:614
  70.5 1.9 %collective-permute-start.17 = (f32[264,128]{1,0:T(8,128)}, f32[264,128]{1,0:T(8,128)}, u32[]{:S(2)}, u32[]{:S(2)}) collective-permute-start(f32[264,128]{1,0:T(8,128)} %get-tuple-element.90), channel_id=1, source_target_pairs={{0,12},{4,8},{8,4},{12,0},{1,13},{5,9},{9,5},{13,1},{2,14},{6,10},... | collective-permute-start | bytes 405512 | tf_op jit(solution)/shard_map/ppermute | solution.py:614
  73.1 2.9 %collective-permute-done.15.a1 = f32[264,128]{1,0:T(8,128)} collective-permute-done((f32[264,128]{1,0:T(8,128)}, f32[264,128]{1,0:T(8,128)}, u32[]{:S(2)}, u32[]{:S(2)}) %collective-permute-start.15) | collective-permute-done | bytes 135200 | tf_op jit(solution)/shard_map/ppermute | solution.py:614
  76.0 5.5 %collective-permute-done.16.a2 = f32[264,128]{1,0:T(8,128)} collective-permute-done((f32[264,128]{1,0:T(8,128)}, f32[264,128]{1,0:T(8,128)}, u32[]{:S(2)}, u32[]{:S(2)}) %collective-permute-start.16) | collective-permute-done | bytes 135200 | tf_op jit(solution)/shard_map/ppermute | solution.py:614
  84.6 2.2 %owner_image.1.refs_2_.refs_6_.image_ref = f32[1032,128]{1,0:T(8,128)S(1)} custom-call(s32[7]{0:T(128)S(1)} %stack.31.info_ref, s32[4,2]{1,0:T(4,128)S(1)} %copy.19.owner_ref, f32[264,128]{1,0:T(8,128)S(1)} %copy-done.19, f32[264,128]{1,0:T(8,128)} %collective-permute-done.15.a1, f32[264,128]{1,0:T(8,128)} %collective-permute-done.16.a2, ...), custom_call_target="tpu_custom_call" | custom-call | flops 3300000000 | bytes 1048576 | tf_op jit(solution)/shard_map/owner_image/pallas_call | solution.py:555
  87.5 11.3 %collective-permute-done.18.refs_3_.refs_7_ = f32[1032,128]{1,0:T(8,128)S(1)} collective-permute-done((f32[1032,128]{1,0:T(8,128)S(1)}, f32[1032,128]{1,0:T(8,128)S(1)}, u32[]{:S(2)}, u32[]{:S(2)}) %collective-permute-start.18) | collective-permute-done | bytes 528416 | tf_op jit(solution)/shard_map/ppermute | solution.py:614
  98.8 1.9 %collective-permute-done.20.refs_5_.refs_9_ = f32[1032,128]{1,0:T(8,128)S(1)} collective-permute-done((f32[1032,128]{1,0:T(8,128)S(1)}, f32[1032,128]{1,0:T(8,128)S(1)}, u32[]{:S(2)}, u32[]{:S(2)}) %collective-permute-start.20) | collective-permute-done | bytes 528416 | tf_op jit(solution)/shard_map/ppermute | solution.py:614
  100.8 14.5 %apply_bonds.7 = (f32[4,264,128]{2,1,0:T(8,128)S(1)}, f32[4,264,128]{2,1,0:T(8,128)S(1)}) custom-call(s32[7]{0:T(128)S(1)} %stack.31.info_ref, s32[6,8]{1,0:T(8,128)S(1)} %copy-done.20, s32[6,8]{1,0:T(8,128)S(1)} %collective-permute-done.refs_1_, f32[1032,128]{1,0:T(8,128)S(1)} %owner_image.1.refs_2_.refs_6_.image_ref, ...), custom_call_target="tpu_custom_call" | custom-call | flops 1100000000 | bytes 1048576 | tf_op jit(solution)/shard_map/apply_bonds/pallas_call | solution.py:488
  117.4 4.0 %collective-permute-start.22 = (f32[264,128]{1,0:T(8,128)S(1)}, f32[264,128]{1,0:T(8,128)S(1)}, u32[]{:S(2)}, u32[]{:S(2)}) collective-permute-start(f32[264,128]{1,0:T(8,128)S(1)} %get-tuple-element.88), channel_id=1, source_target_pairs={{0,4},{4,0},{8,12},{12,8},{1,5},{5,1},{9,13},{13,9},{2,6},{6,2},{1... | collective-permute-start | bytes 405512 | tf_op jit(solution)/shard_map/ppermute | solution.py:614
  122.0 1.9 %collective-permute-start.24 = (f32[264,128]{1,0:T(8,128)S(1)}, f32[264,128]{1,0:T(8,128)S(1)}, u32[]{:S(2)}, u32[]{:S(2)}) collective-permute-start(f32[264,128]{1,0:T(8,128)S(1)} %get-tuple-element.86), channel_id=1, source_target_pairs={{0,12},{4,8},{8,4},{12,0},{1,13},{5,9},{9,5},{13,1},{2,14},{6,10},... | collective-permute-start | bytes 405512 | tf_op jit(solution)/shard_map/ppermute | solution.py:614
  123.9 3.2 %collective-permute-done.22.a1 = f32[264,128]{1,0:T(8,128)S(1)} collective-permute-done((f32[264,128]{1,0:T(8,128)S(1)}, f32[264,128]{1,0:T(8,128)S(1)}, u32[]{:S(2)}, u32[]{:S(2)}) %collective-permute-start.22) | collective-permute-done | bytes 135200 | tf_op jit(solution)/shard_map/ppermute | solution.py:614
  127.1 7.5 %collective-permute-done.23.a2 = f32[264,128]{1,0:T(8,128)S(1)} collective-permute-done((f32[264,128]{1,0:T(8,128)S(1)}, f32[264,128]{1,0:T(8,128)S(1)}, u32[]{:S(2)}, u32[]{:S(2)}) %collective-permute-start.23) | collective-permute-done | bytes 135200 | tf_op jit(solution)/shard_map/ppermute | solution.py:614
  134.6 2.1 %outputs.1 = (f32[8,64,256]{2,1,0:T(8,128)}, f32[8,64,256]{2,1,0:T(8,128)}, f32[8,64,256]{2,1,0:T(8,128)}) custom-call(s32[7]{0:T(128)S(1)} %stack.31.info_ref, s32[4,2]{1,0:T(4,128)S(1)} %copy.19.owner_ref, f32[264,128]{1,0:T(8,128)S(1)} %get-tuple-element.89.a0, f32[264,128]{1,0:T(8,128)S(1)} %collective-permute-done.22.a1, ...), custom_call_target="tpu_custom_call" | custom-call | flops 4400000000 | bytes 1048576 | tf_op jit(solution)/shard_map/outputs/pallas_call | solution.py:595
  (113 shorter events, 26.9 us)
Async XLA Ops:
  5.2 13.0 %collective-permute-start.1 = (f32[2,8,16,128]{3,2,1,0:T(8,128)}, f32[2,8,16,128]{3,2,1,0:T(8,128)S(1)}, u32[]{:S(2)}, u32[]{:S(2)}) collective-permute-start(f32[2,8,16,128]{3,2,1,0:T(8,128)} %get-tuple-element.96), channel_id=1, source_target_pairs={{0,4},{4,0},{8,12},{12,8},{1,5},{5,1},{9,13},{13,9},{2,6},{6,2},{1... | collective-permute-start | bytes 393224 | tf_op jit(solution)/shard_map/ppermute | solution.py:614
  8.3 9.2 %collective-permute-start.8 = (f32[6,16,16]{2,1,0:T(8,128)S(1)}, f32[6,16,16]{2,1,0:T(8,128)S(1)}, u32[]{:S(2)}, u32[]{:S(2)}) collective-permute-start(f32[6,16,16]{2,1,0:T(8,128)S(1)} %copy-done.23), channel_id=1, source_target_pairs={{0,2},{2,0},{1,3},{3,1},{4,6},{6,4},{5,7},{7,5},{8,10},{10,8},{9,1... | collective-permute-start | bytes 18440 | tf_op jit(solution)/shard_map/ppermute | solution.py:614
  9.8 12.2 %collective-permute-start.10 = (f32[2,8,16,128]{3,2,1,0:T(8,128)}, f32[2,8,16,128]{3,2,1,0:T(8,128)S(1)}, u32[]{:S(2)}, u32[]{:S(2)}) collective-permute-start(f32[2,8,16,128]{3,2,1,0:T(8,128)} %get-tuple-element.94), channel_id=1, source_target_pairs={{0,12},{4,8},{8,4},{12,0},{1,13},{5,9},{9,5},{13,1},{2,14},{6,10},... | collective-permute-start | bytes 393224 | tf_op jit(solution)/shard_map/ppermute | solution.py:614
  12.2 19.9 %collective-permute-start.9 = (f32[2,8,16,128]{3,2,1,0:T(8,128)}, f32[2,8,16,128]{3,2,1,0:T(8,128)S(1)}, u32[]{:S(2)}, u32[]{:S(2)}) collective-permute-start(f32[2,8,16,128]{3,2,1,0:T(8,128)} %get-tuple-element.95), channel_id=1, source_target_pairs={{0,8},{4,12},{8,0},{12,4},{1,9},{5,13},{9,1},{13,5},{2,10},{6,14},... | collective-permute-start | bytes 393224 | tf_op jit(solution)/shard_map/ppermute | solution.py:614
  12.3 30.8 %collective-permute-start = (s32[6,8]{1,0:T(8,128)S(1)}, s32[6,8]{1,0:T(8,128)S(1)}, u32[]{:S(2)}, u32[]{:S(2)}) collective-permute-start(s32[6,8]{1,0:T(8,128)S(1)} %copy-done.20), channel_id=1, source_target_pairs={{0,2},{2,0},{1,3},{3,1},{4,6},{6,4},{5,7},{7,5},{8,10},{10,8},{9,1... | collective-permute-start | bytes 584 | tf_op jit(solution)/shard_map/ppermute | solution.py:614
  18.4 15.2 %collective-permute-start.2 = (f32[2,8,16,128]{3,2,1,0:T(8,128)S(1)}, f32[2,8,16,128]{3,2,1,0:T(8,128)S(1)}, u32[]{:S(2)}, u32[]{:S(2)}) collective-permute-start(f32[2,8,16,128]{3,2,1,0:T(8,128)S(1)} %copy-done.33), channel_id=1, source_target_pairs={{0,4},{4,0},{8,12},{12,8},{1,5},{5,1},{9,13},{13,9},{2,6},{6,2},{1... | collective-permute-start | bytes 393224 | tf_op jit(solution)/shard_map/ppermute | solution.py:614
  20.2 15.1 %collective-permute-start.6 = (f32[2,8,16,128]{3,2,1,0:T(8,128)S(1)}, f32[2,8,16,128]{3,2,1,0:T(8,128)S(1)}, u32[]{:S(2)}, u32[]{:S(2)}) collective-permute-start(f32[2,8,16,128]{3,2,1,0:T(8,128)S(1)} %copy-done.32), channel_id=1, source_target_pairs={{0,8},{4,12},{8,0},{12,4},{1,9},{5,13},{9,1},{13,5},{2,10},{6,14},... | collective-permute-start | bytes 393224 | tf_op jit(solution)/shard_map/ppermute | solution.py:614
  21.9 13.4 %collective-permute-start.7 = (f32[2,8,16,128]{3,2,1,0:T(8,128)S(1)}, f32[2,8,16,128]{3,2,1,0:T(8,128)S(1)}, u32[]{:S(2)}, u32[]{:S(2)}) collective-permute-start(f32[2,8,16,128]{3,2,1,0:T(8,128)S(1)} %copy-done.31), channel_id=1, source_target_pairs={{0,12},{4,8},{8,4},{12,0},{1,13},{5,9},{9,5},{13,1},{2,14},{6,10},... | collective-permute-start | bytes 393224 | tf_op jit(solution)/shard_map/ppermute | solution.py:614
  33.5 9.7 %collective-permute-start.11 = (f32[2,8,48,128]{3,2,1,0:T(8,128)S(1)}, f32[2,8,48,128]{3,2,1,0:T(8,128)S(1)}, u32[]{:S(2)}, u32[]{:S(2)}) collective-permute-start(f32[2,8,48,128]{3,2,1,0:T(8,128)S(1)} %get-tuple-element.56), channel_id=1, source_target_pairs={{0,2},{2,0},{1,3},{3,1},{4,6},{6,4},{5,7},{7,5},{8,10},{10,8},{9,1... | collective-permute-start | bytes 1179656 | tf_op jit(solution)/shard_map/ppermute | solution.py:614
  33.6 15.1 %collective-permute-start.5 = (f32[2,8,16,128]{3,2,1,0:T(8,128)S(1)}, f32[2,8,16,128]{3,2,1,0:T(8,128)S(1)}, u32[]{:S(2)}, u32[]{:S(2)}) collective-permute-start(f32[2,8,16,128]{3,2,1,0:T(8,128)S(1)} %get-tuple-element.47), channel_id=1, source_target_pairs={{0,12},{4,8},{8,4},{12,0},{1,13},{5,9},{9,5},{13,1},{2,14},{6,10},... | collective-permute-start | bytes 393224 | tf_op jit(solution)/shard_map/ppermute | solution.py:614
  35.4 13.4 %collective-permute-start.4 = (f32[2,8,16,128]{3,2,1,0:T(8,128)S(1)}, f32[2,8,16,128]{3,2,1,0:T(8,128)S(1)}, u32[]{:S(2)}, u32[]{:S(2)}) collective-permute-start(f32[2,8,16,128]{3,2,1,0:T(8,128)S(1)} %get-tuple-element.46), channel_id=1, source_target_pairs={{0,8},{4,12},{8,0},{12,4},{1,9},{5,13},{9,1},{13,5},{2,10},{6,14},... | collective-permute-start | bytes 393224 | tf_op jit(solution)/shard_map/ppermute | solution.py:614
  35.4 13.4 %collective-permute-start.3 = (f32[2,8,16,128]{3,2,1,0:T(8,128)S(1)}, f32[2,8,16,128]{3,2,1,0:T(8,128)S(1)}, u32[]{:S(2)}, u32[]{:S(2)}) collective-permute-start(f32[2,8,16,128]{3,2,1,0:T(8,128)S(1)} %get-tuple-element.45), channel_id=1, source_target_pairs={{0,4},{4,0},{8,12},{12,8},{1,5},{5,1},{9,13},{13,9},{2,6},{6,2},{1... | collective-permute-start | bytes 393224 | tf_op jit(solution)/shard_map/ppermute | solution.py:614
  43.1 9.4 %collective-permute-start.13 = (f32[2,8,48,128]{3,2,1,0:T(8,128)S(1)}, f32[2,8,48,128]{3,2,1,0:T(8,128)S(1)}, u32[]{:S(2)}, u32[]{:S(2)}) collective-permute-start(f32[2,8,48,128]{3,2,1,0:T(8,128)S(1)} %get-tuple-element.50), channel_id=1, source_target_pairs={{0,2},{2,0},{1,3},{3,1},{4,6},{6,4},{5,7},{7,5},{8,10},{10,8},{9,1... | collective-permute-start | bytes 1179656 | tf_op jit(solution)/shard_map/ppermute | solution.py:614
  50.1 9.2 %collective-permute-start.12 = (f32[2,8,48,128]{3,2,1,0:T(8,128)S(1)}, f32[2,8,48,128]{3,2,1,0:T(8,128)S(1)}, u32[]{:S(2)}, u32[]{:S(2)}) collective-permute-start(f32[2,8,48,128]{3,2,1,0:T(8,128)S(1)} %get-tuple-element.62), channel_id=1, source_target_pairs={{0,2},{2,0},{1,3},{3,1},{4,6},{6,4},{5,7},{7,5},{8,10},{10,8},{9,1... | collective-permute-start | bytes 1179656 | tf_op jit(solution)/shard_map/ppermute | solution.py:614
  65.1 2.0 %collective-permute-start.14 = (f32[4,264,128]{2,1,0:T(8,128)S(1)}, f32[4,264,128]{2,1,0:T(8,128)S(1)}, u32[]{:S(2)}, u32[]{:S(2)}) collective-permute-start(f32[4,264,128]{2,1,0:T(8,128)S(1)} %get-tuple-element.69), channel_id=1, source_target_pairs={{0,1},{1,0},{2,3},{3,2},{4,5},{5,4},{6,7},{7,6},{8,9},{9,8},{10,11... | collective-permute-start | bytes 1622024 | tf_op jit(solution)/shard_map/ppermute | solution.py:614
  68.0 8.1 %collective-permute-start.15 = (f32[264,128]{1,0:T(8,128)}, f32[264,128]{1,0:T(8,128)}, u32[]{:S(2)}, u32[]{:S(2)}) collective-permute-start(f32[264,128]{1,0:T(8,128)} %get-tuple-element.92), channel_id=1, source_target_pairs={{0,4},{4,0},{8,12},{12,8},{1,5},{5,1},{9,13},{13,9},{2,6},{6,2},{1... | collective-permute-start | bytes 405512 | tf_op jit(solution)/shard_map/ppermute | solution.py:614
  68.0 13.5 %collective-permute-start.16 = (f32[264,128]{1,0:T(8,128)}, f32[264,128]{1,0:T(8,128)}, u32[]{:S(2)}, u32[]{:S(2)}) collective-permute-start(f32[264,128]{1,0:T(8,128)} %get-tuple-element.91), channel_id=1, source_target_pairs={{0,8},{4,12},{8,0},{12,4},{1,9},{5,13},{9,1},{13,5},{2,10},{6,14},... | collective-permute-start | bytes 405512 | tf_op jit(solution)/shard_map/ppermute | solution.py:614
  70.5 11.1 %collective-permute-start.17 = (f32[264,128]{1,0:T(8,128)}, f32[264,128]{1,0:T(8,128)}, u32[]{:S(2)}, u32[]{:S(2)}) collective-permute-start(f32[264,128]{1,0:T(8,128)} %get-tuple-element.90), channel_id=1, source_target_pairs={{0,12},{4,8},{8,4},{12,0},{1,13},{5,9},{9,5},{13,1},{2,14},{6,10},... | collective-permute-start | bytes 405512 | tf_op jit(solution)/shard_map/ppermute | solution.py:614
  86.8 12.0 %collective-permute-start.18 = (f32[1032,128]{1,0:T(8,128)S(1)}, f32[1032,128]{1,0:T(8,128)S(1)}, u32[]{:S(2)}, u32[]{:S(2)}) collective-permute-start(f32[1032,128]{1,0:T(8,128)S(1)} %owner_image.1.refs_2_.refs_6_.image_ref), channel_id=1, source_target_pairs={{0,2},{2,0},{1,3},{3,1},{4,6},{6,4},{5,7},{7,5},{8,10},{10,8},{9,1... | collective-permute-start | bytes 1585160 | tf_op jit(solution)/shard_map/ppermute | solution.py:614
  87.5 11.3 %collective-permute-start.19 = (f32[1032,128]{1,0:T(8,128)S(1)}, f32[1032,128]{1,0:T(8,128)S(1)}, u32[]{:S(2)}, u32[]{:S(2)}) collective-permute-start(f32[1032,128]{1,0:T(8,128)S(1)} %owner_image.1.refs_2_.refs_6_.image_ref), channel_id=1, source_target_pairs={{0,1},{1,0},{2,3},{3,2},{4,5},{5,4},{6,7},{7,6},{8,9},{9,8},{10,11... | collective-permute-start | bytes 1585160 | tf_op jit(solution)/shard_map/ppermute | solution.py:614
  115.3 2.0 %collective-permute-start.21 = (f32[4,264,128]{2,1,0:T(8,128)S(1)}, f32[4,264,128]{2,1,0:T(8,128)S(1)}, u32[]{:S(2)}, u32[]{:S(2)}) collective-permute-start(f32[4,264,128]{2,1,0:T(8,128)S(1)} %get-tuple-element.82), channel_id=1, source_target_pairs={{0,1},{1,0},{2,3},{3,2},{4,5},{5,4},{6,7},{7,6},{8,9},{9,8},{10,11... | collective-permute-start | bytes 1622024 | tf_op jit(solution)/shard_map/ppermute | solution.py:614
  117.4 9.7 %collective-permute-start.22 = (f32[264,128]{1,0:T(8,128)S(1)}, f32[264,128]{1,0:T(8,128)S(1)}, u32[]{:S(2)}, u32[]{:S(2)}) collective-permute-start(f32[264,128]{1,0:T(8,128)S(1)} %get-tuple-element.88), channel_id=1, source_target_pairs={{0,4},{4,0},{8,12},{12,8},{1,5},{5,1},{9,13},{13,9},{2,6},{6,2},{1... | collective-permute-start | bytes 405512 | tf_op jit(solution)/shard_map/ppermute | solution.py:614
  121.4 13.2 %collective-permute-start.23 = (f32[264,128]{1,0:T(8,128)S(1)}, f32[264,128]{1,0:T(8,128)S(1)}, u32[]{:S(2)}, u32[]{:S(2)}) collective-permute-start(f32[264,128]{1,0:T(8,128)S(1)} %get-tuple-element.87), channel_id=1, source_target_pairs={{0,8},{4,12},{8,0},{12,4},{1,9},{5,13},{9,1},{13,5},{2,10},{6,14},... | collective-permute-start | bytes 405512 | tf_op jit(solution)/shard_map/ppermute | solution.py:614
  122.0 12.6 %collective-permute-start.24 = (f32[264,128]{1,0:T(8,128)S(1)}, f32[264,128]{1,0:T(8,128)S(1)}, u32[]{:S(2)}, u32[]{:S(2)}) collective-permute-start(f32[264,128]{1,0:T(8,128)S(1)} %get-tuple-element.86), channel_id=1, source_target_pairs={{0,12},{4,8},{8,4},{12,0},{1,13},{5,9},{9,5},{13,1},{2,14},{6,10},... | collective-permute-start | bytes 405512 | tf_op jit(solution)/shard_map/ppermute | solution.py:614
  (35 other events, 295.3 us)

commit v7 on v6

--- a/solution.py
+++ b/solution.py
@@ -266,6 +266,37 @@
         jax.ShapeDtypeStruct((per, blocks, half, lanes), jnp.bfloat16),
         jax.ShapeDtypeStruct((blocks, per * 32, 2 * lanes), jnp.bfloat16),
     ]
+
+
+def cut_kernel(group, info_ref, source, *refs):
+    outs, sems = refs[:3], refs[3]
+    per = outs[0].shape[0]
+    copies = []
+    for k in range(3):
+        part = source.at[pl.ds(group * per, per), info_ref[4] ^ (k + 1)]
+        copies.append(pltpu.make_async_copy(part, outs[k], sems.at[k]))
+    for copy in copies:
+        copy.start()
+    for copy in copies:
+        copy.wait()
+
+
+def cut_pieces(info, by_owner, group, per):
+    shape = jax.ShapeDtypeStruct((per,) + by_owner.shape[2:], jnp.float32)
+    return pl.pallas_call(
+        functools.partial(cut_kernel, group),
+        grid_spec=pltpu.PrefetchScalarGridSpec(
+            num_scalar_prefetch=1,
+            grid=(1,),
+            in_specs=[pl.BlockSpec(memory_space=pl.ANY)],
+            out_specs=[pl.BlockSpec(memory_space=pl.ANY)] * 3,
+            scratch_shapes=[pltpu.SemaphoreType.DMA((3,))],
+        ),
+        out_shape=[shape] * 3,
+        compiler_params=pltpu.CompilerParams(vmem_limit_bytes=SMALL_VMEM),
+        cost_estimate=micros(1),
+        name="cut_pieces",
+    )(info, by_owner)
 
 
 def own_operands(info, by_owner, group, pieces):
@@ -565,7 +596,7 @@
         compiler_params=pltpu.CompilerParams(vmem_limit_bytes=SMALL_VMEM),
         cost_estimate=micros(3),
         name="owner_image",
-    )(info, owners, *arrived, diagonal, own)
+    )(info, owners, *in_hbm(arrived[0]), *arrived[1:], *in_hbm(diagonal, own))
 
 
 def final_kernel(
@@ -609,6 +640,10 @@
     )(info, owners, *arrived, diagonal, own, image)
 
 
+def in_hbm(*arrays):
+    return [pltpu.with_memory_space_constraint(x, pltpu.HBM) for x in arrays]
+
+
 def partner(x, axis, k):
     size = lax.axis_size(axis)
     return lax.ppermute(x, axis, [(i, i ^ k) for i in range(size)])
@@ -644,19 +679,19 @@
     entries = float(blocks * zs * rows * width)
 
     vector, own, diagonal_packed = pack(info, wavefunction, diagonal)
-    mixing = mixing_operand([bond_terms, partner(bond_terms, "mpo", 1)])
-    slots = [term_slot, partner(term_slot, "mpo", 1)]
 
     by_owner = environment.reshape(bonds, zs, blocks, rows // zs, 2 * rows)
-    pieces = [[None] * 4 for _ in range(GROUPS)]
+    pieces = []
     for group in range(GROUPS):
-        mine = by_owner[group * per : (group + 1) * per]
-        for k in range(1, 4):
-            piece = lax.dynamic_index_in_dim(mine, blk ^ k, 1, keepdims=False)
-            if group:
-                piece = after(piece, pieces[group - 1][1])
-            pieces[group][k] = partner(piece, "blk", k)
-    pieces[0][1] = after(pieces[0][1], vector, mixing)
+        cuts = cut_pieces(info, by_owner, group, per)
+        if group:
+            cuts = [after(x, y) for x, y in zip(cuts, pieces[-1][1:])]
+        pieces.append([None] + [partner(x, "blk", k + 1) for k, x in enumerate(cuts)])
+    pieces[0][1] = after(pieces[0][1], vector)
+    other_terms = partner(after(bond_terms, pieces[0][1]), "mpo", 1)
+    mixing = mixing_operand([bond_terms, other_terms])
+    slots = [term_slot, partner(after(term_slot, pieces[0][1]), "mpo", 1)]
+
     made, sent = [], []
     total = None
     operands = []

time: 137 us -> 135 us (0.985)
  local copies, waits for them, and re-layouts: 11 us -> 4.71 us
  starting transfers between devices: 34.1 us -> 38.1 us
  Pallas kernels: 42.5 us -> 46.3 us
  waiting for transfers between devices: 47 us -> 43.3 us
    ppermute x25, starting transfers between devices: 34.1 us -> 38.1 us  [partner(): return lax.ppermute(x, axis, [(i, i ^ k) for i in range(size)])]
    squeeze x3 -> x0, local copies, waits for them, and re-layouts: 3.68 us -> none  [per_device(): piece = lax.dynamic_index_in_dim(mine, blk ^ k, 1, keepdims=False)]
    ppermute x25, waiting for transfers between devices: 47 us -> 43.3 us  [partner(): return lax.ppermute(x, axis, [(i, i ^ k) for i in range(size)])]
    slice x1 -> x0, local copies, waits for them, and re-layouts: 2.68 us -> none  [per_device(): mine = by_owner[group * per:(group + 1) * per]]
    pallas_call x0 -> x3, Pallas kernels: none -> 2.49 us  [cut_pieces(): pl.pallas_call(functools.partial(cut_kernel, group), grid_spec=pltpu.Pref...]
    unnamed x69 -> x57, local copies, waits for them, and re-layouts: 4.54 us -> 4.63 us
  transfers between devices with their start and end apart: 25 -> 25, of which waited for: 11 -> 10; matrix products, arithmetic and copies ran while one was open for 2% -> 1% of each run, Pallas kernels for 13% -> 15%
where the time goes in v7:
time: 135 us; the launch traced here: 134 us
  Pallas kernels  46.3 us (34%)
  waiting for transfers between devices  43.3 us (32%)
  starting transfers between devices  38.1 us (28%)
  local copies, waits for them, and re-layouts  4.71 us (3%)
    ppermute x25, waiting for transfers between devices, partner(): return lax.ppermute(x, axis, [(i, i ^ k) for i in range(size)])  43.3 us
    ppermute x25, starting transfers between devices, partner(): return lax.ppermute(x, axis, [(i, i ^ k) for i in range(size)])  38.1 us
    pallas_call x4, Pallas kernels, apply_bonds(): pl.pallas_call(functools.partial(apply_kernel, plan), grid_spec=pltpu.Pre...  32.1 us
    unnamed x57, local copies, waits for them, and re-layouts  4.63 us
    pallas_call x3, Pallas kernels, own_operands(): pl.pallas_call(own_operands_kernel, grid_spec=pltpu.PrefetchScalarGridSpe...  4.09 us
  transfers between devices with their start and end apart: 25, of which 10 were waited for; matrix products, arithmetic and copies ran while one was open for 1% of the time, Pallas kernels for 15%

profile of v7, /device:TPU:0, one launch (start us, length us, event | category | flops | bytes accessed | tf_op | source)
XLA Modules:
  0.0 134.5 jit_solution(2752935717657014793)
XLA Ops:
  3.1 3.1 %collective-permute-start = (f32[2,8,16,128]{3,2,1,0:T(8,128)S(1)}, f32[2,8,16,128]{3,2,1,0:T(8,128)S(1)}, u32[]{:S(2)}, u32[]{:S(2)}) collective-permute-start(f32[2,8,16,128]{3,2,1,0:T(8,128)S(1)} %get-tuple-element.54), channel_id=1, source_target_pairs={{0,4},{4,0},{8,12},{12,8},{1,5},{5,1},{9,13},{13,9},{2,6},{6,2},{1... | collective-permute-start | bytes 393224 | tf_op jit(solution)/shard_map/ppermute | solution.py:649
  6.2 2.6 %collective-permute-start.4 = (f32[2,8,16,128]{3,2,1,0:T(8,128)S(1)}, f32[2,8,16,128]{3,2,1,0:T(8,128)S(1)}, u32[]{:S(2)}, u32[]{:S(2)}) collective-permute-start(f32[2,8,16,128]{3,2,1,0:T(8,128)S(1)} %get-tuple-element.64), channel_id=1, source_target_pairs={{0,8},{4,12},{8,0},{12,4},{1,9},{5,13},{9,1},{13,5},{2,10},{6,14},... | collective-permute-start | bytes 393224 | tf_op jit(solution)/shard_map/ppermute | solution.py:649
  8.8 2.6 %pack.1 = (bf16[8,128,1024]{2,1,0:T(8,128)(2,1)S(1)}, f32[8,128,128]{2,1,0:T(8,128)S(1)}, f32[8,128,128]{2,1,0:T(8,128)S(1)}) custom-call(s32[7]{0:T(128)S(1)} %stack.31.info_ref, f32[8,64,1024]{2,1,0:T(8,128)S(1)} %copy-done.19, f32[8,64,1024]{2,1,0:T(8,128)S(1)} %copy-done.19, f32[8,64,256]{2,1,0:T(8,128)S(1)} %copy-done.22), custom_call_target="tpu_custom_call" | custom-call | flops 5500000256 | bytes 1048576 | tf_op jit(solution)/shard_map/pack/pallas_call | solution.py:140
  14.8 4.4 %collective-permute-done.4.refs_2_ = f32[2,8,16,128]{3,2,1,0:T(8,128)S(1)} collective-permute-done((f32[2,8,16,128]{3,2,1,0:T(8,128)S(1)}, f32[2,8,16,128]{3,2,1,0:T(8,128)S(1)}, u32[]{:S(2)}, u32[]{:S(2)}) %collective-permute-start.4) | collective-permute-done | bytes 131104 | tf_op jit(solution)/shard_map/ppermute | solution.py:649
  19.2 2.2 %collective-permute-start.8 = (f32[2,8,16,128]{3,2,1,0:T(8,128)S(1)}, f32[2,8,16,128]{3,2,1,0:T(8,128)S(1)}, u32[]{:S(2)}, u32[]{:S(2)}) collective-permute-start(f32[2,8,16,128]{3,2,1,0:T(8,128)S(1)} %get-tuple-element.70), channel_id=1, source_target_pairs={{0,12},{4,8},{8,4},{12,0},{1,13},{5,9},{9,5},{13,1},{2,14},{6,10},... | collective-permute-start | bytes 393224 | tf_op jit(solution)/shard_map/ppermute | solution.py:649
  28.0 1.7 %collective-permute-start.9 = (f32[2,8,16,128]{3,2,1,0:T(8,128)S(1)}, f32[2,8,16,128]{3,2,1,0:T(8,128)S(1)}, u32[]{:S(2)}, u32[]{:S(2)}) collective-permute-start(f32[2,8,16,128]{3,2,1,0:T(8,128)S(1)} %get-tuple-element.71), channel_id=1, source_target_pairs={{0,12},{4,8},{8,4},{12,0},{1,13},{5,9},{9,5},{13,1},{2,14},{6,10},... | collective-permute-start | bytes 393224 | tf_op jit(solution)/shard_map/ppermute | solution.py:649
  29.6 8.6 %collective-permute-start.3 = (f32[2,8,16,128]{3,2,1,0:T(8,128)S(1)}, f32[2,8,16,128]{3,2,1,0:T(8,128)S(1)}, u32[]{:S(2)}, u32[]{:S(2)}) collective-permute-start(f32[2,8,16,128]{3,2,1,0:T(8,128)S(1)} %get-tuple-element.61), channel_id=1, source_target_pairs={{0,4},{4,0},{8,12},{12,8},{1,5},{5,1},{9,13},{13,9},{2,6},{6,2},{1... | collective-permute-start | bytes 393224 | tf_op jit(solution)/shard_map/ppermute | solution.py:649
  40.5 5.6 %apply_bonds.4 = (f32[2,8,128,128]{3,2,1,0:T(8,128)S(1)}, bf16[2,8,64,128]{3,2,1,0:T(8,128)(2,1)S(1)}, bf16[2,8,64,128]{3,2,1,0:T(8,128)(2,1)S(1)}, bf16[8,64,256]{2,1,0:T(8,128)(2,1)S(1)}) custom-call(s32[7]{0:T(128)S(1)} %stack.31.info_ref, s32[6,8]{1,0:T(8,128)S(1)} %copy-done.18, s32[6,8]{1,0:T(8,128)S(1)} %collective-permute-done.1.refs_1_, ...), custom_call_target="tpu_custom_call" | custom-call | flops 1100000000 | bytes 1048576 | tf_op jit(solution)/shard_map/apply_bonds/pallas_call | solution.py:519
  49.1 5.7 %apply_bonds.5 = (f32[2,8,128,128]{3,2,1,0:T(8,128)S(1)}, bf16[2,8,64,128]{3,2,1,0:T(8,128)(2,1)S(1)}, bf16[2,8,64,128]{3,2,1,0:T(8,128)(2,1)S(1)}, bf16[8,64,256]{2,1,0:T(8,128)(2,1)S(1)}) custom-call(s32[7]{0:T(128)S(1)} %stack.31.info_ref, s32[6,8]{1,0:T(8,128)S(1)} %copy-done.18, s32[6,8]{1,0:T(8,128)S(1)} %collective-permute-done.1.refs_1_, ...), custom_call_target="tpu_custom_call" | custom-call | flops 1100000000 | bytes 1048576 | tf_op jit(solution)/shard_map/apply_bonds/pallas_call | solution.py:519
  56.3 5.8 %apply_bonds.6 = (f32[4,264,128]{2,1,0:T(8,128)S(1)}, f32[4,264,128]{2,1,0:T(8,128)S(1)}, bf16[2,8,64,128]{3,2,1,0:T(8,128)(2,1)S(1)}, bf16[2,8,64,128]{3,2,1,0:T(8,128)(2,1)S(1)}, bf16[8,64,256]{2,1,0:T(8,128)(2,1)S(1)}) custom-call(s32[7]{0:T(128)S(1)} %stack.31.info_ref, s32[6,8]{1,0:T(8,128)S(1)} %copy-done.18, ...), custom_call_target="tpu_custom_call" | custom-call | flops 1100000000 | bytes 1048576 | tf_op jit(solution)/shard_map/apply_bonds/pallas_call | solution.py:519
  62.2 1.9 %collective-permute-done.14 = f32[4,264,128]{2,1,0:T(8,128)S(1)} collective-permute-done((f32[4,264,128]{2,1,0:T(8,128)S(1)}, f32[4,264,128]{2,1,0:T(8,128)S(1)}, u32[]{:S(2)}, u32[]{:S(2)}) %collective-permute-start.14) | collective-permute-done | bytes 540704 | tf_op jit(solution)/shard_map/ppermute | solution.py:649
  65.0 3.7 %collective-permute-start.15 = (f32[264,128]{1,0:T(8,128)}, f32[264,128]{1,0:T(8,128)}, u32[]{:S(2)}, u32[]{:S(2)}) collective-permute-start(f32[264,128]{1,0:T(8,128)} %get-tuple-element.111), channel_id=1, source_target_pairs={{0,4},{4,0},{8,12},{12,8},{1,5},{5,1},{9,13},{13,9},{2,6},{6,2},{1... | collective-permute-start | bytes 405512 | tf_op jit(solution)/shard_map/ppermute | solution.py:649
  68.7 2.4 %collective-permute-start.17 = (f32[264,128]{1,0:T(8,128)}, f32[264,128]{1,0:T(8,128)}, u32[]{:S(2)}, u32[]{:S(2)}) collective-permute-start(f32[264,128]{1,0:T(8,128)} %get-tuple-element.109), channel_id=1, source_target_pairs={{0,12},{4,8},{8,4},{12,0},{1,13},{5,9},{9,5},{13,1},{2,14},{6,10},... | collective-permute-start | bytes 405512 | tf_op jit(solution)/shard_map/ppermute | solution.py:649
  73.4 8.1 %collective-permute-done.16.a2 = f32[264,128]{1,0:T(8,128)} collective-permute-done((f32[264,128]{1,0:T(8,128)}, f32[264,128]{1,0:T(8,128)}, u32[]{:S(2)}, u32[]{:S(2)}) %collective-permute-start.16) | collective-permute-done | bytes 135200 | tf_op jit(solution)/shard_map/ppermute | solution.py:649
  81.6 2.6 %owner_image.1.refs_2_.refs_6_.image_ref = f32[1032,128]{1,0:T(8,128)S(1)} custom-call(s32[7]{0:T(128)S(1)} %stack.31.info_ref, s32[4,2]{1,0:T(4,128)S(1)} %copy.10.owner_ref, f32[264,128]{1,0:T(8,128)} %get-tuple-element.112.a0, f32[264,128]{1,0:T(8,128)} %collective-permute-done.15.a1, f32[264,128]{1,0:T(8,128)} %collective-permute-done.16.a2, ...), custom_call_target="tpu_custom_call" | custom-call | flops 3300000000 | bytes 1048576 | tf_op jit(solution)/shard_map/owner_image/pallas_call | solution.py:586
  84.9 12.3 %collective-permute-done.18.refs_3_.refs_7_ = f32[1032,128]{1,0:T(8,128)S(1)} collective-permute-done((f32[1032,128]{1,0:T(8,128)S(1)}, f32[1032,128]{1,0:T(8,128)S(1)}, u32[]{:S(2)}, u32[]{:S(2)}) %collective-permute-start.18) | collective-permute-done | bytes 528416 | tf_op jit(solution)/shard_map/ppermute | solution.py:649
  97.2 1.9 %collective-permute-done.20.refs_5_.refs_9_ = f32[1032,128]{1,0:T(8,128)S(1)} collective-permute-done((f32[1032,128]{1,0:T(8,128)S(1)}, f32[1032,128]{1,0:T(8,128)S(1)}, u32[]{:S(2)}, u32[]{:S(2)}) %collective-permute-start.20) | collective-permute-done | bytes 528416 | tf_op jit(solution)/shard_map/ppermute | solution.py:649
  99.2 15.0 %apply_bonds.7 = (f32[4,264,128]{2,1,0:T(8,128)S(1)}, f32[4,264,128]{2,1,0:T(8,128)S(1)}) custom-call(s32[7]{0:T(128)S(1)} %stack.31.info_ref, s32[6,8]{1,0:T(8,128)S(1)} %copy-done.18, s32[6,8]{1,0:T(8,128)S(1)} %collective-permute-done.1.refs_1_, f32[1032,128]{1,0:T(8,128)S(1)} %owner_image.1.refs_2_.refs_6_.image_ref, ...), custom_call_target="tpu_custom_call" | custom-call | flops 1100000000 | bytes 1048576 | tf_op jit(solution)/shard_map/apply_bonds/pallas_call | solution.py:519
  114.4 1.8 %collective-permute-done.21 = f32[4,264,128]{2,1,0:T(8,128)S(1)} collective-permute-done((f32[4,264,128]{2,1,0:T(8,128)S(1)}, f32[4,264,128]{2,1,0:T(8,128)S(1)}, u32[]{:S(2)}, u32[]{:S(2)}) %collective-permute-start.21) | collective-permute-done | bytes 540704 | tf_op jit(solution)/shard_map/ppermute | solution.py:649
  116.3 3.5 %collective-permute-start.22 = (f32[264,128]{1,0:T(8,128)S(1)}, f32[264,128]{1,0:T(8,128)S(1)}, u32[]{:S(2)}, u32[]{:S(2)}) collective-permute-start(f32[264,128]{1,0:T(8,128)S(1)} %get-tuple-element.107), channel_id=1, source_target_pairs={{0,4},{4,0},{8,12},{12,8},{1,5},{5,1},{9,13},{13,9},{2,6},{6,2},{1... | collective-permute-start | bytes 405512 | tf_op jit(solution)/shard_map/ppermute | solution.py:649
  119.8 2.4 %collective-permute-start.24 = (f32[264,128]{1,0:T(8,128)S(1)}, f32[264,128]{1,0:T(8,128)S(1)}, u32[]{:S(2)}, u32[]{:S(2)}) collective-permute-start(f32[264,128]{1,0:T(8,128)S(1)} %get-tuple-element.105), channel_id=1, source_target_pairs={{0,12},{4,8},{8,4},{12,0},{1,13},{5,9},{9,5},{13,1},{2,14},{6,10},... | collective-permute-start | bytes 405512 | tf_op jit(solution)/shard_map/ppermute | solution.py:649
  122.3 2.0 %collective-permute-done.22.a1 = f32[264,128]{1,0:T(8,128)S(1)} collective-permute-done((f32[264,128]{1,0:T(8,128)S(1)}, f32[264,128]{1,0:T(8,128)S(1)}, u32[]{:S(2)}, u32[]{:S(2)}) %collective-permute-start.22) | collective-permute-done | bytes 135200 | tf_op jit(solution)/shard_map/ppermute | solution.py:649
  124.2 8.1 %collective-permute-done.23.a2 = f32[264,128]{1,0:T(8,128)S(1)} collective-permute-done((f32[264,128]{1,0:T(8,128)S(1)}, f32[264,128]{1,0:T(8,128)S(1)}, u32[]{:S(2)}, u32[]{:S(2)}) %collective-permute-start.23) | collective-permute-done | bytes 135200 | tf_op jit(solution)/shard_map/ppermute | solution.py:649
  132.4 2.1 %outputs.1 = (f32[8,64,256]{2,1,0:T(8,128)}, f32[8,64,256]{2,1,0:T(8,128)}, f32[8,64,256]{2,1,0:T(8,128)}) custom-call(s32[7]{0:T(128)S(1)} %stack.31.info_ref, s32[4,2]{1,0:T(4,128)S(1)} %copy.10.owner_ref, f32[264,128]{1,0:T(8,128)S(1)} %get-tuple-element.108.a0, f32[264,128]{1,0:T(8,128)S(1)} %collective-permute-done.22.a1, ...), custom_call_target="tpu_custom_call" | custom-call | flops 4400000000 | bytes 1048576 | tf_op jit(solution)/shard_map/outputs/pallas_call | solution.py:626
  (100 shorter events, 23.2 us)
Async XLA Ops:
  3.1 10.8 %collective-permute-start = (f32[2,8,16,128]{3,2,1,0:T(8,128)S(1)}, f32[2,8,16,128]{3,2,1,0:T(8,128)S(1)}, u32[]{:S(2)}, u32[]{:S(2)}) collective-permute-start(f32[2,8,16,128]{3,2,1,0:T(8,128)S(1)} %get-tuple-element.54), channel_id=1, source_target_pairs={{0,4},{4,0},{8,12},{12,8},{1,5},{5,1},{9,13},{13,9},{2,6},{6,2},{1... | collective-permute-start | bytes 393224 | tf_op jit(solution)/shard_map/ppermute | solution.py:649
  6.2 13.0 %collective-permute-start.4 = (f32[2,8,16,128]{3,2,1,0:T(8,128)S(1)}, f32[2,8,16,128]{3,2,1,0:T(8,128)S(1)}, u32[]{:S(2)}, u32[]{:S(2)}) collective-permute-start(f32[2,8,16,128]{3,2,1,0:T(8,128)S(1)} %get-tuple-element.64), channel_id=1, source_target_pairs={{0,8},{4,12},{8,0},{12,4},{1,9},{5,13},{9,1},{13,5},{2,10},{6,14},... | collective-permute-start | bytes 393224 | tf_op jit(solution)/shard_map/ppermute | solution.py:649
  8.8 10.4 %collective-permute-start.7 = (f32[2,8,16,128]{3,2,1,0:T(8,128)S(1)}, f32[2,8,16,128]{3,2,1,0:T(8,128)S(1)}, u32[]{:S(2)}, u32[]{:S(2)}) collective-permute-start(f32[2,8,16,128]{3,2,1,0:T(8,128)S(1)} %get-tuple-element.69), channel_id=1, source_target_pairs={{0,12},{4,8},{8,4},{12,0},{1,13},{5,9},{9,5},{13,1},{2,14},{6,10},... | collective-permute-start | bytes 393224 | tf_op jit(solution)/shard_map/ppermute | solution.py:649
  13.9 15.8 %collective-permute-start.2 = (f32[2,8,16,128]{3,2,1,0:T(8,128)S(1)}, f32[2,8,16,128]{3,2,1,0:T(8,128)S(1)}, u32[]{:S(2)}, u32[]{:S(2)}) collective-permute-start(f32[2,8,16,128]{3,2,1,0:T(8,128)S(1)} %get-tuple-element.60), channel_id=1, source_target_pairs={{0,4},{4,0},{8,12},{12,8},{1,5},{5,1},{9,13},{13,9},{2,6},{6,2},{1... | collective-permute-start | bytes 393224 | tf_op jit(solution)/shard_map/ppermute | solution.py:649
  19.2 19.0 %collective-permute-start.5 = (f32[2,8,16,128]{3,2,1,0:T(8,128)S(1)}, f32[2,8,16,128]{3,2,1,0:T(8,128)S(1)}, u32[]{:S(2)}, u32[]{:S(2)}) collective-permute-start(f32[2,8,16,128]{3,2,1,0:T(8,128)S(1)} %get-tuple-element.65), channel_id=1, source_target_pairs={{0,8},{4,12},{8,0},{12,4},{1,9},{5,13},{9,1},{13,5},{2,10},{6,14},... | collective-permute-start | bytes 393224 | tf_op jit(solution)/shard_map/ppermute | solution.py:649
  19.2 8.8 %collective-permute-start.8 = (f32[2,8,16,128]{3,2,1,0:T(8,128)S(1)}, f32[2,8,16,128]{3,2,1,0:T(8,128)S(1)}, u32[]{:S(2)}, u32[]{:S(2)}) collective-permute-start(f32[2,8,16,128]{3,2,1,0:T(8,128)S(1)} %get-tuple-element.70), channel_id=1, source_target_pairs={{0,12},{4,8},{8,4},{12,0},{1,13},{5,9},{9,5},{13,1},{2,14},{6,10},... | collective-permute-start | bytes 393224 | tf_op jit(solution)/shard_map/ppermute | solution.py:649
  21.4 4.7 %collective-permute-start.11 = (f32[6,16,16]{2,1,0:T(8,128)S(1)}, f32[6,16,16]{2,1,0:T(8,128)S(1)}, u32[]{:S(2)}, u32[]{:S(2)}) collective-permute-start(f32[6,16,16]{2,1,0:T(8,128)S(1)} %copy-done.23), channel_id=1, source_target_pairs={{0,2},{2,0},{1,3},{3,1},{4,6},{6,4},{5,7},{7,5},{8,10},{10,8},{9,1... | collective-permute-start | bytes 18440 | tf_op jit(solution)/shard_map/ppermute | solution.py:649
  24.3 16.1 %collective-permute-start.10 = (f32[2,8,48,128]{3,2,1,0:T(8,128)S(1)}, f32[2,8,48,128]{3,2,1,0:T(8,128)S(1)}, u32[]{:S(2)}, u32[]{:S(2)}) collective-permute-start(f32[2,8,48,128]{3,2,1,0:T(8,128)S(1)} %get-tuple-element.77), channel_id=1, source_target_pairs={{0,2},{2,0},{1,3},{3,1},{4,6},{6,4},{5,7},{7,5},{8,10},{10,8},{9,1... | collective-permute-start | bytes 1179656 | tf_op jit(solution)/shard_map/ppermute | solution.py:649
  26.1 13.7 %collective-permute-start.1 = (s32[6,8]{1,0:T(8,128)S(1)}, s32[6,8]{1,0:T(8,128)S(1)}, u32[]{:S(2)}, u32[]{:S(2)}) collective-permute-start(s32[6,8]{1,0:T(8,128)S(1)} %copy-done.18), channel_id=1, source_target_pairs={{0,2},{2,0},{1,3},{3,1},{4,6},{6,4},{5,7},{7,5},{8,10},{10,8},{9,1... | collective-permute-start | bytes 584 | tf_op jit(solution)/shard_map/ppermute | solution.py:649
  28.0 18.1 %collective-permute-start.9 = (f32[2,8,16,128]{3,2,1,0:T(8,128)S(1)}, f32[2,8,16,128]{3,2,1,0:T(8,128)S(1)}, u32[]{:S(2)}, u32[]{:S(2)}) collective-permute-start(f32[2,8,16,128]{3,2,1,0:T(8,128)S(1)} %get-tuple-element.71), channel_id=1, source_target_pairs={{0,12},{4,8},{8,4},{12,0},{1,13},{5,9},{9,5},{13,1},{2,14},{6,10},... | collective-permute-start | bytes 393224 | tf_op jit(solution)/shard_map/ppermute | solution.py:649
  29.6 16.5 %collective-permute-start.3 = (f32[2,8,16,128]{3,2,1,0:T(8,128)S(1)}, f32[2,8,16,128]{3,2,1,0:T(8,128)S(1)}, u32[]{:S(2)}, u32[]{:S(2)}) collective-permute-start(f32[2,8,16,128]{3,2,1,0:T(8,128)S(1)} %get-tuple-element.61), channel_id=1, source_target_pairs={{0,4},{4,0},{8,12},{12,8},{1,5},{5,1},{9,13},{13,9},{2,6},{6,2},{1... | collective-permute-start | bytes 393224 | tf_op jit(solution)/shard_map/ppermute | solution.py:649
  38.2 7.9 %collective-permute-start.6 = (f32[2,8,16,128]{3,2,1,0:T(8,128)S(1)}, f32[2,8,16,128]{3,2,1,0:T(8,128)S(1)}, u32[]{:S(2)}, u32[]{:S(2)}) collective-permute-start(f32[2,8,16,128]{3,2,1,0:T(8,128)S(1)} %get-tuple-element.66), channel_id=1, source_target_pairs={{0,8},{4,12},{8,0},{12,4},{1,9},{5,13},{9,1},{13,5},{2,10},{6,14},... | collective-permute-start | bytes 393224 | tf_op jit(solution)/shard_map/ppermute | solution.py:649
  39.9 9.3 %collective-permute-start.13 = (f32[2,8,48,128]{3,2,1,0:T(8,128)S(1)}, f32[2,8,48,128]{3,2,1,0:T(8,128)S(1)}, u32[]{:S(2)}, u32[]{:S(2)}) collective-permute-start(f32[2,8,48,128]{3,2,1,0:T(8,128)S(1)} %get-tuple-element.72), channel_id=1, source_target_pairs={{0,2},{2,0},{1,3},{3,1},{4,6},{6,4},{5,7},{7,5},{8,10},{10,8},{9,1... | collective-permute-start | bytes 1179656 | tf_op jit(solution)/shard_map/ppermute | solution.py:649
  47.6 8.8 %collective-permute-start.12 = (f32[2,8,48,128]{3,2,1,0:T(8,128)S(1)}, f32[2,8,48,128]{3,2,1,0:T(8,128)S(1)}, u32[]{:S(2)}, u32[]{:S(2)}) collective-permute-start(f32[2,8,48,128]{3,2,1,0:T(8,128)S(1)} %get-tuple-element.84), channel_id=1, source_target_pairs={{0,2},{2,0},{1,3},{3,1},{4,6},{6,4},{5,7},{7,5},{8,10},{10,8},{9,1... | collective-permute-start | bytes 1179656 | tf_op jit(solution)/shard_map/ppermute | solution.py:649
  62.2 2.0 %collective-permute-start.14 = (f32[4,264,128]{2,1,0:T(8,128)S(1)}, f32[4,264,128]{2,1,0:T(8,128)S(1)}, u32[]{:S(2)}, u32[]{:S(2)}) collective-permute-start(f32[4,264,128]{2,1,0:T(8,128)S(1)} %get-tuple-element.91), channel_id=1, source_target_pairs={{0,1},{1,0},{2,3},{3,2},{4,5},{5,4},{6,7},{7,6},{8,9},{9,8},{10,11... | collective-permute-start | bytes 1622024 | tf_op jit(solution)/shard_map/ppermute | solution.py:649
  65.0 8.4 %collective-permute-start.15 = (f32[264,128]{1,0:T(8,128)}, f32[264,128]{1,0:T(8,128)}, u32[]{:S(2)}, u32[]{:S(2)}) collective-permute-start(f32[264,128]{1,0:T(8,128)} %get-tuple-element.111), channel_id=1, source_target_pairs={{0,4},{4,0},{8,12},{12,8},{1,5},{5,1},{9,13},{13,9},{2,6},{6,2},{1... | collective-permute-start | bytes 405512 | tf_op jit(solution)/shard_map/ppermute | solution.py:649
  68.7 12.9 %collective-permute-start.16 = (f32[264,128]{1,0:T(8,128)}, f32[264,128]{1,0:T(8,128)}, u32[]{:S(2)}, u32[]{:S(2)}) collective-permute-start(f32[264,128]{1,0:T(8,128)} %get-tuple-element.110), channel_id=1, source_target_pairs={{0,8},{4,12},{8,0},{12,4},{1,9},{5,13},{9,1},{13,5},{2,10},{6,14},... | collective-permute-start | bytes 405512 | tf_op jit(solution)/shard_map/ppermute | solution.py:649
  68.7 12.9 %collective-permute-start.17 = (f32[264,128]{1,0:T(8,128)}, f32[264,128]{1,0:T(8,128)}, u32[]{:S(2)}, u32[]{:S(2)}) collective-permute-start(f32[264,128]{1,0:T(8,128)} %get-tuple-element.109), channel_id=1, source_target_pairs={{0,12},{4,8},{8,4},{12,0},{1,13},{5,9},{9,5},{13,1},{2,14},{6,10},... | collective-permute-start | bytes 405512 | tf_op jit(solution)/shard_map/ppermute | solution.py:649
  84.3 13.0 %collective-permute-start.18 = (f32[1032,128]{1,0:T(8,128)S(1)}, f32[1032,128]{1,0:T(8,128)S(1)}, u32[]{:S(2)}, u32[]{:S(2)}) collective-permute-start(f32[1032,128]{1,0:T(8,128)S(1)} %owner_image.1.refs_2_.refs_6_.image_ref), channel_id=1, source_target_pairs={{0,2},{2,0},{1,3},{3,1},{4,6},{6,4},{5,7},{7,5},{8,10},{10,8},{9,1... | collective-permute-start | bytes 1585160 | tf_op jit(solution)/shard_map/ppermute | solution.py:649
  84.9 12.4 %collective-permute-start.19 = (f32[1032,128]{1,0:T(8,128)S(1)}, f32[1032,128]{1,0:T(8,128)S(1)}, u32[]{:S(2)}, u32[]{:S(2)}) collective-permute-start(f32[1032,128]{1,0:T(8,128)S(1)} %owner_image.1.refs_2_.refs_6_.image_ref), channel_id=1, source_target_pairs={{0,1},{1,0},{2,3},{3,2},{4,5},{5,4},{6,7},{7,6},{8,9},{9,8},{10,11... | collective-permute-start | bytes 1585160 | tf_op jit(solution)/shard_map/ppermute | solution.py:649
  114.2 2.0 %collective-permute-start.21 = (f32[4,264,128]{2,1,0:T(8,128)S(1)}, f32[4,264,128]{2,1,0:T(8,128)S(1)}, u32[]{:S(2)}, u32[]{:S(2)}) collective-permute-start(f32[4,264,128]{2,1,0:T(8,128)S(1)} %get-tuple-element.104), channel_id=1, source_target_pairs={{0,1},{1,0},{2,3},{3,2},{4,5},{5,4},{6,7},{7,6},{8,9},{9,8},{10,11... | collective-permute-start | bytes 1622024 | tf_op jit(solution)/shard_map/ppermute | solution.py:649
  116.3 7.9 %collective-permute-start.22 = (f32[264,128]{1,0:T(8,128)S(1)}, f32[264,128]{1,0:T(8,128)S(1)}, u32[]{:S(2)}, u32[]{:S(2)}) collective-permute-start(f32[264,128]{1,0:T(8,128)S(1)} %get-tuple-element.107), channel_id=1, source_target_pairs={{0,4},{4,0},{8,12},{12,8},{1,5},{5,1},{9,13},{13,9},{2,6},{6,2},{1... | collective-permute-start | bytes 405512 | tf_op jit(solution)/shard_map/ppermute | solution.py:649
  119.8 12.5 %collective-permute-start.23 = (f32[264,128]{1,0:T(8,128)S(1)}, f32[264,128]{1,0:T(8,128)S(1)}, u32[]{:S(2)}, u32[]{:S(2)}) collective-permute-start(f32[264,128]{1,0:T(8,128)S(1)} %get-tuple-element.106), channel_id=1, source_target_pairs={{0,8},{4,12},{8,0},{12,4},{1,9},{5,13},{9,1},{13,5},{2,10},{6,14},... | collective-permute-start | bytes 405512 | tf_op jit(solution)/shard_map/ppermute | solution.py:649
  119.8 12.5 %collective-permute-start.24 = (f32[264,128]{1,0:T(8,128)S(1)}, f32[264,128]{1,0:T(8,128)S(1)}, u32[]{:S(2)}, u32[]{:S(2)}) collective-permute-start(f32[264,128]{1,0:T(8,128)S(1)} %get-tuple-element.105), channel_id=1, source_target_pairs={{0,12},{4,8},{8,4},{12,0},{1,13},{5,9},{9,5},{13,1},{2,14},{6,10},... | collective-permute-start | bytes 405512 | tf_op jit(solution)/shard_map/ppermute | solution.py:649
  (29 other events, 296.4 us)

commit v8 on v7

--- a/solution.py
+++ b/solution.py
@@ -13,7 +13,7 @@
 TINY = 1e-30
 GROUPS = 3
 SMALL_VMEM = 16 * 1024 * 1024
-APPLY_VMEM = 36 * 1024 * 1024
+APPLY_VMEM = 26 * 1024 * 1024
 
 
 def plain_apply(vector_full, environment, bond_terms, term_slot, slot_block, diagonal):
@@ -117,26 +117,28 @@
             put(row, pair, high, low)
 
 
-def pack_kernel(info_ref, wave_ref, own_wave_ref, diag_ref, vec_ref, own_ref, diag_out, tiles):
+def pack_kernel(info_ref, wave_ref, diag_ref, vec_ref, wave_out, diag_out, start_ref):
     half = LANES // 2
     for j in range(wave_ref.shape[0]):
-        own_ref[j] = pack_tile(own_wave_ref[j])
-        diag_out[j] = pack_tile(diag_ref[j])
         for q in range(4):
-            tiles[q, j] = pack_tile(wave_ref[j, :, 2 * LANES * q : 2 * LANES * (q + 1)])
+            wave_out[q, j] = pack_tile(wave_ref[j, :, 2 * LANES * q : 2 * LANES * (q + 1)])
+        diagonal = pack_tile(diag_ref[j])
+        diag_out[j] = diagonal
+        start_ref[j] = diagonal * wave_out[info_ref[0], j]
 
         def put(row, pair, high, low):
             columns = slice(pair * LANES, (pair + 1) * LANES)
             vec_ref[j, row : row + 16, columns] = high
             vec_ref[j, row + half : row + half + 16, columns] = low
 
-        store_vector([tiles.at[q, j] for q in range(4)], [16 * q for q in range(4)], put)
+        store_vector([wave_out.at[q, j] for q in range(4)], [16 * q for q in range(4)], put)
 
 
 def pack(info, wavefunction, diagonal):
     blocks, rows, width = wavefunction.shape
     step = 2
     tile = pl.BlockSpec((step, LANES, LANES), lambda i, *_: (i, 0, 0))
+    tiles = jax.ShapeDtypeStruct((blocks, LANES, LANES), jnp.float32)
     return pl.pallas_call(
         pack_kernel,
         grid_spec=pltpu.PrefetchScalarGridSpec(
@@ -144,21 +146,25 @@
             grid=(blocks // step,),
             in_specs=[
                 pl.BlockSpec((step, rows, width), lambda i, *_: (i, 0, 0)),
-                pl.BlockSpec((step, rows, width // 4), lambda i, info: (i, 0, info[0])),
                 pl.BlockSpec((step, rows, width // 4), lambda i, *_: (i, 0, 0)),
             ],
-            out_specs=[pl.BlockSpec((step, LANES, width), lambda i, *_: (i, 0, 0)), tile, tile],
-            scratch_shapes=[pltpu.VMEM((4, step, LANES, LANES), jnp.float32)],
+            out_specs=[
+                pl.BlockSpec((step, LANES, width), lambda i, *_: (i, 0, 0)),
+                pl.BlockSpec((4, step, LANES, LANES), lambda i, *_: (0, i, 0, 0)),
+                tile,
+                tile,
+            ],
         ),
         out_shape=[
             jax.ShapeDtypeStruct((blocks, LANES, width), jnp.bfloat16),
-            jax.ShapeDtypeStruct((blocks, LANES, LANES), jnp.float32),
-            jax.ShapeDtypeStruct((blocks, LANES, LANES), jnp.float32),
+            jax.ShapeDtypeStruct((4, blocks, LANES, LANES), jnp.float32),
+            tiles,
+            tiles,
         ],
         compiler_params=pltpu.CompilerParams(vmem_limit_bytes=SMALL_VMEM),
         cost_estimate=micros(5),
         name="pack",
-    )(info, wavefunction, wavefunction, diagonal)
+    )(info, wavefunction, diagonal)
 
 
 def mixing_kernel(*refs):
@@ -296,7 +302,7 @@
         compiler_params=pltpu.CompilerParams(vmem_limit_bytes=SMALL_VMEM),
         cost_estimate=micros(1),
         name="cut_pieces",
-    )(info, by_owner)
+    )(info, *in_hbm(by_owner))
 
 
 def own_operands(info, by_owner, group, pieces):
@@ -326,16 +332,16 @@
         compiler_params=pltpu.CompilerParams(vmem_limit_bytes=SMALL_VMEM),
         cost_estimate=micros(6),
         name="own_operands",
-    )(info, by_owner, *pieces)
+    )(info, *in_hbm(by_owner), *pieces)
 
 
 def apply_kernel(plan, info_ref, *refs):
-    chunks, parts_given, sent_given, before_given, pieces = plan
+    chunks, sent_given, before_given, stats_given, pieces = plan
     refs = list(refs)
     take = lambda n: [refs.pop(0) for _ in range(n)]
     slots = take(2)
-    vector = take(4 if parts_given else 1)
-    tiles = take(4) if parts_given else []
+    vector = take(1)[0]
+    stats = take(1)[0] if stats_given else None
     operands = [take(3) for _ in chunks[: -1 if sent_given else None]]
     sent = take(1)[0] if sent_given else None
     mixes = take(len(chunks))
@@ -343,7 +349,7 @@
     outs = take(2 if pieces else 1)
     if sent_given:
         operands.append(take(3))
-    total_ref, vec, mid = take(3)
+    total_ref, mid = take(2)
     if before_given:
         prior, arrival = take(2)
     step = mid.shape[0]
@@ -352,7 +358,6 @@
     first_half = lane_is_first(half)
     keep_first = jnp.where(first_half, 1.0, 0.0).astype(jnp.bfloat16)
     keep_second = jnp.where(first_half, 0.0, 1.0).astype(jnp.bfloat16)
-    nothing = jnp.zeros((lanes, lanes), jnp.bfloat16)
     me = info_ref[4]
 
     @pl.when(pl.program_id(0) == 0)
@@ -364,18 +369,7 @@
     def right_side(j):
         if sent_given:
             other_operands(sent, *operands[-1], j)
-        if parts_given:
-
-            def put(row, pair, high, low):
-                columns = slice(pair * lanes, (pair + 1) * lanes)
-                vec[j, pl.ds(row, 16), columns] = high
-                vec[j, pl.ds(row + half, 16), columns] = low
-
-            rows_of = [pl.multiple_of(info_ref[g] * 16, 16) for g in range(4)]
-            store_vector([x.at[pl.ds(j * lanes, lanes)] for x in vector], rows_of, put)
-            source = vec[j]
-        else:
-            source = vector[0][j]
+        source = vector[j]
         source = jnp.concatenate([source, source], axis=0)
         at = 0
         for left_high, left_low, right in operands:
@@ -400,14 +394,8 @@
         lh, ll = left_high[w, j], left_low[w, j]
         wide_high = jnp.concatenate([lh * keep_first, lh * keep_second], axis=0)
         wide_low = jnp.concatenate([ll * keep_first, ll * keep_second], axis=0)
-        weights = jnp.concatenate(
-            [
-                jnp.concatenate([wide_high, wide_low], axis=1),
-                jnp.concatenate([wide_high, nothing], axis=1),
-            ],
-            axis=0,
-        )
-        return jnp.concatenate([t_high, t_low], axis=1), weights
+        weights = jnp.concatenate([wide_high, wide_high, wide_low], axis=0)
+        return jnp.concatenate([t_high, t_low, t_high], axis=1), weights
 
     def mix_unit(mixing, w, z):
         z_high, z_low = [jnp.concatenate([x[:lanes], x[lanes:]], axis=1) for x in z]
@@ -449,7 +437,7 @@
         if waiting is not None:
             before_j, before_mixing, before_w, before_table, before_bond, before_z = waiting
             mixed = mix_unit(before_mixing, before_w, before_z)
-        z = split_two(z[:, :lanes] + z[:, lanes:])
+        z = split_two(z)
         if waiting is not None:
             add_up(before_j, before_table, before_bond, mixed)
         waiting = (j, mixing, w, table, bond, z)
@@ -462,30 +450,26 @@
             pltpu.make_async_copy(before, prior, arrival).wait()
             total_ref[...] += prior[...]
         if pieces:
-            stats = jnp.zeros((SUB, lanes), jnp.float32)
-            if parts_given:
-                stats = stacked_rows(*merged([tile[...] for tile in tiles]))
+            nil = jnp.zeros((SUB, lanes), jnp.float32)
+            row = stats[...] if stats_given else nil
             for out, part in ((outs[0], info_ref[5]), (outs[1], 1 - info_ref[5])):
                 for k in range(4):
                     for i in range(2):
                         out[k, i * lanes : (i + 1) * lanes] = total_ref[part, 2 * k + i]
-                    out[k, 2 * lanes :] = stats
-                stats = jnp.zeros((SUB, lanes), jnp.float32)
+                    out[k, 2 * lanes :] = row
+                row = nil
         else:
             outs[0][...] = total_ref[...]
 
 
-def apply_bonds(info, slots, vector, chunks, operands, sent, mixing, before, pieces):
+def apply_bonds(info, slots, vector, stats, chunks, operands, sent, mixing, before, pieces):
     count, blocks, half, lanes = operands[0][0].shape
     step = 4
-    parts_given = len(vector) == 4
-    if parts_given:
-        last = vector[0].shape[0] // SUB - 1
-        in_specs = [pl.BlockSpec((step * lanes, lanes), lambda i, *_: (i, 0))] * 4
-        in_specs += [pl.BlockSpec((SUB, lanes), lambda i, *_: (last, 0))] * 4
-    else:
-        in_specs = [pl.BlockSpec((step,) + vector[0].shape[1:], lambda i, *_: (i, 0, 0))]
-    arguments = list(vector) * (2 if parts_given else 1)
+    in_specs = [pl.BlockSpec((step,) + vector.shape[1:], lambda i, *_: (i, 0, 0))]
+    arguments = [vector]
+    if stats is not None:
+        in_specs.append(whole(*stats.shape))
+        arguments.append(stats)
     for made in operands:
         in_specs += operand_specs(count, step, half, lanes)
         arguments += made
@@ -502,7 +486,6 @@
     total = count * len(chunks)
     scratch = [
         pltpu.VMEM((2, 8, lanes, lanes), jnp.float32),
-        pltpu.VMEM((step, lanes, PHYS * half), jnp.bfloat16),
         pltpu.VMEM((step, total * 32, PHYS * half), jnp.float32),
     ]
     if before is not None:
@@ -515,7 +498,7 @@
     if sent is not None:
         out_specs += operand_specs(count, step, half, lanes)
         out_shape += operand_shapes(count, blocks, half, lanes)
-    plan = (tuple(chunks), parts_given, sent is not None, before is not None, pieces)
+    plan = (tuple(chunks), sent is not None, before is not None, stats is not None, pieces)
     out = pl.pallas_call(
         functools.partial(apply_kernel, plan),
         grid_spec=pltpu.PrefetchScalarGridSpec(
@@ -560,47 +543,68 @@
     return cross, square, rest
 
 
-def image_kernel(info_ref, owner_ref, a0, a1, a2, a3, diag_ref, own_ref, image_ref, total):
-    total[...] = diag_ref[...] * own_ref[...]
-    add_arrived(info_ref, owner_ref, (a0, a1, a2, a3), total)
-    blocks = total.shape[0]
+def image_kernel(info_ref, owner_ref, *refs):
+    arrived = [refs[4 * g : 4 * g + 4][::-1] for g in range(4)]
+    starts, wave_ref, image_ref, vec_ref, stats_ref, total = refs[16:20], *refs[20:]
+    half = LANES // 2
+    blocks = image_ref.shape[0]
     cross = jnp.zeros((LANES, LANES), jnp.float32)
     square = jnp.zeros((LANES, LANES), jnp.float32)
-    for k in range(blocks):
-        own, image = own_ref[k], total[k]
-        image_ref[k * LANES : (k + 1) * LANES] = image
-        cross += own * image
-        square += own * own
+    for g in range(4):
+        total[g] = starts[g][...]
+        add_arrived(info_ref, owner_ref, arrived[g], total.at[g])
+        for k in range(blocks):
+            wave = wave_ref[info_ref[g], k]
+            cross += wave * total[g, k]
+            square += wave * wave
+    image_ref[...] = total[0]
     cross = jnp.sum(cross, keepdims=True)
     square = jnp.sum(square, keepdims=True)
     ratio = cross / jnp.maximum(square, TINY)
     rest = jnp.zeros((LANES, LANES), jnp.float32)
-    for k in range(blocks):
-        apart = total[k] - ratio * own_ref[k]
-        rest += apart * apart
-    image_ref[blocks * LANES :] = stacked_rows(cross, square, jnp.sum(rest, keepdims=True))
-
-
-def owner_image(info, owners, arrived, diagonal, own):
-    rows = own.shape[0] * LANES + SUB
+    for g in range(4):
+        for k in range(blocks):
+            apart = total[g, k] - ratio * wave_ref[info_ref[g], k]
+            rest += apart * apart
+    stats_ref[...] = stacked_rows(cross, square, jnp.sum(rest, keepdims=True))
+    rows_of = [pl.multiple_of(info_ref[g] * 16, 16) for g in range(4)]
+    for j in range(blocks):
+
+        def put(row, pair, high, low):
+            columns = slice(pair * LANES, (pair + 1) * LANES)
+            vec_ref[j, pl.ds(row, 16), columns] = high
+            vec_ref[j, pl.ds(row + half, 16), columns] = low
+
+        store_vector([total.at[g, j] for g in range(4)], rows_of, put)
+
+
+def whole_image(info, owners, arrived, starts, waves):
+    blocks = waves.shape[1]
+    pieces = [piece for part in arrived for piece in part]
+    arguments = (*pieces, *starts, waves)
+    shapes = [
+        jax.ShapeDtypeStruct((blocks, LANES, LANES), jnp.float32),
+        jax.ShapeDtypeStruct((blocks, LANES, 8 * LANES), jnp.bfloat16),
+        jax.ShapeDtypeStruct((SUB, LANES), jnp.float32),
+    ]
     return pl.pallas_call(
         image_kernel,
         grid_spec=pltpu.PrefetchScalarGridSpec(
             num_scalar_prefetch=2,
             grid=(1,),
-            in_specs=[whole(*x.shape) for x in (*arrived, diagonal, own)],
-            out_specs=whole(rows, LANES),
-            scratch_shapes=[pltpu.VMEM(own.shape, jnp.float32)],
+            in_specs=[whole(*x.shape) for x in arguments],
+            out_specs=[whole(*x.shape) for x in shapes],
+            scratch_shapes=[pltpu.VMEM(waves.shape, jnp.float32)],
         ),
-        out_shape=jax.ShapeDtypeStruct((rows, LANES), jnp.float32),
-        compiler_params=pltpu.CompilerParams(vmem_limit_bytes=SMALL_VMEM),
+        out_shape=shapes,
+        compiler_params=pltpu.CompilerParams(vmem_limit_bytes=APPLY_VMEM),
         cost_estimate=micros(3),
-        name="owner_image",
-    )(info, owners, *in_hbm(arrived[0]), *arrived[1:], *in_hbm(diagonal, own))
+        name="whole_image",
+    )(info, owners, *arguments)
 
 
 def final_kernel(
-    entries, info_ref, owner_ref, a0, a1, a2, a3, diag_ref, own_ref, image_ref, first_ref,
+    entries, info_ref, owner_ref, a0, a1, a2, a3, diag_ref, wave_ref, image_ref, first_ref,
     vector_ref, second_ref, total,
 ):
     arrived = (a0, a1, a2, a3)
@@ -611,16 +615,16 @@
     mean = scale * scale * ((rest + apart * apart) / entries)
     second_scale = scale * lax.rsqrt(mean + 1e-06)
     for k in range(total.shape[0]):
-        image = image_ref[k * LANES : (k + 1) * LANES]
+        image = image_ref[k]
         total[k] = (diag_ref[k] - rayleigh) * image
         first_ref[k] = unpack_tile(scale * image)
-        vector_ref[k] = unpack_tile(second_scale * (image - rayleigh * own_ref[k]))
+        vector_ref[k] = unpack_tile(second_scale * (image - rayleigh * wave_ref[0, k]))
     add_arrived(info_ref, owner_ref, arrived, total)
     for k in range(total.shape[0]):
         second_ref[k] = unpack_tile(second_scale * total[k])
 
 
-def outputs(info, owners, arrived, diagonal, own, image, entries):
+def outputs(info, owners, arrived, diagonal, waves, image, entries):
     blocks = diagonal.shape[0]
     shape = (blocks, LANES // 2, 2 * LANES)
     return pl.pallas_call(
@@ -628,8 +632,9 @@
         grid_spec=pltpu.PrefetchScalarGridSpec(
             num_scalar_prefetch=2,
             grid=(1,),
-            in_specs=[whole(*x.shape) for x in (*arrived, diagonal, own)]
-            + [whole(blocks * LANES, LANES)],
+            in_specs=[whole(*x.shape) for x in (*arrived, diagonal)]
+            + [pl.BlockSpec((1,) + waves.shape[1:], lambda i, info, _: (info[0], 0, 0, 0))]
+            + [whole(*image.shape)],
             out_specs=[whole(*shape)] * 3,
             scratch_shapes=[pltpu.VMEM(diagonal.shape, jnp.float32)],
         ),
@@ -637,7 +642,7 @@
         compiler_params=pltpu.CompilerParams(vmem_limit_bytes=SMALL_VMEM),
         cost_estimate=micros(4),
         name="outputs",
-    )(info, owners, *arrived, diagonal, own, image)
+    )(info, owners, *arrived, diagonal, waves, image)
 
 
 def in_hbm(*arrays):
@@ -659,7 +664,8 @@
 
 
 def everyone_of(pieces, axis):
-    return [pieces[0]] + [partner(pieces[k], axis, k) for k in range(1, 4)]
+    sent = {k: partner(pieces[k], axis, k) for k in (3, 2, 1)}
+    return [pieces[0], sent[1], sent[2], sent[3]]
 
 
 def to_owners(mine, theirs):
@@ -678,19 +684,23 @@
     per = bonds // GROUPS
     entries = float(blocks * zs * rows * width)
 
-    vector, own, diagonal_packed = pack(info, wavefunction, diagonal)
 
     by_owner = environment.reshape(bonds, zs, blocks, rows // zs, 2 * rows)
     pieces = []
     for group in range(GROUPS):
         cuts = cut_pieces(info, by_owner, group, per)
-        if group:
+        if group == 0:
+            first_cut = cuts[0]
+        else:
             cuts = [after(x, y) for x, y in zip(cuts, pieces[-1][1:])]
         pieces.append([None] + [partner(x, "blk", k + 1) for k, x in enumerate(cuts)])
+    vector, waves, diagonal_packed, start = pack(after(info, pieces[0][1]), wavefunction, diagonal)
     pieces[0][1] = after(pieces[0][1], vector)
     other_terms = partner(after(bond_terms, pieces[0][1]), "mpo", 1)
     mixing = mixing_operand([bond_terms, other_terms])
     slots = [term_slot, partner(after(term_slot, pieces[0][1]), "mpo", 1)]
+    starts = gathered(start)
+    vector = after(vector, *starts[1:])
 
     made, sent = [], []
     total = None
@@ -700,7 +710,7 @@
     def apply_group(group, vector):
         last = group == GROUPS - 1
         out, other = apply_bonds(
-            info, slots, [vector], [group, GROUPS + group], [made[group]],
+            info, slots, vector, None, [group, GROUPS + group], [made[group]],
             partner(sent[group], "mpo", 1), mixing, total, last,
         )
         operands.extend([made[group], other])
@@ -715,13 +725,14 @@
         sent.append(send)
     total = apply_group(GROUPS - 2, after(vector, sent[-1]))[0]
     out = apply_group(GROUPS - 1, vector)
-    image = owner_image(info, slot_block, to_owners(*out), diagonal_packed, own)
-
-    parts = gathered(image)
+    arrived = to_owners(*out)
+    by_part = list(zip(*[gathered(piece) for piece in arrived[::-1]]))
+    image, vector, stats = whole_image(info, slot_block, by_part, starts, waves)
+
     chunks = [group + GROUPS * source for group in range(GROUPS) for source in range(2)]
-    out, _ = apply_bonds(info, slots, parts, chunks, operands, None, mixing, None, True)
+    out, _ = apply_bonds(info, slots, vector, stats, chunks, operands, None, mixing, None, True)
     return tuple(
-        outputs(info, slot_block, to_owners(*out), diagonal_packed, own, image, entries)
+        outputs(info, slot_block, to_owners(*out), diagonal_packed, waves, image, entries)
     )
 
 

time: 135 us -> 158 us (1.17)
  Pallas kernels: 46.3 us -> 58.8 us
  local copies, waits for them, and re-layouts: 4.71 us -> 16.9 us
  starting transfers between devices: 38.1 us -> 35.8 us
    unnamed x57 -> x93, local copies, waits for them, and re-layouts: 4.63 us -> 16.8 us
    pallas_call x4, Pallas kernels: 32.1 us -> 38.1 us  [apply_bonds(): pl.pallas_call(functools.partial(apply_kernel, plan), grid_spec=pltpu.Pre...]
    pallas_call x3, Pallas kernels: 2.49 us -> 5.02 us  [cut_pieces(): pl.pallas_call(functools.partial(cut_kernel, group), grid_spec=pltpu.Pref...]
    pallas_call x3, Pallas kernels: 4.09 us -> 6.46 us  [own_operands(): pl.pallas_call(own_operands_kernel, grid_spec=pltpu.PrefetchScalarGridSpe...]
    ppermute x25 -> x37, starting transfers between devices: 38.1 us -> 35.8 us  [partner(): return lax.ppermute(x, axis, [(i, i ^ k) for i in range(size)])]
    pallas_call x1, Pallas kernels: 2.64 us -> 4.35 us  [whole_image(): pl.pallas_call(image_kernel, grid_spec=pltpu.PrefetchScalarGridSpec(num_s...]
    ppermute x25 -> x37, waiting for transfers between devices: 43.3 us -> 44.3 us  [partner(): return lax.ppermute(x, axis, [(i, i ^ k) for i in range(size)])]
  transfers between devices with their start and end apart: 25 -> 37, of which waited for: 10 -> 15; matrix products, arithmetic and copies ran while one was open for 1% -> 0% of each run, Pallas kernels for 15% -> 16%
where the time goes in v8:
time: 158 us; the launch traced here: 157 us
  Pallas kernels  58.8 us (37%)
  waiting for transfers between devices  44.3 us (28%)
  starting transfers between devices  35.8 us (23%)
  local copies, waits for them, and re-layouts  16.9 us (11%)
    ppermute x37, waiting for transfers between devices, partner(): return lax.ppermute(x, axis, [(i, i ^ k) for i in range(size)])  44.3 us
    pallas_call x4, Pallas kernels, apply_bonds(): pl.pallas_call(functools.partial(apply_kernel, plan), grid_spec=pltpu.Pre...  38.1 us
    ppermute x37, starting transfers between devices, partner(): return lax.ppermute(x, axis, [(i, i ^ k) for i in range(size)])  35.8 us
    unnamed x93, local copies, waits for them, and re-layouts  16.8 us
    pallas_call x3, Pallas kernels, own_operands(): pl.pallas_call(own_operands_kernel, grid_spec=pltpu.PrefetchScalarGridSpe...  6.46 us
    pallas_call x3, Pallas kernels, cut_pieces(): pl.pallas_call(functools.partial(cut_kernel, group), grid_spec=pltpu.Pref...  5.02 us
    pallas_call x1, Pallas kernels, whole_image(): pl.pallas_call(image_kernel, grid_spec=pltpu.PrefetchScalarGridSpec(num_s...  4.35 us
  transfers between devices with their start and end apart: 37, of which 15 were waited for; matrix products, arithmetic and copies ran while one was open for 0% of the time, Pallas kernels for 16%

profile of v8, /device:TPU:0, one launch (start us, length us, event | category | flops | bytes accessed | tf_op | source)
XLA Modules:
  0.0 157.2 jit_solution(8375322403205875588)
XLA Ops:
  2.3 3.1 %collective-permute-start = (f32[2,8,16,128]{3,2,1,0:T(8,128)S(1)}, f32[2,8,16,128]{3,2,1,0:T(8,128)S(1)}, u32[]{:S(2)}, u32[]{:S(2)}) collective-permute-start(f32[2,8,16,128]{3,2,1,0:T(8,128)S(1)} %get-tuple-element.60), channel_id=1, source_target_pairs={{0,4},{4,0},{8,12},{12,8},{1,5},{5,1},{9,13},{13,9},{2,6},{6,2},{1... | collective-permute-start | bytes 393224 | tf_op jit(solution)/shard_map/ppermute | solution.py:654
  5.4 2.6 %collective-permute-start.7 = (f32[2,8,16,128]{3,2,1,0:T(8,128)S(1)}, f32[2,8,16,128]{3,2,1,0:T(8,128)S(1)}, u32[]{:S(2)}, u32[]{:S(2)}) collective-permute-start(f32[2,8,16,128]{3,2,1,0:T(8,128)S(1)} %get-tuple-element.73), channel_id=1, source_target_pairs={{0,8},{4,12},{8,0},{12,4},{1,9},{5,13},{9,1},{13,5},{2,10},{6,14},... | collective-permute-start | bytes 393224 | tf_op jit(solution)/shard_map/ppermute | solution.py:654
  11.5 2.5 %pack.1 = (bf16[8,128,1024]{2,1,0:T(8,128)(2,1)S(1)}, f32[4,8,128,128]{3,2,1,0:T(8,128)S(1)}, f32[8,128,128]{2,1,0:T(8,128)S(1)}, f32[8,128,128]{2,1,0:T(8,128)S(1)}) custom-call(s32[7]{0:T(128)S(1)} %stack.31.info_ref, f32[8,64,1024]{2,1,0:T(8,128)S(1)} %copy-done.21, f32[8,64,256]{2,1,0:T(8,128)S(1)} %copy-done.22), custom_call_target="tpu_custom_call" | custom-call | flops 5500000256 | bytes 1048576 | tf_op jit(solution)/shard_map/pack/pallas_call | solution.py:142
  20.6 2.2 %own_operands.4 = (bf16[2,8,64,128]{3,2,1,0:T(8,128)(2,1)S(1)}, bf16[2,8,64,128]{3,2,1,0:T(8,128)(2,1)S(1)}, bf16[8,64,256]{2,1,0:T(8,128)(2,1)S(1)}, f32[2,8,48,128]{3,2,1,0:T(8,128)S(1)}) custom-call(s32[7]{0:T(128)S(1)} %stack.31.info_ref, f32[6,4,8,16,128]{4,3,2,1,0:T(8,128)} %bitcast.27, f32[2,8,16,128]{3,2,1,0:T(8,128)S(1)} %collective-permute-done.refs_1_, ...), custom_call_target="tpu_custom_call" | custom-call | flops 6600000000 | bytes 1048576 | tf_op jit(solution)/shard_map/own_operands/pallas_call | solution.py:312
  22.8 6.7 %collective-permute-done.14.refs_1_ = f32[6,16,16]{2,1,0:T(8,128)S(1)} collective-permute-done((f32[6,16,16]{2,1,0:T(8,128)S(1)}, f32[6,16,16]{2,1,0:T(8,128)S(1)}, u32[]{:S(2)}, u32[]{:S(2)}) %collective-permute-start.14) | collective-permute-done | bytes 6176 | tf_op jit(solution)/shard_map/ppermute | solution.py:654
  29.5 3.8 %collective-permute-start.11 = (f32[2,8,16,128]{3,2,1,0:T(8,128)S(1)}, f32[2,8,16,128]{3,2,1,0:T(8,128)S(1)}, u32[]{:S(2)}, u32[]{:S(2)}) collective-permute-start(f32[2,8,16,128]{3,2,1,0:T(8,128)S(1)} %get-tuple-element.79), channel_id=1, source_target_pairs={{0,12},{4,8},{8,4},{12,0},{1,13},{5,9},{9,5},{13,1},{2,14},{6,10},... | collective-permute-start | bytes 393224 | tf_op jit(solution)/shard_map/ppermute | solution.py:654
  35.2 2.4 %collective-permute-done.11.refs_3_ = f32[2,8,16,128]{3,2,1,0:T(8,128)S(1)} collective-permute-done((f32[2,8,16,128]{3,2,1,0:T(8,128)S(1)}, f32[2,8,16,128]{3,2,1,0:T(8,128)S(1)}, u32[]{:S(2)}, u32[]{:S(2)}) %collective-permute-start.11) | collective-permute-done | bytes 131104 | tf_op jit(solution)/shard_map/ppermute | solution.py:654
  37.7 3.7 %collective-permute-start.12 = (f32[2,8,16,128]{3,2,1,0:T(8,128)S(1)}, f32[2,8,16,128]{3,2,1,0:T(8,128)S(1)}, u32[]{:S(2)}, u32[]{:S(2)}) collective-permute-start(f32[2,8,16,128]{3,2,1,0:T(8,128)S(1)} %get-tuple-element.80), channel_id=1, source_target_pairs={{0,12},{4,8},{8,4},{12,0},{1,13},{5,9},{9,5},{13,1},{2,14},{6,10},... | collective-permute-start | bytes 393224 | tf_op jit(solution)/shard_map/ppermute | solution.py:654
  41.4 2.2 %own_operands.3 = (bf16[2,8,64,128]{3,2,1,0:T(8,128)(2,1)S(1)}, bf16[2,8,64,128]{3,2,1,0:T(8,128)(2,1)S(1)}, bf16[8,64,256]{2,1,0:T(8,128)(2,1)S(1)}, f32[2,8,48,128]{3,2,1,0:T(8,128)S(1)}) custom-call(s32[7]{0:T(128)S(1)} %stack.31.info_ref, f32[6,4,8,16,128]{4,3,2,1,0:T(8,128)} %bitcast.28, f32[2,8,16,128]{3,2,1,0:T(8,128)S(1)} %collective-permute-done.5.refs_1_, ...), custom_call_target="tpu_custom_call" | custom-call | flops 6600000000 | bytes 1048576 | tf_op jit(solution)/shard_map/own_operands/pallas_call | solution.py:312
  49.7 6.5 %apply_bonds.4 = (f32[2,8,128,128]{3,2,1,0:T(8,128)S(1)}, bf16[2,8,64,128]{3,2,1,0:T(8,128)(2,1)S(1)}, bf16[2,8,64,128]{3,2,1,0:T(8,128)(2,1)S(1)}, bf16[8,64,256]{2,1,0:T(8,128)(2,1)S(1)}) custom-call(s32[7]{0:T(128)S(1)} %stack.31.info_ref, s32[6,8]{1,0:T(8,128)S(1)} %copy-done.20, s32[6,8]{1,0:T(8,128)S(1)} %collective-permute-done.1.refs_1_, ...), custom_call_target="tpu_custom_call" | custom-call | flops 1100000000 | bytes 1048576 | tf_op jit(solution)/shard_map/apply_bonds/pallas_call | solution.py:502
  56.3 2.2 %own_operands.5 = (bf16[2,8,64,128]{3,2,1,0:T(8,128)(2,1)S(1)}, bf16[2,8,64,128]{3,2,1,0:T(8,128)(2,1)S(1)}, bf16[8,64,256]{2,1,0:T(8,128)(2,1)S(1)}, f32[2,8,48,128]{3,2,1,0:T(8,128)S(1)}) custom-call(s32[7]{0:T(128)S(1)} %stack.31.info_ref, f32[6,4,8,16,128]{4,3,2,1,0:T(8,128)} %bitcast.29, f32[2,8,16,128]{3,2,1,0:T(8,128)S(1)} %collective-permute-done.6.refs_1_, ...), custom_call_target="tpu_custom_call" | custom-call | flops 6600000000 | bytes 1048576 | tf_op jit(solution)/shard_map/own_operands/pallas_call | solution.py:312
  58.9 6.7 %apply_bonds.5 = (f32[2,8,128,128]{3,2,1,0:T(8,128)S(1)}, bf16[2,8,64,128]{3,2,1,0:T(8,128)(2,1)S(1)}, bf16[2,8,64,128]{3,2,1,0:T(8,128)(2,1)S(1)}, bf16[8,64,256]{2,1,0:T(8,128)(2,1)S(1)}) custom-call(s32[7]{0:T(128)S(1)} %stack.31.info_ref, s32[6,8]{1,0:T(8,128)S(1)} %copy-done.20, s32[6,8]{1,0:T(8,128)S(1)} %collective-permute-done.1.refs_1_, ...), custom_call_target="tpu_custom_call" | custom-call | flops 1100000000 | bytes 1048576 | tf_op jit(solution)/shard_map/apply_bonds/pallas_call | solution.py:502
  65.7 3.3 %collective-permute-done.15.refs_6_ = f32[2,8,48,128]{3,2,1,0:T(8,128)S(1)} collective-permute-done((f32[2,8,48,128]{3,2,1,0:T(8,128)S(1)}, f32[2,8,48,128]{3,2,1,0:T(8,128)S(1)}, u32[]{:S(2)}, u32[]{:S(2)}) %collective-permute-start.15) | collective-permute-done | bytes 393248 | tf_op jit(solution)/shard_map/ppermute | solution.py:654
  69.0 6.9 %apply_bonds.6 = (f32[4,264,128]{2,1,0:T(8,128)S(1)}, f32[4,264,128]{2,1,0:T(8,128)S(1)}, bf16[2,8,64,128]{3,2,1,0:T(8,128)(2,1)S(1)}, bf16[2,8,64,128]{3,2,1,0:T(8,128)(2,1)S(1)}, bf16[8,64,256]{2,1,0:T(8,128)(2,1)S(1)}) custom-call(s32[7]{0:T(128)S(1)} %stack.31.info_ref, s32[6,8]{1,0:T(8,128)S(1)} %copy-done.20, ...), custom_call_target="tpu_custom_call" | custom-call | flops 1100000000 | bytes 1048576 | tf_op jit(solution)/shard_map/apply_bonds/pallas_call | solution.py:502
  79.9 2.7 %collective-permute-start.18 = (f32[264,128]{1,0:T(8,128)S(1)}, f32[264,128]{1,0:T(8,128)}, u32[]{:S(2)}, u32[]{:S(2)}) collective-permute-start(f32[264,128]{1,0:T(8,128)S(1)} %get-tuple-element.124), channel_id=1, source_target_pairs={{0,12},{4,8},{8,4},{12,0},{1,13},{5,9},{9,5},{13,1},{2,14},{6,10},... | collective-permute-start | bytes 405512 | tf_op jit(solution)/shard_map/ppermute | solution.py:654
  83.5 2.7 %collective-permute-done.20.refs_2_ = f32[264,128]{1,0:T(8,128)S(1)} collective-permute-done((f32[264,128]{1,0:T(8,128)S(1)}, f32[264,128]{1,0:T(8,128)S(1)}, u32[]{:S(2)}, u32[]{:S(2)}) %collective-permute-start.20) | collective-permute-done | bytes 135200 | tf_op jit(solution)/shard_map/ppermute | solution.py:654
  86.2 5.3 %collective-permute-done.19.refs_1_ = f32[264,128]{1,0:T(8,128)S(1)} collective-permute-done((f32[264,128]{1,0:T(8,128)S(1)}, f32[264,128]{1,0:T(8,128)S(1)}, u32[]{:S(2)}, u32[]{:S(2)}) %collective-permute-start.19) | collective-permute-done | bytes 135200 | tf_op jit(solution)/shard_map/ppermute | solution.py:654
  99.8 2.6 %collective-permute-done.21.refs_4_ = f32[264,128]{1,0:T(8,128)} collective-permute-done((f32[264,128]{1,0:T(8,128)}, f32[264,128]{1,0:T(8,128)}, u32[]{:S(2)}, u32[]{:S(2)}) %collective-permute-start.21) | collective-permute-done | bytes 135200 | tf_op jit(solution)/shard_map/ppermute | solution.py:654
  115.4 4.3 %whole_image.1 = (f32[8,128,128]{2,1,0:T(8,128)S(1)}, bf16[8,128,1024]{2,1,0:T(8,128)(2,1)S(1)}, f32[8,128]{1,0:T(8,128)S(1)}) custom-call(s32[7]{0:T(128)S(1)} %stack.31.info_ref, s32[4,2]{1,0:T(4,128)S(1)} %copy.10.owner_ref, f32[264,128]{1,0:T(8,128)} %collective-permute-done.18.refs_0_, f32[264,128]{1,0:T(8,128)S(1)} %copy-done.34, ...), custom_call_target="tpu_custom_call" | custom-call | flops 3300000000 | bytes 1048576 | tf_op jit(solution)/shard_map/whole_image/pallas_call | solution.py:590
  119.9 17.9 %apply_bonds.7 = (f32[4,264,128]{2,1,0:T(8,128)S(1)}, f32[4,264,128]{2,1,0:T(8,128)S(1)}) custom-call(s32[7]{0:T(128)S(1)} %stack.31.info_ref, s32[6,8]{1,0:T(8,128)S(1)} %copy-done.20, s32[6,8]{1,0:T(8,128)S(1)} %collective-permute-done.1.refs_1_, bf16[8,128,1024]{2,1,0:T(8,128)(2,1)S(1)} %get-tuple-element.102.refs_2_, ...), custom_call_target="tpu_custom_call" | custom-call | flops 1100000000 | bytes 1048576 | tf_op jit(solution)/shard_map/apply_bonds/pallas_call | solution.py:502
  139.9 2.6 %collective-permute-start.36 = (f32[264,128]{1,0:T(8,128)S(1)}, f32[264,128]{1,0:T(8,128)S(1)}, u32[]{:S(2)}, u32[]{:S(2)}) collective-permute-start(f32[264,128]{1,0:T(8,128)S(1)} %get-tuple-element.117), channel_id=1, source_target_pairs={{0,12},{4,8},{8,4},{12,0},{1,13},{5,9},{9,5},{13,1},{2,14},{6,10},... | collective-permute-start | bytes 405512 | tf_op jit(solution)/shard_map/ppermute | solution.py:654
  144.3 4.0 %collective-permute-done.36.a3 = f32[264,128]{1,0:T(8,128)S(1)} collective-permute-done((f32[264,128]{1,0:T(8,128)S(1)}, f32[264,128]{1,0:T(8,128)S(1)}, u32[]{:S(2)}, u32[]{:S(2)}) %collective-permute-start.36) | collective-permute-done | bytes 135200 | tf_op jit(solution)/shard_map/ppermute | solution.py:654
  148.3 6.8 %collective-permute-done.35.a2 = f32[264,128]{1,0:T(8,128)S(1)} collective-permute-done((f32[264,128]{1,0:T(8,128)S(1)}, f32[264,128]{1,0:T(8,128)S(1)}, u32[]{:S(2)}, u32[]{:S(2)}) %collective-permute-start.35) | collective-permute-done | bytes 135200 | tf_op jit(solution)/shard_map/ppermute | solution.py:654
  155.1 2.1 %outputs.1 = (f32[8,64,256]{2,1,0:T(8,128)}, f32[8,64,256]{2,1,0:T(8,128)}, f32[8,64,256]{2,1,0:T(8,128)}) custom-call(s32[7]{0:T(128)S(1)} %stack.31.info_ref, s32[4,2]{1,0:T(4,128)S(1)} %copy.10.owner_ref, f32[264,128]{1,0:T(8,128)S(1)} %get-tuple-element.120.a0, f32[264,128]{1,0:T(8,128)S(1)} %collective-permute-done.34.a1, ...), custom_call_target="tpu_custom_call" | custom-call | flops 4400000000 | bytes 1048576 | tf_op jit(solution)/shard_map/outputs/pallas_call | solution.py:630
  (160 shorter events, 50.1 us)
Async XLA Ops:
  2.3 9.2 %collective-permute-start = (f32[2,8,16,128]{3,2,1,0:T(8,128)S(1)}, f32[2,8,16,128]{3,2,1,0:T(8,128)S(1)}, u32[]{:S(2)}, u32[]{:S(2)}) collective-permute-start(f32[2,8,16,128]{3,2,1,0:T(8,128)S(1)} %get-tuple-element.60), channel_id=1, source_target_pairs={{0,4},{4,0},{8,12},{12,8},{1,5},{5,1},{9,13},{13,9},{2,6},{6,2},{1... | collective-permute-start | bytes 393224 | tf_op jit(solution)/shard_map/ppermute | solution.py:654
  5.4 12.9 %collective-permute-start.7 = (f32[2,8,16,128]{3,2,1,0:T(8,128)S(1)}, f32[2,8,16,128]{3,2,1,0:T(8,128)S(1)}, u32[]{:S(2)}, u32[]{:S(2)}) collective-permute-start(f32[2,8,16,128]{3,2,1,0:T(8,128)S(1)} %get-tuple-element.73), channel_id=1, source_target_pairs={{0,8},{4,12},{8,0},{12,4},{1,9},{5,13},{9,1},{13,5},{2,10},{6,14},... | collective-permute-start | bytes 393224 | tf_op jit(solution)/shard_map/ppermute | solution.py:654
  8.0 12.0 %collective-permute-start.10 = (f32[2,8,16,128]{3,2,1,0:T(8,128)S(1)}, f32[2,8,16,128]{3,2,1,0:T(8,128)S(1)}, u32[]{:S(2)}, u32[]{:S(2)}) collective-permute-start(f32[2,8,16,128]{3,2,1,0:T(8,128)S(1)} %get-tuple-element.78), channel_id=1, source_target_pairs={{0,12},{4,8},{8,4},{12,0},{1,13},{5,9},{9,5},{13,1},{2,14},{6,10},... | collective-permute-start | bytes 393224 | tf_op jit(solution)/shard_map/ppermute | solution.py:654
  14.0 23.7 %collective-permute-start.3 = (f32[8,128,128]{2,1,0:T(8,128)S(1)}, f32[8,128,128]{2,1,0:T(8,128)S(1)}, u32[]{:S(2)}, u32[]{:S(2)}) collective-permute-start(f32[8,128,128]{2,1,0:T(8,128)S(1)} %get-tuple-element.65.refs_16_), channel_id=1, source_target_pairs={{0,1},{1,0},{2,3},{3,2},{4,5},{5,4},{6,7},{7,6},{8,9},{9,8},{10,11... | collective-permute-start | bytes 1572872 | tf_op jit(solution)/shard_map/ppermute | solution.py:654
  14.1 27.3 %collective-permute-start.2 = (f32[8,128,128]{2,1,0:T(8,128)S(1)}, f32[8,128,128]{2,1,0:T(8,128)S(1)}, u32[]{:S(2)}, u32[]{:S(2)}) collective-permute-start(f32[8,128,128]{2,1,0:T(8,128)S(1)} %get-tuple-element.65.refs_16_), channel_id=1, source_target_pairs={{0,2},{2,0},{1,3},{3,1},{4,6},{6,4},{5,7},{7,5},{8,10},{10,8},{9,1... | collective-permute-start | bytes 1572872 | tf_op jit(solution)/shard_map/ppermute | solution.py:654
  15.9 17.8 %collective-permute-start.5 = (f32[2,8,16,128]{3,2,1,0:T(8,128)S(1)}, f32[2,8,16,128]{3,2,1,0:T(8,128)S(1)}, u32[]{:S(2)}, u32[]{:S(2)}) collective-permute-start(f32[2,8,16,128]{3,2,1,0:T(8,128)S(1)} %get-tuple-element.69), channel_id=1, source_target_pairs={{0,4},{4,0},{8,12},{12,8},{1,5},{5,1},{9,13},{13,9},{2,6},{6,2},{1... | collective-permute-start | bytes 393224 | tf_op jit(solution)/shard_map/ppermute | solution.py:654
  18.3 16.9 %collective-permute-start.8 = (f32[2,8,16,128]{3,2,1,0:T(8,128)S(1)}, f32[2,8,16,128]{3,2,1,0:T(8,128)S(1)}, u32[]{:S(2)}, u32[]{:S(2)}) collective-permute-start(f32[2,8,16,128]{3,2,1,0:T(8,128)S(1)} %get-tuple-element.74), channel_id=1, source_target_pairs={{0,8},{4,12},{8,0},{12,4},{1,9},{5,13},{9,1},{13,5},{2,10},{6,14},... | collective-permute-start | bytes 393224 | tf_op jit(solution)/shard_map/ppermute | solution.py:654
  20.1 9.4 %collective-permute-start.14 = (f32[6,16,16]{2,1,0:T(8,128)S(1)}, f32[6,16,16]{2,1,0:T(8,128)S(1)}, u32[]{:S(2)}, u32[]{:S(2)}) collective-permute-start(f32[6,16,16]{2,1,0:T(8,128)S(1)} %copy-done.41), channel_id=1, source_target_pairs={{0,2},{2,0},{1,3},{3,1},{4,6},{6,4},{5,7},{7,5},{8,10},{10,8},{9,1... | collective-permute-start | bytes 18440 | tf_op jit(solution)/shard_map/ppermute | solution.py:654
  29.5 8.2 %collective-permute-start.11 = (f32[2,8,16,128]{3,2,1,0:T(8,128)S(1)}, f32[2,8,16,128]{3,2,1,0:T(8,128)S(1)}, u32[]{:S(2)}, u32[]{:S(2)}) collective-permute-start(f32[2,8,16,128]{3,2,1,0:T(8,128)S(1)} %get-tuple-element.79), channel_id=1, source_target_pairs={{0,12},{4,8},{8,4},{12,0},{1,13},{5,9},{9,5},{13,1},{2,14},{6,10},... | collective-permute-start | bytes 393224 | tf_op jit(solution)/shard_map/ppermute | solution.py:654
  33.7 16.0 %collective-permute-start.13 = (f32[2,8,48,128]{3,2,1,0:T(8,128)S(1)}, f32[2,8,48,128]{3,2,1,0:T(8,128)S(1)}, u32[]{:S(2)}, u32[]{:S(2)}) collective-permute-start(f32[2,8,48,128]{3,2,1,0:T(8,128)S(1)} %get-tuple-element.86), channel_id=1, source_target_pairs={{0,2},{2,0},{1,3},{3,1},{4,6},{6,4},{5,7},{7,5},{8,10},{10,8},{9,1... | collective-permute-start | bytes 1179656 | tf_op jit(solution)/shard_map/ppermute | solution.py:654
  35.2 21.0 %collective-permute-start.6 = (f32[2,8,16,128]{3,2,1,0:T(8,128)S(1)}, f32[2,8,16,128]{3,2,1,0:T(8,128)S(1)}, u32[]{:S(2)}, u32[]{:S(2)}) collective-permute-start(f32[2,8,16,128]{3,2,1,0:T(8,128)S(1)} %get-tuple-element.70), channel_id=1, source_target_pairs={{0,4},{4,0},{8,12},{12,8},{1,5},{5,1},{9,13},{13,9},{2,6},{6,2},{1... | collective-permute-start | bytes 393224 | tf_op jit(solution)/shard_map/ppermute | solution.py:654
  37.7 18.6 %collective-permute-start.9 = (f32[2,8,16,128]{3,2,1,0:T(8,128)S(1)}, f32[2,8,16,128]{3,2,1,0:T(8,128)S(1)}, u32[]{:S(2)}, u32[]{:S(2)}) collective-permute-start(f32[2,8,16,128]{3,2,1,0:T(8,128)S(1)} %get-tuple-element.75), channel_id=1, source_target_pairs={{0,8},{4,12},{8,0},{12,4},{1,9},{5,13},{9,1},{13,5},{2,10},{6,14},... | collective-permute-start | bytes 393224 | tf_op jit(solution)/shard_map/ppermute | solution.py:654
  37.7 18.6 %collective-permute-start.12 = (f32[2,8,16,128]{3,2,1,0:T(8,128)S(1)}, f32[2,8,16,128]{3,2,1,0:T(8,128)S(1)}, u32[]{:S(2)}, u32[]{:S(2)}) collective-permute-start(f32[2,8,16,128]{3,2,1,0:T(8,128)S(1)} %get-tuple-element.80), channel_id=1, source_target_pairs={{0,12},{4,8},{8,4},{12,0},{1,13},{5,9},{9,5},{13,1},{2,14},{6,10},... | collective-permute-start | bytes 393224 | tf_op jit(solution)/shard_map/ppermute | solution.py:654
  48.0 10.9 %collective-permute-start.16 = (f32[2,8,48,128]{3,2,1,0:T(8,128)S(1)}, f32[2,8,48,128]{3,2,1,0:T(8,128)S(1)}, u32[]{:S(2)}, u32[]{:S(2)}) collective-permute-start(f32[2,8,48,128]{3,2,1,0:T(8,128)S(1)} %get-tuple-element.81), channel_id=1, source_target_pairs={{0,2},{2,0},{1,3},{3,1},{4,6},{6,4},{5,7},{7,5},{8,10},{10,8},{9,1... | collective-permute-start | bytes 1179656 | tf_op jit(solution)/shard_map/ppermute | solution.py:654
  58.5 10.5 %collective-permute-start.15 = (f32[2,8,48,128]{3,2,1,0:T(8,128)S(1)}, f32[2,8,48,128]{3,2,1,0:T(8,128)S(1)}, u32[]{:S(2)}, u32[]{:S(2)}) collective-permute-start(f32[2,8,48,128]{3,2,1,0:T(8,128)S(1)} %get-tuple-element.93), channel_id=1, source_target_pairs={{0,2},{2,0},{1,3},{3,1},{4,6},{6,4},{5,7},{7,5},{8,10},{10,8},{9,1... | collective-permute-start | bytes 1179656 | tf_op jit(solution)/shard_map/ppermute | solution.py:654
  78.1 8.2 %collective-permute-start.20 = (f32[264,128]{1,0:T(8,128)S(1)}, f32[264,128]{1,0:T(8,128)S(1)}, u32[]{:S(2)}, u32[]{:S(2)}) collective-permute-start(f32[264,128]{1,0:T(8,128)S(1)} %get-tuple-element.122), channel_id=1, source_target_pairs={{0,4},{4,0},{8,12},{12,8},{1,5},{5,1},{9,13},{13,9},{2,6},{6,2},{1... | collective-permute-start | bytes 405512 | tf_op jit(solution)/shard_map/ppermute | solution.py:654
  78.4 13.1 %collective-permute-start.19 = (f32[264,128]{1,0:T(8,128)S(1)}, f32[264,128]{1,0:T(8,128)S(1)}, u32[]{:S(2)}, u32[]{:S(2)}) collective-permute-start(f32[264,128]{1,0:T(8,128)S(1)} %get-tuple-element.123), channel_id=1, source_target_pairs={{0,8},{4,12},{8,0},{12,4},{1,9},{5,13},{9,1},{13,5},{2,10},{6,14},... | collective-permute-start | bytes 405512 | tf_op jit(solution)/shard_map/ppermute | solution.py:654
  79.9 12.7 %collective-permute-start.18 = (f32[264,128]{1,0:T(8,128)S(1)}, f32[264,128]{1,0:T(8,128)}, u32[]{:S(2)}, u32[]{:S(2)}) collective-permute-start(f32[264,128]{1,0:T(8,128)S(1)} %get-tuple-element.124), channel_id=1, source_target_pairs={{0,12},{4,8},{8,4},{12,0},{1,13},{5,9},{9,5},{13,1},{2,14},{6,10},... | collective-permute-start | bytes 405512 | tf_op jit(solution)/shard_map/ppermute | solution.py:654
  82.5 10.1 %collective-permute-start.28 = (f32[264,128]{1,0:T(8,128)S(1)}, f32[264,128]{1,0:T(8,128)S(1)}, u32[]{:S(2)}, u32[]{:S(2)}) collective-permute-start(f32[264,128]{1,0:T(8,128)S(1)} %get-tuple-element.121.refs_3_), channel_id=1, source_target_pairs={{0,1},{1,0},{2,3},{3,2},{4,5},{5,4},{6,7},{7,6},{8,9},{9,8},{10,11... | collective-permute-start | bytes 405512 | tf_op jit(solution)/shard_map/ppermute | solution.py:654
  82.5 13.1 %collective-permute-start.24 = (f32[264,128]{1,0:T(8,128)S(1)}, f32[264,128]{1,0:T(8,128)}, u32[]{:S(2)}, u32[]{:S(2)}) collective-permute-start(f32[264,128]{1,0:T(8,128)S(1)} %get-tuple-element.121.refs_3_), channel_id=1, source_target_pairs={{0,2},{2,0},{1,3},{3,1},{4,6},{6,4},{5,7},{7,5},{8,10},{10,8},{9,1... | collective-permute-start | bytes 405512 | tf_op jit(solution)/shard_map/ppermute | solution.py:654
  86.2 9.7 %collective-permute-start.27 = (f32[264,128]{1,0:T(8,128)S(1)}, f32[264,128]{1,0:T(8,128)S(1)}, u32[]{:S(2)}, u32[]{:S(2)}) collective-permute-start(f32[264,128]{1,0:T(8,128)S(1)} %collective-permute-done.20.refs_2_), channel_id=1, source_target_pairs={{0,1},{1,0},{2,3},{3,2},{4,5},{5,4},{6,7},{7,6},{8,9},{9,8},{10,11... | collective-permute-start | bytes 405512 | tf_op jit(solution)/shard_map/ppermute | solution.py:654
  139.9 8.4 %collective-permute-start.36 = (f32[264,128]{1,0:T(8,128)S(1)}, f32[264,128]{1,0:T(8,128)S(1)}, u32[]{:S(2)}, u32[]{:S(2)}) collective-permute-start(f32[264,128]{1,0:T(8,128)S(1)} %get-tuple-element.117), channel_id=1, source_target_pairs={{0,12},{4,8},{8,4},{12,0},{1,13},{5,9},{9,5},{13,1},{2,14},{6,10},... | collective-permute-start | bytes 405512 | tf_op jit(solution)/shard_map/ppermute | solution.py:654
  142.4 12.7 %collective-permute-start.35 = (f32[264,128]{1,0:T(8,128)S(1)}, f32[264,128]{1,0:T(8,128)S(1)}, u32[]{:S(2)}, u32[]{:S(2)}) collective-permute-start(f32[264,128]{1,0:T(8,128)S(1)} %get-tuple-element.118), channel_id=1, source_target_pairs={{0,8},{4,12},{8,0},{12,4},{1,9},{5,13},{9,1},{13,5},{2,10},{6,14},... | collective-permute-start | bytes 405512 | tf_op jit(solution)/shard_map/ppermute | solution.py:654
  142.7 12.4 %collective-permute-start.34 = (f32[264,128]{1,0:T(8,128)S(1)}, f32[264,128]{1,0:T(8,128)S(1)}, u32[]{:S(2)}, u32[]{:S(2)}) collective-permute-start(f32[264,128]{1,0:T(8,128)S(1)} %get-tuple-element.119), channel_id=1, source_target_pairs={{0,4},{4,0},{8,12},{12,8},{1,5},{5,1},{9,13},{13,9},{2,6},{6,2},{1... | collective-permute-start | bytes 405512 | tf_op jit(solution)/shard_map/ppermute | solution.py:654
  (59 other events, 245.4 us)

commit v9 on v7

--- a/solution.py
+++ b/solution.py
@@ -13,7 +13,7 @@
 TINY = 1e-30
 GROUPS = 3
 SMALL_VMEM = 16 * 1024 * 1024
-APPLY_VMEM = 36 * 1024 * 1024
+APPLY_VMEM = 26 * 1024 * 1024
 
 
 def plain_apply(vector_full, environment, bond_terms, term_slot, slot_block, diagonal):
@@ -174,12 +174,12 @@
     for source in sources:
         for k in range(source.shape[0]):
             high, low = split_two(source[k].T)
-            for term, places in ((high, (0, 1)), (low, (2,))):
+            for place, term in enumerate((high, low)):
                 wide = jnp.dot(term, spread, preferred_element_type=jnp.float32)
                 tall = jnp.concatenate([wide] * SUB, axis=0)
                 tall = jnp.where(same, tall, 0.0).astype(jnp.bfloat16)
-                for place in places:
-                    out_ref[at, :, place * LANES : (place + 1) * LANES] = tall
+                rows = slice(place * LANES, (place + 1) * LANES)
+                out_ref[at, rows] = jnp.concatenate([tall, tall], axis=1)
             at += 1
 
 
@@ -187,7 +187,7 @@
     count = sources[0].shape[0] * len(sources)
     return pl.pallas_call(
         mixing_kernel,
-        out_shape=jax.ShapeDtypeStruct((count, LANES, 3 * LANES), jnp.bfloat16),
+        out_shape=jax.ShapeDtypeStruct((count, 2 * LANES, 2 * LANES), jnp.bfloat16),
         compiler_params=pltpu.CompilerParams(vmem_limit_bytes=SMALL_VMEM),
         cost_estimate=micros(2),
         name="mixing",
@@ -296,7 +296,7 @@
         compiler_params=pltpu.CompilerParams(vmem_limit_bytes=SMALL_VMEM),
         cost_estimate=micros(1),
         name="cut_pieces",
-    )(info, by_owner)
+    )(info, *(in_hbm(by_owner) if group == 0 else [by_owner]))
 
 
 def own_operands(info, by_owner, group, pieces):
@@ -352,7 +352,6 @@
     first_half = lane_is_first(half)
     keep_first = jnp.where(first_half, 1.0, 0.0).astype(jnp.bfloat16)
     keep_second = jnp.where(first_half, 0.0, 1.0).astype(jnp.bfloat16)
-    nothing = jnp.zeros((lanes, lanes), jnp.bfloat16)
     me = info_ref[4]
 
     @pl.when(pl.program_id(0) == 0)
@@ -400,20 +399,15 @@
         lh, ll = left_high[w, j], left_low[w, j]
         wide_high = jnp.concatenate([lh * keep_first, lh * keep_second], axis=0)
         wide_low = jnp.concatenate([ll * keep_first, ll * keep_second], axis=0)
-        weights = jnp.concatenate(
-            [
-                jnp.concatenate([wide_high, wide_low], axis=1),
-                jnp.concatenate([wide_high, nothing], axis=1),
-            ],
-            axis=0,
-        )
+        weights = jnp.concatenate([wide_high, wide_low], axis=1)
+        weights = jnp.concatenate([weights, weights], axis=0)
         return jnp.concatenate([t_high, t_low], axis=1), weights
 
     def mix_unit(mixing, w, z):
         z_high, z_low = [jnp.concatenate([x[:lanes], x[lanes:]], axis=1) for x in z]
         return jnp.dot(
             mixing[w],
-            jnp.concatenate([z_high, z_low, z_high], axis=0),
+            jnp.concatenate([z_high, z_low], axis=0),
             preferred_element_type=jnp.float32,
         )
 
@@ -421,7 +415,8 @@
         slot = table[bond, pl.program_id(0) * step + j]
         slot = ((slot >> 1) ^ me) * 2 + (slot & 1)
         for part in range(2):
-            total_ref[part, slot] += mixed[:, part * lanes : (part + 1) * lanes]
+            columns = slice(part * lanes, (part + 1) * lanes)
+            total_ref[part, slot] += mixed[:lanes, columns] + mixed[lanes:, columns]
 
     bonds = []
     for chunk, refs_of, mix in zip(chunks, operands, mixes):

time: 135 us -> 136 us (level)
  local copies, waits for them, and re-layouts: 4.71 us -> 1.7 us
  waiting for transfers between devices: 43.3 us -> 46.1 us
  starting transfers between devices: 38.1 us -> 39.7 us
    unnamed x57 -> x65, local copies, waits for them, and re-layouts: 4.63 us -> 1.61 us
    ppermute x25, waiting for transfers between devices: 43.3 us -> 46.1 us  [partner(): return lax.ppermute(x, axis, [(i, i ^ k) for i in range(size)])]
    ppermute x25, starting transfers between devices: 38.1 us -> 39.7 us  [partner(): return lax.ppermute(x, axis, [(i, i ^ k) for i in range(size)])]
  transfers between devices with their start and end apart: 25 -> 25, of which waited for: 10 -> 11; matrix products, arithmetic and copies ran while one was open for 1% -> 0% of each run, Pallas kernels for 15% -> 14%
where the time goes in v9:
time: 136 us
  Pallas kernels  46.3 us (34%)
  waiting for transfers between devices  46.1 us (34%)
  starting transfers between devices  39.7 us (29%)
  local copies, waits for them, and re-layouts  1.7 us (1%)
    ppermute x25, waiting for transfers between devices, partner(): return lax.ppermute(x, axis, [(i, i ^ k) for i in range(size)])  46.1 us
    ppermute x25, starting transfers between devices, partner(): return lax.ppermute(x, axis, [(i, i ^ k) for i in range(size)])  39.7 us
    pallas_call x4, Pallas kernels, apply_bonds(): pl.pallas_call(functools.partial(apply_kernel, plan), grid_spec=pltpu.Pre...  31.1 us
    pallas_call x3, Pallas kernels, own_operands(): pl.pallas_call(own_operands_kernel, grid_spec=pltpu.PrefetchScalarGridSpe...  4.09 us
    pallas_call x3, Pallas kernels, cut_pieces(): pl.pallas_call(functools.partial(cut_kernel, group), grid_spec=pltpu.Pref...  3.4 us
    pallas_call x1, Pallas kernels, owner_image(): pl.pallas_call(image_kernel, grid_spec=pltpu.PrefetchScalarGridSpec(num_s...  2.77 us
  transfers between devices with their start and end apart: 25, of which 11 were waited for; matrix products, arithmetic and copies ran while one was open for 0% of the time, Pallas kernels for 14%

profile of v9, /device:TPU:0, one launch (start us, length us, event | category | flops | bytes accessed | tf_op | source)
XLA Modules:
  0.0 135.9 jit_solution(9095272933389763529)
XLA Ops:
  2.5 3.1 %collective-permute-start = (f32[2,8,16,128]{3,2,1,0:T(8,128)S(1)}, f32[2,8,16,128]{3,2,1,0:T(8,128)S(1)}, u32[]{:S(2)}, u32[]{:S(2)}) collective-permute-start(f32[2,8,16,128]{3,2,1,0:T(8,128)S(1)} %get-tuple-element.54), channel_id=1, source_target_pairs={{0,4},{4,0},{8,12},{12,8},{1,5},{5,1},{9,13},{13,9},{2,6},{6,2},{1... | collective-permute-start | bytes 393224 | tf_op jit(solution)/shard_map/ppermute | solution.py:644
  5.6 2.6 %collective-permute-start.4 = (f32[2,8,16,128]{3,2,1,0:T(8,128)S(1)}, f32[2,8,16,128]{3,2,1,0:T(8,128)S(1)}, u32[]{:S(2)}, u32[]{:S(2)}) collective-permute-start(f32[2,8,16,128]{3,2,1,0:T(8,128)S(1)} %get-tuple-element.64), channel_id=1, source_target_pairs={{0,8},{4,12},{8,0},{12,4},{1,9},{5,13},{9,1},{13,5},{2,10},{6,14},... | collective-permute-start | bytes 393224 | tf_op jit(solution)/shard_map/ppermute | solution.py:644
  8.2 2.5 %pack.1 = (bf16[8,128,1024]{2,1,0:T(8,128)(2,1)S(1)}, f32[8,128,128]{2,1,0:T(8,128)S(1)}, f32[8,128,128]{2,1,0:T(8,128)S(1)}) custom-call(s32[7]{0:T(128)S(1)} %stack.31.info_ref, f32[8,64,1024]{2,1,0:T(8,128)S(1)} %copy-done.23, f32[8,64,1024]{2,1,0:T(8,128)S(1)} %copy-done.23, f32[8,64,256]{2,1,0:T(8,128)S(1)} %copy-done.25), custom_call_target="tpu_custom_call" | custom-call | flops 5500000256 | bytes 1048576 | tf_op jit(solution)/shard_map/pack/pallas_call | solution.py:140
  13.4 5.1 %collective-permute-done.4.refs_2_ = f32[2,8,16,128]{3,2,1,0:T(8,128)S(1)} collective-permute-done((f32[2,8,16,128]{3,2,1,0:T(8,128)S(1)}, f32[2,8,16,128]{3,2,1,0:T(8,128)S(1)}, u32[]{:S(2)}, u32[]{:S(2)}) %collective-permute-start.4) | collective-permute-done | bytes 131104 | tf_op jit(solution)/shard_map/ppermute | solution.py:644
  18.6 2.9 %collective-permute-start.8 = (f32[2,8,16,128]{3,2,1,0:T(8,128)S(1)}, f32[2,8,16,128]{3,2,1,0:T(8,128)S(1)}, u32[]{:S(2)}, u32[]{:S(2)}) collective-permute-start(f32[2,8,16,128]{3,2,1,0:T(8,128)S(1)} %get-tuple-element.70), channel_id=1, source_target_pairs={{0,12},{4,8},{8,4},{12,0},{1,13},{5,9},{9,5},{13,1},{2,14},{6,10},... | collective-permute-start | bytes 393224 | tf_op jit(solution)/shard_map/ppermute | solution.py:644
  29.0 8.6 %collective-permute-start.3 = (f32[2,8,16,128]{3,2,1,0:T(8,128)S(1)}, f32[2,8,16,128]{3,2,1,0:T(8,128)S(1)}, u32[]{:S(2)}, u32[]{:S(2)}) collective-permute-start(f32[2,8,16,128]{3,2,1,0:T(8,128)S(1)} %get-tuple-element.61), channel_id=1, source_target_pairs={{0,4},{4,0},{8,12},{12,8},{1,5},{5,1},{9,13},{13,9},{2,6},{6,2},{1... | collective-permute-start | bytes 393224 | tf_op jit(solution)/shard_map/ppermute | solution.py:644
  40.5 5.5 %apply_bonds.4 = (f32[2,8,128,128]{3,2,1,0:T(8,128)S(1)}, bf16[2,8,64,128]{3,2,1,0:T(8,128)(2,1)S(1)}, bf16[2,8,64,128]{3,2,1,0:T(8,128)(2,1)S(1)}, bf16[8,64,256]{2,1,0:T(8,128)(2,1)S(1)}) custom-call(s32[7]{0:T(128)S(1)} %stack.31.info_ref, s32[6,8]{1,0:T(8,128)S(1)} %copy-done.22, s32[6,8]{1,0:T(8,128)S(1)} %collective-permute-done.1.refs_1_, ...), custom_call_target="tpu_custom_call" | custom-call | flops 1100000000 | bytes 1048576 | tf_op jit(solution)/shard_map/apply_bonds/pallas_call | solution.py:514
  49.2 5.6 %apply_bonds.5 = (f32[2,8,128,128]{3,2,1,0:T(8,128)S(1)}, bf16[2,8,64,128]{3,2,1,0:T(8,128)(2,1)S(1)}, bf16[2,8,64,128]{3,2,1,0:T(8,128)(2,1)S(1)}, bf16[8,64,256]{2,1,0:T(8,128)(2,1)S(1)}) custom-call(s32[7]{0:T(128)S(1)} %stack.31.info_ref, s32[6,8]{1,0:T(8,128)S(1)} %copy-done.22, s32[6,8]{1,0:T(8,128)S(1)} %collective-permute-done.1.refs_1_, ...), custom_call_target="tpu_custom_call" | custom-call | flops 1100000000 | bytes 1048576 | tf_op jit(solution)/shard_map/apply_bonds/pallas_call | solution.py:514
  56.2 5.7 %apply_bonds.6 = (f32[4,264,128]{2,1,0:T(8,128)S(1)}, f32[4,264,128]{2,1,0:T(8,128)S(1)}, bf16[2,8,64,128]{3,2,1,0:T(8,128)(2,1)S(1)}, bf16[2,8,64,128]{3,2,1,0:T(8,128)(2,1)S(1)}, bf16[8,64,256]{2,1,0:T(8,128)(2,1)S(1)}) custom-call(s32[7]{0:T(128)S(1)} %stack.31.info_ref, s32[6,8]{1,0:T(8,128)S(1)} %copy-done.22, ...), custom_call_target="tpu_custom_call" | custom-call | flops 1100000000 | bytes 1048576 | tf_op jit(solution)/shard_map/apply_bonds/pallas_call | solution.py:514
  62.0 1.9 %collective-permute-done.14 = f32[4,264,128]{2,1,0:T(8,128)S(1)} collective-permute-done((f32[4,264,128]{2,1,0:T(8,128)S(1)}, f32[4,264,128]{2,1,0:T(8,128)S(1)}, u32[]{:S(2)}, u32[]{:S(2)}) %collective-permute-start.14) | collective-permute-done | bytes 540704 | tf_op jit(solution)/shard_map/ppermute | solution.py:644
  64.7 5.8 %collective-permute-start.15 = (f32[264,128]{1,0:T(8,128)}, f32[264,128]{1,0:T(8,128)}, u32[]{:S(2)}, u32[]{:S(2)}) collective-permute-start(f32[264,128]{1,0:T(8,128)} %get-tuple-element.111), channel_id=1, source_target_pairs={{0,4},{4,0},{8,12},{12,8},{1,5},{5,1},{9,13},{13,9},{2,6},{6,2},{1... | collective-permute-start | bytes 405512 | tf_op jit(solution)/shard_map/ppermute | solution.py:644
  70.6 2.4 %collective-permute-start.17 = (f32[264,128]{1,0:T(8,128)}, f32[264,128]{1,0:T(8,128)}, u32[]{:S(2)}, u32[]{:S(2)}) collective-permute-start(f32[264,128]{1,0:T(8,128)} %get-tuple-element.109), channel_id=1, source_target_pairs={{0,12},{4,8},{8,4},{12,0},{1,13},{5,9},{9,5},{13,1},{2,14},{6,10},... | collective-permute-start | bytes 405512 | tf_op jit(solution)/shard_map/ppermute | solution.py:644
  73.1 2.3 %collective-permute-done.15.a1 = f32[264,128]{1,0:T(8,128)} collective-permute-done((f32[264,128]{1,0:T(8,128)}, f32[264,128]{1,0:T(8,128)}, u32[]{:S(2)}, u32[]{:S(2)}) %collective-permute-start.15) | collective-permute-done | bytes 135200 | tf_op jit(solution)/shard_map/ppermute | solution.py:644
  75.4 8.1 %collective-permute-done.16.a2 = f32[264,128]{1,0:T(8,128)} collective-permute-done((f32[264,128]{1,0:T(8,128)}, f32[264,128]{1,0:T(8,128)}, u32[]{:S(2)}, u32[]{:S(2)}) %collective-permute-start.16) | collective-permute-done | bytes 135200 | tf_op jit(solution)/shard_map/ppermute | solution.py:644
  83.6 2.8 %owner_image.1.refs_2_.refs_6_.image_ref = f32[1032,128]{1,0:T(8,128)S(1)} custom-call(s32[7]{0:T(128)S(1)} %stack.31.info_ref, s32[4,2]{1,0:T(4,128)S(1)} %copy.10.owner_ref, f32[264,128]{1,0:T(8,128)} %get-tuple-element.112.a0, f32[264,128]{1,0:T(8,128)} %collective-permute-done.15.a1, f32[264,128]{1,0:T(8,128)} %collective-permute-done.16.a2, ...), custom_call_target="tpu_custom_call" | custom-call | flops 3300000000 | bytes 1048576 | tf_op jit(solution)/shard_map/owner_image/pallas_call | solution.py:581
  86.6 12.7 %collective-permute-done.18.refs_3_.refs_7_ = f32[1032,128]{1,0:T(8,128)S(1)} collective-permute-done((f32[1032,128]{1,0:T(8,128)S(1)}, f32[1032,128]{1,0:T(8,128)S(1)}, u32[]{:S(2)}, u32[]{:S(2)}) %collective-permute-start.18) | collective-permute-done | bytes 528416 | tf_op jit(solution)/shard_map/ppermute | solution.py:644
  99.2 1.9 %collective-permute-done.20.refs_5_.refs_9_ = f32[1032,128]{1,0:T(8,128)S(1)} collective-permute-done((f32[1032,128]{1,0:T(8,128)S(1)}, f32[1032,128]{1,0:T(8,128)S(1)}, u32[]{:S(2)}, u32[]{:S(2)}) %collective-permute-start.20) | collective-permute-done | bytes 528416 | tf_op jit(solution)/shard_map/ppermute | solution.py:644
  101.3 14.4 %apply_bonds.7 = (f32[4,264,128]{2,1,0:T(8,128)S(1)}, f32[4,264,128]{2,1,0:T(8,128)S(1)}) custom-call(s32[7]{0:T(128)S(1)} %stack.31.info_ref, s32[6,8]{1,0:T(8,128)S(1)} %copy-done.22, s32[6,8]{1,0:T(8,128)S(1)} %collective-permute-done.1.refs_1_, f32[1032,128]{1,0:T(8,128)S(1)} %owner_image.1.refs_2_.refs_6_.image_ref, ...), custom_call_target="tpu_custom_call" | custom-call | flops 1100000000 | bytes 1048576 | tf_op jit(solution)/shard_map/apply_bonds/pallas_call | solution.py:514
  115.8 1.8 %collective-permute-done.21 = f32[4,264,128]{2,1,0:T(8,128)S(1)} collective-permute-done((f32[4,264,128]{2,1,0:T(8,128)S(1)}, f32[4,264,128]{2,1,0:T(8,128)S(1)}, u32[]{:S(2)}, u32[]{:S(2)}) %collective-permute-start.21) | collective-permute-done | bytes 540704 | tf_op jit(solution)/shard_map/ppermute | solution.py:644
  117.7 3.5 %collective-permute-start.22 = (f32[264,128]{1,0:T(8,128)S(1)}, f32[264,128]{1,0:T(8,128)S(1)}, u32[]{:S(2)}, u32[]{:S(2)}) collective-permute-start(f32[264,128]{1,0:T(8,128)S(1)} %get-tuple-element.107), channel_id=1, source_target_pairs={{0,4},{4,0},{8,12},{12,8},{1,5},{5,1},{9,13},{13,9},{2,6},{6,2},{1... | collective-permute-start | bytes 405512 | tf_op jit(solution)/shard_map/ppermute | solution.py:644
  121.2 2.4 %collective-permute-start.24 = (f32[264,128]{1,0:T(8,128)S(1)}, f32[264,128]{1,0:T(8,128)S(1)}, u32[]{:S(2)}, u32[]{:S(2)}) collective-permute-start(f32[264,128]{1,0:T(8,128)S(1)} %get-tuple-element.105), channel_id=1, source_target_pairs={{0,12},{4,8},{8,4},{12,0},{1,13},{5,9},{9,5},{13,1},{2,14},{6,10},... | collective-permute-start | bytes 405512 | tf_op jit(solution)/shard_map/ppermute | solution.py:644
  123.7 2.0 %collective-permute-done.22.a1 = f32[264,128]{1,0:T(8,128)S(1)} collective-permute-done((f32[264,128]{1,0:T(8,128)S(1)}, f32[264,128]{1,0:T(8,128)S(1)}, u32[]{:S(2)}, u32[]{:S(2)}) %collective-permute-start.22) | collective-permute-done | bytes 135200 | tf_op jit(solution)/shard_map/ppermute | solution.py:644
  125.6 8.1 %collective-permute-done.23.a2 = f32[264,128]{1,0:T(8,128)S(1)} collective-permute-done((f32[264,128]{1,0:T(8,128)S(1)}, f32[264,128]{1,0:T(8,128)S(1)}, u32[]{:S(2)}, u32[]{:S(2)}) %collective-permute-start.23) | collective-permute-done | bytes 135200 | tf_op jit(solution)/shard_map/ppermute | solution.py:644
  133.8 2.1 %outputs.1 = (f32[8,64,256]{2,1,0:T(8,128)}, f32[8,64,256]{2,1,0:T(8,128)}, f32[8,64,256]{2,1,0:T(8,128)}) custom-call(s32[7]{0:T(128)S(1)} %stack.31.info_ref, s32[4,2]{1,0:T(4,128)S(1)} %copy.10.owner_ref, f32[264,128]{1,0:T(8,128)S(1)} %get-tuple-element.108.a0, f32[264,128]{1,0:T(8,128)S(1)} %collective-permute-done.22.a1, ...), custom_call_target="tpu_custom_call" | custom-call | flops 4400000000 | bytes 1048576 | tf_op jit(solution)/shard_map/outputs/pallas_call | solution.py:621
  (108 shorter events, 20.8 us)
Async XLA Ops:
  2.5 10.0 %collective-permute-start = (f32[2,8,16,128]{3,2,1,0:T(8,128)S(1)}, f32[2,8,16,128]{3,2,1,0:T(8,128)S(1)}, u32[]{:S(2)}, u32[]{:S(2)}) collective-permute-start(f32[2,8,16,128]{3,2,1,0:T(8,128)S(1)} %get-tuple-element.54), channel_id=1, source_target_pairs={{0,4},{4,0},{8,12},{12,8},{1,5},{5,1},{9,13},{13,9},{2,6},{6,2},{1... | collective-permute-start | bytes 393224 | tf_op jit(solution)/shard_map/ppermute | solution.py:644
  5.6 13.0 %collective-permute-start.4 = (f32[2,8,16,128]{3,2,1,0:T(8,128)S(1)}, f32[2,8,16,128]{3,2,1,0:T(8,128)S(1)}, u32[]{:S(2)}, u32[]{:S(2)}) collective-permute-start(f32[2,8,16,128]{3,2,1,0:T(8,128)S(1)} %get-tuple-element.64), channel_id=1, source_target_pairs={{0,8},{4,12},{8,0},{12,4},{1,9},{5,13},{9,1},{13,5},{2,10},{6,14},... | collective-permute-start | bytes 393224 | tf_op jit(solution)/shard_map/ppermute | solution.py:644
  8.2 10.4 %collective-permute-start.7 = (f32[2,8,16,128]{3,2,1,0:T(8,128)S(1)}, f32[2,8,16,128]{3,2,1,0:T(8,128)S(1)}, u32[]{:S(2)}, u32[]{:S(2)}) collective-permute-start(f32[2,8,16,128]{3,2,1,0:T(8,128)S(1)} %get-tuple-element.69), channel_id=1, source_target_pairs={{0,12},{4,8},{8,4},{12,0},{1,13},{5,9},{9,5},{13,1},{2,14},{6,10},... | collective-permute-start | bytes 393224 | tf_op jit(solution)/shard_map/ppermute | solution.py:644
  12.5 16.5 %collective-permute-start.2 = (f32[2,8,16,128]{3,2,1,0:T(8,128)S(1)}, f32[2,8,16,128]{3,2,1,0:T(8,128)S(1)}, u32[]{:S(2)}, u32[]{:S(2)}) collective-permute-start(f32[2,8,16,128]{3,2,1,0:T(8,128)S(1)} %get-tuple-element.60), channel_id=1, source_target_pairs={{0,4},{4,0},{8,12},{12,8},{1,5},{5,1},{9,13},{13,9},{2,6},{6,2},{1... | collective-permute-start | bytes 393224 | tf_op jit(solution)/shard_map/ppermute | solution.py:644
  18.6 19.0 %collective-permute-start.5 = (f32[2,8,16,128]{3,2,1,0:T(8,128)S(1)}, f32[2,8,16,128]{3,2,1,0:T(8,128)S(1)}, u32[]{:S(2)}, u32[]{:S(2)}) collective-permute-start(f32[2,8,16,128]{3,2,1,0:T(8,128)S(1)} %get-tuple-element.65), channel_id=1, source_target_pairs={{0,8},{4,12},{8,0},{12,4},{1,9},{5,13},{9,1},{13,5},{2,10},{6,14},... | collective-permute-start | bytes 393224 | tf_op jit(solution)/shard_map/ppermute | solution.py:644
  18.6 9.4 %collective-permute-start.8 = (f32[2,8,16,128]{3,2,1,0:T(8,128)S(1)}, f32[2,8,16,128]{3,2,1,0:T(8,128)S(1)}, u32[]{:S(2)}, u32[]{:S(2)}) collective-permute-start(f32[2,8,16,128]{3,2,1,0:T(8,128)S(1)} %get-tuple-element.70), channel_id=1, source_target_pairs={{0,12},{4,8},{8,4},{12,0},{1,13},{5,9},{9,5},{13,1},{2,14},{6,10},... | collective-permute-start | bytes 393224 | tf_op jit(solution)/shard_map/ppermute | solution.py:644
  21.5 4.7 %collective-permute-start.11 = (f32[6,16,16]{2,1,0:T(8,128)S(1)}, f32[6,16,16]{2,1,0:T(8,128)S(1)}, u32[]{:S(2)}, u32[]{:S(2)}) collective-permute-start(f32[6,16,16]{2,1,0:T(8,128)S(1)} %copy-done.26), channel_id=1, source_target_pairs={{0,2},{2,0},{1,3},{3,1},{4,6},{6,4},{5,7},{7,5},{8,10},{10,8},{9,1... | collective-permute-start | bytes 18440 | tf_op jit(solution)/shard_map/ppermute | solution.py:644
  24.3 16.2 %collective-permute-start.10 = (f32[2,8,48,128]{3,2,1,0:T(8,128)S(1)}, f32[2,8,48,128]{3,2,1,0:T(8,128)S(1)}, u32[]{:S(2)}, u32[]{:S(2)}) collective-permute-start(f32[2,8,48,128]{3,2,1,0:T(8,128)S(1)} %get-tuple-element.77), channel_id=1, source_target_pairs={{0,2},{2,0},{1,3},{3,1},{4,6},{6,4},{5,7},{7,5},{8,10},{10,8},{9,1... | collective-permute-start | bytes 1179656 | tf_op jit(solution)/shard_map/ppermute | solution.py:644
  26.2 13.0 %collective-permute-start.1 = (s32[6,8]{1,0:T(8,128)S(1)}, s32[6,8]{1,0:T(8,128)S(1)}, u32[]{:S(2)}, u32[]{:S(2)}) collective-permute-start(s32[6,8]{1,0:T(8,128)S(1)} %copy-done.22), channel_id=1, source_target_pairs={{0,2},{2,0},{1,3},{3,1},{4,6},{6,4},{5,7},{7,5},{8,10},{10,8},{9,1... | collective-permute-start | bytes 584 | tf_op jit(solution)/shard_map/ppermute | solution.py:644
  28.0 18.0 %collective-permute-start.9 = (f32[2,8,16,128]{3,2,1,0:T(8,128)S(1)}, f32[2,8,16,128]{3,2,1,0:T(8,128)S(1)}, u32[]{:S(2)}, u32[]{:S(2)}) collective-permute-start(f32[2,8,16,128]{3,2,1,0:T(8,128)S(1)} %get-tuple-element.71), channel_id=1, source_target_pairs={{0,12},{4,8},{8,4},{12,0},{1,13},{5,9},{9,5},{13,1},{2,14},{6,10},... | collective-permute-start | bytes 393224 | tf_op jit(solution)/shard_map/ppermute | solution.py:644
  29.0 17.1 %collective-permute-start.3 = (f32[2,8,16,128]{3,2,1,0:T(8,128)S(1)}, f32[2,8,16,128]{3,2,1,0:T(8,128)S(1)}, u32[]{:S(2)}, u32[]{:S(2)}) collective-permute-start(f32[2,8,16,128]{3,2,1,0:T(8,128)S(1)} %get-tuple-element.61), channel_id=1, source_target_pairs={{0,4},{4,0},{8,12},{12,8},{1,5},{5,1},{9,13},{13,9},{2,6},{6,2},{1... | collective-permute-start | bytes 393224 | tf_op jit(solution)/shard_map/ppermute | solution.py:644
  37.6 8.5 %collective-permute-start.6 = (f32[2,8,16,128]{3,2,1,0:T(8,128)S(1)}, f32[2,8,16,128]{3,2,1,0:T(8,128)S(1)}, u32[]{:S(2)}, u32[]{:S(2)}) collective-permute-start(f32[2,8,16,128]{3,2,1,0:T(8,128)S(1)} %get-tuple-element.66), channel_id=1, source_target_pairs={{0,8},{4,12},{8,0},{12,4},{1,9},{5,13},{9,1},{13,5},{2,10},{6,14},... | collective-permute-start | bytes 393224 | tf_op jit(solution)/shard_map/ppermute | solution.py:644
  39.2 10.0 %collective-permute-start.13 = (f32[2,8,48,128]{3,2,1,0:T(8,128)S(1)}, f32[2,8,48,128]{3,2,1,0:T(8,128)S(1)}, u32[]{:S(2)}, u32[]{:S(2)}) collective-permute-start(f32[2,8,48,128]{3,2,1,0:T(8,128)S(1)} %get-tuple-element.72), channel_id=1, source_target_pairs={{0,2},{2,0},{1,3},{3,1},{4,6},{6,4},{5,7},{7,5},{8,10},{10,8},{9,1... | collective-permute-start | bytes 1179656 | tf_op jit(solution)/shard_map/ppermute | solution.py:644
  47.5 8.7 %collective-permute-start.12 = (f32[2,8,48,128]{3,2,1,0:T(8,128)S(1)}, f32[2,8,48,128]{3,2,1,0:T(8,128)S(1)}, u32[]{:S(2)}, u32[]{:S(2)}) collective-permute-start(f32[2,8,48,128]{3,2,1,0:T(8,128)S(1)} %get-tuple-element.84), channel_id=1, source_target_pairs={{0,2},{2,0},{1,3},{3,1},{4,6},{6,4},{5,7},{7,5},{8,10},{10,8},{9,1... | collective-permute-start | bytes 1179656 | tf_op jit(solution)/shard_map/ppermute | solution.py:644
  61.9 2.0 %collective-permute-start.14 = (f32[4,264,128]{2,1,0:T(8,128)S(1)}, f32[4,264,128]{2,1,0:T(8,128)S(1)}, u32[]{:S(2)}, u32[]{:S(2)}) collective-permute-start(f32[4,264,128]{2,1,0:T(8,128)S(1)} %get-tuple-element.91), channel_id=1, source_target_pairs={{0,1},{1,0},{2,3},{3,2},{4,5},{5,4},{6,7},{7,6},{8,9},{9,8},{10,11... | collective-permute-start | bytes 1622024 | tf_op jit(solution)/shard_map/ppermute | solution.py:644
  64.7 10.7 %collective-permute-start.15 = (f32[264,128]{1,0:T(8,128)}, f32[264,128]{1,0:T(8,128)}, u32[]{:S(2)}, u32[]{:S(2)}) collective-permute-start(f32[264,128]{1,0:T(8,128)} %get-tuple-element.111), channel_id=1, source_target_pairs={{0,4},{4,0},{8,12},{12,8},{1,5},{5,1},{9,13},{13,9},{2,6},{6,2},{1... | collective-permute-start | bytes 405512 | tf_op jit(solution)/shard_map/ppermute | solution.py:644
  70.6 13.0 %collective-permute-start.16 = (f32[264,128]{1,0:T(8,128)}, f32[264,128]{1,0:T(8,128)}, u32[]{:S(2)}, u32[]{:S(2)}) collective-permute-start(f32[264,128]{1,0:T(8,128)} %get-tuple-element.110), channel_id=1, source_target_pairs={{0,8},{4,12},{8,0},{12,4},{1,9},{5,13},{9,1},{13,5},{2,10},{6,14},... | collective-permute-start | bytes 405512 | tf_op jit(solution)/shard_map/ppermute | solution.py:644
  70.6 13.0 %collective-permute-start.17 = (f32[264,128]{1,0:T(8,128)}, f32[264,128]{1,0:T(8,128)}, u32[]{:S(2)}, u32[]{:S(2)}) collective-permute-start(f32[264,128]{1,0:T(8,128)} %get-tuple-element.109), channel_id=1, source_target_pairs={{0,12},{4,8},{8,4},{12,0},{1,13},{5,9},{9,5},{13,1},{2,14},{6,10},... | collective-permute-start | bytes 405512 | tf_op jit(solution)/shard_map/ppermute | solution.py:644
  86.4 12.8 %collective-permute-start.18 = (f32[1032,128]{1,0:T(8,128)S(1)}, f32[1032,128]{1,0:T(8,128)S(1)}, u32[]{:S(2)}, u32[]{:S(2)}) collective-permute-start(f32[1032,128]{1,0:T(8,128)S(1)} %owner_image.1.refs_2_.refs_6_.image_ref), channel_id=1, source_target_pairs={{0,2},{2,0},{1,3},{3,1},{4,6},{6,4},{5,7},{7,5},{8,10},{10,8},{9,1... | collective-permute-start | bytes 1585160 | tf_op jit(solution)/shard_map/ppermute | solution.py:644
  86.5 12.7 %collective-permute-start.19 = (f32[1032,128]{1,0:T(8,128)S(1)}, f32[1032,128]{1,0:T(8,128)S(1)}, u32[]{:S(2)}, u32[]{:S(2)}) collective-permute-start(f32[1032,128]{1,0:T(8,128)S(1)} %owner_image.1.refs_2_.refs_6_.image_ref), channel_id=1, source_target_pairs={{0,1},{1,0},{2,3},{3,2},{4,5},{5,4},{6,7},{7,6},{8,9},{9,8},{10,11... | collective-permute-start | bytes 1585160 | tf_op jit(solution)/shard_map/ppermute | solution.py:644
  115.6 2.0 %collective-permute-start.21 = (f32[4,264,128]{2,1,0:T(8,128)S(1)}, f32[4,264,128]{2,1,0:T(8,128)S(1)}, u32[]{:S(2)}, u32[]{:S(2)}) collective-permute-start(f32[4,264,128]{2,1,0:T(8,128)S(1)} %get-tuple-element.104), channel_id=1, source_target_pairs={{0,1},{1,0},{2,3},{3,2},{4,5},{5,4},{6,7},{7,6},{8,9},{9,8},{10,11... | collective-permute-start | bytes 1622024 | tf_op jit(solution)/shard_map/ppermute | solution.py:644
  117.7 7.9 %collective-permute-start.22 = (f32[264,128]{1,0:T(8,128)S(1)}, f32[264,128]{1,0:T(8,128)S(1)}, u32[]{:S(2)}, u32[]{:S(2)}) collective-permute-start(f32[264,128]{1,0:T(8,128)S(1)} %get-tuple-element.107), channel_id=1, source_target_pairs={{0,4},{4,0},{8,12},{12,8},{1,5},{5,1},{9,13},{13,9},{2,6},{6,2},{1... | collective-permute-start | bytes 405512 | tf_op jit(solution)/shard_map/ppermute | solution.py:644
  121.2 12.5 %collective-permute-start.23 = (f32[264,128]{1,0:T(8,128)S(1)}, f32[264,128]{1,0:T(8,128)S(1)}, u32[]{:S(2)}, u32[]{:S(2)}) collective-permute-start(f32[264,128]{1,0:T(8,128)S(1)} %get-tuple-element.106), channel_id=1, source_target_pairs={{0,8},{4,12},{8,0},{12,4},{1,9},{5,13},{9,1},{13,5},{2,10},{6,14},... | collective-permute-start | bytes 405512 | tf_op jit(solution)/shard_map/ppermute | solution.py:644
  121.2 12.5 %collective-permute-start.24 = (f32[264,128]{1,0:T(8,128)S(1)}, f32[264,128]{1,0:T(8,128)S(1)}, u32[]{:S(2)}, u32[]{:S(2)}) collective-permute-start(f32[264,128]{1,0:T(8,128)S(1)} %get-tuple-element.105), channel_id=1, source_target_pairs={{0,12},{4,8},{8,4},{12,0},{1,13},{5,9},{9,5},{13,1},{2,14},{6,10},... | collective-permute-start | bytes 405512 | tf_op jit(solution)/shard_map/ppermute | solution.py:644
  (33 other events, 356.2 us)

commit v10 on v9

--- a/solution.py
+++ b/solution.py
@@ -11,7 +11,6 @@
 SUB = 8
 PHYS = 16
 TINY = 1e-30
-GROUPS = 3
 SMALL_VMEM = 16 * 1024 * 1024
 APPLY_VMEM = 26 * 1024 * 1024
 
@@ -161,8 +160,8 @@
     )(info, wavefunction, wavefunction, diagonal)
 
 
-def mixing_kernel(*refs):
-    sources, out_ref = refs[:-1], refs[-1]
+def mixing_kernel(sizes, *refs):
+    sources, outs = refs[:2], refs[2:]
     spread = (
         lax.broadcasted_iota(jnp.int32, (PHYS, LANES), 1) // SUB
         == lax.broadcasted_iota(jnp.int32, (PHYS, LANES), 0)
@@ -170,28 +169,33 @@
     row = lax.broadcasted_iota(jnp.int32, (LANES, LANES), 0) // PHYS
     column = lax.broadcasted_iota(jnp.int32, (LANES, LANES), 1) % SUB
     same = row == column
-    at = 0
-    for source in sources:
-        for k in range(source.shape[0]):
-            high, low = split_two(source[k].T)
-            for place, term in enumerate((high, low)):
-                wide = jnp.dot(term, spread, preferred_element_type=jnp.float32)
-                tall = jnp.concatenate([wide] * SUB, axis=0)
-                tall = jnp.where(same, tall, 0.0).astype(jnp.bfloat16)
-                rows = slice(place * LANES, (place + 1) * LANES)
-                out_ref[at, rows] = jnp.concatenate([tall, tall], axis=1)
-            at += 1
-
-
-def mixing_operand(sources):
-    count = sources[0].shape[0] * len(sources)
-    return pl.pallas_call(
-        mixing_kernel,
-        out_shape=jax.ShapeDtypeStruct((count, 2 * LANES, 2 * LANES), jnp.bfloat16),
+    for n, source in enumerate(sources):
+        start = 0
+        for group, size in enumerate(sizes):
+            out_ref = outs[n * len(sizes) + group]
+            for at in range(size):
+                for place, term in enumerate(split_two(source[start + at].T)):
+                    wide = jnp.dot(term, spread, preferred_element_type=jnp.float32)
+                    tall = jnp.concatenate([wide] * SUB, axis=0)
+                    tall = jnp.where(same, tall, 0.0).astype(jnp.bfloat16)
+                    rows = slice(place * LANES, (place + 1) * LANES)
+                    out_ref[at, rows] = jnp.concatenate([tall, tall], axis=1)
+            start += size
+
+
+def mixing_operands(sources, sizes):
+    out = pl.pallas_call(
+        functools.partial(mixing_kernel, sizes),
+        out_shape=[
+            jax.ShapeDtypeStruct((size, 2 * LANES, 2 * LANES), jnp.bfloat16)
+            for _ in sources
+            for size in sizes
+        ],
         compiler_params=pltpu.CompilerParams(vmem_limit_bytes=SMALL_VMEM),
         cost_estimate=micros(2),
         name="mixing",
     )(*sources)
+    return [out[: len(sizes)], out[len(sizes) :]]
 
 
 def own_operands_kernel(info_ref, *refs):
@@ -208,8 +212,7 @@
         for w in range(per):
             for z in range(4):
                 row = pl.multiple_of((info_ref[4] ^ z) * rows, rows)
-                piece = pieces[z][w, 0, j] if z == 0 else pieces[z][w, j]
-                blocks_ref[w, j, pl.ds(row, rows), :] = piece
+                blocks_ref[w, j, pl.ds(row, rows), :] = pieces[z][w, j]
         for w in range(per):
             block = blocks_ref[w, j]
             upright_ref[w, j] = jnp.concatenate([block, block], axis=0).T
@@ -252,11 +255,11 @@
         right_out[j, wide * w : wide * (w + 1), lanes:] = low
 
 
-def operand_specs(per, step, half, lanes):
+def operand_specs(per, step, half, lanes, at=0):
     return [
-        pl.BlockSpec((per, step, half, lanes), lambda i, *_: (0, i, 0, 0)),
-        pl.BlockSpec((per, step, half, lanes), lambda i, *_: (0, i, 0, 0)),
-        pl.BlockSpec((step, per * 32, 2 * lanes), lambda i, *_: (i, 0, 0)),
+        pl.BlockSpec((per, step, half, lanes), lambda i, *_: (0, at + i, 0, 0)),
+        pl.BlockSpec((per, step, half, lanes), lambda i, *_: (0, at + i, 0, 0)),
+        pl.BlockSpec((step, per * 32, 2 * lanes), lambda i, *_: (at + i, 0, 0)),
     ]
 
 
@@ -268,12 +271,12 @@
     ]
 
 
-def cut_kernel(group, info_ref, source, *refs):
-    outs, sems = refs[:3], refs[3]
+def cut_kernel(first, info_ref, source, *refs):
+    outs, sems = refs[:4], refs[4]
     per = outs[0].shape[0]
     copies = []
-    for k in range(3):
-        part = source.at[pl.ds(group * per, per), info_ref[4] ^ (k + 1)]
+    for k in range(4):
+        part = source.at[pl.ds(first, per), info_ref[4] ^ k]
         copies.append(pltpu.make_async_copy(part, outs[k], sems.at[k]))
     for copy in copies:
         copy.start()
@@ -281,25 +284,25 @@
         copy.wait()
 
 
-def cut_pieces(info, by_owner, group, per):
+def cut_pieces(info, by_owner, first, per):
     shape = jax.ShapeDtypeStruct((per,) + by_owner.shape[2:], jnp.float32)
     return pl.pallas_call(
-        functools.partial(cut_kernel, group),
+        functools.partial(cut_kernel, first),
         grid_spec=pltpu.PrefetchScalarGridSpec(
             num_scalar_prefetch=1,
             grid=(1,),
             in_specs=[pl.BlockSpec(memory_space=pl.ANY)],
-            out_specs=[pl.BlockSpec(memory_space=pl.ANY)] * 3,
-            scratch_shapes=[pltpu.SemaphoreType.DMA((3,))],
+            out_specs=[pl.BlockSpec(memory_space=pl.ANY)] * 4,
+            scratch_shapes=[pltpu.SemaphoreType.DMA((4,))],
         ),
-        out_shape=[shape] * 3,
+        out_shape=[shape] * 4,
         compiler_params=pltpu.CompilerParams(vmem_limit_bytes=SMALL_VMEM),
         cost_estimate=micros(1),
         name="cut_pieces",
-    )(info, *(in_hbm(by_owner) if group == 0 else [by_owner]))
-
-
-def own_operands(info, by_owner, group, pieces):
+    )(info, *(in_hbm(by_owner) if first == 0 else [by_owner]))
+
+
+def own_operands(info, pieces):
     per, blocks, rows, lanes = pieces[0].shape
     half = lanes // 2
     step = 4
@@ -308,12 +311,7 @@
         grid_spec=pltpu.PrefetchScalarGridSpec(
             num_scalar_prefetch=1,
             grid=(blocks // step,),
-            in_specs=[
-                pl.BlockSpec(
-                    (per, 1, step, rows, lanes), lambda i, info: (group, info[4], i, 0, 0)
-                )
-            ]
-            + [pl.BlockSpec((per, step, rows, lanes), lambda i, *_: (0, i, 0, 0))] * 3,
+            in_specs=[pl.BlockSpec((per, step, rows, lanes), lambda i, *_: (0, i, 0, 0))] * 4,
             out_specs=operand_specs(per, step, half, lanes)
             + [pl.BlockSpec((per, step, 3 * rows, lanes), lambda i, *_: (0, i, 0, 0))],
             scratch_shapes=[
@@ -324,18 +322,18 @@
         out_shape=operand_shapes(per, blocks, half, lanes)
         + [jax.ShapeDtypeStruct((per, blocks, 3 * rows, lanes), jnp.float32)],
         compiler_params=pltpu.CompilerParams(vmem_limit_bytes=SMALL_VMEM),
-        cost_estimate=micros(6),
+        cost_estimate=micros(12),
         name="own_operands",
-    )(info, by_owner, *pieces)
+    )(info, *pieces)
 
 
 def apply_kernel(plan, info_ref, *refs):
-    chunks, parts_given, sent_given, before_given, pieces = plan
+    chunks, first_block, parts_given, sent_given, before_given, pieces = plan
     refs = list(refs)
     take = lambda n: [refs.pop(0) for _ in range(n)]
     slots = take(2)
     vector = take(4 if parts_given else 1)
-    tiles = take(4) if parts_given else []
+    tiles = take(4) if parts_given and pieces else []
     operands = [take(3) for _ in chunks[: -1 if sent_given else None]]
     sent = take(1)[0] if sent_given else None
     mixes = take(len(chunks))
@@ -412,18 +410,16 @@
         )
 
     def add_up(j, table, bond, mixed):
-        slot = table[bond, pl.program_id(0) * step + j]
+        slot = table[bond, first_block + pl.program_id(0) * step + j]
         slot = ((slot >> 1) ^ me) * 2 + (slot & 1)
         for part in range(2):
             columns = slice(part * lanes, (part + 1) * lanes)
             total_ref[part, slot] += mixed[:lanes, columns] + mixed[lanes:, columns]
 
     bonds = []
-    for chunk, refs_of, mix in zip(chunks, operands, mixes):
-        count = mix.shape[0]
-        source, group = chunk // GROUPS, chunk % GROUPS
-        for w in range(count):
-            bonds.append((refs_of, mix, w, slots[source], group * count + w))
+    for (source, start), refs_of, mix in zip(chunks, operands, mixes):
+        for w in range(mix.shape[0]):
+            bonds.append((refs_of, mix, w, slots[source], start + w))
     right_side(0)
     units = [(j, at) for j in range(step) for at in range(len(bonds))]
 
@@ -458,7 +454,7 @@
             total_ref[...] += prior[...]
         if pieces:
             stats = jnp.zeros((SUB, lanes), jnp.float32)
-            if parts_given:
+            if tiles:
                 stats = stacked_rows(*merged([tile[...] for tile in tiles]))
             for out, part in ((outs[0], info_ref[5]), (outs[1], 1 - info_ref[5])):
                 for k in range(4):
@@ -470,35 +466,37 @@
             outs[0][...] = total_ref[...]
 
 
-def apply_bonds(info, slots, vector, chunks, operands, sent, mixing, before, pieces):
-    count, blocks, half, lanes = operands[0][0].shape
+def apply_bonds(info, slots, vector, chunks, operands, sent, mixes, before, pieces, half_of=None):
+    blocks, half, lanes = operands[0][0].shape[1:]
     step = 4
-    parts_given = len(vector) == 4
+    parts_given = half_of is not None
+    at = half_of or 0
     if parts_given:
-        last = vector[0].shape[0] // SUB - 1
-        in_specs = [pl.BlockSpec((step * lanes, lanes), lambda i, *_: (i, 0))] * 4
-        in_specs += [pl.BlockSpec((SUB, lanes), lambda i, *_: (last, 0))] * 4
+        in_specs = [whole(step * lanes, lanes)] * 4
+        arguments = list(vector)
+        if pieces:
+            last = vector[0].shape[0] // SUB - 1
+            in_specs += [pl.BlockSpec((SUB, lanes), lambda i, *_: (last, 0))] * 4
+            arguments += list(vector)
     else:
-        in_specs = [pl.BlockSpec((step,) + vector[0].shape[1:], lambda i, *_: (i, 0, 0))]
-    arguments = list(vector) * (2 if parts_given else 1)
+        in_specs = [pl.BlockSpec((step,) + vector.shape[1:], lambda i, *_: (i, 0, 0))]
+        arguments = [vector]
     for made in operands:
-        in_specs += operand_specs(count, step, half, lanes)
+        in_specs += operand_specs(made[0].shape[0], step, half, lanes, at)
         arguments += made
+    counts = [mix.shape[0] for mix in mixes]
     if sent is not None:
         in_specs.append(
-            pl.BlockSpec((count, step) + sent.shape[2:], lambda i, *_: (0, i, 0, 0))
+            pl.BlockSpec((counts[-1], step) + sent.shape[2:], lambda i, *_: (0, i, 0, 0))
         )
         arguments.append(sent)
-    for chunk in chunks:
-        in_specs.append(
-            pl.BlockSpec((count,) + mixing.shape[1:], lambda i, *_, at=chunk: (at, 0, 0))
-        )
-        arguments.append(mixing)
-    total = count * len(chunks)
+    for mix in mixes:
+        in_specs.append(whole(*mix.shape))
+        arguments.append(mix)
     scratch = [
         pltpu.VMEM((2, 8, lanes, lanes), jnp.float32),
         pltpu.VMEM((step, lanes, PHYS * half), jnp.bfloat16),
-        pltpu.VMEM((step, total * 32, PHYS * half), jnp.float32),
+        pltpu.VMEM((step, sum(counts) * 32, PHYS * half), jnp.float32),
     ]
     if before is not None:
         in_specs.append(pl.BlockSpec(memory_space=pl.ANY))
@@ -508,21 +506,23 @@
     out_specs = [whole(*shape) for shape in shapes]
     out_shape = [jax.ShapeDtypeStruct(shape, jnp.float32) for shape in shapes]
     if sent is not None:
-        out_specs += operand_specs(count, step, half, lanes)
-        out_shape += operand_shapes(count, blocks, half, lanes)
-    plan = (tuple(chunks), parts_given, sent is not None, before is not None, pieces)
+        out_specs += operand_specs(counts[-1], step, half, lanes)
+        out_shape += operand_shapes(counts[-1], blocks, half, lanes)
+    plan = (
+        tuple(chunks), at * step, parts_given, sent is not None, before is not None, pieces,
+    )
     out = pl.pallas_call(
         functools.partial(apply_kernel, plan),
         grid_spec=pltpu.PrefetchScalarGridSpec(
             num_scalar_prefetch=3,
-            grid=(blocks // step,),
+            grid=(1 if parts_given else blocks // step,),
             in_specs=in_specs,
             out_specs=out_specs,
             scratch_shapes=scratch,
         ),
         out_shape=out_shape,
         compiler_params=pltpu.CompilerParams(vmem_limit_bytes=APPLY_VMEM),
-        cost_estimate=micros(1),
+        cost_estimate=micros(10 if parts_given else 1),
         name="apply_bonds",
     )(info, *slots, *arguments)
     return out[: len(shapes)], out[len(shapes) :]
@@ -555,7 +555,9 @@
     return cross, square, rest
 
 
-def image_kernel(info_ref, owner_ref, a0, a1, a2, a3, diag_ref, own_ref, image_ref, total):
+def image_kernel(
+    info_ref, owner_ref, a0, a1, a2, a3, diag_ref, own_ref, lower_ref, upper_ref, total
+):
     total[...] = diag_ref[...] * own_ref[...]
     add_arrived(info_ref, owner_ref, (a0, a1, a2, a3), total)
     blocks = total.shape[0]
@@ -563,7 +565,9 @@
     square = jnp.zeros((LANES, LANES), jnp.float32)
     for k in range(blocks):
         own, image = own_ref[k], total[k]
-        image_ref[k * LANES : (k + 1) * LANES] = image
+        half = lower_ref if k < blocks // 2 else upper_ref
+        at = k % (blocks // 2) * LANES
+        half[at : at + LANES] = image
         cross += own * image
         square += own * own
     cross = jnp.sum(cross, keepdims=True)
@@ -573,21 +577,22 @@
     for k in range(blocks):
         apart = total[k] - ratio * own_ref[k]
         rest += apart * apart
-    image_ref[blocks * LANES :] = stacked_rows(cross, square, jnp.sum(rest, keepdims=True))
+    upper_ref[blocks // 2 * LANES :] = stacked_rows(cross, square, jnp.sum(rest, keepdims=True))
 
 
 def owner_image(info, owners, arrived, diagonal, own):
-    rows = own.shape[0] * LANES + SUB
+    rows = own.shape[0] // 2 * LANES
+    shapes = [jax.ShapeDtypeStruct((n, LANES), jnp.float32) for n in (rows, rows + SUB)]
     return pl.pallas_call(
         image_kernel,
         grid_spec=pltpu.PrefetchScalarGridSpec(
             num_scalar_prefetch=2,
             grid=(1,),
             in_specs=[whole(*x.shape) for x in (*arrived, diagonal, own)],
-            out_specs=whole(rows, LANES),
+            out_specs=[whole(*x.shape) for x in shapes],
             scratch_shapes=[pltpu.VMEM(own.shape, jnp.float32)],
         ),
-        out_shape=jax.ShapeDtypeStruct((rows, LANES), jnp.float32),
+        out_shape=shapes,
         compiler_params=pltpu.CompilerParams(vmem_limit_bytes=SMALL_VMEM),
         cost_estimate=micros(3),
         name="owner_image",
@@ -595,8 +600,8 @@
 
 
 def final_kernel(
-    entries, info_ref, owner_ref, a0, a1, a2, a3, diag_ref, own_ref, image_ref, first_ref,
-    vector_ref, second_ref, total,
+    entries, info_ref, owner_ref, a0, a1, a2, a3, diag_ref, own_ref, lower_ref, upper_ref,
+    first_ref, vector_ref, second_ref, total,
 ):
     arrived = (a0, a1, a2, a3)
     cross, square, rest = merged([ref[2 * LANES :] for ref in arrived])
@@ -606,7 +611,8 @@
     mean = scale * scale * ((rest + apart * apart) / entries)
     second_scale = scale * lax.rsqrt(mean + 1e-06)
     for k in range(total.shape[0]):
-        image = image_ref[k * LANES : (k + 1) * LANES]
+        at = k % (total.shape[0] // 2) * LANES
+        image = (lower_ref if k < total.shape[0] // 2 else upper_ref)[at : at + LANES]
         total[k] = (diag_ref[k] - rayleigh) * image
         first_ref[k] = unpack_tile(scale * image)
         vector_ref[k] = unpack_tile(second_scale * (image - rayleigh * own_ref[k]))
@@ -615,7 +621,7 @@
         second_ref[k] = unpack_tile(second_scale * total[k])
 
 
-def outputs(info, owners, arrived, diagonal, own, image, entries):
+def outputs(info, owners, arrived, diagonal, own, images, entries):
     blocks = diagonal.shape[0]
     shape = (blocks, LANES // 2, 2 * LANES)
     return pl.pallas_call(
@@ -624,7 +630,7 @@
             num_scalar_prefetch=2,
             grid=(1,),
             in_specs=[whole(*x.shape) for x in (*arrived, diagonal, own)]
-            + [whole(blocks * LANES, LANES)],
+            + [whole(blocks // 2 * LANES, LANES)] * 2,
             out_specs=[whole(*shape)] * 3,
             scratch_shapes=[pltpu.VMEM(diagonal.shape, jnp.float32)],
         ),
@@ -632,7 +638,7 @@
         compiler_params=pltpu.CompilerParams(vmem_limit_bytes=SMALL_VMEM),
         cost_estimate=micros(4),
         name="outputs",
-    )(info, owners, *arrived, diagonal, own, image)
+    )(info, owners, *arrived, diagonal, own, *images)
 
 
 def in_hbm(*arrays):
@@ -670,21 +676,22 @@
     place = 2 * mpo + rep
     info = jnp.stack([place, place ^ 2, place ^ 1, place ^ 3, blk, rep, mpo]).astype(jnp.int32)
     bonds = environment.shape[0]
-    per = bonds // GROUPS
+    sizes = tuple(bonds * part // 6 for part in (2, 2, 1, 1))
+    firsts = tuple(sum(sizes[:group]) for group in range(len(sizes)))
     entries = float(blocks * zs * rows * width)
 
     vector, own, diagonal_packed = pack(info, wavefunction, diagonal)
 
     by_owner = environment.reshape(bonds, zs, blocks, rows // zs, 2 * rows)
     pieces = []
-    for group in range(GROUPS):
-        cuts = cut_pieces(info, by_owner, group, per)
+    for group in range(len(sizes)):
+        cuts = list(cut_pieces(info, by_owner, firsts[group], sizes[group]))
         if group:
-            cuts = [after(x, y) for x, y in zip(cuts, pieces[-1][1:])]
-        pieces.append([None] + [partner(x, "blk", k + 1) for k, x in enumerate(cuts)])
+            cuts[1:] = [after(x, y) for x, y in zip(cuts[1:], pieces[-1][1:])]
+        pieces.append(cuts[:1] + [partner(cuts[k], "blk", k) for k in range(1, 4)])
     pieces[0][1] = after(pieces[0][1], vector)
     other_terms = partner(after(bond_terms, pieces[0][1]), "mpo", 1)
-    mixing = mixing_operand([bond_terms, other_terms])
+    mixing = mixing_operands([bond_terms, other_terms], sizes)
     slots = [term_slot, partner(after(term_slot, pieces[0][1]), "mpo", 1)]
 
     made, sent = [], []
@@ -693,30 +700,43 @@
     done = 0
 
     def apply_group(group, vector):
-        last = group == GROUPS - 1
         out, other = apply_bonds(
-            info, slots, [vector], [group, GROUPS + group], [made[group]],
-            partner(sent[group], "mpo", 1), mixing, total, last,
+            info, slots, vector, [(0, firsts[group]), (1, firsts[group])], [made[group]],
+            partner(sent[group], "mpo", 1), [terms[group] for terms in mixing], total,
+            group == len(sizes) - 1,
         )
         operands.extend([made[group], other])
         return out
 
-    for group in range(GROUPS):
+    for group in range(len(sizes)):
         if group >= 2:
             total = apply_group(group - 2, after(vector, sent[group - 1]))[0]
             pieces[group][3] = after(pieces[group][3], total)
-        *own_set, send = own_operands(info, by_owner, group, pieces[group][1:])
+        if group + 1 < len(sizes):
+            pieces[group][1] = after(pieces[group][1], pieces[group + 1][1])
+        *own_set, send = own_operands(info, pieces[group])
         made.append(own_set)
         sent.append(send)
-    total = apply_group(GROUPS - 2, after(vector, sent[-1]))[0]
-    out = apply_group(GROUPS - 1, vector)
-    image = owner_image(info, slot_block, to_owners(*out), diagonal_packed, own)
-
-    parts = gathered(image)
-    chunks = [group + GROUPS * source for group in range(GROUPS) for source in range(2)]
-    out, _ = apply_bonds(info, slots, parts, chunks, operands, None, mixing, None, True)
+    total = apply_group(len(sizes) - 2, after(vector, sent[-1]))[0]
+    out = apply_group(len(sizes) - 1, vector)
+    lower, upper = owner_image(info, slot_block, to_owners(*out), diagonal_packed, own)
+
+    chunks = [(source, first) for first in firsts for source in range(2)]
+    mixes = [mixing[source][group] for group in range(len(sizes)) for source in range(2)]
+    lower_parts = gathered(lower)
+    across = partner(after(upper, lower_parts[1]), "mpo", 1)
+    out, _ = apply_bonds(
+        info, slots, lower_parts, chunks, operands, None, mixes, None, False, 0
+    )
+    upper_parts = [upper, across, partner(upper, "rep", 1)]
+    upper_parts.append(partner(after(across, out[0]), "rep", 1))
+    out, _ = apply_bonds(
+        info, slots, upper_parts, chunks, operands, None, mixes, out[0], True, 1
+    )
     return tuple(
-        outputs(info, slot_block, to_owners(*out), diagonal_packed, own, image, entries)
+        outputs(
+            info, slot_block, to_owners(*out), diagonal_packed, own, (lower, upper), entries
+        )
     )
 
 

time: 136 us -> 135 us (level)
  waiting for transfers between devices: 46.1 us -> 38 us
  Pallas kernels: 46.3 us -> 52.6 us
    ppermute x25 -> x32, waiting for transfers between devices: 46.1 us -> 38 us  [partner(): return lax.ppermute(x, axis, [(i, i ^ k) for i in range(size)])]
    pallas_call x4 -> x6, Pallas kernels: 31.1 us -> 35.7 us  [apply_bonds(): pl.pallas_call(functools.partial(apply_kernel, plan), grid_spec=pltpu.Pre...]
    pallas_call x4 -> x5, Pallas kernels: 3.7 us -> 4.89 us  [the longest x4 4.58 us: cut_pieces(): pl.pallas_call(functools.partial(cut_kernel, first), grid_spec=pltpu.Pref...]
    ppermute x25 -> x32, starting transfers between devices: 39.7 us -> 40.6 us  [partner(): return lax.ppermute(x, axis, [(i, i ^ k) for i in range(size)])]
    pallas_call x3 -> x4, Pallas kernels: 4.09 us -> 4.69 us  [own_operands(): pl.pallas_call(own_operands_kernel, grid_spec=pltpu.PrefetchScalarGridSpe...]
  transfers between devices with their start and end apart: 25 -> 32, of which waited for: 11 -> 12; matrix products, arithmetic and copies ran while one was open for 0% -> 0% of each run, Pallas kernels for 14% -> 25%
where the time goes in v10:
time: 135 us
  Pallas kernels  52.6 us (39%)
  starting transfers between devices  40.6 us (30%)
  waiting for transfers between devices  38 us (28%)
  between operations  1.48 us (1%)
    ppermute x32, starting transfers between devices, partner(): return lax.ppermute(x, axis, [(i, i ^ k) for i in range(size)])  40.6 us
    ppermute x32, waiting for transfers between devices, partner(): return lax.ppermute(x, axis, [(i, i ^ k) for i in range(size)])  38 us
    pallas_call x6, Pallas kernels, apply_bonds(): pl.pallas_call(functools.partial(apply_kernel, plan), grid_spec=pltpu.Pre...  35.7 us
    pallas_call x4, Pallas kernels, own_operands(): pl.pallas_call(own_operands_kernel, grid_spec=pltpu.PrefetchScalarGridSpe...  4.69 us
    pallas_call x4, Pallas kernels, cut_pieces(): pl.pallas_call(functools.partial(cut_kernel, first), grid_spec=pltpu.Pref...  4.58 us
    pallas_call x1, Pallas kernels, owner_image(): pl.pallas_call(image_kernel, grid_spec=pltpu.PrefetchScalarGridSpec(num_s...  2.71 us
  transfers between devices with their start and end apart: 32, of which 12 were waited for; matrix products, arithmetic and copies ran while one was open for 0% of the time, Pallas kernels for 25%

profile of v10, /device:TPU:0, one launch (start us, length us, event | category | flops | bytes accessed | tf_op | source)
XLA Modules:
  0.0 134.7 jit_solution(13267143314409065861)
XLA Ops:
  2.6 3.1 %collective-permute-start = (f32[2,8,16,128]{3,2,1,0:T(8,128)S(1)}, f32[2,8,16,128]{3,2,1,0:T(8,128)S(1)}, u32[]{:S(2)}, u32[]{:S(2)}) collective-permute-start(f32[2,8,16,128]{3,2,1,0:T(8,128)S(1)} %get-tuple-element.89), channel_id=1, source_target_pairs={{0,4},{4,0},{8,12},{12,8},{1,5},{5,1},{9,13},{13,9},{2,6},{6,2},{1... | collective-permute-start | bytes 393224 | tf_op jit(solution)/shard_map/ppermute | solution.py:650
  5.6 2.6 %collective-permute-start.5 = (f32[2,8,16,128]{3,2,1,0:T(8,128)S(1)}, f32[2,8,16,128]{3,2,1,0:T(8,128)S(1)}, u32[]{:S(2)}, u32[]{:S(2)}) collective-permute-start(f32[2,8,16,128]{3,2,1,0:T(8,128)S(1)} %get-tuple-element.103), channel_id=1, source_target_pairs={{0,8},{4,12},{8,0},{12,4},{1,9},{5,13},{9,1},{13,5},{2,10},{6,14},... | collective-permute-start | bytes 393224 | tf_op jit(solution)/shard_map/ppermute | solution.py:650
  8.2 2.5 %pack.1 = (bf16[8,128,1024]{2,1,0:T(8,128)(2,1)S(1)}, f32[8,128,128]{2,1,0:T(8,128)S(1)}, f32[8,128,128]{2,1,0:T(8,128)S(1)}) custom-call(s32[7]{0:T(128)S(1)} %stack.31.info_ref, f32[8,64,1024]{2,1,0:T(8,128)S(1)} %copy-done.1, f32[8,64,1024]{2,1,0:T(8,128)S(1)} %copy-done.1, f32[8,64,256]{2,1,0:T(8,128)S(1)} %copy-done.3), custom_call_target="tpu_custom_call" | custom-call | flops 5500000256 | bytes 1048576 | tf_op jit(solution)/shard_map/pack/pallas_call | solution.py:139
  17.0 2.9 %collective-permute-start.10 = (f32[2,8,16,128]{3,2,1,0:T(8,128)S(1)}, f32[2,8,16,128]{3,2,1,0:T(8,128)S(1)}, u32[]{:S(2)}, u32[]{:S(2)}) collective-permute-start(f32[2,8,16,128]{3,2,1,0:T(8,128)S(1)} %get-tuple-element.111), channel_id=1, source_target_pairs={{0,12},{4,8},{8,4},{12,0},{1,13},{5,9},{9,5},{13,1},{2,14},{6,10},... | collective-permute-start | bytes 393224 | tf_op jit(solution)/shard_map/ppermute | solution.py:650
  20.0 2.0 %collective-permute-start.6 = (f32[2,8,16,128]{3,2,1,0:T(8,128)S(1)}, f32[2,8,16,128]{3,2,1,0:T(8,128)S(1)}, u32[]{:S(2)}, u32[]{:S(2)}) collective-permute-start(f32[2,8,16,128]{3,2,1,0:T(8,128)S(1)} %get-tuple-element.104), channel_id=1, source_target_pairs={{0,8},{4,12},{8,0},{12,4},{1,9},{5,13},{9,1},{13,5},{2,10},{6,14},... | collective-permute-start | bytes 393224 | tf_op jit(solution)/shard_map/ppermute | solution.py:650
  26.5 2.5 %collective-permute-start.11 = (f32[1,8,16,128]{3,2,1,0:T(8,128)S(1)}, f32[1,8,16,128]{3,2,1,0:T(8,128)S(1)}, u32[]{:S(2)}, u32[]{:S(2)}) collective-permute-start(f32[1,8,16,128]{3,2,1,0:T(8,128)S(1)} %get-tuple-element.112), channel_id=1, source_target_pairs={{0,12},{4,8},{8,4},{12,0},{1,13},{5,9},{9,5},{13,1},{2,14},{6,10},... | collective-permute-start | bytes 196616 | tf_op jit(solution)/shard_map/ppermute | solution.py:650
  29.1 5.1 %collective-permute-done.6.refs_2_ = f32[2,8,16,128]{3,2,1,0:T(8,128)S(1)} collective-permute-done((f32[2,8,16,128]{3,2,1,0:T(8,128)S(1)}, f32[2,8,16,128]{3,2,1,0:T(8,128)S(1)}, u32[]{:S(2)}, u32[]{:S(2)}) %collective-permute-start.6) | collective-permute-done | bytes 131104 | tf_op jit(solution)/shard_map/ppermute | solution.py:650
  34.2 3.6 %collective-permute-start.4 = (f32[1,8,16,128]{3,2,1,0:T(8,128)S(1)}, f32[1,8,16,128]{3,2,1,0:T(8,128)S(1)}, u32[]{:S(2)}, u32[]{:S(2)}) collective-permute-start(f32[1,8,16,128]{3,2,1,0:T(8,128)S(1)} %get-tuple-element.99), channel_id=1, source_target_pairs={{0,4},{4,0},{8,12},{12,8},{1,5},{5,1},{9,13},{13,9},{2,6},{6,2},{1... | collective-permute-start | bytes 196616 | tf_op jit(solution)/shard_map/ppermute | solution.py:650
  40.2 2.9 %collective-permute-start.12 = (f32[1,8,16,128]{3,2,1,0:T(8,128)S(1)}, f32[1,8,16,128]{3,2,1,0:T(8,128)S(1)}, u32[]{:S(2)}, u32[]{:S(2)}) collective-permute-start(f32[1,8,16,128]{3,2,1,0:T(8,128)S(1)} %get-tuple-element.113), channel_id=1, source_target_pairs={{0,12},{4,8},{8,4},{12,0},{1,13},{5,9},{9,5},{13,1},{2,14},{6,10},... | collective-permute-start | bytes 196616 | tf_op jit(solution)/shard_map/ppermute | solution.py:650
  43.2 5.6 %apply_bonds.6 = (f32[2,8,128,128]{3,2,1,0:T(8,128)S(1)}, bf16[2,8,64,128]{3,2,1,0:T(8,128)(2,1)S(1)}, bf16[2,8,64,128]{3,2,1,0:T(8,128)(2,1)S(1)}, bf16[8,64,256]{2,1,0:T(8,128)(2,1)S(1)}) custom-call(s32[7]{0:T(128)S(1)} %stack.31.info_ref, s32[6,8]{1,0:T(8,128)S(1)} %copy-done, s32[6,8]{1,0:T(8,128)S(1)} %collective-permute-done.1.refs_1_, ...), custom_call_target="tpu_custom_call" | custom-call | flops 1100000000 | bytes 1048576 | tf_op jit(solution)/shard_map/apply_bonds/pallas_call | solution.py:514
  49.9 5.6 %apply_bonds.7 = (f32[2,8,128,128]{3,2,1,0:T(8,128)S(1)}, bf16[2,8,64,128]{3,2,1,0:T(8,128)(2,1)S(1)}, bf16[2,8,64,128]{3,2,1,0:T(8,128)(2,1)S(1)}, bf16[8,64,256]{2,1,0:T(8,128)(2,1)S(1)}) custom-call(s32[7]{0:T(128)S(1)} %stack.31.info_ref, s32[6,8]{1,0:T(8,128)S(1)} %copy-done, s32[6,8]{1,0:T(8,128)S(1)} %collective-permute-done.1.refs_1_, ...), custom_call_target="tpu_custom_call" | custom-call | flops 1100000000 | bytes 1048576 | tf_op jit(solution)/shard_map/apply_bonds/pallas_call | solution.py:514
  56.6 2.1 %collective-permute-start.16 = (f32[1,8,48,128]{3,2,1,0:T(8,128)S(1)}, f32[1,8,48,128]{3,2,1,0:T(8,128)S(1)}, u32[]{:S(2)}, u32[]{:S(2)}) collective-permute-start(f32[1,8,48,128]{3,2,1,0:T(8,128)S(1)} %get-tuple-element.143), channel_id=1, source_target_pairs={{0,2},{2,0},{1,3},{3,1},{4,6},{6,4},{5,7},{7,5},{8,10},{10,8},{9,1... | collective-permute-start | bytes 589832 | tf_op jit(solution)/shard_map/ppermute | solution.py:650
  58.7 4.2 %apply_bonds.8 = (f32[2,8,128,128]{3,2,1,0:T(8,128)S(1)}, bf16[1,8,64,128]{3,2,1,0:T(8,128)(2,1)S(1)}, bf16[1,8,64,128]{3,2,1,0:T(8,128)(2,1)S(1)}, bf16[8,32,256]{2,1,0:T(8,128)(2,1)S(1)}) custom-call(s32[7]{0:T(128)S(1)} %stack.31.info_ref, s32[6,8]{1,0:T(8,128)S(1)} %copy-done, s32[6,8]{1,0:T(8,128)S(1)} %collective-permute-done.1.refs_1_, ...), custom_call_target="tpu_custom_call" | custom-call | flops 1100000000 | bytes 1048576 | tf_op jit(solution)/shard_map/apply_bonds/pallas_call | solution.py:514
  63.0 4.4 %apply_bonds.9 = (f32[4,264,128]{2,1,0:T(8,128)S(1)}, f32[4,264,128]{2,1,0:T(8,128)S(1)}, bf16[1,8,64,128]{3,2,1,0:T(8,128)(2,1)S(1)}, bf16[1,8,64,128]{3,2,1,0:T(8,128)(2,1)S(1)}, bf16[8,32,256]{2,1,0:T(8,128)(2,1)S(1)}) custom-call(s32[7]{0:T(128)S(1)} %stack.31.info_ref, s32[6,8]{1,0:T(8,128)S(1)} %copy-done, s32[6,8]{1,0:T(8,128)S(1)} %collective-permute-done.1.refs_1_, ...), custom_call_target="tpu_custom_call" | custom-call | flops 1100000000 | bytes 1048576 | tf_op jit(solution)/shard_map/apply_bonds/pallas_call | solution.py:514
  74.9 3.4 %collective-permute-done.19.a1 = f32[264,128]{1,0:T(8,128)S(1)} collective-permute-done((f32[264,128]{1,0:T(8,128)}, f32[264,128]{1,0:T(8,128)S(1)}, u32[]{:S(2)}, u32[]{:S(2)}) %collective-permute-start.19) | collective-permute-done | bytes 135200 | tf_op jit(solution)/shard_map/ppermute | solution.py:650
  78.3 7.3 %collective-permute-done.20.a2 = f32[264,128]{1,0:T(8,128)S(1)} collective-permute-done((f32[264,128]{1,0:T(8,128)}, f32[264,128]{1,0:T(8,128)S(1)}, u32[]{:S(2)}, u32[]{:S(2)}) %collective-permute-start.20) | collective-permute-done | bytes 135200 | tf_op jit(solution)/shard_map/ppermute | solution.py:650
  85.8 2.7 %owner_image.1 = (f32[512,128]{1,0:T(8,128)S(1)}, f32[520,128]{1,0:T(8,128)S(1)}) custom-call(s32[7]{0:T(128)S(1)} %stack.31.info_ref, s32[4,2]{1,0:T(4,128)S(1)} %copy.10.owner_ref, f32[264,128]{1,0:T(8,128)} %get-tuple-element.182.a0, f32[264,128]{1,0:T(8,128)S(1)} %collective-permute-done.19.a1, f32[264,128]{1,0:T(8,128)S(1)} %collective-permute-done.20.a2, ...), custom_call_target="tpu_custom_call" | custom-call | flops 3300000000 | bytes 1048576 | tf_op jit(solution)/shard_map/owner_image/pallas_call | solution.py:586
  89.5 5.4 %collective-permute-done.22.refs_3_ = f32[512,128]{1,0:T(8,128)S(1)} collective-permute-done((f32[512,128]{1,0:T(8,128)S(1)}, f32[512,128]{1,0:T(8,128)S(1)}, u32[]{:S(2)}, u32[]{:S(2)}) %collective-permute-start.22) | collective-permute-done | bytes 262176 | tf_op jit(solution)/shard_map/ppermute | solution.py:650
  96.9 7.7 %apply_bonds.10.refs_42_ = f32[2,8,128,128]{3,2,1,0:T(8,128)S(1)} custom-call(s32[7]{0:T(128)S(1)} %stack.31.info_ref, s32[6,8]{1,0:T(8,128)S(1)} %copy-done, s32[6,8]{1,0:T(8,128)S(1)} %collective-permute-done.1.refs_1_, f32[512,128]{1,0:T(8,128)S(1)} %get-tuple-element.158.refs_2_.lower_ref, f32[512,128]{1,0:T(8,128)S(1)} %collective-permute-done.22.refs_3_, ...), custom_call_target="tpu_custom_call" | custom-call | flops 11000000512 | bytes 1048576 | tf_op jit(solution)/shard_map/apply_bonds/pallas_call | solution.py:514
  106.3 8.2 %apply_bonds.11 = (f32[4,264,128]{2,1,0:T(8,128)S(1)}, f32[4,264,128]{2,1,0:T(8,128)S(1)}) custom-call(s32[7]{0:T(128)S(1)} %stack.31.info_ref, s32[6,8]{1,0:T(8,128)S(1)} %copy-done, s32[6,8]{1,0:T(8,128)S(1)} %collective-permute-done.1.refs_1_, f32[520,128]{1,0:T(8,128)S(1)} %get-tuple-element.159.refs_2_.refs_6_.upper_ref, ...), custom_call_target="tpu_custom_call" | custom-call | flops 11000000512 | bytes 1048576 | tf_op jit(solution)/shard_map/apply_bonds/pallas_call | solution.py:514
  116.5 3.0 %collective-permute-start.29 = (f32[264,128]{1,0:T(8,128)S(1)}, f32[264,128]{1,0:T(8,128)S(1)}, u32[]{:S(2)}, u32[]{:S(2)}) collective-permute-start(f32[264,128]{1,0:T(8,128)S(1)} %get-tuple-element.177), channel_id=1, source_target_pairs={{0,4},{4,0},{8,12},{12,8},{1,5},{5,1},{9,13},{13,9},{2,6},{6,2},{1... | collective-permute-start | bytes 405512 | tf_op jit(solution)/shard_map/ppermute | solution.py:650
  122.7 3.0 %collective-permute-done.29.a1 = f32[264,128]{1,0:T(8,128)S(1)} collective-permute-done((f32[264,128]{1,0:T(8,128)S(1)}, f32[264,128]{1,0:T(8,128)S(1)}, u32[]{:S(2)}, u32[]{:S(2)}) %collective-permute-start.29) | collective-permute-done | bytes 135200 | tf_op jit(solution)/shard_map/ppermute | solution.py:650
  125.7 6.9 %collective-permute-done.30.a2 = f32[264,128]{1,0:T(8,128)S(1)} collective-permute-done((f32[264,128]{1,0:T(8,128)S(1)}, f32[264,128]{1,0:T(8,128)S(1)}, u32[]{:S(2)}, u32[]{:S(2)}) %collective-permute-start.30) | collective-permute-done | bytes 135200 | tf_op jit(solution)/shard_map/ppermute | solution.py:650
  132.7 2.1 %outputs.1 = (f32[8,64,256]{2,1,0:T(8,128)}, f32[8,64,256]{2,1,0:T(8,128)}, f32[8,64,256]{2,1,0:T(8,128)}) custom-call(s32[7]{0:T(128)S(1)} %stack.31.info_ref, s32[4,2]{1,0:T(4,128)S(1)} %copy.10.owner_ref, f32[264,128]{1,0:T(8,128)S(1)} %get-tuple-element.178.a0, f32[264,128]{1,0:T(8,128)S(1)} %collective-permute-done.29.a1, ...), custom_call_target="tpu_custom_call" | custom-call | flops 4400000000 | bytes 1048576 | tf_op jit(solution)/shard_map/outputs/pallas_call | solution.py:627
  (150 shorter events, 34.2 us)
Async XLA Ops:
  2.6 11.0 %collective-permute-start = (f32[2,8,16,128]{3,2,1,0:T(8,128)S(1)}, f32[2,8,16,128]{3,2,1,0:T(8,128)S(1)}, u32[]{:S(2)}, u32[]{:S(2)}) collective-permute-start(f32[2,8,16,128]{3,2,1,0:T(8,128)S(1)} %get-tuple-element.89), channel_id=1, source_target_pairs={{0,4},{4,0},{8,12},{12,8},{1,5},{5,1},{9,13},{13,9},{2,6},{6,2},{1... | collective-permute-start | bytes 393224 | tf_op jit(solution)/shard_map/ppermute | solution.py:650
  5.6 14.3 %collective-permute-start.5 = (f32[2,8,16,128]{3,2,1,0:T(8,128)S(1)}, f32[2,8,16,128]{3,2,1,0:T(8,128)S(1)}, u32[]{:S(2)}, u32[]{:S(2)}) collective-permute-start(f32[2,8,16,128]{3,2,1,0:T(8,128)S(1)} %get-tuple-element.103), channel_id=1, source_target_pairs={{0,8},{4,12},{8,0},{12,4},{1,9},{5,13},{9,1},{13,5},{2,10},{6,14},... | collective-permute-start | bytes 393224 | tf_op jit(solution)/shard_map/ppermute | solution.py:650
  8.2 8.8 %collective-permute-start.9 = (f32[2,8,16,128]{3,2,1,0:T(8,128)S(1)}, f32[2,8,16,128]{3,2,1,0:T(8,128)S(1)}, u32[]{:S(2)}, u32[]{:S(2)}) collective-permute-start(f32[2,8,16,128]{3,2,1,0:T(8,128)S(1)} %get-tuple-element.110), channel_id=1, source_target_pairs={{0,12},{4,8},{8,4},{12,0},{1,13},{5,9},{9,5},{13,1},{2,14},{6,10},... | collective-permute-start | bytes 393224 | tf_op jit(solution)/shard_map/ppermute | solution.py:650
  13.5 10.0 %collective-permute-start.14 = (f32[6,16,16]{2,1,0:T(8,128)S(1)}, f32[6,16,16]{2,1,0:T(8,128)S(1)}, u32[]{:S(2)}, u32[]{:S(2)}) collective-permute-start(f32[6,16,16]{2,1,0:T(8,128)S(1)} %copy-done.4), channel_id=1, source_target_pairs={{0,2},{2,0},{1,3},{3,1},{4,6},{6,4},{5,7},{7,5},{8,10},{10,8},{9,1... | collective-permute-start | bytes 18440 | tf_op jit(solution)/shard_map/ppermute | solution.py:650
  16.2 7.6 %collective-permute-start.2 = (f32[2,8,16,128]{3,2,1,0:T(8,128)S(1)}, f32[2,8,16,128]{3,2,1,0:T(8,128)S(1)}, u32[]{:S(2)}, u32[]{:S(2)}) collective-permute-start(f32[2,8,16,128]{3,2,1,0:T(8,128)S(1)} %get-tuple-element.97), channel_id=1, source_target_pairs={{0,4},{4,0},{8,12},{12,8},{1,5},{5,1},{9,13},{13,9},{2,6},{6,2},{1... | collective-permute-start | bytes 393224 | tf_op jit(solution)/shard_map/ppermute | solution.py:650
  17.0 9.5 %collective-permute-start.10 = (f32[2,8,16,128]{3,2,1,0:T(8,128)S(1)}, f32[2,8,16,128]{3,2,1,0:T(8,128)S(1)}, u32[]{:S(2)}, u32[]{:S(2)}) collective-permute-start(f32[2,8,16,128]{3,2,1,0:T(8,128)S(1)} %get-tuple-element.111), channel_id=1, source_target_pairs={{0,12},{4,8},{8,4},{12,0},{1,13},{5,9},{9,5},{13,1},{2,14},{6,10},... | collective-permute-start | bytes 393224 | tf_op jit(solution)/shard_map/ppermute | solution.py:650
  20.0 14.2 %collective-permute-start.6 = (f32[2,8,16,128]{3,2,1,0:T(8,128)S(1)}, f32[2,8,16,128]{3,2,1,0:T(8,128)S(1)}, u32[]{:S(2)}, u32[]{:S(2)}) collective-permute-start(f32[2,8,16,128]{3,2,1,0:T(8,128)S(1)} %get-tuple-element.104), channel_id=1, source_target_pairs={{0,8},{4,12},{8,0},{12,4},{1,9},{5,13},{9,1},{13,5},{2,10},{6,14},... | collective-permute-start | bytes 393224 | tf_op jit(solution)/shard_map/ppermute | solution.py:650
  22.0 21.1 %collective-permute-start.1 = (s32[6,8]{1,0:T(8,128)S(1)}, s32[6,8]{1,0:T(8,128)S(1)}, u32[]{:S(2)}, u32[]{:S(2)}) collective-permute-start(s32[6,8]{1,0:T(8,128)S(1)} %copy-done), channel_id=1, source_target_pairs={{0,2},{2,0},{1,3},{3,1},{4,6},{6,4},{5,7},{7,5},{8,10},{10,8},{9,1... | collective-permute-start | bytes 584 | tf_op jit(solution)/shard_map/ppermute | solution.py:650
  23.8 10.4 %collective-permute-start.3 = (f32[1,8,16,128]{3,2,1,0:T(8,128)S(1)}, f32[1,8,16,128]{3,2,1,0:T(8,128)S(1)}, u32[]{:S(2)}, u32[]{:S(2)}) collective-permute-start(f32[1,8,16,128]{3,2,1,0:T(8,128)S(1)} %get-tuple-element.98), channel_id=1, source_target_pairs={{0,4},{4,0},{8,12},{12,8},{1,5},{5,1},{9,13},{13,9},{2,6},{6,2},{1... | collective-permute-start | bytes 196616 | tf_op jit(solution)/shard_map/ppermute | solution.py:650
  25.8 17.3 %collective-permute-start.13 = (f32[2,8,48,128]{3,2,1,0:T(8,128)S(1)}, f32[2,8,48,128]{3,2,1,0:T(8,128)S(1)}, u32[]{:S(2)}, u32[]{:S(2)}) collective-permute-start(f32[2,8,48,128]{3,2,1,0:T(8,128)S(1)} %get-tuple-element.125), channel_id=1, source_target_pairs={{0,2},{2,0},{1,3},{3,1},{4,6},{6,4},{5,7},{7,5},{8,10},{10,8},{9,1... | collective-permute-start | bytes 1179656 | tf_op jit(solution)/shard_map/ppermute | solution.py:650
  26.5 12.6 %collective-permute-start.11 = (f32[1,8,16,128]{3,2,1,0:T(8,128)S(1)}, f32[1,8,16,128]{3,2,1,0:T(8,128)S(1)}, u32[]{:S(2)}, u32[]{:S(2)}) collective-permute-start(f32[1,8,16,128]{3,2,1,0:T(8,128)S(1)} %get-tuple-element.112), channel_id=1, source_target_pairs={{0,12},{4,8},{8,4},{12,0},{1,13},{5,9},{9,5},{13,1},{2,14},{6,10},... | collective-permute-start | bytes 196616 | tf_op jit(solution)/shard_map/ppermute | solution.py:650
  34.2 8.9 %collective-permute-start.4 = (f32[1,8,16,128]{3,2,1,0:T(8,128)S(1)}, f32[1,8,16,128]{3,2,1,0:T(8,128)S(1)}, u32[]{:S(2)}, u32[]{:S(2)}) collective-permute-start(f32[1,8,16,128]{3,2,1,0:T(8,128)S(1)} %get-tuple-element.99), channel_id=1, source_target_pairs={{0,4},{4,0},{8,12},{12,8},{1,5},{5,1},{9,13},{13,9},{2,6},{6,2},{1... | collective-permute-start | bytes 196616 | tf_op jit(solution)/shard_map/ppermute | solution.py:650
  39.2 10.7 %collective-permute-start.15 = (f32[2,8,48,128]{3,2,1,0:T(8,128)S(1)}, f32[2,8,48,128]{3,2,1,0:T(8,128)S(1)}, u32[]{:S(2)}, u32[]{:S(2)}) collective-permute-start(f32[2,8,48,128]{3,2,1,0:T(8,128)S(1)} %get-tuple-element.118), channel_id=1, source_target_pairs={{0,2},{2,0},{1,3},{3,1},{4,6},{6,4},{5,7},{7,5},{8,10},{10,8},{9,1... | collective-permute-start | bytes 1179656 | tf_op jit(solution)/shard_map/ppermute | solution.py:650
  40.2 15.4 %collective-permute-start.12 = (f32[1,8,16,128]{3,2,1,0:T(8,128)S(1)}, f32[1,8,16,128]{3,2,1,0:T(8,128)S(1)}, u32[]{:S(2)}, u32[]{:S(2)}) collective-permute-start(f32[1,8,16,128]{3,2,1,0:T(8,128)S(1)} %get-tuple-element.113), channel_id=1, source_target_pairs={{0,12},{4,8},{8,4},{12,0},{1,13},{5,9},{9,5},{13,1},{2,14},{6,10},... | collective-permute-start | bytes 196616 | tf_op jit(solution)/shard_map/ppermute | solution.py:650
  43.1 12.5 %collective-permute-start.8 = (f32[1,8,16,128]{3,2,1,0:T(8,128)S(1)}, f32[1,8,16,128]{3,2,1,0:T(8,128)S(1)}, u32[]{:S(2)}, u32[]{:S(2)}) collective-permute-start(f32[1,8,16,128]{3,2,1,0:T(8,128)S(1)} %get-tuple-element.106), channel_id=1, source_target_pairs={{0,8},{4,12},{8,0},{12,4},{1,9},{5,13},{9,1},{13,5},{2,10},{6,14},... | collective-permute-start | bytes 196616 | tf_op jit(solution)/shard_map/ppermute | solution.py:650
  49.8 8.9 %collective-permute-start.17 = (f32[1,8,48,128]{3,2,1,0:T(8,128)S(1)}, f32[1,8,48,128]{3,2,1,0:T(8,128)S(1)}, u32[]{:S(2)}, u32[]{:S(2)}) collective-permute-start(f32[1,8,48,128]{3,2,1,0:T(8,128)S(1)} %get-tuple-element.131), channel_id=1, source_target_pairs={{0,2},{2,0},{1,3},{3,1},{4,6},{6,4},{5,7},{7,5},{8,10},{10,8},{9,1... | collective-permute-start | bytes 589832 | tf_op jit(solution)/shard_map/ppermute | solution.py:650
  70.3 8.1 %collective-permute-start.19 = (f32[264,128]{1,0:T(8,128)}, f32[264,128]{1,0:T(8,128)S(1)}, u32[]{:S(2)}, u32[]{:S(2)}) collective-permute-start(f32[264,128]{1,0:T(8,128)} %get-tuple-element.181), channel_id=1, source_target_pairs={{0,4},{4,0},{8,12},{12,8},{1,5},{5,1},{9,13},{13,9},{2,6},{6,2},{1... | collective-permute-start | bytes 405512 | tf_op jit(solution)/shard_map/ppermute | solution.py:650
  72.3 13.4 %collective-permute-start.20 = (f32[264,128]{1,0:T(8,128)}, f32[264,128]{1,0:T(8,128)S(1)}, u32[]{:S(2)}, u32[]{:S(2)}) collective-permute-start(f32[264,128]{1,0:T(8,128)} %get-tuple-element.180), channel_id=1, source_target_pairs={{0,8},{4,12},{8,0},{12,4},{1,9},{5,13},{9,1},{13,5},{2,10},{6,14},... | collective-permute-start | bytes 405512 | tf_op jit(solution)/shard_map/ppermute | solution.py:650
  73.3 12.3 %collective-permute-start.21 = (f32[264,128]{1,0:T(8,128)}, f32[264,128]{1,0:T(8,128)S(1)}, u32[]{:S(2)}, u32[]{:S(2)}) collective-permute-start(f32[264,128]{1,0:T(8,128)} %get-tuple-element.179), channel_id=1, source_target_pairs={{0,12},{4,8},{8,4},{12,0},{1,13},{5,9},{9,5},{13,1},{2,14},{6,10},... | collective-permute-start | bytes 405512 | tf_op jit(solution)/shard_map/ppermute | solution.py:650
  94.9 9.8 %collective-permute-start.24 = (f32[520,128]{1,0:T(8,128)S(1)}, f32[520,128]{1,0:T(8,128)S(1)}, u32[]{:S(2)}, u32[]{:S(2)}) collective-permute-start(f32[520,128]{1,0:T(8,128)S(1)} %get-tuple-element.159.refs_2_.refs_6_.upper_ref), channel_id=1, source_target_pairs={{0,1},{1,0},{2,3},{3,2},{4,5},{5,4},{6,7},{7,6},{8,9},{9,8},{10,11... | collective-permute-start | bytes 798728 | tf_op jit(solution)/shard_map/ppermute | solution.py:650
  95.4 9.2 %collective-permute-start.23 = (f32[520,128]{1,0:T(8,128)S(1)}, f32[520,128]{1,0:T(8,128)S(1)}, u32[]{:S(2)}, u32[]{:S(2)}) collective-permute-start(f32[520,128]{1,0:T(8,128)S(1)} %get-tuple-element.159.refs_2_.refs_6_.upper_ref), channel_id=1, source_target_pairs={{0,2},{2,0},{1,3},{3,1},{4,6},{6,4},{5,7},{7,5},{8,10},{10,8},{9,1... | collective-permute-start | bytes 798728 | tf_op jit(solution)/shard_map/ppermute | solution.py:650
  116.5 9.2 %collective-permute-start.29 = (f32[264,128]{1,0:T(8,128)S(1)}, f32[264,128]{1,0:T(8,128)S(1)}, u32[]{:S(2)}, u32[]{:S(2)}) collective-permute-start(f32[264,128]{1,0:T(8,128)S(1)} %get-tuple-element.177), channel_id=1, source_target_pairs={{0,4},{4,0},{8,12},{12,8},{1,5},{5,1},{9,13},{13,9},{2,6},{6,2},{1... | collective-permute-start | bytes 405512 | tf_op jit(solution)/shard_map/ppermute | solution.py:650
  119.6 13.1 %collective-permute-start.30 = (f32[264,128]{1,0:T(8,128)S(1)}, f32[264,128]{1,0:T(8,128)S(1)}, u32[]{:S(2)}, u32[]{:S(2)}) collective-permute-start(f32[264,128]{1,0:T(8,128)S(1)} %get-tuple-element.176), channel_id=1, source_target_pairs={{0,8},{4,12},{8,0},{12,4},{1,9},{5,13},{9,1},{13,5},{2,10},{6,14},... | collective-permute-start | bytes 405512 | tf_op jit(solution)/shard_map/ppermute | solution.py:650
  121.3 11.3 %collective-permute-start.31 = (f32[264,128]{1,0:T(8,128)S(1)}, f32[264,128]{1,0:T(8,128)S(1)}, u32[]{:S(2)}, u32[]{:S(2)}) collective-permute-start(f32[264,128]{1,0:T(8,128)S(1)} %get-tuple-element.175), channel_id=1, source_target_pairs={{0,12},{4,8},{8,4},{12,0},{1,13},{5,9},{9,5},{13,1},{2,14},{6,10},... | collective-permute-start | bytes 405512 | tf_op jit(solution)/shard_map/ppermute | solution.py:650
  (52 other events, 487.2 us)

commit v11 on v10

--- a/solution.py
+++ b/solution.py
@@ -12,7 +12,7 @@
 PHYS = 16
 TINY = 1e-30
 SMALL_VMEM = 16 * 1024 * 1024
-APPLY_VMEM = 26 * 1024 * 1024
+APPLY_VMEM = 16 * 1024 * 1024
 
 
 def plain_apply(vector_full, environment, bond_terms, term_slot, slot_block, diagonal):
@@ -333,7 +333,6 @@
     take = lambda n: [refs.pop(0) for _ in range(n)]
     slots = take(2)
     vector = take(4 if parts_given else 1)
-    tiles = take(4) if parts_given and pieces else []
     operands = [take(3) for _ in chunks[: -1 if sent_given else None]]
     sent = take(1)[0] if sent_given else None
     mixes = take(len(chunks))
@@ -341,9 +340,9 @@
     outs = take(2 if pieces else 1)
     if sent_given:
         operands.append(take(3))
-    total_ref, vec, mid = take(3)
-    if before_given:
-        prior, arrival = take(2)
+    scratch = take(2)
+    vec, mid = scratch
+    total_ref = take(1)[0] if pieces else outs[0]
     step = mid.shape[0]
     lanes, half = LANES, LANES // 2
     first = lane_is_first(SUB)
@@ -352,15 +351,14 @@
     keep_second = jnp.where(first_half, 0.0, 1.0).astype(jnp.bfloat16)
     me = info_ref[4]
 
-    @pl.when(pl.program_id(0) == 0)
-    def _():
-        if before_given:
-            pltpu.make_async_copy(before, prior, arrival).start()
+    if not before_given:
         total_ref[...] = jnp.zeros_like(total_ref)
+    else:
+        total_ref[...] = before[...]
 
     def right_side(j):
         if sent_given:
-            other_operands(sent, *operands[-1], j)
+            other_operands(sent, *operands[-1], first_block + j)
         if parts_given:
 
             def put(row, pair, high, low):
@@ -372,13 +370,13 @@
             store_vector([x.at[pl.ds(j * lanes, lanes)] for x in vector], rows_of, put)
             source = vec[j]
         else:
-            source = vector[0][j]
+            source = vector[0][first_block + j]
         source = jnp.concatenate([source, source], axis=0)
         at = 0
         for left_high, left_low, right in operands:
             count = right.shape[1]
             mid[j, at : at + count, :] = jnp.dot(
-                right[j], source, preferred_element_type=jnp.float32
+                right[first_block + j], source, preferred_element_type=jnp.float32
             )
             at += count
 
@@ -394,7 +392,7 @@
                 tiles.append(jnp.where(first, upper, pltpu.roll(lower, half, 1)))
                 tiles.append(jnp.where(first, pltpu.roll(upper, half, 1), lower))
         t_high, t_low = split_two(jnp.concatenate(tiles, axis=0))
-        lh, ll = left_high[w, j], left_low[w, j]
+        lh, ll = left_high[w, first_block + j], left_low[w, first_block + j]
         wide_high = jnp.concatenate([lh * keep_first, lh * keep_second], axis=0)
         wide_low = jnp.concatenate([ll * keep_first, ll * keep_second], axis=0)
         weights = jnp.concatenate([wide_high, wide_low], axis=1)
@@ -410,7 +408,7 @@
         )
 
     def add_up(j, table, bond, mixed):
-        slot = table[bond, first_block + pl.program_id(0) * step + j]
+        slot = table[bond, first_block + j]
         slot = ((slot >> 1) ^ me) * 2 + (slot & 1)
         for part in range(2):
             columns = slice(part * lanes, (part + 1) * lanes)
@@ -447,80 +445,57 @@
     j, mixing, w, table, bond, z = waiting
     add_up(j, table, bond, mix_unit(mixing, w, z))
 
-    @pl.when(pl.program_id(0) == pl.num_programs(0) - 1)
-    def _():
-        if before_given:
-            pltpu.make_async_copy(before, prior, arrival).wait()
-            total_ref[...] += prior[...]
-        if pieces:
+    if pieces:
+        stats = jnp.zeros((SUB, lanes), jnp.float32)
+        if parts_given:
+            tail = vector[0].shape[0] - SUB
+            stats = stacked_rows(*merged([x[tail:] for x in vector]))
+        for out, part in ((outs[0], info_ref[5]), (outs[1], 1 - info_ref[5])):
+            for k in range(4):
+                for i in range(2):
+                    out[k, i * lanes : (i + 1) * lanes] = total_ref[part, 2 * k + i]
+                out[k, 2 * lanes :] = stats
             stats = jnp.zeros((SUB, lanes), jnp.float32)
-            if tiles:
-                stats = stacked_rows(*merged([tile[...] for tile in tiles]))
-            for out, part in ((outs[0], info_ref[5]), (outs[1], 1 - info_ref[5])):
-                for k in range(4):
-                    for i in range(2):
-                        out[k, i * lanes : (i + 1) * lanes] = total_ref[part, 2 * k + i]
-                    out[k, 2 * lanes :] = stats
-                stats = jnp.zeros((SUB, lanes), jnp.float32)
-        else:
-            outs[0][...] = total_ref[...]
 
 
 def apply_bonds(info, slots, vector, chunks, operands, sent, mixes, before, pieces, half_of=None):
     blocks, half, lanes = operands[0][0].shape[1:]
-    step = 4
     parts_given = half_of is not None
-    at = half_of or 0
-    if parts_given:
-        in_specs = [whole(step * lanes, lanes)] * 4
-        arguments = list(vector)
-        if pieces:
-            last = vector[0].shape[0] // SUB - 1
-            in_specs += [pl.BlockSpec((SUB, lanes), lambda i, *_: (last, 0))] * 4
-            arguments += list(vector)
-    else:
-        in_specs = [pl.BlockSpec((step,) + vector.shape[1:], lambda i, *_: (i, 0, 0))]
-        arguments = [vector]
+    step = 4 if parts_given else blocks
+    arguments = list(vector) if parts_given else [vector]
     for made in operands:
-        in_specs += operand_specs(made[0].shape[0], step, half, lanes, at)
         arguments += made
+    if sent is not None:
+        arguments.append(sent)
+    arguments += mixes
+    aliases = {}
+    if before is not None:
+        if not pieces:
+            aliases[3 + len(arguments)] = 0
+        arguments.append(before)
     counts = [mix.shape[0] for mix in mixes]
+    shapes = [(4, 2 * lanes + SUB, lanes)] * 2 if pieces else [(2, 8, lanes, lanes)]
+    out_shape = [jax.ShapeDtypeStruct(shape, jnp.float32) for shape in shapes]
     if sent is not None:
-        in_specs.append(
-            pl.BlockSpec((counts[-1], step) + sent.shape[2:], lambda i, *_: (0, i, 0, 0))
-        )
-        arguments.append(sent)
-    for mix in mixes:
-        in_specs.append(whole(*mix.shape))
-        arguments.append(mix)
+        out_shape += operand_shapes(counts[-1], blocks, half, lanes)
     scratch = [
-        pltpu.VMEM((2, 8, lanes, lanes), jnp.float32),
-        pltpu.VMEM((step, lanes, PHYS * half), jnp.bfloat16),
+        pltpu.VMEM((step if parts_given else 1, lanes, PHYS * half), jnp.bfloat16),
         pltpu.VMEM((step, sum(counts) * 32, PHYS * half), jnp.float32),
     ]
-    if before is not None:
-        in_specs.append(pl.BlockSpec(memory_space=pl.ANY))
-        arguments.append(before)
-        scratch += [pltpu.VMEM(before.shape, jnp.float32), pltpu.SemaphoreType.DMA]
-    shapes = [(4, 2 * lanes + SUB, lanes)] * 2 if pieces else [(2, 8, lanes, lanes)]
-    out_specs = [whole(*shape) for shape in shapes]
-    out_shape = [jax.ShapeDtypeStruct(shape, jnp.float32) for shape in shapes]
-    if sent is not None:
-        out_specs += operand_specs(counts[-1], step, half, lanes)
-        out_shape += operand_shapes(counts[-1], blocks, half, lanes)
+    if pieces:
+        scratch.append(pltpu.VMEM((2, 8, lanes, lanes), jnp.float32))
     plan = (
-        tuple(chunks), at * step, parts_given, sent is not None, before is not None, pieces,
+        tuple(chunks), (half_of or 0) * step, parts_given, sent is not None, before is not None,
+        pieces,
     )
     out = pl.pallas_call(
         functools.partial(apply_kernel, plan),
-        grid_spec=pltpu.PrefetchScalarGridSpec(
-            num_scalar_prefetch=3,
-            grid=(1 if parts_given else blocks // step,),
-            in_specs=in_specs,
-            out_specs=out_specs,
-            scratch_shapes=scratch,
-        ),
+        in_specs=[pl.BlockSpec(memory_space=pltpu.SMEM)] * 3
+        + [pl.BlockSpec(memory_space=pltpu.VMEM)] * len(arguments),
+        out_specs=[pl.BlockSpec(memory_space=pltpu.VMEM)] * len(out_shape),
+        scratch_shapes=scratch,
         out_shape=out_shape,
+        input_output_aliases=aliases,
         compiler_params=pltpu.CompilerParams(vmem_limit_bytes=APPLY_VMEM),
         cost_estimate=micros(10 if parts_given else 1),
         name="apply_bonds",
@@ -585,18 +560,15 @@
     shapes = [jax.ShapeDtypeStruct((n, LANES), jnp.float32) for n in (rows, rows + SUB)]
     return pl.pallas_call(
         image_kernel,
-        grid_spec=pltpu.PrefetchScalarGridSpec(
-            num_scalar_prefetch=2,
-            grid=(1,),
-            in_specs=[whole(*x.shape) for x in (*arrived, diagonal, own)],
-            out_specs=[whole(*x.shape) for x in shapes],
-            scratch_shapes=[pltpu.VMEM(own.shape, jnp.float32)],
-        ),
+        in_specs=[pl.BlockSpec(memory_space=pltpu.SMEM)] * 2
+        + [pl.BlockSpec(memory_space=pltpu.VMEM)] * 6,
+        out_specs=[pl.BlockSpec(memory_space=pltpu.VMEM)] * 2,
+        scratch_shapes=[pltpu.VMEM(own.shape, jnp.float32)],
         out_shape=shapes,
         compiler_params=pltpu.CompilerParams(vmem_limit_bytes=SMALL_VMEM),
         cost_estimate=micros(3),
         name="owner_image",
-    )(info, owners, *in_hbm(arrived[0]), *arrived[1:], *in_hbm(diagonal, own))
+    )(info, owners, *arrived, diagonal, own)
 
 
 def final_kernel(

time: 135 us -> 134 us (level)
  Pallas kernels: 52.6 us -> 48.2 us
  local copies, waits for them, and re-layouts: 1.16 us -> 4.03 us
  waiting for transfers between devices: 38 us -> 40.2 us
  starting transfers between devices: 40.6 us -> 39.1 us
    pallas_call x7, Pallas kernels: 38.4 us -> 33.8 us  [the longest x6 32.7 us: apply_bonds(): pl.pallas_call(functools.partial(apply_kernel, plan), in_specs=[pl.BlockS...]
    unnamed x89 -> x95, local copies, waits for them, and re-layouts: 1.07 us -> 3.94 us
    ppermute x32, waiting for transfers between devices: 38 us -> 40.2 us  [partner(): return lax.ppermute(x, axis, [(i, i ^ k) for i in range(size)])]
    ppermute x32, starting transfers between devices: 40.6 us -> 39.1 us  [partner(): return lax.ppermute(x, axis, [(i, i ^ k) for i in range(size)])]
  transfers between devices with their start and end apart: 32 -> 32, of which waited for: 12 -> 13; matrix products, arithmetic and copies ran while one was open for 0% -> 0% of each run, Pallas kernels for 25% -> 24%
where the time goes in v11:
time: 134 us
  Pallas kernels  48.2 us (36%)
  waiting for transfers between devices  40.2 us (30%)
  starting transfers between devices  39.1 us (29%)
  local copies, waits for them, and re-layouts  4.03 us (3%)
  between operations  1.41 us (1%)
    ppermute x32, waiting for transfers between devices, partner(): return lax.ppermute(x, axis, [(i, i ^ k) for i in range(size)])  40.2 us
    ppermute x32, starting transfers between devices, partner(): return lax.ppermute(x, axis, [(i, i ^ k) for i in range(size)])  39.1 us
    pallas_call x6, Pallas kernels, apply_bonds(): pl.pallas_call(functools.partial(apply_kernel, plan), in_specs=[pl.BlockS...  32.7 us
    pallas_call x4, Pallas kernels, own_operands(): pl.pallas_call(own_operands_kernel, grid_spec=pltpu.PrefetchScalarGridSpe...  4.87 us
    pallas_call x4, Pallas kernels, cut_pieces(): pl.pallas_call(functools.partial(cut_kernel, first), grid_spec=pltpu.Pref...  4.58 us
    unnamed x95, local copies, waits for them, and re-layouts  3.94 us
  transfers between devices with their start and end apart: 32, of which 13 were waited for; matrix products, arithmetic and copies ran while one was open for 0% of the time, Pallas kernels for 24%

profile of v11, /device:TPU:0, one launch (start us, length us, event | category | flops | bytes accessed | tf_op | source)
XLA Modules:
  0.0 133.8 jit_solution(14502385558097295070)
XLA Ops:
  2.6 3.1 %collective-permute-start = (f32[2,8,16,128]{3,2,1,0:T(8,128)S(1)}, f32[2,8,16,128]{3,2,1,0:T(8,128)S(1)}, u32[]{:S(2)}, u32[]{:S(2)}) collective-permute-start(f32[2,8,16,128]{3,2,1,0:T(8,128)S(1)} %get-tuple-element.89), channel_id=1, source_target_pairs={{0,4},{4,0},{8,12},{12,8},{1,5},{5,1},{9,13},{13,9},{2,6},{6,2},{1... | collective-permute-start | bytes 393224 | tf_op jit(solution)/shard_map/ppermute | solution.py:622
  5.6 2.6 %collective-permute-start.5 = (f32[2,8,16,128]{3,2,1,0:T(8,128)S(1)}, f32[2,8,16,128]{3,2,1,0:T(8,128)S(1)}, u32[]{:S(2)}, u32[]{:S(2)}) collective-permute-start(f32[2,8,16,128]{3,2,1,0:T(8,128)S(1)} %get-tuple-element.103), channel_id=1, source_target_pairs={{0,8},{4,12},{8,0},{12,4},{1,9},{5,13},{9,1},{13,5},{2,10},{6,14},... | collective-permute-start | bytes 393224 | tf_op jit(solution)/shard_map/ppermute | solution.py:622
  8.2 2.5 %pack.1 = (bf16[8,128,1024]{2,1,0:T(8,128)(2,1)S(1)}, f32[8,128,128]{2,1,0:T(8,128)S(1)}, f32[8,128,128]{2,1,0:T(8,128)S(1)}) custom-call(s32[7]{0:T(128)S(1)} %stack.31.info_ref, f32[8,64,1024]{2,1,0:T(8,128)S(1)} %copy-done.1, f32[8,64,1024]{2,1,0:T(8,128)S(1)} %copy-done.1, f32[8,64,256]{2,1,0:T(8,128)S(1)} %copy-done.3), custom_call_target="tpu_custom_call" | custom-call | flops 5500000256 | bytes 1048576 | tf_op jit(solution)/shard_map/pack/pallas_call | solution.py:139
  17.7 3.0 %collective-permute-start.10 = (f32[2,8,16,128]{3,2,1,0:T(8,128)S(1)}, f32[2,8,16,128]{3,2,1,0:T(8,128)S(1)}, u32[]{:S(2)}, u32[]{:S(2)}) collective-permute-start(f32[2,8,16,128]{3,2,1,0:T(8,128)S(1)} %get-tuple-element.111), channel_id=1, source_target_pairs={{0,12},{4,8},{8,4},{12,0},{1,13},{5,9},{9,5},{13,1},{2,14},{6,10},... | collective-permute-start | bytes 393224 | tf_op jit(solution)/shard_map/ppermute | solution.py:622
  26.1 1.8 %collective-permute-done.10.refs_3_ = f32[2,8,16,128]{3,2,1,0:T(8,128)S(1)} collective-permute-done((f32[2,8,16,128]{3,2,1,0:T(8,128)S(1)}, f32[2,8,16,128]{3,2,1,0:T(8,128)S(1)}, u32[]{:S(2)}, u32[]{:S(2)}) %collective-permute-start.10) | collective-permute-done | bytes 131104 | tf_op jit(solution)/shard_map/ppermute | solution.py:622
  29.6 5.0 %collective-permute-done.6.refs_2_ = f32[2,8,16,128]{3,2,1,0:T(8,128)S(1)} collective-permute-done((f32[2,8,16,128]{3,2,1,0:T(8,128)S(1)}, f32[2,8,16,128]{3,2,1,0:T(8,128)S(1)}, u32[]{:S(2)}, u32[]{:S(2)}) %collective-permute-start.6) | collective-permute-done | bytes 131104 | tf_op jit(solution)/shard_map/ppermute | solution.py:622
  34.6 4.0 %collective-permute-start.4 = (f32[1,8,16,128]{3,2,1,0:T(8,128)S(1)}, f32[1,8,16,128]{3,2,1,0:T(8,128)S(1)}, u32[]{:S(2)}, u32[]{:S(2)}) collective-permute-start(f32[1,8,16,128]{3,2,1,0:T(8,128)S(1)} %get-tuple-element.99), channel_id=1, source_target_pairs={{0,4},{4,0},{8,12},{12,8},{1,5},{5,1},{9,13},{13,9},{2,6},{6,2},{1... | collective-permute-start | bytes 196616 | tf_op jit(solution)/shard_map/ppermute | solution.py:622
  40.6 2.6 %collective-permute-start.12 = (f32[1,8,16,128]{3,2,1,0:T(8,128)S(1)}, f32[1,8,16,128]{3,2,1,0:T(8,128)S(1)}, u32[]{:S(2)}, u32[]{:S(2)}) collective-permute-start(f32[1,8,16,128]{3,2,1,0:T(8,128)S(1)} %get-tuple-element.113), channel_id=1, source_target_pairs={{0,12},{4,8},{8,4},{12,0},{1,13},{5,9},{9,5},{13,1},{2,14},{6,10},... | collective-permute-start | bytes 196616 | tf_op jit(solution)/shard_map/ppermute | solution.py:622
  43.3 4.9 %apply_bonds.6 = (f32[2,8,128,128]{3,2,1,0:T(8,128)S(1)}, bf16[2,8,64,128]{3,2,1,0:T(8,128)(2,1)S(1)}, bf16[2,8,64,128]{3,2,1,0:T(8,128)(2,1)S(1)}, bf16[8,64,256]{2,1,0:T(8,128)(2,1)S(1)}) custom-call(s32[7]{0:T(128)S(1)} %stack.31.info_ref, s32[6,8]{1,0:T(8,128)S(1)} %copy-done, s32[6,8]{1,0:T(8,128)S(1)} %collective-permute-done.1.refs_1_, ...), custom_call_target="tpu_custom_call" | custom-call | flops 1100000000 | bytes 1048576 | tf_op jit(solution)/shard_map/apply_bonds/pallas_call | solution.py:491
  49.8 5.1 %apply_bonds.7 = (f32[2,8,128,128]{3,2,1,0:T(8,128)S(1)}, bf16[2,8,64,128]{3,2,1,0:T(8,128)(2,1)S(1)}, bf16[2,8,64,128]{3,2,1,0:T(8,128)(2,1)S(1)}, bf16[8,64,256]{2,1,0:T(8,128)(2,1)S(1)}) custom-call(s32[7]{0:T(128)S(1)} %stack.31.info_ref, s32[6,8]{1,0:T(8,128)S(1)} %copy-done, ...), custom_call_target="tpu_custom_call", output_to_operand_aliasing={{0}: (10, {})} | custom-call | flops 1100000000 | bytes 1048576 | tf_op jit(solution)/shard_map/apply_bonds/pallas_call | solution.py:491
  57.8 3.7 %apply_bonds.8 = (f32[2,8,128,128]{3,2,1,0:T(8,128)S(1)}, bf16[1,8,64,128]{3,2,1,0:T(8,128)(2,1)S(1)}, bf16[1,8,64,128]{3,2,1,0:T(8,128)(2,1)S(1)}, bf16[8,32,256]{2,1,0:T(8,128)(2,1)S(1)}) custom-call(s32[7]{0:T(128)S(1)} %stack.31.info_ref, s32[6,8]{1,0:T(8,128)S(1)} %copy-done, ...), custom_call_target="tpu_custom_call", output_to_operand_aliasing={{0}: (10, {})} | custom-call | flops 1100000000 | bytes 1048576 | tf_op jit(solution)/shard_map/apply_bonds/pallas_call | solution.py:491
  61.9 3.6 %apply_bonds.9 = (f32[4,264,128]{2,1,0:T(8,128)S(1)}, f32[4,264,128]{2,1,0:T(8,128)S(1)}, bf16[1,8,64,128]{3,2,1,0:T(8,128)(2,1)S(1)}, bf16[1,8,64,128]{3,2,1,0:T(8,128)(2,1)S(1)}, bf16[8,32,256]{2,1,0:T(8,128)(2,1)S(1)}) custom-call(s32[7]{0:T(128)S(1)} %stack.31.info_ref, s32[6,8]{1,0:T(8,128)S(1)} %copy-done, s32[6,8]{1,0:T(8,128)S(1)} %collective-permute-done.1.refs_1_, ...), custom_call_target="tpu_custom_call" | custom-call | flops 1100000000 | bytes 1048576 | tf_op jit(solution)/shard_map/apply_bonds/pallas_call | solution.py:491
  65.6 1.9 %collective-permute-done.18 = f32[4,264,128]{2,1,0:T(8,128)S(1)} collective-permute-done((f32[4,264,128]{2,1,0:T(8,128)S(1)}, f32[4,264,128]{2,1,0:T(8,128)S(1)}, u32[]{:S(2)}, u32[]{:S(2)}) %collective-permute-start.18) | collective-permute-done | bytes 540704 | tf_op jit(solution)/shard_map/ppermute | solution.py:622
  68.3 2.8 %collective-permute-start.19 = (f32[264,128]{1,0:T(8,128)}, f32[264,128]{1,0:T(8,128)S(1)}, u32[]{:S(2)}, u32[]{:S(2)}) collective-permute-start(f32[264,128]{1,0:T(8,128)} %get-tuple-element.181), channel_id=1, source_target_pairs={{0,4},{4,0},{8,12},{12,8},{1,5},{5,1},{9,13},{13,9},{2,6},{6,2},{1... | collective-permute-start | bytes 405512 | tf_op jit(solution)/shard_map/ppermute | solution.py:622
  71.4 2.2 %collective-permute-start.21 = (f32[264,128]{1,0:T(8,128)}, f32[264,128]{1,0:T(8,128)S(1)}, u32[]{:S(2)}, u32[]{:S(2)}) collective-permute-start(f32[264,128]{1,0:T(8,128)} %get-tuple-element.179), channel_id=1, source_target_pairs={{0,12},{4,8},{8,4},{12,0},{1,13},{5,9},{9,5},{13,1},{2,14},{6,10},... | collective-permute-start | bytes 405512 | tf_op jit(solution)/shard_map/ppermute | solution.py:622
  73.7 3.0 %collective-permute-done.19.a1 = f32[264,128]{1,0:T(8,128)S(1)} collective-permute-done((f32[264,128]{1,0:T(8,128)}, f32[264,128]{1,0:T(8,128)S(1)}, u32[]{:S(2)}, u32[]{:S(2)}) %collective-permute-start.19) | collective-permute-done | bytes 135200 | tf_op jit(solution)/shard_map/ppermute | solution.py:622
  76.8 7.7 %collective-permute-done.20.a2 = f32[264,128]{1,0:T(8,128)S(1)} collective-permute-done((f32[264,128]{1,0:T(8,128)}, f32[264,128]{1,0:T(8,128)S(1)}, u32[]{:S(2)}, u32[]{:S(2)}) %collective-permute-start.20) | collective-permute-done | bytes 135200 | tf_op jit(solution)/shard_map/ppermute | solution.py:622
  88.5 5.8 %collective-permute-done.22.refs_3_ = f32[512,128]{1,0:T(8,128)S(1)} collective-permute-done((f32[512,128]{1,0:T(8,128)S(1)}, f32[512,128]{1,0:T(8,128)S(1)}, u32[]{:S(2)}, u32[]{:S(2)}) %collective-permute-start.22) | collective-permute-done | bytes 262176 | tf_op jit(solution)/shard_map/ppermute | solution.py:622
  96.0 7.9 %apply_bonds.10.refs_38_ = f32[2,8,128,128]{3,2,1,0:T(8,128)S(1)} custom-call(s32[7]{0:T(128)S(1)} %stack.31.info_ref, s32[6,8]{1,0:T(8,128)S(1)} %copy-done, s32[6,8]{1,0:T(8,128)S(1)} %collective-permute-done.1.refs_1_, f32[512,128]{1,0:T(8,128)S(1)} %get-tuple-element.158.refs_2_.lower_ref, f32[512,128]{1,0:T(8,128)S(1)} %collective-permute-done.22.refs_3_, ...), custom_call_target="tpu_custom_call" | custom-call | flops 11000000512 | bytes 1048576 | tf_op jit(solution)/shard_map/apply_bonds/pallas_call | solution.py:491
  105.5 7.6 %apply_bonds.11 = (f32[4,264,128]{2,1,0:T(8,128)S(1)}, f32[4,264,128]{2,1,0:T(8,128)S(1)}) custom-call(s32[7]{0:T(128)S(1)} %stack.31.info_ref, s32[6,8]{1,0:T(8,128)S(1)} %copy-done, s32[6,8]{1,0:T(8,128)S(1)} %collective-permute-done.1.refs_1_, f32[520,128]{1,0:T(8,128)S(1)} %get-tuple-element.159.refs_2_.upper_ref, ...), custom_call_target="tpu_custom_call" | custom-call | flops 11000000512 | bytes 1048576 | tf_op jit(solution)/shard_map/apply_bonds/pallas_call | solution.py:491
  115.2 3.3 %collective-permute-start.29 = (f32[264,128]{1,0:T(8,128)S(1)}, f32[264,128]{1,0:T(8,128)S(1)}, u32[]{:S(2)}, u32[]{:S(2)}) collective-permute-start(f32[264,128]{1,0:T(8,128)S(1)} %get-tuple-element.177), channel_id=1, source_target_pairs={{0,4},{4,0},{8,12},{12,8},{1,5},{5,1},{9,13},{13,9},{2,6},{6,2},{1... | collective-permute-start | bytes 405512 | tf_op jit(solution)/shard_map/ppermute | solution.py:622
  121.0 3.4 %collective-permute-done.29.a1 = f32[264,128]{1,0:T(8,128)S(1)} collective-permute-done((f32[264,128]{1,0:T(8,128)S(1)}, f32[264,128]{1,0:T(8,128)S(1)}, u32[]{:S(2)}, u32[]{:S(2)}) %collective-permute-start.29) | collective-permute-done | bytes 135200 | tf_op jit(solution)/shard_map/ppermute | solution.py:622
  124.4 7.3 %collective-permute-done.30.a2 = f32[264,128]{1,0:T(8,128)S(1)} collective-permute-done((f32[264,128]{1,0:T(8,128)S(1)}, f32[264,128]{1,0:T(8,128)S(1)}, u32[]{:S(2)}, u32[]{:S(2)}) %collective-permute-start.30) | collective-permute-done | bytes 135200 | tf_op jit(solution)/shard_map/ppermute | solution.py:622
  131.7 2.1 %outputs.1 = (f32[8,64,256]{2,1,0:T(8,128)}, f32[8,64,256]{2,1,0:T(8,128)}, f32[8,64,256]{2,1,0:T(8,128)}) custom-call(s32[7]{0:T(128)S(1)} %stack.31.info_ref, s32[4,2]{1,0:T(4,128)S(1)} %copy.12.owner_ref, f32[264,128]{1,0:T(8,128)S(1)} %get-tuple-element.178.a0, f32[264,128]{1,0:T(8,128)S(1)} %collective-permute-done.29.a1, ...), custom_call_target="tpu_custom_call" | custom-call | flops 4400000000 | bytes 1048576 | tf_op jit(solution)/shard_map/outputs/pallas_call | solution.py:599
  (156 shorter events, 35.4 us)
Async XLA Ops:
  2.6 11.7 %collective-permute-start = (f32[2,8,16,128]{3,2,1,0:T(8,128)S(1)}, f32[2,8,16,128]{3,2,1,0:T(8,128)S(1)}, u32[]{:S(2)}, u32[]{:S(2)}) collective-permute-start(f32[2,8,16,128]{3,2,1,0:T(8,128)S(1)} %get-tuple-element.89), channel_id=1, source_target_pairs={{0,4},{4,0},{8,12},{12,8},{1,5},{5,1},{9,13},{13,9},{2,6},{6,2},{1... | collective-permute-start | bytes 393224 | tf_op jit(solution)/shard_map/ppermute | solution.py:622
  5.6 15.1 %collective-permute-start.5 = (f32[2,8,16,128]{3,2,1,0:T(8,128)S(1)}, f32[2,8,16,128]{3,2,1,0:T(8,128)S(1)}, u32[]{:S(2)}, u32[]{:S(2)}) collective-permute-start(f32[2,8,16,128]{3,2,1,0:T(8,128)S(1)} %get-tuple-element.103), channel_id=1, source_target_pairs={{0,8},{4,12},{8,0},{12,4},{1,9},{5,13},{9,1},{13,5},{2,10},{6,14},... | collective-permute-start | bytes 393224 | tf_op jit(solution)/shard_map/ppermute | solution.py:622
  8.2 9.5 %collective-permute-start.9 = (f32[2,8,16,128]{3,2,1,0:T(8,128)S(1)}, f32[2,8,16,128]{3,2,1,0:T(8,128)S(1)}, u32[]{:S(2)}, u32[]{:S(2)}) collective-permute-start(f32[2,8,16,128]{3,2,1,0:T(8,128)S(1)} %get-tuple-element.110), channel_id=1, source_target_pairs={{0,12},{4,8},{8,4},{12,0},{1,13},{5,9},{9,5},{13,1},{2,14},{6,10},... | collective-permute-start | bytes 393224 | tf_op jit(solution)/shard_map/ppermute | solution.py:622
  14.3 9.2 %collective-permute-start.14 = (f32[6,16,16]{2,1,0:T(8,128)S(1)}, f32[6,16,16]{2,1,0:T(8,128)S(1)}, u32[]{:S(2)}, u32[]{:S(2)}) collective-permute-start(f32[6,16,16]{2,1,0:T(8,128)S(1)} %copy-done.4), channel_id=1, source_target_pairs={{0,2},{2,0},{1,3},{3,1},{4,6},{6,4},{5,7},{7,5},{8,10},{10,8},{9,1... | collective-permute-start | bytes 18440 | tf_op jit(solution)/shard_map/ppermute | solution.py:622
  17.7 10.2 %collective-permute-start.10 = (f32[2,8,16,128]{3,2,1,0:T(8,128)S(1)}, f32[2,8,16,128]{3,2,1,0:T(8,128)S(1)}, u32[]{:S(2)}, u32[]{:S(2)}) collective-permute-start(f32[2,8,16,128]{3,2,1,0:T(8,128)S(1)} %get-tuple-element.111), channel_id=1, source_target_pairs={{0,12},{4,8},{8,4},{12,0},{1,13},{5,9},{9,5},{13,1},{2,14},{6,10},... | collective-permute-start | bytes 393224 | tf_op jit(solution)/shard_map/ppermute | solution.py:622
  20.8 13.9 %collective-permute-start.6 = (f32[2,8,16,128]{3,2,1,0:T(8,128)S(1)}, f32[2,8,16,128]{3,2,1,0:T(8,128)S(1)}, u32[]{:S(2)}, u32[]{:S(2)}) collective-permute-start(f32[2,8,16,128]{3,2,1,0:T(8,128)S(1)} %get-tuple-element.104), channel_id=1, source_target_pairs={{0,8},{4,12},{8,0},{12,4},{1,9},{5,13},{9,1},{13,5},{2,10},{6,14},... | collective-permute-start | bytes 393224 | tf_op jit(solution)/shard_map/ppermute | solution.py:622
  22.0 21.2 %collective-permute-start.1 = (s32[6,8]{1,0:T(8,128)S(1)}, s32[6,8]{1,0:T(8,128)S(1)}, u32[]{:S(2)}, u32[]{:S(2)}) collective-permute-start(s32[6,8]{1,0:T(8,128)S(1)} %copy-done), channel_id=1, source_target_pairs={{0,2},{2,0},{1,3},{3,1},{4,6},{6,4},{5,7},{7,5},{8,10},{10,8},{9,1... | collective-permute-start | bytes 584 | tf_op jit(solution)/shard_map/ppermute | solution.py:622
  23.8 10.8 %collective-permute-start.3 = (f32[1,8,16,128]{3,2,1,0:T(8,128)S(1)}, f32[1,8,16,128]{3,2,1,0:T(8,128)S(1)}, u32[]{:S(2)}, u32[]{:S(2)}) collective-permute-start(f32[1,8,16,128]{3,2,1,0:T(8,128)S(1)} %get-tuple-element.98), channel_id=1, source_target_pairs={{0,4},{4,0},{8,12},{12,8},{1,5},{5,1},{9,13},{13,9},{2,6},{6,2},{1... | collective-permute-start | bytes 196616 | tf_op jit(solution)/shard_map/ppermute | solution.py:622
  25.5 17.8 %collective-permute-start.13 = (f32[2,8,48,128]{3,2,1,0:T(8,128)S(1)}, f32[2,8,48,128]{3,2,1,0:T(8,128)S(1)}, u32[]{:S(2)}, u32[]{:S(2)}) collective-permute-start(f32[2,8,48,128]{3,2,1,0:T(8,128)S(1)} %get-tuple-element.125), channel_id=1, source_target_pairs={{0,2},{2,0},{1,3},{3,1},{4,6},{6,4},{5,7},{7,5},{8,10},{10,8},{9,1... | collective-permute-start | bytes 1179656 | tf_op jit(solution)/shard_map/ppermute | solution.py:622
  27.9 12.0 %collective-permute-start.11 = (f32[1,8,16,128]{3,2,1,0:T(8,128)S(1)}, f32[1,8,16,128]{3,2,1,0:T(8,128)S(1)}, u32[]{:S(2)}, u32[]{:S(2)}) collective-permute-start(f32[1,8,16,128]{3,2,1,0:T(8,128)S(1)} %get-tuple-element.112), channel_id=1, source_target_pairs={{0,12},{4,8},{8,4},{12,0},{1,13},{5,9},{9,5},{13,1},{2,14},{6,10},... | collective-permute-start | bytes 196616 | tf_op jit(solution)/shard_map/ppermute | solution.py:622
  34.6 8.6 %collective-permute-start.4 = (f32[1,8,16,128]{3,2,1,0:T(8,128)S(1)}, f32[1,8,16,128]{3,2,1,0:T(8,128)S(1)}, u32[]{:S(2)}, u32[]{:S(2)}) collective-permute-start(f32[1,8,16,128]{3,2,1,0:T(8,128)S(1)} %get-tuple-element.99), channel_id=1, source_target_pairs={{0,4},{4,0},{8,12},{12,8},{1,5},{5,1},{9,13},{13,9},{2,6},{6,2},{1... | collective-permute-start | bytes 196616 | tf_op jit(solution)/shard_map/ppermute | solution.py:622
  40.0 9.9 %collective-permute-start.15 = (f32[2,8,48,128]{3,2,1,0:T(8,128)S(1)}, f32[2,8,48,128]{3,2,1,0:T(8,128)S(1)}, u32[]{:S(2)}, u32[]{:S(2)}) collective-permute-start(f32[2,8,48,128]{3,2,1,0:T(8,128)S(1)} %get-tuple-element.118), channel_id=1, source_target_pairs={{0,2},{2,0},{1,3},{3,1},{4,6},{6,4},{5,7},{7,5},{8,10},{10,8},{9,1... | collective-permute-start | bytes 1179656 | tf_op jit(solution)/shard_map/ppermute | solution.py:622
  40.6 14.3 %collective-permute-start.12 = (f32[1,8,16,128]{3,2,1,0:T(8,128)S(1)}, f32[1,8,16,128]{3,2,1,0:T(8,128)S(1)}, u32[]{:S(2)}, u32[]{:S(2)}) collective-permute-start(f32[1,8,16,128]{3,2,1,0:T(8,128)S(1)} %get-tuple-element.113), channel_id=1, source_target_pairs={{0,12},{4,8},{8,4},{12,0},{1,13},{5,9},{9,5},{13,1},{2,14},{6,10},... | collective-permute-start | bytes 196616 | tf_op jit(solution)/shard_map/ppermute | solution.py:622
  43.2 11.7 %collective-permute-start.8 = (f32[1,8,16,128]{3,2,1,0:T(8,128)S(1)}, f32[1,8,16,128]{3,2,1,0:T(8,128)S(1)}, u32[]{:S(2)}, u32[]{:S(2)}) collective-permute-start(f32[1,8,16,128]{3,2,1,0:T(8,128)S(1)} %get-tuple-element.106), channel_id=1, source_target_pairs={{0,8},{4,12},{8,0},{12,4},{1,9},{5,13},{9,1},{13,5},{2,10},{6,14},... | collective-permute-start | bytes 196616 | tf_op jit(solution)/shard_map/ppermute | solution.py:622
  49.3 8.5 %collective-permute-start.17 = (f32[1,8,48,128]{3,2,1,0:T(8,128)S(1)}, f32[1,8,48,128]{3,2,1,0:T(8,128)S(1)}, u32[]{:S(2)}, u32[]{:S(2)}) collective-permute-start(f32[1,8,48,128]{3,2,1,0:T(8,128)S(1)} %get-tuple-element.131), channel_id=1, source_target_pairs={{0,2},{2,0},{1,3},{3,1},{4,6},{6,4},{5,7},{7,5},{8,10},{10,8},{9,1... | collective-permute-start | bytes 589832 | tf_op jit(solution)/shard_map/ppermute | solution.py:622
  68.3 8.4 %collective-permute-start.19 = (f32[264,128]{1,0:T(8,128)}, f32[264,128]{1,0:T(8,128)S(1)}, u32[]{:S(2)}, u32[]{:S(2)}) collective-permute-start(f32[264,128]{1,0:T(8,128)} %get-tuple-element.181), channel_id=1, source_target_pairs={{0,4},{4,0},{8,12},{12,8},{1,5},{5,1},{9,13},{13,9},{2,6},{6,2},{1... | collective-permute-start | bytes 405512 | tf_op jit(solution)/shard_map/ppermute | solution.py:622
  71.1 13.4 %collective-permute-start.20 = (f32[264,128]{1,0:T(8,128)}, f32[264,128]{1,0:T(8,128)S(1)}, u32[]{:S(2)}, u32[]{:S(2)}) collective-permute-start(f32[264,128]{1,0:T(8,128)} %get-tuple-element.180), channel_id=1, source_target_pairs={{0,8},{4,12},{8,0},{12,4},{1,9},{5,13},{9,1},{13,5},{2,10},{6,14},... | collective-permute-start | bytes 405512 | tf_op jit(solution)/shard_map/ppermute | solution.py:622
  71.4 13.1 %collective-permute-start.21 = (f32[264,128]{1,0:T(8,128)}, f32[264,128]{1,0:T(8,128)S(1)}, u32[]{:S(2)}, u32[]{:S(2)}) collective-permute-start(f32[264,128]{1,0:T(8,128)} %get-tuple-element.179), channel_id=1, source_target_pairs={{0,12},{4,8},{8,4},{12,0},{1,13},{5,9},{9,5},{13,1},{2,14},{6,10},... | collective-permute-start | bytes 405512 | tf_op jit(solution)/shard_map/ppermute | solution.py:622
  88.5 6.9 %collective-permute-start.25 = (f32[512,128]{1,0:T(8,128)S(1)}, f32[512,128]{1,0:T(8,128)S(1)}, u32[]{:S(2)}, u32[]{:S(2)}) collective-permute-start(f32[512,128]{1,0:T(8,128)S(1)} %get-tuple-element.158.refs_2_.lower_ref), channel_id=1, source_target_pairs={{0,1},{1,0},{2,3},{3,2},{4,5},{5,4},{6,7},{7,6},{8,9},{9,8},{10,11... | collective-permute-start | bytes 786440 | tf_op jit(solution)/shard_map/ppermute | solution.py:622
  94.3 9.8 %collective-permute-start.24 = (f32[520,128]{1,0:T(8,128)S(1)}, f32[520,128]{1,0:T(8,128)S(1)}, u32[]{:S(2)}, u32[]{:S(2)}) collective-permute-start(f32[520,128]{1,0:T(8,128)S(1)} %get-tuple-element.159.refs_2_.upper_ref), channel_id=1, source_target_pairs={{0,1},{1,0},{2,3},{3,2},{4,5},{5,4},{6,7},{7,6},{8,9},{9,8},{10,11... | collective-permute-start | bytes 798728 | tf_op jit(solution)/shard_map/ppermute | solution.py:622
  94.8 9.1 %collective-permute-start.23 = (f32[520,128]{1,0:T(8,128)S(1)}, f32[520,128]{1,0:T(8,128)S(1)}, u32[]{:S(2)}, u32[]{:S(2)}) collective-permute-start(f32[520,128]{1,0:T(8,128)S(1)} %get-tuple-element.159.refs_2_.upper_ref), channel_id=1, source_target_pairs={{0,2},{2,0},{1,3},{3,1},{4,6},{6,4},{5,7},{7,5},{8,10},{10,8},{9,1... | collective-permute-start | bytes 798728 | tf_op jit(solution)/shard_map/ppermute | solution.py:622
  115.2 9.2 %collective-permute-start.29 = (f32[264,128]{1,0:T(8,128)S(1)}, f32[264,128]{1,0:T(8,128)S(1)}, u32[]{:S(2)}, u32[]{:S(2)}) collective-permute-start(f32[264,128]{1,0:T(8,128)S(1)} %get-tuple-element.177), channel_id=1, source_target_pairs={{0,4},{4,0},{8,12},{12,8},{1,5},{5,1},{9,13},{13,9},{2,6},{6,2},{1... | collective-permute-start | bytes 405512 | tf_op jit(solution)/shard_map/ppermute | solution.py:622
  118.6 13.2 %collective-permute-start.30 = (f32[264,128]{1,0:T(8,128)S(1)}, f32[264,128]{1,0:T(8,128)S(1)}, u32[]{:S(2)}, u32[]{:S(2)}) collective-permute-start(f32[264,128]{1,0:T(8,128)S(1)} %get-tuple-element.176), channel_id=1, source_target_pairs={{0,8},{4,12},{8,0},{12,4},{1,9},{5,13},{9,1},{13,5},{2,10},{6,14},... | collective-permute-start | bytes 405512 | tf_op jit(solution)/shard_map/ppermute | solution.py:622
  119.5 12.2 %collective-permute-start.31 = (f32[264,128]{1,0:T(8,128)S(1)}, f32[264,128]{1,0:T(8,128)S(1)}, u32[]{:S(2)}, u32[]{:S(2)}) collective-permute-start(f32[264,128]{1,0:T(8,128)S(1)} %get-tuple-element.175), channel_id=1, source_target_pairs={{0,12},{4,8},{8,4},{12,0},{1,13},{5,9},{9,5},{13,1},{2,14},{6,10},... | collective-permute-start | bytes 405512 | tf_op jit(solution)/shard_map/ppermute | solution.py:622
  (55 other events, 440.7 us)

commit v12 on v11

--- a/solution.py
+++ b/solution.py
@@ -531,10 +531,20 @@
 
 
 def image_kernel(
-    info_ref, owner_ref, a0, a1, a2, a3, diag_ref, own_ref, lower_ref, upper_ref, total
+    info_ref, owner_ref, a0, a1, a2, a3, diag_hbm, own_hbm, lower_ref, upper_ref, total,
+    diag_ref, own_ref, sems,
 ):
-    total[...] = diag_ref[...] * own_ref[...]
+    copies = [
+        pltpu.make_async_copy(diag_hbm, diag_ref, sems.at[0]),
+        pltpu.make_async_copy(own_hbm, own_ref, sems.at[1]),
+    ]
+    for copy in copies:
+        copy.start()
+    total[...] = jnp.zeros_like(total)
     add_arrived(info_ref, owner_ref, (a0, a1, a2, a3), total)
+    for copy in copies:
+        copy.wait()
+    total[...] += diag_ref[...] * own_ref[...]
     blocks = total.shape[0]
     cross = jnp.zeros((LANES, LANES), jnp.float32)
     square = jnp.zeros((LANES, LANES), jnp.float32)
@@ -561,14 +571,15 @@
     return pl.pallas_call(
         image_kernel,
         in_specs=[pl.BlockSpec(memory_space=pltpu.SMEM)] * 2
-        + [pl.BlockSpec(memory_space=pltpu.VMEM)] * 6,
+        + [pl.BlockSpec(memory_space=pltpu.VMEM)] * 4
+        + [pl.BlockSpec(memory_space=pl.ANY)] * 2,
         out_specs=[pl.BlockSpec(memory_space=pltpu.VMEM)] * 2,
-        scratch_shapes=[pltpu.VMEM(own.shape, jnp.float32)],
+        scratch_shapes=[pltpu.VMEM(own.shape, jnp.float32)] * 3 + [pltpu.SemaphoreType.DMA((2,))],
         out_shape=shapes,
         compiler_params=pltpu.CompilerParams(vmem_limit_bytes=SMALL_VMEM),
         cost_estimate=micros(3),
         name="owner_image",
-    )(info, owners, *arrived, diagonal, own)
+    )(info, owners, *arrived, *in_hbm(diagonal, own))
 
 
 def final_kernel(
@@ -648,7 +659,7 @@
     place = 2 * mpo + rep
     info = jnp.stack([place, place ^ 2, place ^ 1, place ^ 3, blk, rep, mpo]).astype(jnp.int32)
     bonds = environment.shape[0]
-    sizes = tuple(bonds * part // 6 for part in (2, 2, 1, 1))
+    sizes = tuple(bonds * part // 6 for part in (2, 2, 2))
     firsts = tuple(sum(sizes[:group]) for group in range(len(sizes)))
     entries = float(blocks * zs * rows * width)
 
@@ -684,7 +695,7 @@
         if group >= 2:
             total = apply_group(group - 2, after(vector, sent[group - 1]))[0]
             pieces[group][3] = after(pieces[group][3], total)
-        if group + 1 < len(sizes):
+        if group < 1:
             pieces[group][1] = after(pieces[group][1], pieces[group + 1][1])
         *own_set, send = own_operands(info, pieces[group])
         made.append(own_set)

time: 134 us -> 127 us (0.948)
  Pallas kernels: 48.2 us -> 45.3 us
  local copies, waits for them, and re-layouts: 4.03 us -> 1.82 us
    pallas_call x6 -> x5, Pallas kernels: 32.7 us -> 29.6 us  [apply_bonds(): pl.pallas_call(functools.partial(apply_kernel, plan), in_specs=[pl.BlockS...]
    unnamed x95 -> x69, local copies, waits for them, and re-layouts: 3.94 us -> 1.73 us
    pallas_call x1, Pallas kernels: 1.12 us -> 2.89 us  [owner_image(): pl.pallas_call(image_kernel, in_specs=[pl.BlockSpec(memory_space=pltpu.SM...]
    pallas_call x4 -> x3, Pallas kernels: 4.58 us -> 3.65 us  [cut_pieces(): pl.pallas_call(functools.partial(cut_kernel, first), grid_spec=pltpu.Pref...]
    ppermute x32 -> x28, starting transfers between devices: 39.1 us -> 38.3 us  [partner(): return lax.ppermute(x, axis, [(i, i ^ k) for i in range(size)])]
    ppermute x32 -> x28, waiting for transfers between devices: 40.2 us -> 39.5 us  [partner(): return lax.ppermute(x, axis, [(i, i ^ k) for i in range(size)])]
    pallas_call x4 -> x3, Pallas kernels: 4.87 us -> 4.23 us  [own_operands(): pl.pallas_call(own_operands_kernel, grid_spec=pltpu.PrefetchScalarGridSpe...]
  transfers between devices with their start and end apart: 32 -> 28, of which waited for: 13 -> 12; matrix products, arithmetic and copies ran while one was open for 0% -> 0% of each run, Pallas kernels for 24% -> 21%
where the time goes in v12:
time: 127 us
  Pallas kernels  45.3 us (36%)
  waiting for transfers between devices  39.5 us (31%)
  starting transfers between devices  38.3 us (30%)
  local copies, waits for them, and re-layouts  1.82 us (1%)
    ppermute x28, waiting for transfers between devices, partner(): return lax.ppermute(x, axis, [(i, i ^ k) for i in range(size)])  39.5 us
    ppermute x28, starting transfers between devices, partner(): return lax.ppermute(x, axis, [(i, i ^ k) for i in range(size)])  38.3 us
    pallas_call x5, Pallas kernels, apply_bonds(): pl.pallas_call(functools.partial(apply_kernel, plan), in_specs=[pl.BlockS...  29.6 us
    pallas_call x3, Pallas kernels, own_operands(): pl.pallas_call(own_operands_kernel, grid_spec=pltpu.PrefetchScalarGridSpe...  4.23 us
    pallas_call x3, Pallas kernels, cut_pieces(): pl.pallas_call(functools.partial(cut_kernel, first), grid_spec=pltpu.Pref...  3.65 us
    pallas_call x1, Pallas kernels, owner_image(): pl.pallas_call(image_kernel, in_specs=[pl.BlockSpec(memory_space=pltpu.SM...  2.89 us
  transfers between devices with their start and end apart: 28, of which 12 were waited for; matrix products, arithmetic and copies ran while one was open for 0% of the time, Pallas kernels for 21%

profile of v12, /device:TPU:0, one launch (start us, length us, event | category | flops | bytes accessed | tf_op | source)
XLA Modules:
  0.0 127.1 jit_solution(18387566243775990200)
XLA Ops:
  0.7 1.8 %cut_pieces.3 = (f32[2,8,16,128]{3,2,1,0:T(8,128)S(1)}, f32[2,8,16,128]{3,2,1,0:T(8,128)S(1)}, f32[2,8,16,128]{3,2,1,0:T(8,128)S(1)}, f32[2,8,16,128]{3,2,1,0:T(8,128)S(1)}) custom-call(s32[7]{0:T(128)S(1)} %stack.31.info_ref, f32[6,4,8,16,128]{4,3,2,1,0:T(8,128)} %bitcast.24), custom_call_target="tpu_custom_call" | custom-call | flops 1100000000 | bytes 1048576 | tf_op jit(solution)/shard_map/cut_pieces/pallas_call | solution.py:289
  2.6 3.1 %collective-permute-start = (f32[2,8,16,128]{3,2,1,0:T(8,128)S(1)}, f32[2,8,16,128]{3,2,1,0:T(8,128)S(1)}, u32[]{:S(2)}, u32[]{:S(2)}) collective-permute-start(f32[2,8,16,128]{3,2,1,0:T(8,128)S(1)} %get-tuple-element.68), channel_id=1, source_target_pairs={{0,4},{4,0},{8,12},{12,8},{1,5},{5,1},{9,13},{13,9},{2,6},{6,2},{1... | collective-permute-start | bytes 393224 | tf_op jit(solution)/shard_map/ppermute | solution.py:633
  5.6 2.6 %collective-permute-start.4 = (f32[2,8,16,128]{3,2,1,0:T(8,128)S(1)}, f32[2,8,16,128]{3,2,1,0:T(8,128)S(1)}, u32[]{:S(2)}, u32[]{:S(2)}) collective-permute-start(f32[2,8,16,128]{3,2,1,0:T(8,128)S(1)} %get-tuple-element.79), channel_id=1, source_target_pairs={{0,8},{4,12},{8,0},{12,4},{1,9},{5,13},{9,1},{13,5},{2,10},{6,14},... | collective-permute-start | bytes 393224 | tf_op jit(solution)/shard_map/ppermute | solution.py:633
  8.2 2.5 %pack.1 = (bf16[8,128,1024]{2,1,0:T(8,128)(2,1)S(1)}, f32[8,128,128]{2,1,0:T(8,128)S(1)}, f32[8,128,128]{2,1,0:T(8,128)S(1)}) custom-call(s32[7]{0:T(128)S(1)} %stack.31.info_ref, f32[8,64,1024]{2,1,0:T(8,128)S(1)} %copy-done.1, f32[8,64,1024]{2,1,0:T(8,128)S(1)} %copy-done.1, f32[8,64,256]{2,1,0:T(8,128)S(1)} %copy-done.3), custom_call_target="tpu_custom_call" | custom-call | flops 5500000256 | bytes 1048576 | tf_op jit(solution)/shard_map/pack/pallas_call | solution.py:139
  16.0 2.6 %collective-permute-done.4.refs_2_ = f32[2,8,16,128]{3,2,1,0:T(8,128)S(1)} collective-permute-done((f32[2,8,16,128]{3,2,1,0:T(8,128)S(1)}, f32[2,8,16,128]{3,2,1,0:T(8,128)S(1)}, u32[]{:S(2)}, u32[]{:S(2)}) %collective-permute-start.4) | collective-permute-done | bytes 131104 | tf_op jit(solution)/shard_map/ppermute | solution.py:633
  24.7 2.2 %collective-permute-done.8.refs_3_ = f32[2,8,16,128]{3,2,1,0:T(8,128)S(1)} collective-permute-done((f32[2,8,16,128]{3,2,1,0:T(8,128)S(1)}, f32[2,8,16,128]{3,2,1,0:T(8,128)S(1)}, u32[]{:S(2)}, u32[]{:S(2)}) %collective-permute-start.8) | collective-permute-done | bytes 131104 | tf_op jit(solution)/shard_map/ppermute | solution.py:633
  28.4 7.8 %collective-permute-start.3 = (f32[2,8,16,128]{3,2,1,0:T(8,128)S(1)}, f32[2,8,16,128]{3,2,1,0:T(8,128)S(1)}, u32[]{:S(2)}, u32[]{:S(2)}) collective-permute-start(f32[2,8,16,128]{3,2,1,0:T(8,128)S(1)} %get-tuple-element.76), channel_id=1, source_target_pairs={{0,4},{4,0},{8,12},{12,8},{1,5},{5,1},{9,13},{13,9},{2,6},{6,2},{1... | collective-permute-start | bytes 393224 | tf_op jit(solution)/shard_map/ppermute | solution.py:633
  39.1 5.0 %apply_bonds.5 = (f32[2,8,128,128]{3,2,1,0:T(8,128)S(1)}, bf16[2,8,64,128]{3,2,1,0:T(8,128)(2,1)S(1)}, bf16[2,8,64,128]{3,2,1,0:T(8,128)(2,1)S(1)}, bf16[8,64,256]{2,1,0:T(8,128)(2,1)S(1)}) custom-call(s32[7]{0:T(128)S(1)} %stack.31.info_ref, s32[6,8]{1,0:T(8,128)S(1)} %copy-done, s32[6,8]{1,0:T(8,128)S(1)} %collective-permute-done.1.refs_1_, ...), custom_call_target="tpu_custom_call" | custom-call | flops 1100000000 | bytes 1048576 | tf_op jit(solution)/shard_map/apply_bonds/pallas_call | solution.py:491
  47.8 5.1 %apply_bonds.6 = (f32[2,8,128,128]{3,2,1,0:T(8,128)S(1)}, bf16[2,8,64,128]{3,2,1,0:T(8,128)(2,1)S(1)}, bf16[2,8,64,128]{3,2,1,0:T(8,128)(2,1)S(1)}, bf16[8,64,256]{2,1,0:T(8,128)(2,1)S(1)}) custom-call(s32[7]{0:T(128)S(1)} %stack.31.info_ref, s32[6,8]{1,0:T(8,128)S(1)} %copy-done, ...), custom_call_target="tpu_custom_call", output_to_operand_aliasing={{0}: (10, {})} | custom-call | flops 1100000000 | bytes 1048576 | tf_op jit(solution)/shard_map/apply_bonds/pallas_call | solution.py:491
  52.9 3.9 %collective-permute-done.12.refs_6_ = f32[2,8,48,128]{3,2,1,0:T(8,128)S(1)} collective-permute-done((f32[2,8,48,128]{3,2,1,0:T(8,128)S(1)}, f32[2,8,48,128]{3,2,1,0:T(8,128)S(1)}, u32[]{:S(2)}, u32[]{:S(2)}) %collective-permute-start.12) | collective-permute-done | bytes 393248 | tf_op jit(solution)/shard_map/ppermute | solution.py:633
  56.8 4.9 %apply_bonds.7 = (f32[4,264,128]{2,1,0:T(8,128)S(1)}, f32[4,264,128]{2,1,0:T(8,128)S(1)}, bf16[2,8,64,128]{3,2,1,0:T(8,128)(2,1)S(1)}, bf16[2,8,64,128]{3,2,1,0:T(8,128)(2,1)S(1)}, bf16[8,64,256]{2,1,0:T(8,128)(2,1)S(1)}) custom-call(s32[7]{0:T(128)S(1)} %stack.31.info_ref, s32[6,8]{1,0:T(8,128)S(1)} %copy-done, s32[6,8]{1,0:T(8,128)S(1)} %collective-permute-done.1.refs_1_, ...), custom_call_target="tpu_custom_call" | custom-call | flops 1100000000 | bytes 1048576 | tf_op jit(solution)/shard_map/apply_bonds/pallas_call | solution.py:491
  61.8 1.9 %collective-permute-done.14 = f32[4,264,128]{2,1,0:T(8,128)S(1)} collective-permute-done((f32[4,264,128]{2,1,0:T(8,128)S(1)}, f32[4,264,128]{2,1,0:T(8,128)S(1)}, u32[]{:S(2)}, u32[]{:S(2)}) %collective-permute-start.14) | collective-permute-done | bytes 540704 | tf_op jit(solution)/shard_map/ppermute | solution.py:633
  67.1 1.9 %collective-permute-start.17 = (f32[264,128]{1,0:T(8,128)}, f32[264,128]{1,0:T(8,128)}, u32[]{:S(2)}, u32[]{:S(2)}) collective-permute-start(f32[264,128]{1,0:T(8,128)} %get-tuple-element.137), channel_id=1, source_target_pairs={{0,12},{4,8},{8,4},{12,0},{1,13},{5,9},{9,5},{13,1},{2,14},{6,10},... | collective-permute-start | bytes 405512 | tf_op jit(solution)/shard_map/ppermute | solution.py:633
  69.1 3.6 %collective-permute-done.15.a1 = f32[264,128]{1,0:T(8,128)S(1)} collective-permute-done((f32[264,128]{1,0:T(8,128)}, f32[264,128]{1,0:T(8,128)S(1)}, u32[]{:S(2)}, u32[]{:S(2)}) %collective-permute-start.15) | collective-permute-done | bytes 135200 | tf_op jit(solution)/shard_map/ppermute | solution.py:633
  72.7 6.2 %collective-permute-done.16.a2 = f32[264,128]{1,0:T(8,128)} collective-permute-done((f32[264,128]{1,0:T(8,128)}, f32[264,128]{1,0:T(8,128)}, u32[]{:S(2)}, u32[]{:S(2)}) %collective-permute-start.16) | collective-permute-done | bytes 135200 | tf_op jit(solution)/shard_map/ppermute | solution.py:633
  79.0 2.9 %owner_image.1 = (f32[512,128]{1,0:T(8,128)S(1)}, f32[520,128]{1,0:T(8,128)S(1)}) custom-call(s32[7]{0:T(128)S(1)} %stack.31.info_ref, s32[4,2]{1,0:T(4,128)S(1)} %copy.11.owner_ref, f32[264,128]{1,0:T(8,128)S(1)} %get-tuple-element.140.a0, f32[264,128]{1,0:T(8,128)S(1)} %collective-permute-done.15.a1, f32[264,128]{1,0:T(8,128)} %collective-permute-done.16.a2, ...), custom_call_target="tpu_custom_call" | custom-call | flops 3300000000 | bytes 1048576 | tf_op jit(solution)/shard_map/owner_image/pallas_call | solution.py:571
  83.1 5.3 %collective-permute-done.18.refs_3_ = f32[512,128]{1,0:T(8,128)S(1)} collective-permute-done((f32[512,128]{1,0:T(8,128)S(1)}, f32[512,128]{1,0:T(8,128)S(1)}, u32[]{:S(2)}, u32[]{:S(2)}) %collective-permute-start.18) | collective-permute-done | bytes 262176 | tf_op jit(solution)/shard_map/ppermute | solution.py:633
  90.2 7.5 %apply_bonds.8.refs_30_ = f32[2,8,128,128]{3,2,1,0:T(8,128)S(1)} custom-call(s32[7]{0:T(128)S(1)} %stack.31.info_ref, s32[6,8]{1,0:T(8,128)S(1)} %copy-done, s32[6,8]{1,0:T(8,128)S(1)} %collective-permute-done.1.refs_1_, f32[512,128]{1,0:T(8,128)S(1)} %get-tuple-element.119.refs_2_.lower_ref, f32[512,128]{1,0:T(8,128)S(1)} %collective-permute-done.18.refs_3_, ...), custom_call_target="tpu_custom_call" | custom-call | flops 11000000512 | bytes 1048576 | tf_op jit(solution)/shard_map/apply_bonds/pallas_call | solution.py:491
  99.3 7.1 %apply_bonds.9 = (f32[4,264,128]{2,1,0:T(8,128)S(1)}, f32[4,264,128]{2,1,0:T(8,128)S(1)}) custom-call(s32[7]{0:T(128)S(1)} %stack.31.info_ref, s32[6,8]{1,0:T(8,128)S(1)} %copy-done, s32[6,8]{1,0:T(8,128)S(1)} %collective-permute-done.1.refs_1_, f32[520,128]{1,0:T(8,128)S(1)} %get-tuple-element.120.refs_2_.upper_ref, ...), custom_call_target="tpu_custom_call" | custom-call | flops 11000000512 | bytes 1048576 | tf_op jit(solution)/shard_map/apply_bonds/pallas_call | solution.py:491
  106.7 1.8 %collective-permute-done.24 = f32[4,264,128]{2,1,0:T(8,128)S(1)} collective-permute-done((f32[4,264,128]{2,1,0:T(8,128)S(1)}, f32[4,264,128]{2,1,0:T(8,128)S(1)}, u32[]{:S(2)}, u32[]{:S(2)}) %collective-permute-start.24) | collective-permute-done | bytes 540704 | tf_op jit(solution)/shard_map/ppermute | solution.py:633
  108.6 3.2 %collective-permute-start.25 = (f32[264,128]{1,0:T(8,128)S(1)}, f32[264,128]{1,0:T(8,128)S(1)}, u32[]{:S(2)}, u32[]{:S(2)}) collective-permute-start(f32[264,128]{1,0:T(8,128)S(1)} %get-tuple-element.135), channel_id=1, source_target_pairs={{0,4},{4,0},{8,12},{12,8},{1,5},{5,1},{9,13},{13,9},{2,6},{6,2},{1... | collective-permute-start | bytes 405512 | tf_op jit(solution)/shard_map/ppermute | solution.py:633
  114.6 3.2 %collective-permute-done.25.a1 = f32[264,128]{1,0:T(8,128)S(1)} collective-permute-done((f32[264,128]{1,0:T(8,128)S(1)}, f32[264,128]{1,0:T(8,128)S(1)}, u32[]{:S(2)}, u32[]{:S(2)}) %collective-permute-start.25) | collective-permute-done | bytes 135200 | tf_op jit(solution)/shard_map/ppermute | solution.py:633
  117.8 7.2 %collective-permute-done.26.a2 = f32[264,128]{1,0:T(8,128)S(1)} collective-permute-done((f32[264,128]{1,0:T(8,128)S(1)}, f32[264,128]{1,0:T(8,128)S(1)}, u32[]{:S(2)}, u32[]{:S(2)}) %collective-permute-start.26) | collective-permute-done | bytes 135200 | tf_op jit(solution)/shard_map/ppermute | solution.py:633
  125.0 2.1 %outputs.1 = (f32[8,64,256]{2,1,0:T(8,128)}, f32[8,64,256]{2,1,0:T(8,128)}, f32[8,64,256]{2,1,0:T(8,128)}) custom-call(s32[7]{0:T(128)S(1)} %stack.31.info_ref, s32[4,2]{1,0:T(4,128)S(1)} %copy.11.owner_ref, f32[264,128]{1,0:T(8,128)S(1)} %get-tuple-element.136.a0, f32[264,128]{1,0:T(8,128)S(1)} %collective-permute-done.25.a1, ...), custom_call_target="tpu_custom_call" | custom-call | flops 4400000000 | bytes 1048576 | tf_op jit(solution)/shard_map/outputs/pallas_call | solution.py:610
  (119 shorter events, 30.5 us)
Async XLA Ops:
  2.6 10.0 %collective-permute-start = (f32[2,8,16,128]{3,2,1,0:T(8,128)S(1)}, f32[2,8,16,128]{3,2,1,0:T(8,128)S(1)}, u32[]{:S(2)}, u32[]{:S(2)}) collective-permute-start(f32[2,8,16,128]{3,2,1,0:T(8,128)S(1)} %get-tuple-element.68), channel_id=1, source_target_pairs={{0,4},{4,0},{8,12},{12,8},{1,5},{5,1},{9,13},{13,9},{2,6},{6,2},{1... | collective-permute-start | bytes 393224 | tf_op jit(solution)/shard_map/ppermute | solution.py:633
  5.6 12.9 %collective-permute-start.4 = (f32[2,8,16,128]{3,2,1,0:T(8,128)S(1)}, f32[2,8,16,128]{3,2,1,0:T(8,128)S(1)}, u32[]{:S(2)}, u32[]{:S(2)}) collective-permute-start(f32[2,8,16,128]{3,2,1,0:T(8,128)S(1)} %get-tuple-element.79), channel_id=1, source_target_pairs={{0,8},{4,12},{8,0},{12,4},{1,9},{5,13},{9,1},{13,5},{2,10},{6,14},... | collective-permute-start | bytes 393224 | tf_op jit(solution)/shard_map/ppermute | solution.py:633
  8.2 11.3 %collective-permute-start.7 = (f32[2,8,16,128]{3,2,1,0:T(8,128)S(1)}, f32[2,8,16,128]{3,2,1,0:T(8,128)S(1)}, u32[]{:S(2)}, u32[]{:S(2)}) collective-permute-start(f32[2,8,16,128]{3,2,1,0:T(8,128)S(1)} %get-tuple-element.84), channel_id=1, source_target_pairs={{0,12},{4,8},{8,4},{12,0},{1,13},{5,9},{9,5},{13,1},{2,14},{6,10},... | collective-permute-start | bytes 393224 | tf_op jit(solution)/shard_map/ppermute | solution.py:633
  12.6 9.8 %collective-permute-start.11 = (f32[6,16,16]{2,1,0:T(8,128)S(1)}, f32[6,16,16]{2,1,0:T(8,128)S(1)}, u32[]{:S(2)}, u32[]{:S(2)}) collective-permute-start(f32[6,16,16]{2,1,0:T(8,128)S(1)} %copy-done.12), channel_id=1, source_target_pairs={{0,2},{2,0},{1,3},{3,1},{4,6},{6,4},{5,7},{7,5},{8,10},{10,8},{9,1... | collective-permute-start | bytes 18440 | tf_op jit(solution)/shard_map/ppermute | solution.py:633
  15.3 7.4 %collective-permute-start.2 = (f32[2,8,16,128]{3,2,1,0:T(8,128)S(1)}, f32[2,8,16,128]{3,2,1,0:T(8,128)S(1)}, u32[]{:S(2)}, u32[]{:S(2)}) collective-permute-start(f32[2,8,16,128]{3,2,1,0:T(8,128)S(1)} %get-tuple-element.75), channel_id=1, source_target_pairs={{0,4},{4,0},{8,12},{12,8},{1,5},{5,1},{9,13},{13,9},{2,6},{6,2},{1... | collective-permute-start | bytes 393224 | tf_op jit(solution)/shard_map/ppermute | solution.py:633
  18.6 17.6 %collective-permute-start.5 = (f32[2,8,16,128]{3,2,1,0:T(8,128)S(1)}, f32[2,8,16,128]{3,2,1,0:T(8,128)S(1)}, u32[]{:S(2)}, u32[]{:S(2)}) collective-permute-start(f32[2,8,16,128]{3,2,1,0:T(8,128)S(1)} %get-tuple-element.80), channel_id=1, source_target_pairs={{0,8},{4,12},{8,0},{12,4},{1,9},{5,13},{9,1},{13,5},{2,10},{6,14},... | collective-permute-start | bytes 393224 | tf_op jit(solution)/shard_map/ppermute | solution.py:633
  19.5 7.4 %collective-permute-start.8 = (f32[2,8,16,128]{3,2,1,0:T(8,128)S(1)}, f32[2,8,16,128]{3,2,1,0:T(8,128)S(1)}, u32[]{:S(2)}, u32[]{:S(2)}) collective-permute-start(f32[2,8,16,128]{3,2,1,0:T(8,128)S(1)} %get-tuple-element.85), channel_id=1, source_target_pairs={{0,12},{4,8},{8,4},{12,0},{1,13},{5,9},{9,5},{13,1},{2,14},{6,10},... | collective-permute-start | bytes 393224 | tf_op jit(solution)/shard_map/ppermute | solution.py:633
  20.9 16.6 %collective-permute-start.1 = (s32[6,8]{1,0:T(8,128)S(1)}, s32[6,8]{1,0:T(8,128)S(1)}, u32[]{:S(2)}, u32[]{:S(2)}) collective-permute-start(s32[6,8]{1,0:T(8,128)S(1)} %copy-done), channel_id=1, source_target_pairs={{0,2},{2,0},{1,3},{3,1},{4,6},{6,4},{5,7},{7,5},{8,10},{10,8},{9,1... | collective-permute-start | bytes 584 | tf_op jit(solution)/shard_map/ppermute | solution.py:633
  24.1 15.0 %collective-permute-start.10 = (f32[2,8,48,128]{3,2,1,0:T(8,128)S(1)}, f32[2,8,48,128]{3,2,1,0:T(8,128)S(1)}, u32[]{:S(2)}, u32[]{:S(2)}) collective-permute-start(f32[2,8,48,128]{3,2,1,0:T(8,128)S(1)} %get-tuple-element.95), channel_id=1, source_target_pairs={{0,2},{2,0},{1,3},{3,1},{4,6},{6,4},{5,7},{7,5},{8,10},{10,8},{9,1... | collective-permute-start | bytes 1179656 | tf_op jit(solution)/shard_map/ppermute | solution.py:633
  26.9 17.9 %collective-permute-start.9 = (f32[2,8,16,128]{3,2,1,0:T(8,128)S(1)}, f32[2,8,16,128]{3,2,1,0:T(8,128)S(1)}, u32[]{:S(2)}, u32[]{:S(2)}) collective-permute-start(f32[2,8,16,128]{3,2,1,0:T(8,128)S(1)} %get-tuple-element.86), channel_id=1, source_target_pairs={{0,12},{4,8},{8,4},{12,0},{1,13},{5,9},{9,5},{13,1},{2,14},{6,10},... | collective-permute-start | bytes 393224 | tf_op jit(solution)/shard_map/ppermute | solution.py:633
  28.4 16.5 %collective-permute-start.3 = (f32[2,8,16,128]{3,2,1,0:T(8,128)S(1)}, f32[2,8,16,128]{3,2,1,0:T(8,128)S(1)}, u32[]{:S(2)}, u32[]{:S(2)}) collective-permute-start(f32[2,8,16,128]{3,2,1,0:T(8,128)S(1)} %get-tuple-element.76), channel_id=1, source_target_pairs={{0,4},{4,0},{8,12},{12,8},{1,5},{5,1},{9,13},{13,9},{2,6},{6,2},{1... | collective-permute-start | bytes 393224 | tf_op jit(solution)/shard_map/ppermute | solution.py:633
  36.2 8.7 %collective-permute-start.6 = (f32[2,8,16,128]{3,2,1,0:T(8,128)S(1)}, f32[2,8,16,128]{3,2,1,0:T(8,128)S(1)}, u32[]{:S(2)}, u32[]{:S(2)}) collective-permute-start(f32[2,8,16,128]{3,2,1,0:T(8,128)S(1)} %get-tuple-element.81), channel_id=1, source_target_pairs={{0,8},{4,12},{8,0},{12,4},{1,9},{5,13},{9,1},{13,5},{2,10},{6,14},... | collective-permute-start | bytes 393224 | tf_op jit(solution)/shard_map/ppermute | solution.py:633
  37.5 10.3 %collective-permute-start.13 = (f32[2,8,48,128]{3,2,1,0:T(8,128)S(1)}, f32[2,8,48,128]{3,2,1,0:T(8,128)S(1)}, u32[]{:S(2)}, u32[]{:S(2)}) collective-permute-start(f32[2,8,48,128]{3,2,1,0:T(8,128)S(1)} %get-tuple-element.88), channel_id=1, source_target_pairs={{0,2},{2,0},{1,3},{3,1},{4,6},{6,4},{5,7},{7,5},{8,10},{10,8},{9,1... | collective-permute-start | bytes 1179656 | tf_op jit(solution)/shard_map/ppermute | solution.py:633
  46.4 10.3 %collective-permute-start.12 = (f32[2,8,48,128]{3,2,1,0:T(8,128)S(1)}, f32[2,8,48,128]{3,2,1,0:T(8,128)S(1)}, u32[]{:S(2)}, u32[]{:S(2)}) collective-permute-start(f32[2,8,48,128]{3,2,1,0:T(8,128)S(1)} %get-tuple-element.104), channel_id=1, source_target_pairs={{0,2},{2,0},{1,3},{3,1},{4,6},{6,4},{5,7},{7,5},{8,10},{10,8},{9,1... | collective-permute-start | bytes 1179656 | tf_op jit(solution)/shard_map/ppermute | solution.py:633
  64.5 8.2 %collective-permute-start.15 = (f32[264,128]{1,0:T(8,128)}, f32[264,128]{1,0:T(8,128)S(1)}, u32[]{:S(2)}, u32[]{:S(2)}) collective-permute-start(f32[264,128]{1,0:T(8,128)} %get-tuple-element.139), channel_id=1, source_target_pairs={{0,4},{4,0},{8,12},{12,8},{1,5},{5,1},{9,13},{13,9},{2,6},{6,2},{1... | collective-permute-start | bytes 405512 | tf_op jit(solution)/shard_map/ppermute | solution.py:633
  65.4 13.5 %collective-permute-start.16 = (f32[264,128]{1,0:T(8,128)}, f32[264,128]{1,0:T(8,128)}, u32[]{:S(2)}, u32[]{:S(2)}) collective-permute-start(f32[264,128]{1,0:T(8,128)} %get-tuple-element.138), channel_id=1, source_target_pairs={{0,8},{4,12},{8,0},{12,4},{1,9},{5,13},{9,1},{13,5},{2,10},{6,14},... | collective-permute-start | bytes 405512 | tf_op jit(solution)/shard_map/ppermute | solution.py:633
  67.1 11.8 %collective-permute-start.17 = (f32[264,128]{1,0:T(8,128)}, f32[264,128]{1,0:T(8,128)}, u32[]{:S(2)}, u32[]{:S(2)}) collective-permute-start(f32[264,128]{1,0:T(8,128)} %get-tuple-element.137), channel_id=1, source_target_pairs={{0,12},{4,8},{8,4},{12,0},{1,13},{5,9},{9,5},{13,1},{2,14},{6,10},... | collective-permute-start | bytes 405512 | tf_op jit(solution)/shard_map/ppermute | solution.py:633
  81.9 6.5 %collective-permute-start.18 = (f32[512,128]{1,0:T(8,128)S(1)}, f32[512,128]{1,0:T(8,128)S(1)}, u32[]{:S(2)}, u32[]{:S(2)}) collective-permute-start(f32[512,128]{1,0:T(8,128)S(1)} %get-tuple-element.119.refs_2_.lower_ref), channel_id=1, source_target_pairs={{0,2},{2,0},{1,3},{3,1},{4,6},{6,4},{5,7},{7,5},{8,10},{10,8},{9,1... | collective-permute-start | bytes 786440 | tf_op jit(solution)/shard_map/ppermute | solution.py:633
  83.1 6.9 %collective-permute-start.21 = (f32[512,128]{1,0:T(8,128)S(1)}, f32[512,128]{1,0:T(8,128)S(1)}, u32[]{:S(2)}, u32[]{:S(2)}) collective-permute-start(f32[512,128]{1,0:T(8,128)S(1)} %get-tuple-element.119.refs_2_.lower_ref), channel_id=1, source_target_pairs={{0,1},{1,0},{2,3},{3,2},{4,5},{5,4},{6,7},{7,6},{8,9},{9,8},{10,11... | collective-permute-start | bytes 786440 | tf_op jit(solution)/shard_map/ppermute | solution.py:633
  88.4 9.4 %collective-permute-start.20 = (f32[520,128]{1,0:T(8,128)S(1)}, f32[520,128]{1,0:T(8,128)S(1)}, u32[]{:S(2)}, u32[]{:S(2)}) collective-permute-start(f32[520,128]{1,0:T(8,128)S(1)} %get-tuple-element.120.refs_2_.upper_ref), channel_id=1, source_target_pairs={{0,1},{1,0},{2,3},{3,2},{4,5},{5,4},{6,7},{7,6},{8,9},{9,8},{10,11... | collective-permute-start | bytes 798728 | tf_op jit(solution)/shard_map/ppermute | solution.py:633
  88.9 8.8 %collective-permute-start.19 = (f32[520,128]{1,0:T(8,128)S(1)}, f32[520,128]{1,0:T(8,128)S(1)}, u32[]{:S(2)}, u32[]{:S(2)}) collective-permute-start(f32[520,128]{1,0:T(8,128)S(1)} %get-tuple-element.120.refs_2_.upper_ref), channel_id=1, source_target_pairs={{0,2},{2,0},{1,3},{3,1},{4,6},{6,4},{5,7},{7,5},{8,10},{10,8},{9,1... | collective-permute-start | bytes 798728 | tf_op jit(solution)/shard_map/ppermute | solution.py:633
  108.6 9.2 %collective-permute-start.25 = (f32[264,128]{1,0:T(8,128)S(1)}, f32[264,128]{1,0:T(8,128)S(1)}, u32[]{:S(2)}, u32[]{:S(2)}) collective-permute-start(f32[264,128]{1,0:T(8,128)S(1)} %get-tuple-element.135), channel_id=1, source_target_pairs={{0,4},{4,0},{8,12},{12,8},{1,5},{5,1},{9,13},{13,9},{2,6},{6,2},{1... | collective-permute-start | bytes 405512 | tf_op jit(solution)/shard_map/ppermute | solution.py:633
  111.8 13.2 %collective-permute-start.26 = (f32[264,128]{1,0:T(8,128)S(1)}, f32[264,128]{1,0:T(8,128)S(1)}, u32[]{:S(2)}, u32[]{:S(2)}) collective-permute-start(f32[264,128]{1,0:T(8,128)S(1)} %get-tuple-element.134), channel_id=1, source_target_pairs={{0,8},{4,12},{8,0},{12,4},{1,9},{5,13},{9,1},{13,5},{2,10},{6,14},... | collective-permute-start | bytes 405512 | tf_op jit(solution)/shard_map/ppermute | solution.py:633
  113.2 11.8 %collective-permute-start.27 = (f32[264,128]{1,0:T(8,128)S(1)}, f32[264,128]{1,0:T(8,128)S(1)}, u32[]{:S(2)}, u32[]{:S(2)}) collective-permute-start(f32[264,128]{1,0:T(8,128)S(1)} %get-tuple-element.133), channel_id=1, source_target_pairs={{0,12},{4,8},{8,4},{12,0},{1,13},{5,9},{9,5},{13,1},{2,14},{6,10},... | collective-permute-start | bytes 405512 | tf_op jit(solution)/shard_map/ppermute | solution.py:633
  (38 other events, 347.1 us)

commit v13 on v12

--- a/solution.py
+++ b/solution.py
@@ -116,11 +116,14 @@
             put(row, pair, high, low)
 
 
-def pack_kernel(info_ref, wave_ref, own_wave_ref, diag_ref, vec_ref, own_ref, diag_out, tiles):
+def pack_kernel(
+    info_ref, wave_ref, own_wave_ref, diag_ref, vec_ref, own_ref, diag_out, start_ref, tiles
+):
     half = LANES // 2
     for j in range(wave_ref.shape[0]):
         own_ref[j] = pack_tile(own_wave_ref[j])
         diag_out[j] = pack_tile(diag_ref[j])
+        start_ref[j] = diag_out[j] * own_ref[j]
         for q in range(4):
             tiles[q, j] = pack_tile(wave_ref[j, :, 2 * LANES * q : 2 * LANES * (q + 1)])
 
@@ -146,14 +149,13 @@
                 pl.BlockSpec((step, rows, width // 4), lambda i, info: (i, 0, info[0])),
                 pl.BlockSpec((step, rows, width // 4), lambda i, *_: (i, 0, 0)),
             ],
-            out_specs=[pl.BlockSpec((step, LANES, width), lambda i, *_: (i, 0, 0)), tile, tile],
+            out_specs=[pl.BlockSpec((step, LANES, width), lambda i, *_: (i, 0, 0))] + [tile] * 3,
             scratch_shapes=[pltpu.VMEM((4, step, LANES, LANES), jnp.float32)],
         ),
         out_shape=[
             jax.ShapeDtypeStruct((blocks, LANES, width), jnp.bfloat16),
-            jax.ShapeDtypeStruct((blocks, LANES, LANES), jnp.float32),
-            jax.ShapeDtypeStruct((blocks, LANES, LANES), jnp.float32),
-        ],
+        ]
+        + [jax.ShapeDtypeStruct((blocks, LANES, LANES), jnp.float32)] * 3,
         compiler_params=pltpu.CompilerParams(vmem_limit_bytes=SMALL_VMEM),
         cost_estimate=micros(5),
         name="pack",
@@ -531,59 +533,83 @@
 
 
 def image_kernel(
-    info_ref, owner_ref, a0, a1, a2, a3, diag_hbm, own_hbm, lower_ref, upper_ref, total,
-    diag_ref, own_ref, sems,
+    info_ref, owner_ref, a3, a2, a1, a0, start_hbm, lower_ref, upper_ref, total, start_ref, sems
 ):
+    blocks = total.shape[0]
     copies = [
-        pltpu.make_async_copy(diag_hbm, diag_ref, sems.at[0]),
-        pltpu.make_async_copy(own_hbm, own_ref, sems.at[1]),
+        pltpu.make_async_copy(start_hbm.at[k], start_ref.at[k], sems.at[k]) for k in range(blocks)
     ]
     for copy in copies:
         copy.start()
     total[...] = jnp.zeros_like(total)
     add_arrived(info_ref, owner_ref, (a0, a1, a2, a3), total)
-    for copy in copies:
-        copy.wait()
-    total[...] += diag_ref[...] * own_ref[...]
-    blocks = total.shape[0]
+    for k in range(blocks):
+        copies[k].wait()
+        half = lower_ref if k < blocks // 2 else upper_ref
+        at = k % (blocks // 2) * LANES
+        half[at : at + LANES] = total[k] + start_ref[k]
+
+
+def owner_image(info, owners, arrived, start):
+    blocks = start.shape[0]
+    shape = jax.ShapeDtypeStruct((blocks // 2 * LANES, LANES), jnp.float32)
+    return pl.pallas_call(
+        image_kernel,
+        in_specs=[pl.BlockSpec(memory_space=pltpu.SMEM)] * 2
+        + [pl.BlockSpec(memory_space=pltpu.VMEM)] * 4
+        + [pl.BlockSpec(memory_space=pl.ANY)],
+        out_specs=[pl.BlockSpec(memory_space=pltpu.VMEM)] * 2,
+        scratch_shapes=[pltpu.VMEM(start.shape, jnp.float32)] * 2
+        + [pltpu.SemaphoreType.DMA((blocks,))],
+        out_shape=[shape, shape],
+        compiler_params=pltpu.CompilerParams(vmem_limit_bytes=SMALL_VMEM),
+        cost_estimate=micros(1),
+        name="owner_image",
+    )(info, owners, *arrived[::-1], *in_hbm(start))
+
+
+def statistics_kernel(own_hbm, lower_ref, upper_ref, out_ref, own_ref, sem):
+    copy = pltpu.make_async_copy(own_hbm, own_ref, sem)
+    copy.start()
+    rows = upper_ref.shape[0]
+    out_ref[0:rows] = upper_ref[...]
+    copy.wait()
+    blocks = own_ref.shape[0]
+    images = []
+    for half in (lower_ref, upper_ref):
+        images += [half.at[pl.ds(k * LANES, LANES)] for k in range(blocks // 2)]
     cross = jnp.zeros((LANES, LANES), jnp.float32)
     square = jnp.zeros((LANES, LANES), jnp.float32)
     for k in range(blocks):
-        own, image = own_ref[k], total[k]
-        half = lower_ref if k < blocks // 2 else upper_ref
-        at = k % (blocks // 2) * LANES
-        half[at : at + LANES] = image
-        cross += own * image
+        own = own_ref[k]
+        cross += own * images[k][...]
         square += own * own
     cross = jnp.sum(cross, keepdims=True)
     square = jnp.sum(square, keepdims=True)
     ratio = cross / jnp.maximum(square, TINY)
     rest = jnp.zeros((LANES, LANES), jnp.float32)
     for k in range(blocks):
-        apart = total[k] - ratio * own_ref[k]
+        apart = images[k][...] - ratio * own_ref[k]
         rest += apart * apart
-    upper_ref[blocks // 2 * LANES :] = stacked_rows(cross, square, jnp.sum(rest, keepdims=True))
-
-
-def owner_image(info, owners, arrived, diagonal, own):
-    rows = own.shape[0] // 2 * LANES
-    shapes = [jax.ShapeDtypeStruct((n, LANES), jnp.float32) for n in (rows, rows + SUB)]
+    out_ref[rows:] = stacked_rows(cross, square, jnp.sum(rest, keepdims=True))
+
+
+def with_statistics(own, lower, upper):
     return pl.pallas_call(
-        image_kernel,
-        in_specs=[pl.BlockSpec(memory_space=pltpu.SMEM)] * 2
-        + [pl.BlockSpec(memory_space=pltpu.VMEM)] * 4
-        + [pl.BlockSpec(memory_space=pl.ANY)] * 2,
-        out_specs=[pl.BlockSpec(memory_space=pltpu.VMEM)] * 2,
-        scratch_shapes=[pltpu.VMEM(own.shape, jnp.float32)] * 3 + [pltpu.SemaphoreType.DMA((2,))],
-        out_shape=shapes,
+        statistics_kernel,
+        in_specs=[pl.BlockSpec(memory_space=pl.ANY)]
+        + [pl.BlockSpec(memory_space=pltpu.VMEM)] * 2,
+        out_specs=pl.BlockSpec(memory_space=pltpu.VMEM),
+        scratch_shapes=[pltpu.VMEM(own.shape, jnp.float32), pltpu.SemaphoreType.DMA],
+        out_shape=jax.ShapeDtypeStruct((upper.shape[0] + SUB, LANES), jnp.float32),
         compiler_params=pltpu.CompilerParams(vmem_limit_bytes=SMALL_VMEM),
         cost_estimate=micros(3),
-        name="owner_image",
-    )(info, owners, *arrived, *in_hbm(diagonal, own))
+        name="statistics",
+    )(*in_hbm(own), lower, upper)
 
 
 def final_kernel(
-    entries, info_ref, owner_ref, a0, a1, a2, a3, diag_ref, own_ref, lower_ref, upper_ref,
+    entries, info_ref, owner_ref, a3, a2, a1, a0, diag_ref, own_ref, lower_ref, upper_ref,
     first_ref, vector_ref, second_ref, total,
 ):
     arrived = (a0, a1, a2, a3)
@@ -621,7 +647,7 @@
         compiler_params=pltpu.CompilerParams(vmem_limit_bytes=SMALL_VMEM),
         cost_estimate=micros(4),
         name="outputs",
-    )(info, owners, *arrived, diagonal, own, *images)
+    )(info, owners, *arrived[::-1], diagonal, own, *images)
 
 
 def in_hbm(*arrays):
@@ -663,7 +689,7 @@
     firsts = tuple(sum(sizes[:group]) for group in range(len(sizes)))
     entries = float(blocks * zs * rows * width)
 
-    vector, own, diagonal_packed = pack(info, wavefunction, diagonal)
+    vector, own, diagonal_packed, start = pack(info, wavefunction, diagonal)
 
     by_owner = environment.reshape(bonds, zs, blocks, rows // zs, 2 * rows)
     pieces = []
@@ -702,11 +728,13 @@
         sent.append(send)
     total = apply_group(len(sizes) - 2, after(vector, sent[-1]))[0]
     out = apply_group(len(sizes) - 1, vector)
-    lower, upper = owner_image(info, slot_block, to_owners(*out), diagonal_packed, own)
+    lower, upper = owner_image(info, slot_block, to_owners(*out), start)
+    upper = with_statistics(own, lower, upper)
 
     chunks = [(source, first) for first in firsts for source in range(2)]
     mixes = [mixing[source][group] for group in range(len(sizes)) for source in range(2)]
-    lower_parts = gathered(lower)
+    lower_parts = [lower, partner(lower, "mpo", 1), partner(lower, "rep", 1)]
+    lower_parts.append(partner(after(lower_parts[1], upper), "rep", 1))
     across = partner(after(upper, lower_parts[1]), "mpo", 1)
     out, _ = apply_bonds(
         info, slots, lower_parts, chunks, operands, None, mixes, None, False, 0

time: 127 us -> 125 us (0.984)
  starting transfers between devices: 38.3 us -> 35.8 us
    ppermute x28, starting transfers between devices: 38.3 us -> 35.8 us  [partner(): return lax.ppermute(x, axis, [(i, i ^ k) for i in range(size)])]
    pallas_call x0 -> x1, Pallas kernels: none -> 1.6 us  [with_statistics(): pl.pallas_call(statistics_kernel, in_specs=[pl.BlockSpec(memory_space=pl....]
  transfers between devices with their start and end apart: 28 -> 28, of which waited for: 12 -> 12; matrix products, arithmetic and copies ran while one was open for 0% -> 0% of each run, Pallas kernels for 21% -> 22%
where the time goes in v13:
time: 125 us
  Pallas kernels  46 us (37%)
  waiting for transfers between devices  39.5 us (32%)
  starting transfers between devices  35.8 us (29%)
  local copies, waits for them, and re-layouts  1.73 us (1%)
    ppermute x28, waiting for transfers between devices, partner(): return lax.ppermute(x, axis, [(i, i ^ k) for i in range(size)])  39.5 us
    ppermute x28, starting transfers between devices, partner(): return lax.ppermute(x, axis, [(i, i ^ k) for i in range(size)])  35.8 us
    pallas_call x5, Pallas kernels, apply_bonds(): pl.pallas_call(functools.partial(apply_kernel, plan), in_specs=[pl.BlockS...  29.5 us
    pallas_call x3, Pallas kernels, own_operands(): pl.pallas_call(own_operands_kernel, grid_spec=pltpu.PrefetchScalarGridSpe...  4.23 us
    pallas_call x3, Pallas kernels, cut_pieces(): pl.pallas_call(functools.partial(cut_kernel, first), grid_spec=pltpu.Pref...  3.66 us
    pallas_call x1, Pallas kernels, pack(): pl.pallas_call(pack_kernel, grid_spec=pltpu.PrefetchScalarGridSpec(num_sc...  2.55 us
  transfers between devices with their start and end apart: 28, of which 12 were waited for; matrix products, arithmetic and copies ran while one was open for 0% of the time, Pallas kernels for 22%

profile of v13, /device:TPU:0, one launch (start us, length us, event | category | flops | bytes accessed | tf_op | source)
XLA Modules:
  0.0 125.2 jit_solution(1502791800520512093)
XLA Ops:
  0.7 1.8 %cut_pieces.3 = (f32[2,8,16,128]{3,2,1,0:T(8,128)S(1)}, f32[2,8,16,128]{3,2,1,0:T(8,128)S(1)}, f32[2,8,16,128]{3,2,1,0:T(8,128)S(1)}, f32[2,8,16,128]{3,2,1,0:T(8,128)S(1)}) custom-call(s32[7]{0:T(128)S(1)} %stack.31.info_ref, f32[6,4,8,16,128]{4,3,2,1,0:T(8,128)} %bitcast.24), custom_call_target="tpu_custom_call" | custom-call | flops 1100000000 | bytes 1048576 | tf_op jit(solution)/shard_map/cut_pieces/pallas_call | solution.py:291
  2.6 3.1 %collective-permute-start = (f32[2,8,16,128]{3,2,1,0:T(8,128)S(1)}, f32[2,8,16,128]{3,2,1,0:T(8,128)S(1)}, u32[]{:S(2)}, u32[]{:S(2)}) collective-permute-start(f32[2,8,16,128]{3,2,1,0:T(8,128)S(1)} %get-tuple-element.70), channel_id=1, source_target_pairs={{0,4},{4,0},{8,12},{12,8},{1,5},{5,1},{9,13},{13,9},{2,6},{6,2},{1... | collective-permute-start | bytes 393224 | tf_op jit(solution)/shard_map/ppermute | solution.py:659
  5.6 2.6 %collective-permute-start.4 = (f32[2,8,16,128]{3,2,1,0:T(8,128)S(1)}, f32[2,8,16,128]{3,2,1,0:T(8,128)S(1)}, u32[]{:S(2)}, u32[]{:S(2)}) collective-permute-start(f32[2,8,16,128]{3,2,1,0:T(8,128)S(1)} %get-tuple-element.82), channel_id=1, source_target_pairs={{0,8},{4,12},{8,0},{12,4},{1,9},{5,13},{9,1},{13,5},{2,10},{6,14},... | collective-permute-start | bytes 393224 | tf_op jit(solution)/shard_map/ppermute | solution.py:659
  8.2 2.5 %pack.1 = (bf16[8,128,1024]{2,1,0:T(8,128)(2,1)S(1)}, f32[8,128,128]{2,1,0:T(8,128)S(1)}, f32[8,128,128]{2,1,0:T(8,128)S(1)}, f32[8,128,128]{2,1,0:T(8,128)S(1)}) custom-call(s32[7]{0:T(128)S(1)} %stack.31.info_ref, f32[8,64,1024]{2,1,0:T(8,128)S(1)} %copy-done.1, f32[8,64,1024]{2,1,0:T(8,128)S(1)} %copy-done.1, f32[8,64,256]{2,1,0:T(8,128)S(1)} %copy-done.3), custom_call_target="tpu_custom_call" | custom-call | flops 5500000256 | bytes 1048576 | tf_op jit(solution)/shard_map/pack/pallas_call | solution.py:142
  15.3 3.3 %collective-permute-done.4.refs_2_ = f32[2,8,16,128]{3,2,1,0:T(8,128)S(1)} collective-permute-done((f32[2,8,16,128]{3,2,1,0:T(8,128)S(1)}, f32[2,8,16,128]{3,2,1,0:T(8,128)S(1)}, u32[]{:S(2)}, u32[]{:S(2)}) %collective-permute-start.4) | collective-permute-done | bytes 131104 | tf_op jit(solution)/shard_map/ppermute | solution.py:659
  18.8 2.1 %collective-permute-start.8 = (f32[2,8,16,128]{3,2,1,0:T(8,128)S(1)}, f32[2,8,16,128]{3,2,1,0:T(8,128)S(1)}, u32[]{:S(2)}, u32[]{:S(2)}) collective-permute-start(f32[2,8,16,128]{3,2,1,0:T(8,128)S(1)} %get-tuple-element.88), channel_id=1, source_target_pairs={{0,12},{4,8},{8,4},{12,0},{1,13},{5,9},{9,5},{13,1},{2,14},{6,10},... | collective-permute-start | bytes 393224 | tf_op jit(solution)/shard_map/ppermute | solution.py:659
  27.7 8.5 %collective-permute-start.3 = (f32[2,8,16,128]{3,2,1,0:T(8,128)S(1)}, f32[2,8,16,128]{3,2,1,0:T(8,128)S(1)}, u32[]{:S(2)}, u32[]{:S(2)}) collective-permute-start(f32[2,8,16,128]{3,2,1,0:T(8,128)S(1)} %get-tuple-element.79), channel_id=1, source_target_pairs={{0,4},{4,0},{8,12},{12,8},{1,5},{5,1},{9,13},{13,9},{2,6},{6,2},{1... | collective-permute-start | bytes 393224 | tf_op jit(solution)/shard_map/ppermute | solution.py:659
  39.1 5.0 %apply_bonds.5 = (f32[2,8,128,128]{3,2,1,0:T(8,128)S(1)}, bf16[2,8,64,128]{3,2,1,0:T(8,128)(2,1)S(1)}, bf16[2,8,64,128]{3,2,1,0:T(8,128)(2,1)S(1)}, bf16[8,64,256]{2,1,0:T(8,128)(2,1)S(1)}) custom-call(s32[7]{0:T(128)S(1)} %stack.31.info_ref, s32[6,8]{1,0:T(8,128)S(1)} %copy-done, s32[6,8]{1,0:T(8,128)S(1)} %collective-permute-done.1.refs_1_, ...), custom_call_target="tpu_custom_call" | custom-call | flops 1100000000 | bytes 1048576 | tf_op jit(solution)/shard_map/apply_bonds/pallas_call | solution.py:493
  47.8 5.1 %apply_bonds.6 = (f32[2,8,128,128]{3,2,1,0:T(8,128)S(1)}, bf16[2,8,64,128]{3,2,1,0:T(8,128)(2,1)S(1)}, bf16[2,8,64,128]{3,2,1,0:T(8,128)(2,1)S(1)}, bf16[8,64,256]{2,1,0:T(8,128)(2,1)S(1)}) custom-call(s32[7]{0:T(128)S(1)} %stack.31.info_ref, s32[6,8]{1,0:T(8,128)S(1)} %copy-done, ...), custom_call_target="tpu_custom_call", output_to_operand_aliasing={{0}: (10, {})} | custom-call | flops 1100000000 | bytes 1048576 | tf_op jit(solution)/shard_map/apply_bonds/pallas_call | solution.py:493
  52.9 4.1 %collective-permute-done.12.refs_6_ = f32[2,8,48,128]{3,2,1,0:T(8,128)S(1)} collective-permute-done((f32[2,8,48,128]{3,2,1,0:T(8,128)S(1)}, f32[2,8,48,128]{3,2,1,0:T(8,128)S(1)}, u32[]{:S(2)}, u32[]{:S(2)}) %collective-permute-start.12) | collective-permute-done | bytes 393248 | tf_op jit(solution)/shard_map/ppermute | solution.py:659
  57.0 4.9 %apply_bonds.7 = (f32[4,264,128]{2,1,0:T(8,128)S(1)}, f32[4,264,128]{2,1,0:T(8,128)S(1)}, bf16[2,8,64,128]{3,2,1,0:T(8,128)(2,1)S(1)}, bf16[2,8,64,128]{3,2,1,0:T(8,128)(2,1)S(1)}, bf16[8,64,256]{2,1,0:T(8,128)(2,1)S(1)}) custom-call(s32[7]{0:T(128)S(1)} %stack.31.info_ref, s32[6,8]{1,0:T(8,128)S(1)} %copy-done, s32[6,8]{1,0:T(8,128)S(1)} %collective-permute-done.1.refs_1_, ...), custom_call_target="tpu_custom_call" | custom-call | flops 1100000000 | bytes 1048576 | tf_op jit(solution)/shard_map/apply_bonds/pallas_call | solution.py:493
  62.1 1.9 %collective-permute-done.14 = f32[4,264,128]{2,1,0:T(8,128)S(1)} collective-permute-done((f32[4,264,128]{2,1,0:T(8,128)S(1)}, f32[4,264,128]{2,1,0:T(8,128)S(1)}, u32[]{:S(2)}, u32[]{:S(2)}) %collective-permute-start.14) | collective-permute-done | bytes 540704 | tf_op jit(solution)/shard_map/ppermute | solution.py:659
  69.3 4.0 %collective-permute-done.15.a3 = f32[264,128]{1,0:T(8,128)S(1)} collective-permute-done((f32[264,128]{1,0:T(8,128)}, f32[264,128]{1,0:T(8,128)S(1)}, u32[]{:S(2)}, u32[]{:S(2)}) %collective-permute-start.15) | collective-permute-done | bytes 135200 | tf_op jit(solution)/shard_map/ppermute | solution.py:659
  73.4 6.8 %collective-permute-done.16.a2 = f32[264,128]{1,0:T(8,128)} collective-permute-done((f32[264,128]{1,0:T(8,128)}, f32[264,128]{1,0:T(8,128)}, u32[]{:S(2)}, u32[]{:S(2)}) %collective-permute-start.16) | collective-permute-done | bytes 135200 | tf_op jit(solution)/shard_map/ppermute | solution.py:659
  80.2 2.1 %owner_image.1 = (f32[512,128]{1,0:T(8,128)S(1)}, f32[512,128]{1,0:T(8,128)S(1)}) custom-call(s32[7]{0:T(128)S(1)} %stack.31.info_ref, s32[4,2]{1,0:T(4,128)S(1)} %copy.11.owner_ref, f32[264,128]{1,0:T(8,128)S(1)} %collective-permute-done.15.a3, f32[264,128]{1,0:T(8,128)} %collective-permute-done.16.a2, f32[264,128]{1,0:T(8,128)} %collective-permute-done.17.a1, ...), custom_call_target="tpu_custom_call" | custom-call | flops 1100000000 | bytes 1048576 | tf_op jit(solution)/shard_map/owner_image/pallas_call | solution.py:556
  84.7 5.1 %collective-permute-done.18.refs_3_ = f32[512,128]{1,0:T(8,128)S(1)} collective-permute-done((f32[512,128]{1,0:T(8,128)S(1)}, f32[512,128]{1,0:T(8,128)S(1)}, u32[]{:S(2)}, u32[]{:S(2)}) %collective-permute-start.18) | collective-permute-done | bytes 262176 | tf_op jit(solution)/shard_map/ppermute | solution.py:659
  91.5 7.3 %apply_bonds.8.refs_30_ = f32[2,8,128,128]{3,2,1,0:T(8,128)S(1)} custom-call(s32[7]{0:T(128)S(1)} %stack.31.info_ref, s32[6,8]{1,0:T(8,128)S(1)} %copy-done, s32[6,8]{1,0:T(8,128)S(1)} %collective-permute-done.1.refs_1_, f32[512,128]{1,0:T(8,128)S(1)} %get-tuple-element.120.lower_ref.refs_2_, f32[512,128]{1,0:T(8,128)S(1)} %collective-permute-done.18.refs_3_, ...), custom_call_target="tpu_custom_call" | custom-call | flops 11000000512 | bytes 1048576 | tf_op jit(solution)/shard_map/apply_bonds/pallas_call | solution.py:493
  100.5 7.1 %apply_bonds.9 = (f32[4,264,128]{2,1,0:T(8,128)S(1)}, f32[4,264,128]{2,1,0:T(8,128)S(1)}) custom-call(s32[7]{0:T(128)S(1)} %stack.31.info_ref, s32[6,8]{1,0:T(8,128)S(1)} %copy-done, s32[6,8]{1,0:T(8,128)S(1)} %collective-permute-done.1.refs_1_, f32[520,128]{1,0:T(8,128)S(1)} %statistics.1.refs_2_.upper_ref, f32[520,128]{1,0:T(8,128)S(1)} %collective-permute-done.19.refs_3_, ...), custom_call_target="tpu_custom_call" | custom-call | flops 11000000512 | bytes 1048576 | tf_op jit(solution)/shard_map/apply_bonds/pallas_call | solution.py:493
  107.8 1.8 %collective-permute-done.24 = f32[4,264,128]{2,1,0:T(8,128)S(1)} collective-permute-done((f32[4,264,128]{2,1,0:T(8,128)S(1)}, f32[4,264,128]{2,1,0:T(8,128)S(1)}, u32[]{:S(2)}, u32[]{:S(2)}) %collective-permute-start.24) | collective-permute-done | bytes 540704 | tf_op jit(solution)/shard_map/ppermute | solution.py:659
  109.7 2.5 %collective-permute-start.25 = (f32[264,128]{1,0:T(8,128)S(1)}, f32[264,128]{1,0:T(8,128)S(1)}, u32[]{:S(2)}, u32[]{:S(2)}) collective-permute-start(f32[264,128]{1,0:T(8,128)S(1)} %get-tuple-element.140), channel_id=1, source_target_pairs={{0,12},{4,8},{8,4},{12,0},{1,13},{5,9},{9,5},{13,1},{2,14},{6,10},... | collective-permute-start | bytes 405512 | tf_op jit(solution)/shard_map/ppermute | solution.py:659
  112.2 2.0 %collective-permute-start.27 = (f32[264,128]{1,0:T(8,128)S(1)}, f32[264,128]{1,0:T(8,128)S(1)}, u32[]{:S(2)}, u32[]{:S(2)}) collective-permute-start(f32[264,128]{1,0:T(8,128)S(1)} %get-tuple-element.138), channel_id=1, source_target_pairs={{0,4},{4,0},{8,12},{12,8},{1,5},{5,1},{9,13},{13,9},{2,6},{6,2},{1... | collective-permute-start | bytes 405512 | tf_op jit(solution)/shard_map/ppermute | solution.py:659
  114.1 4.0 %collective-permute-done.25.a3 = f32[264,128]{1,0:T(8,128)S(1)} collective-permute-done((f32[264,128]{1,0:T(8,128)S(1)}, f32[264,128]{1,0:T(8,128)S(1)}, u32[]{:S(2)}, u32[]{:S(2)}) %collective-permute-start.25) | collective-permute-done | bytes 135200 | tf_op jit(solution)/shard_map/ppermute | solution.py:659
  118.1 5.0 %collective-permute-done.26.a2 = f32[264,128]{1,0:T(8,128)S(1)} collective-permute-done((f32[264,128]{1,0:T(8,128)S(1)}, f32[264,128]{1,0:T(8,128)S(1)}, u32[]{:S(2)}, u32[]{:S(2)}) %collective-permute-start.26) | collective-permute-done | bytes 135200 | tf_op jit(solution)/shard_map/ppermute | solution.py:659
  123.1 2.1 %outputs.1 = (f32[8,64,256]{2,1,0:T(8,128)}, f32[8,64,256]{2,1,0:T(8,128)}, f32[8,64,256]{2,1,0:T(8,128)}) custom-call(s32[7]{0:T(128)S(1)} %stack.31.info_ref, s32[4,2]{1,0:T(4,128)S(1)} %copy.11.owner_ref, f32[264,128]{1,0:T(8,128)S(1)} %collective-permute-done.25.a3, f32[264,128]{1,0:T(8,128)S(1)} %collective-permute-done.26.a2, ...), custom_call_target="tpu_custom_call" | custom-call | flops 4400000000 | bytes 1048576 | tf_op jit(solution)/shard_map/outputs/pallas_call | solution.py:636
  (122 shorter events, 29.2 us)
Async XLA Ops:
  2.6 9.3 %collective-permute-start = (f32[2,8,16,128]{3,2,1,0:T(8,128)S(1)}, f32[2,8,16,128]{3,2,1,0:T(8,128)S(1)}, u32[]{:S(2)}, u32[]{:S(2)}) collective-permute-start(f32[2,8,16,128]{3,2,1,0:T(8,128)S(1)} %get-tuple-element.70), channel_id=1, source_target_pairs={{0,4},{4,0},{8,12},{12,8},{1,5},{5,1},{9,13},{13,9},{2,6},{6,2},{1... | collective-permute-start | bytes 393224 | tf_op jit(solution)/shard_map/ppermute | solution.py:659
  5.6 12.9 %collective-permute-start.4 = (f32[2,8,16,128]{3,2,1,0:T(8,128)S(1)}, f32[2,8,16,128]{3,2,1,0:T(8,128)S(1)}, u32[]{:S(2)}, u32[]{:S(2)}) collective-permute-start(f32[2,8,16,128]{3,2,1,0:T(8,128)S(1)} %get-tuple-element.82), channel_id=1, source_target_pairs={{0,8},{4,12},{8,0},{12,4},{1,9},{5,13},{9,1},{13,5},{2,10},{6,14},... | collective-permute-start | bytes 393224 | tf_op jit(solution)/shard_map/ppermute | solution.py:659
  8.2 10.6 %collective-permute-start.7 = (f32[2,8,16,128]{3,2,1,0:T(8,128)S(1)}, f32[2,8,16,128]{3,2,1,0:T(8,128)S(1)}, u32[]{:S(2)}, u32[]{:S(2)}) collective-permute-start(f32[2,8,16,128]{3,2,1,0:T(8,128)S(1)} %get-tuple-element.87), channel_id=1, source_target_pairs={{0,12},{4,8},{8,4},{12,0},{1,13},{5,9},{9,5},{13,1},{2,14},{6,10},... | collective-permute-start | bytes 393224 | tf_op jit(solution)/shard_map/ppermute | solution.py:659
  11.8 10.7 %collective-permute-start.11 = (f32[6,16,16]{2,1,0:T(8,128)S(1)}, f32[6,16,16]{2,1,0:T(8,128)S(1)}, u32[]{:S(2)}, u32[]{:S(2)}) collective-permute-start(f32[6,16,16]{2,1,0:T(8,128)S(1)} %copy-done.12), channel_id=1, source_target_pairs={{0,2},{2,0},{1,3},{3,1},{4,6},{6,4},{5,7},{7,5},{8,10},{10,8},{9,1... | collective-permute-start | bytes 18440 | tf_op jit(solution)/shard_map/ppermute | solution.py:659
  14.6 8.3 %collective-permute-start.2 = (f32[2,8,16,128]{3,2,1,0:T(8,128)S(1)}, f32[2,8,16,128]{3,2,1,0:T(8,128)S(1)}, u32[]{:S(2)}, u32[]{:S(2)}) collective-permute-start(f32[2,8,16,128]{3,2,1,0:T(8,128)S(1)} %get-tuple-element.78), channel_id=1, source_target_pairs={{0,4},{4,0},{8,12},{12,8},{1,5},{5,1},{9,13},{13,9},{2,6},{6,2},{1... | collective-permute-start | bytes 393224 | tf_op jit(solution)/shard_map/ppermute | solution.py:659
  18.6 17.6 %collective-permute-start.5 = (f32[2,8,16,128]{3,2,1,0:T(8,128)S(1)}, f32[2,8,16,128]{3,2,1,0:T(8,128)S(1)}, u32[]{:S(2)}, u32[]{:S(2)}) collective-permute-start(f32[2,8,16,128]{3,2,1,0:T(8,128)S(1)} %get-tuple-element.83), channel_id=1, source_target_pairs={{0,8},{4,12},{8,0},{12,4},{1,9},{5,13},{9,1},{13,5},{2,10},{6,14},... | collective-permute-start | bytes 393224 | tf_op jit(solution)/shard_map/ppermute | solution.py:659
  18.8 7.6 %collective-permute-start.8 = (f32[2,8,16,128]{3,2,1,0:T(8,128)S(1)}, f32[2,8,16,128]{3,2,1,0:T(8,128)S(1)}, u32[]{:S(2)}, u32[]{:S(2)}) collective-permute-start(f32[2,8,16,128]{3,2,1,0:T(8,128)S(1)} %get-tuple-element.88), channel_id=1, source_target_pairs={{0,12},{4,8},{8,4},{12,0},{1,13},{5,9},{9,5},{13,1},{2,14},{6,10},... | collective-permute-start | bytes 393224 | tf_op jit(solution)/shard_map/ppermute | solution.py:659
  20.9 16.6 %collective-permute-start.1 = (s32[6,8]{1,0:T(8,128)S(1)}, s32[6,8]{1,0:T(8,128)S(1)}, u32[]{:S(2)}, u32[]{:S(2)}) collective-permute-start(s32[6,8]{1,0:T(8,128)S(1)} %copy-done), channel_id=1, source_target_pairs={{0,2},{2,0},{1,3},{3,1},{4,6},{6,4},{5,7},{7,5},{8,10},{10,8},{9,1... | collective-permute-start | bytes 584 | tf_op jit(solution)/shard_map/ppermute | solution.py:659
  24.3 14.8 %collective-permute-start.10 = (f32[2,8,48,128]{3,2,1,0:T(8,128)S(1)}, f32[2,8,48,128]{3,2,1,0:T(8,128)S(1)}, u32[]{:S(2)}, u32[]{:S(2)}) collective-permute-start(f32[2,8,48,128]{3,2,1,0:T(8,128)S(1)} %get-tuple-element.98), channel_id=1, source_target_pairs={{0,2},{2,0},{1,3},{3,1},{4,6},{6,4},{5,7},{7,5},{8,10},{10,8},{9,1... | collective-permute-start | bytes 1179656 | tf_op jit(solution)/shard_map/ppermute | solution.py:659
  26.4 19.2 %collective-permute-start.9 = (f32[2,8,16,128]{3,2,1,0:T(8,128)S(1)}, f32[2,8,16,128]{3,2,1,0:T(8,128)S(1)}, u32[]{:S(2)}, u32[]{:S(2)}) collective-permute-start(f32[2,8,16,128]{3,2,1,0:T(8,128)S(1)} %get-tuple-element.89), channel_id=1, source_target_pairs={{0,12},{4,8},{8,4},{12,0},{1,13},{5,9},{9,5},{13,1},{2,14},{6,10},... | collective-permute-start | bytes 393224 | tf_op jit(solution)/shard_map/ppermute | solution.py:659
  27.7 17.9 %collective-permute-start.3 = (f32[2,8,16,128]{3,2,1,0:T(8,128)S(1)}, f32[2,8,16,128]{3,2,1,0:T(8,128)S(1)}, u32[]{:S(2)}, u32[]{:S(2)}) collective-permute-start(f32[2,8,16,128]{3,2,1,0:T(8,128)S(1)} %get-tuple-element.79), channel_id=1, source_target_pairs={{0,4},{4,0},{8,12},{12,8},{1,5},{5,1},{9,13},{13,9},{2,6},{6,2},{1... | collective-permute-start | bytes 393224 | tf_op jit(solution)/shard_map/ppermute | solution.py:659
  36.2 9.5 %collective-permute-start.6 = (f32[2,8,16,128]{3,2,1,0:T(8,128)S(1)}, f32[2,8,16,128]{3,2,1,0:T(8,128)S(1)}, u32[]{:S(2)}, u32[]{:S(2)}) collective-permute-start(f32[2,8,16,128]{3,2,1,0:T(8,128)S(1)} %get-tuple-element.84), channel_id=1, source_target_pairs={{0,8},{4,12},{8,0},{12,4},{1,9},{5,13},{9,1},{13,5},{2,10},{6,14},... | collective-permute-start | bytes 393224 | tf_op jit(solution)/shard_map/ppermute | solution.py:659
  37.5 10.2 %collective-permute-start.13 = (f32[2,8,48,128]{3,2,1,0:T(8,128)S(1)}, f32[2,8,48,128]{3,2,1,0:T(8,128)S(1)}, u32[]{:S(2)}, u32[]{:S(2)}) collective-permute-start(f32[2,8,48,128]{3,2,1,0:T(8,128)S(1)} %get-tuple-element.91), channel_id=1, source_target_pairs={{0,2},{2,0},{1,3},{3,1},{4,6},{6,4},{5,7},{7,5},{8,10},{10,8},{9,1... | collective-permute-start | bytes 1179656 | tf_op jit(solution)/shard_map/ppermute | solution.py:659
  47.2 9.8 %collective-permute-start.12 = (f32[2,8,48,128]{3,2,1,0:T(8,128)S(1)}, f32[2,8,48,128]{3,2,1,0:T(8,128)S(1)}, u32[]{:S(2)}, u32[]{:S(2)}) collective-permute-start(f32[2,8,48,128]{3,2,1,0:T(8,128)S(1)} %get-tuple-element.107), channel_id=1, source_target_pairs={{0,2},{2,0},{1,3},{3,1},{4,6},{6,4},{5,7},{7,5},{8,10},{10,8},{9,1... | collective-permute-start | bytes 1179656 | tf_op jit(solution)/shard_map/ppermute | solution.py:659
  64.8 8.6 %collective-permute-start.15 = (f32[264,128]{1,0:T(8,128)}, f32[264,128]{1,0:T(8,128)S(1)}, u32[]{:S(2)}, u32[]{:S(2)}) collective-permute-start(f32[264,128]{1,0:T(8,128)} %get-tuple-element.144), channel_id=1, source_target_pairs={{0,12},{4,8},{8,4},{12,0},{1,13},{5,9},{9,5},{13,1},{2,14},{6,10},... | collective-permute-start | bytes 405512 | tf_op jit(solution)/shard_map/ppermute | solution.py:659
  66.5 13.7 %collective-permute-start.16 = (f32[264,128]{1,0:T(8,128)}, f32[264,128]{1,0:T(8,128)}, u32[]{:S(2)}, u32[]{:S(2)}) collective-permute-start(f32[264,128]{1,0:T(8,128)} %get-tuple-element.143), channel_id=1, source_target_pairs={{0,8},{4,12},{8,0},{12,4},{1,9},{5,13},{9,1},{13,5},{2,10},{6,14},... | collective-permute-start | bytes 405512 | tf_op jit(solution)/shard_map/ppermute | solution.py:659
  67.6 12.6 %collective-permute-start.17 = (f32[264,128]{1,0:T(8,128)}, f32[264,128]{1,0:T(8,128)}, u32[]{:S(2)}, u32[]{:S(2)}) collective-permute-start(f32[264,128]{1,0:T(8,128)} %get-tuple-element.142), channel_id=1, source_target_pairs={{0,4},{4,0},{8,12},{12,8},{1,5},{5,1},{9,13},{13,9},{2,6},{6,2},{1... | collective-permute-start | bytes 405512 | tf_op jit(solution)/shard_map/ppermute | solution.py:659
  82.3 7.6 %collective-permute-start.18 = (f32[512,128]{1,0:T(8,128)S(1)}, f32[512,128]{1,0:T(8,128)S(1)}, u32[]{:S(2)}, u32[]{:S(2)}) collective-permute-start(f32[512,128]{1,0:T(8,128)S(1)} %get-tuple-element.120.lower_ref.refs_2_), channel_id=1, source_target_pairs={{0,2},{2,0},{1,3},{3,1},{4,6},{6,4},{5,7},{7,5},{8,10},{10,8},{9,1... | collective-permute-start | bytes 786440 | tf_op jit(solution)/shard_map/ppermute | solution.py:659
  83.0 8.0 %collective-permute-start.21 = (f32[512,128]{1,0:T(8,128)S(1)}, f32[512,128]{1,0:T(8,128)S(1)}, u32[]{:S(2)}, u32[]{:S(2)}) collective-permute-start(f32[512,128]{1,0:T(8,128)S(1)} %get-tuple-element.120.lower_ref.refs_2_), channel_id=1, source_target_pairs={{0,1},{1,0},{2,3},{3,2},{4,5},{5,4},{6,7},{7,6},{8,9},{9,8},{10,11... | collective-permute-start | bytes 786440 | tf_op jit(solution)/shard_map/ppermute | solution.py:659
  89.9 9.2 %collective-permute-start.20 = (f32[520,128]{1,0:T(8,128)S(1)}, f32[520,128]{1,0:T(8,128)S(1)}, u32[]{:S(2)}, u32[]{:S(2)}) collective-permute-start(f32[520,128]{1,0:T(8,128)S(1)} %statistics.1.refs_2_.upper_ref), channel_id=1, source_target_pairs={{0,1},{1,0},{2,3},{3,2},{4,5},{5,4},{6,7},{7,6},{8,9},{9,8},{10,11... | collective-permute-start | bytes 798728 | tf_op jit(solution)/shard_map/ppermute | solution.py:659
  90.4 8.4 %collective-permute-start.19 = (f32[520,128]{1,0:T(8,128)S(1)}, f32[520,128]{1,0:T(8,128)S(1)}, u32[]{:S(2)}, u32[]{:S(2)}) collective-permute-start(f32[520,128]{1,0:T(8,128)S(1)} %statistics.1.refs_2_.upper_ref), channel_id=1, source_target_pairs={{0,2},{2,0},{1,3},{3,1},{4,6},{6,4},{5,7},{7,5},{8,10},{10,8},{9,1... | collective-permute-start | bytes 798728 | tf_op jit(solution)/shard_map/ppermute | solution.py:659
  109.7 8.4 %collective-permute-start.25 = (f32[264,128]{1,0:T(8,128)S(1)}, f32[264,128]{1,0:T(8,128)S(1)}, u32[]{:S(2)}, u32[]{:S(2)}) collective-permute-start(f32[264,128]{1,0:T(8,128)S(1)} %get-tuple-element.140), channel_id=1, source_target_pairs={{0,12},{4,8},{8,4},{12,0},{1,13},{5,9},{9,5},{13,1},{2,14},{6,10},... | collective-permute-start | bytes 405512 | tf_op jit(solution)/shard_map/ppermute | solution.py:659
  112.2 10.9 %collective-permute-start.26 = (f32[264,128]{1,0:T(8,128)S(1)}, f32[264,128]{1,0:T(8,128)S(1)}, u32[]{:S(2)}, u32[]{:S(2)}) collective-permute-start(f32[264,128]{1,0:T(8,128)S(1)} %get-tuple-element.139), channel_id=1, source_target_pairs={{0,8},{4,12},{8,0},{12,4},{1,9},{5,13},{9,1},{13,5},{2,10},{6,14},... | collective-permute-start | bytes 405512 | tf_op jit(solution)/shard_map/ppermute | solution.py:659
  112.2 10.9 %collective-permute-start.27 = (f32[264,128]{1,0:T(8,128)S(1)}, f32[264,128]{1,0:T(8,128)S(1)}, u32[]{:S(2)}, u32[]{:S(2)}) collective-permute-start(f32[264,128]{1,0:T(8,128)S(1)} %get-tuple-element.138), channel_id=1, source_target_pairs={{0,4},{4,0},{8,12},{12,8},{1,5},{5,1},{9,13},{13,9},{2,6},{6,2},{1... | collective-permute-start | bytes 405512 | tf_op jit(solution)/shard_map/ppermute | solution.py:659
  (39 other events, 310.7 us)

commit v14 on v13

--- a/solution.py
+++ b/solution.py
@@ -116,14 +116,11 @@
             put(row, pair, high, low)
 
 
-def pack_kernel(
-    info_ref, wave_ref, own_wave_ref, diag_ref, vec_ref, own_ref, diag_out, start_ref, tiles
-):
+def pack_kernel(info_ref, wave_ref, own_wave_ref, diag_ref, vec_ref, own_ref, diag_out, tiles):
     half = LANES // 2
     for j in range(wave_ref.shape[0]):
         own_ref[j] = pack_tile(own_wave_ref[j])
         diag_out[j] = pack_tile(diag_ref[j])
-        start_ref[j] = diag_out[j] * own_ref[j]
         for q in range(4):
             tiles[q, j] = pack_tile(wave_ref[j, :, 2 * LANES * q : 2 * LANES * (q + 1)])
 
@@ -149,13 +146,13 @@
                 pl.BlockSpec((step, rows, width // 4), lambda i, info: (i, 0, info[0])),
                 pl.BlockSpec((step, rows, width // 4), lambda i, *_: (i, 0, 0)),
             ],
-            out_specs=[pl.BlockSpec((step, LANES, width), lambda i, *_: (i, 0, 0))] + [tile] * 3,
+            out_specs=[pl.BlockSpec((step, LANES, width), lambda i, *_: (i, 0, 0))] + [tile] * 2,
             scratch_shapes=[pltpu.VMEM((4, step, LANES, LANES), jnp.float32)],
         ),
         out_shape=[
             jax.ShapeDtypeStruct((blocks, LANES, width), jnp.bfloat16),
         ]
-        + [jax.ShapeDtypeStruct((blocks, LANES, LANES), jnp.float32)] * 3,
+        + [jax.ShapeDtypeStruct((blocks, LANES, LANES), jnp.float32)] * 2,
         compiler_params=pltpu.CompilerParams(vmem_limit_bytes=SMALL_VMEM),
         cost_estimate=micros(5),
         name="pack",
@@ -176,7 +173,7 @@
         for group, size in enumerate(sizes):
             out_ref = outs[n * len(sizes) + group]
             for at in range(size):
-                for place, term in enumerate(split_two(source[start + at].T)):
+                for place, term in enumerate(split_two(source[start + at, 0:PHYS].T)):
                     wide = jnp.dot(term, spread, preferred_element_type=jnp.float32)
                     tall = jnp.concatenate([wide] * SUB, axis=0)
                     tall = jnp.where(same, tall, 0.0).astype(jnp.bfloat16)
@@ -340,11 +337,17 @@
     mixes = take(len(chunks))
     before = take(1)[0] if before_given else None
     outs = take(2 if pieces else 1)
-    if sent_given:
-        operands.append(take(3))
+    made = take(3) if sent_given else []
     scratch = take(2)
     vec, mid = scratch
     total_ref = take(1)[0] if pieces else outs[0]
+    kept = []
+    if sent_given:
+        operands.append(take(3))
+        sems = take(1)[0]
+        kept = [
+            pltpu.make_async_copy(operands[-1][i], made[i], sems.at[i]) for i in range(3)
+        ]
     step = mid.shape[0]
     lanes, half = LANES, LANES // 2
     first = lane_is_first(SUB)
@@ -435,6 +438,9 @@
         z = jnp.dot(*ready, preferred_element_type=jnp.float32)
         if j + 1 < step and at == len(bonds) // 3:
             right_side(j + 1)
+            if j + 2 == step:
+                for copy in kept:
+                    copy.start()
         if n + 1 < len(units):
             ready = prepare_unit(n + 1)
         if waiting is not None:
@@ -446,6 +452,8 @@
         waiting = (j, mixing, w, table, bond, z)
     j, mixing, w, table, bond, z = waiting
     add_up(j, table, bond, mix_unit(mixing, w, z))
+    for copy in kept:
+        copy.wait()
 
     if pieces:
         stats = jnp.zeros((SUB, lanes), jnp.float32)
@@ -486,6 +494,11 @@
     ]
     if pieces:
         scratch.append(pltpu.VMEM((2, 8, lanes, lanes), jnp.float32))
+    out_specs = [pl.BlockSpec(memory_space=pltpu.VMEM)] * len(shapes)
+    if sent is not None:
+        out_specs += [pl.BlockSpec(memory_space=pltpu.HBM)] * 3
+        scratch += [pltpu.VMEM(x.shape, x.dtype) for x in out_shape[len(shapes) :]]
+        scratch.append(pltpu.SemaphoreType.DMA((3,)))
     plan = (
         tuple(chunks), (half_of or 0) * step, parts_given, sent is not None, before is not None,
         pieces,
@@ -494,7 +507,7 @@
         functools.partial(apply_kernel, plan),
         in_specs=[pl.BlockSpec(memory_space=pltpu.SMEM)] * 3
         + [pl.BlockSpec(memory_space=pltpu.VMEM)] * len(arguments),
-        out_specs=[pl.BlockSpec(memory_space=pltpu.VMEM)] * len(out_shape),
+        out_specs=out_specs,
         scratch_shapes=scratch,
         out_shape=out_shape,
         input_output_aliases=aliases,
@@ -532,22 +545,14 @@
     return cross, square, rest
 
 
-def image_kernel(
-    info_ref, owner_ref, a3, a2, a1, a0, start_hbm, lower_ref, upper_ref, total, start_ref, sems
-):
+def image_kernel(info_ref, owner_ref, a3, a2, a1, a0, start_ref, lower_ref, upper_ref, total):
+    total[...] = start_ref[...]
+    add_arrived(info_ref, owner_ref, (a0, a1, a2, a3), total)
     blocks = total.shape[0]
-    copies = [
-        pltpu.make_async_copy(start_hbm.at[k], start_ref.at[k], sems.at[k]) for k in range(blocks)
-    ]
-    for copy in copies:
-        copy.start()
-    total[...] = jnp.zeros_like(total)
-    add_arrived(info_ref, owner_ref, (a0, a1, a2, a3), total)
     for k in range(blocks):
-        copies[k].wait()
         half = lower_ref if k < blocks // 2 else upper_ref
         at = k % (blocks // 2) * LANES
-        half[at : at + LANES] = total[k] + start_ref[k]
+        half[at : at + LANES] = total[k]
 
 
 def owner_image(info, owners, arrived, start):
@@ -556,16 +561,14 @@
     return pl.pallas_call(
         image_kernel,
         in_specs=[pl.BlockSpec(memory_space=pltpu.SMEM)] * 2
-        + [pl.BlockSpec(memory_space=pltpu.VMEM)] * 4
-        + [pl.BlockSpec(memory_space=pl.ANY)],
+        + [pl.BlockSpec(memory_space=pltpu.VMEM)] * 5,
         out_specs=[pl.BlockSpec(memory_space=pltpu.VMEM)] * 2,
-        scratch_shapes=[pltpu.VMEM(start.shape, jnp.float32)] * 2
-        + [pltpu.SemaphoreType.DMA((blocks,))],
+        scratch_shapes=[pltpu.VMEM(start.shape, jnp.float32)],
         out_shape=[shape, shape],
         compiler_params=pltpu.CompilerParams(vmem_limit_bytes=SMALL_VMEM),
         cost_estimate=micros(1),
         name="owner_image",
-    )(info, owners, *arrived[::-1], *in_hbm(start))
+    )(info, owners, *arrived[::-1], start)
 
 
 def statistics_kernel(own_hbm, lower_ref, upper_ref, out_ref, own_ref, sem):
@@ -689,7 +692,7 @@
     firsts = tuple(sum(sizes[:group]) for group in range(len(sizes)))
     entries = float(blocks * zs * rows * width)
 
-    vector, own, diagonal_packed, start = pack(info, wavefunction, diagonal)
+    vector, own, diagonal_packed = pack(info, wavefunction, diagonal)
 
     by_owner = environment.reshape(bonds, zs, blocks, rows // zs, 2 * rows)
     pieces = []
@@ -699,9 +702,13 @@
             cuts[1:] = [after(x, y) for x, y in zip(cuts[1:], pieces[-1][1:])]
         pieces.append(cuts[:1] + [partner(cuts[k], "blk", k) for k in range(1, 4)])
     pieces[0][1] = after(pieces[0][1], vector)
-    other_terms = partner(after(bond_terms, pieces[0][1]), "mpo", 1)
+    phys = bond_terms.shape[-1]
+    table = jnp.pad(term_slot.astype(jnp.float32), ((0, 0), (0, phys - blocks)))
+    tables = jnp.pad(table[:, None], ((0, 0), (0, SUB - 1), (0, 0)))
+    both = jnp.concatenate([bond_terms, tables], axis=1)
+    other_terms = partner(after(both, pieces[0][1]), "mpo", 1)
     mixing = mixing_operands([bond_terms, other_terms], sizes)
-    slots = [term_slot, partner(after(term_slot, pieces[0][1]), "mpo", 1)]
+    slots = [term_slot, other_terms[:, phys, :blocks].astype(jnp.int32)]
 
     made, sent = [], []
     total = None
@@ -728,7 +735,9 @@
         sent.append(send)
     total = apply_group(len(sizes) - 2, after(vector, sent[-1]))[0]
     out = apply_group(len(sizes) - 1, vector)
-    lower, upper = owner_image(info, slot_block, to_owners(*out), start)
+    arrived = to_owners(*out)
+    start = after(diagonal_packed, arrived[0]) * own
+    lower, upper = owner_image(info, slot_block, arrived, start)
     upper = with_statistics(own, lower, upper)
 
     chunks = [(source, first) for first in firsts for source in range(2)]

time: 125 us -> 125 us (level)
  waiting for transfers between devices: 39.5 us -> 37.8 us
  local copies, waits for them, and re-layouts: 1.73 us -> 2.98 us
    ppermute x28 -> x27, waiting for transfers between devices: 39.5 us -> 37.8 us  [partner(): return lax.ppermute(x, axis, [(i, i ^ k) for i in range(size)])]
    unnamed x71 -> x80, local copies, waits for them, and re-layouts: 1.65 us -> 2.89 us
    ppermute x28 -> x27, starting transfers between devices: 35.8 us -> 36 us  [partner(): return lax.ppermute(x, axis, [(i, i ^ k) for i in range(size)])]
  transfers between devices with their start and end apart: 28 -> 27, of which waited for: 12 -> 13; matrix products, arithmetic and copies ran while one was open for 0% -> 1% of each run, Pallas kernels for 22% -> 23%
where the time goes in v14:
time: 125 us
  Pallas kernels  46 us (37%)
  waiting for transfers between devices  37.8 us (30%)
  starting transfers between devices  36 us (29%)
  local copies, waits for them, and re-layouts  2.98 us (2%)
  between operations  1.33 us (1%)
    ppermute x27, waiting for transfers between devices, partner(): return lax.ppermute(x, axis, [(i, i ^ k) for i in range(size)])  37.8 us
    ppermute x27, starting transfers between devices, partner(): return lax.ppermute(x, axis, [(i, i ^ k) for i in range(size)])  36 us
    pallas_call x5, Pallas kernels, apply_bonds(): pl.pallas_call(functools.partial(apply_kernel, plan), in_specs=[pl.BlockS...  30.5 us
    pallas_call x3, Pallas kernels, own_operands(): pl.pallas_call(own_operands_kernel, grid_spec=pltpu.PrefetchScalarGridSpe...  4.05 us
    pallas_call x3, Pallas kernels, cut_pieces(): pl.pallas_call(functools.partial(cut_kernel, first), grid_spec=pltpu.Pref...  3.67 us
    unnamed x80, local copies, waits for them, and re-layouts  2.89 us
    pallas_call x1, Pallas kernels, pack(): pl.pallas_call(pack_kernel, grid_spec=pltpu.PrefetchScalarGridSpec(num_sc...  2.54 us
  transfers between devices with their start and end apart: 27, of which 13 were waited for; matrix products, arithmetic and copies ran while one was open for 1% of the time, Pallas kernels for 23%

profile of v14, /device:TPU:0, one launch (start us, length us, event | category | flops | bytes accessed | tf_op | source)
XLA Modules:
  0.0 125.0 jit_solution(14888079427670049506)
XLA Ops:
  0.7 1.8 %cut_pieces.3 = (f32[2,8,16,128]{3,2,1,0:T(8,128)S(1)}, f32[2,8,16,128]{3,2,1,0:T(8,128)S(1)}, f32[2,8,16,128]{3,2,1,0:T(8,128)S(1)}, f32[2,8,16,128]{3,2,1,0:T(8,128)S(1)}) custom-call(s32[7]{0:T(128)S(1)} %stack.31.info_ref, f32[6,4,8,16,128]{4,3,2,1,0:T(8,128)} %bitcast.34), custom_call_target="tpu_custom_call" | custom-call | flops 1100000000 | bytes 1048576 | tf_op jit(solution)/shard_map/cut_pieces/pallas_call | solution.py:288
  2.6 3.1 %collective-permute-start = (f32[2,8,16,128]{3,2,1,0:T(8,128)S(1)}, f32[2,8,16,128]{3,2,1,0:T(8,128)S(1)}, u32[]{:S(2)}, u32[]{:S(2)}) collective-permute-start(f32[2,8,16,128]{3,2,1,0:T(8,128)S(1)} %get-tuple-element.69), channel_id=1, source_target_pairs={{0,4},{4,0},{8,12},{12,8},{1,5},{5,1},{9,13},{13,9},{2,6},{6,2},{1... | collective-permute-start | bytes 393224 | tf_op jit(solution)/shard_map/ppermute | solution.py:662
  5.7 2.6 %collective-permute-start.4 = (f32[2,8,16,128]{3,2,1,0:T(8,128)S(1)}, f32[2,8,16,128]{3,2,1,0:T(8,128)S(1)}, u32[]{:S(2)}, u32[]{:S(2)}) collective-permute-start(f32[2,8,16,128]{3,2,1,0:T(8,128)S(1)} %get-tuple-element.81), channel_id=1, source_target_pairs={{0,8},{4,12},{8,0},{12,4},{1,9},{5,13},{9,1},{13,5},{2,10},{6,14},... | collective-permute-start | bytes 393224 | tf_op jit(solution)/shard_map/ppermute | solution.py:662
  8.3 2.5 %pack.1 = (bf16[8,128,1024]{2,1,0:T(8,128)(2,1)S(1)}, f32[8,128,128]{2,1,0:T(8,128)S(1)}, f32[8,128,128]{2,1,0:T(8,128)S(1)}) custom-call(s32[7]{0:T(128)S(1)} %stack.31.info_ref, f32[8,64,1024]{2,1,0:T(8,128)S(1)} %copy-done.8, f32[8,64,1024]{2,1,0:T(8,128)S(1)} %copy-done.8, f32[8,64,256]{2,1,0:T(8,128)S(1)} %copy-done.10), custom_call_target="tpu_custom_call" | custom-call | flops 5500000256 | bytes 1048576 | tf_op jit(solution)/shard_map/pack/pallas_call | solution.py:139
  15.3 3.3 %collective-permute-done.4.refs_2_ = f32[2,8,16,128]{3,2,1,0:T(8,128)S(1)} collective-permute-done((f32[2,8,16,128]{3,2,1,0:T(8,128)S(1)}, f32[2,8,16,128]{3,2,1,0:T(8,128)S(1)}, u32[]{:S(2)}, u32[]{:S(2)}) %collective-permute-start.4) | collective-permute-done | bytes 131104 | tf_op jit(solution)/shard_map/ppermute | solution.py:662
  18.8 2.1 %collective-permute-start.8 = (f32[2,8,16,128]{3,2,1,0:T(8,128)S(1)}, f32[2,8,16,128]{3,2,1,0:T(8,128)S(1)}, u32[]{:S(2)}, u32[]{:S(2)}) collective-permute-start(f32[2,8,16,128]{3,2,1,0:T(8,128)S(1)} %get-tuple-element.87), channel_id=1, source_target_pairs={{0,12},{4,8},{8,4},{12,0},{1,13},{5,9},{9,5},{13,1},{2,14},{6,10},... | collective-permute-start | bytes 393224 | tf_op jit(solution)/shard_map/ppermute | solution.py:662
  24.4 2.0 %collective-permute-done.8.refs_3_ = f32[2,8,16,128]{3,2,1,0:T(8,128)S(1)} collective-permute-done((f32[2,8,16,128]{3,2,1,0:T(8,128)S(1)}, f32[2,8,16,128]{3,2,1,0:T(8,128)S(1)}, u32[]{:S(2)}, u32[]{:S(2)}) %collective-permute-start.8) | collective-permute-done | bytes 131104 | tf_op jit(solution)/shard_map/ppermute | solution.py:662
  27.7 8.5 %collective-permute-start.3 = (f32[2,8,16,128]{3,2,1,0:T(8,128)S(1)}, f32[2,8,16,128]{3,2,1,0:T(8,128)S(1)}, u32[]{:S(2)}, u32[]{:S(2)}) collective-permute-start(f32[2,8,16,128]{3,2,1,0:T(8,128)S(1)} %get-tuple-element.78), channel_id=1, source_target_pairs={{0,4},{4,0},{8,12},{12,8},{1,5},{5,1},{9,13},{13,9},{2,6},{6,2},{1... | collective-permute-start | bytes 393224 | tf_op jit(solution)/shard_map/ppermute | solution.py:662
  39.1 5.2 %apply_bonds.5 = (f32[2,8,128,128]{3,2,1,0:T(8,128)S(1)}, bf16[2,8,64,128]{3,2,1,0:T(8,128)(2,1)S(1)}, bf16[2,8,64,128]{3,2,1,0:T(8,128)(2,1)S(1)}, bf16[8,64,256]{2,1,0:T(8,128)(2,1)S(1)}) custom-call(s32[7]{0:T(128)S(1)} %stack.31.info_ref, s32[6,8]{1,0:T(8,128)S(1)} %copy-done.5, s32[6,8]{1,0:T(8,128)S(1)} %bitcast.29, ...), custom_call_target="tpu_custom_call" | custom-call | flops 1100000000 | bytes 1048576 | tf_op jit(solution)/shard_map/apply_bonds/pallas_call | solution.py:506
  47.6 5.4 %apply_bonds.6 = (f32[2,8,128,128]{3,2,1,0:T(8,128)S(1)}, bf16[2,8,64,128]{3,2,1,0:T(8,128)(2,1)S(1)}, bf16[2,8,64,128]{3,2,1,0:T(8,128)(2,1)S(1)}, bf16[8,64,256]{2,1,0:T(8,128)(2,1)S(1)}) custom-call(s32[7]{0:T(128)S(1)} %stack.31.info_ref, s32[6,8]{1,0:T(8,128)S(1)} %copy-done.5, s32[6,8]{1,0:T(8,128)S(1)} %bitcast.30, ...), custom_call_target="tpu_custom_call", output_to_operand_aliasing={{0}: (10, {})} | custom-call | flops 1100000000 | bytes 1048576 | tf_op jit(solution)/shard_map/apply_bonds/pallas_call | solution.py:506
  53.1 3.8 %collective-permute-done.11.refs_6_ = f32[2,8,48,128]{3,2,1,0:T(8,128)S(1)} collective-permute-done((f32[2,8,48,128]{3,2,1,0:T(8,128)S(1)}, f32[2,8,48,128]{3,2,1,0:T(8,128)S(1)}, u32[]{:S(2)}, u32[]{:S(2)}) %collective-permute-start.11) | collective-permute-done | bytes 393248 | tf_op jit(solution)/shard_map/ppermute | solution.py:662
  56.8 5.2 %apply_bonds.7 = (f32[4,264,128]{2,1,0:T(8,128)S(1)}, f32[4,264,128]{2,1,0:T(8,128)S(1)}, bf16[2,8,64,128]{3,2,1,0:T(8,128)(2,1)S(1)}, bf16[2,8,64,128]{3,2,1,0:T(8,128)(2,1)S(1)}, bf16[8,64,256]{2,1,0:T(8,128)(2,1)S(1)}) custom-call(s32[7]{0:T(128)S(1)} %stack.31.info_ref, s32[6,8]{1,0:T(8,128)S(1)} %copy-done.5, s32[6,8]{1,0:T(8,128)S(1)} %bitcast.31, ...), custom_call_target="tpu_custom_call" | custom-call | flops 1100000000 | bytes 1048576 | tf_op jit(solution)/shard_map/apply_bonds/pallas_call | solution.py:506
  62.2 1.9 %collective-permute-done.13 = f32[4,264,128]{2,1,0:T(8,128)S(1)} collective-permute-done((f32[4,264,128]{2,1,0:T(8,128)S(1)}, f32[4,264,128]{2,1,0:T(8,128)S(1)}, u32[]{:S(2)}, u32[]{:S(2)}) %collective-permute-start.13) | collective-permute-done | bytes 540704 | tf_op jit(solution)/shard_map/ppermute | solution.py:662
  67.0 2.3 %collective-permute-start.16 = (f32[264,128]{1,0:T(8,128)}, f32[264,128]{1,0:T(8,128)}, u32[]{:S(2)}, u32[]{:S(2)}) collective-permute-start(f32[264,128]{1,0:T(8,128)} %get-tuple-element.140), channel_id=1, source_target_pairs={{0,4},{4,0},{8,12},{12,8},{1,5},{5,1},{9,13},{13,9},{2,6},{6,2},{1... | collective-permute-start | bytes 405512 | tf_op jit(solution)/shard_map/ppermute | solution.py:662
  70.7 2.9 %collective-permute-done.14.a3 = f32[264,128]{1,0:T(8,128)} collective-permute-done((f32[264,128]{1,0:T(8,128)}, f32[264,128]{1,0:T(8,128)}, u32[]{:S(2)}, u32[]{:S(2)}) %collective-permute-start.14) | collective-permute-done | bytes 135200 | tf_op jit(solution)/shard_map/ppermute | solution.py:662
  73.6 6.0 %collective-permute-done.15.a2 = f32[264,128]{1,0:T(8,128)} collective-permute-done((f32[264,128]{1,0:T(8,128)}, f32[264,128]{1,0:T(8,128)}, u32[]{:S(2)}, u32[]{:S(2)}) %collective-permute-start.15) | collective-permute-done | bytes 135200 | tf_op jit(solution)/shard_map/ppermute | solution.py:662
  84.1 4.9 %collective-permute-done.17.refs_3_ = f32[512,128]{1,0:T(8,128)S(1)} collective-permute-done((f32[512,128]{1,0:T(8,128)S(1)}, f32[512,128]{1,0:T(8,128)S(1)}, u32[]{:S(2)}, u32[]{:S(2)}) %collective-permute-start.17) | collective-permute-done | bytes 262176 | tf_op jit(solution)/shard_map/ppermute | solution.py:662
  90.7 7.3 %apply_bonds.8.refs_30_ = f32[2,8,128,128]{3,2,1,0:T(8,128)S(1)} custom-call(s32[7]{0:T(128)S(1)} %stack.31.info_ref, s32[6,8]{1,0:T(8,128)S(1)} %copy-done.5, s32[6,8]{1,0:T(8,128)S(1)} %bitcast.32, f32[512,128]{1,0:T(8,128)S(1)} %get-tuple-element.119.lower_ref.refs_2_, f32[512,128]{1,0:T(8,128)S(1)} %collective-permute-done.17.refs_3_, ...), custom_call_target="tpu_custom_call" | custom-call | flops 11000000512 | bytes 1048576 | tf_op jit(solution)/shard_map/apply_bonds/pallas_call | solution.py:506
  99.7 7.4 %apply_bonds.9 = (f32[4,264,128]{2,1,0:T(8,128)S(1)}, f32[4,264,128]{2,1,0:T(8,128)S(1)}) custom-call(s32[7]{0:T(128)S(1)} %stack.31.info_ref, s32[6,8]{1,0:T(8,128)S(1)} %copy-done.5, s32[6,8]{1,0:T(8,128)S(1)} %bitcast.33, f32[520,128]{1,0:T(8,128)S(1)} %statistics.1.refs_2_.upper_ref, f32[520,128]{1,0:T(8,128)S(1)} %collective-permute-done.18.refs_3_, ...), custom_call_target="tpu_custom_call" | custom-call | flops 11000000512 | bytes 1048576 | tf_op jit(solution)/shard_map/apply_bonds/pallas_call | solution.py:506
  107.3 1.8 %collective-permute-done.23 = f32[4,264,128]{2,1,0:T(8,128)S(1)} collective-permute-done((f32[4,264,128]{2,1,0:T(8,128)S(1)}, f32[4,264,128]{2,1,0:T(8,128)S(1)}, u32[]{:S(2)}, u32[]{:S(2)}) %collective-permute-start.23) | collective-permute-done | bytes 540704 | tf_op jit(solution)/shard_map/ppermute | solution.py:662
  109.2 2.8 %collective-permute-start.24 = (f32[264,128]{1,0:T(8,128)S(1)}, f32[264,128]{1,0:T(8,128)S(1)}, u32[]{:S(2)}, u32[]{:S(2)}) collective-permute-start(f32[264,128]{1,0:T(8,128)S(1)} %get-tuple-element.138), channel_id=1, source_target_pairs={{0,12},{4,8},{8,4},{12,0},{1,13},{5,9},{9,5},{13,1},{2,14},{6,10},... | collective-permute-start | bytes 405512 | tf_op jit(solution)/shard_map/ppermute | solution.py:662
  113.6 3.9 %collective-permute-done.24.a3 = f32[264,128]{1,0:T(8,128)S(1)} collective-permute-done((f32[264,128]{1,0:T(8,128)S(1)}, f32[264,128]{1,0:T(8,128)S(1)}, u32[]{:S(2)}, u32[]{:S(2)}) %collective-permute-start.24) | collective-permute-done | bytes 135200 | tf_op jit(solution)/shard_map/ppermute | solution.py:662
  117.6 5.4 %collective-permute-done.25.a2 = f32[264,128]{1,0:T(8,128)S(1)} collective-permute-done((f32[264,128]{1,0:T(8,128)S(1)}, f32[264,128]{1,0:T(8,128)S(1)}, u32[]{:S(2)}, u32[]{:S(2)}) %collective-permute-start.25) | collective-permute-done | bytes 135200 | tf_op jit(solution)/shard_map/ppermute | solution.py:662
  123.0 2.1 %outputs.1 = (f32[8,64,256]{2,1,0:T(8,128)}, f32[8,64,256]{2,1,0:T(8,128)}, f32[8,64,256]{2,1,0:T(8,128)}) custom-call(s32[7]{0:T(128)S(1)} %stack.31.info_ref, s32[4,2]{1,0:T(4,128)S(1)} %copy-done.7, f32[264,128]{1,0:T(8,128)S(1)} %collective-permute-done.24.a3, f32[264,128]{1,0:T(8,128)S(1)} %collective-permute-done.25.a2, ...), custom_call_target="tpu_custom_call" | custom-call | flops 4400000000 | bytes 1048576 | tf_op jit(solution)/shard_map/outputs/pallas_call | solution.py:639
  (135 shorter events, 29.5 us)
Async XLA Ops:
  2.6 9.3 %collective-permute-start = (f32[2,8,16,128]{3,2,1,0:T(8,128)S(1)}, f32[2,8,16,128]{3,2,1,0:T(8,128)S(1)}, u32[]{:S(2)}, u32[]{:S(2)}) collective-permute-start(f32[2,8,16,128]{3,2,1,0:T(8,128)S(1)} %get-tuple-element.69), channel_id=1, source_target_pairs={{0,4},{4,0},{8,12},{12,8},{1,5},{5,1},{9,13},{13,9},{2,6},{6,2},{1... | collective-permute-start | bytes 393224 | tf_op jit(solution)/shard_map/ppermute | solution.py:662
  5.7 12.9 %collective-permute-start.4 = (f32[2,8,16,128]{3,2,1,0:T(8,128)S(1)}, f32[2,8,16,128]{3,2,1,0:T(8,128)S(1)}, u32[]{:S(2)}, u32[]{:S(2)}) collective-permute-start(f32[2,8,16,128]{3,2,1,0:T(8,128)S(1)} %get-tuple-element.81), channel_id=1, source_target_pairs={{0,8},{4,12},{8,0},{12,4},{1,9},{5,13},{9,1},{13,5},{2,10},{6,14},... | collective-permute-start | bytes 393224 | tf_op jit(solution)/shard_map/ppermute | solution.py:662
  8.2 10.6 %collective-permute-start.7 = (f32[2,8,16,128]{3,2,1,0:T(8,128)S(1)}, f32[2,8,16,128]{3,2,1,0:T(8,128)S(1)}, u32[]{:S(2)}, u32[]{:S(2)}) collective-permute-start(f32[2,8,16,128]{3,2,1,0:T(8,128)S(1)} %get-tuple-element.86), channel_id=1, source_target_pairs={{0,12},{4,8},{8,4},{12,0},{1,13},{5,9},{9,5},{13,1},{2,14},{6,10},... | collective-permute-start | bytes 393224 | tf_op jit(solution)/shard_map/ppermute | solution.py:662
  11.9 9.0 %collective-permute-start.1 = (f32[6,24,16]{2,1,0:T(8,128)S(1)}, f32[6,24,16]{2,1,0:T(8,128)S(1)}, u32[]{:S(2)}, u32[]{:S(2)}) collective-permute-start(f32[6,24,16]{2,1,0:T(8,128)S(1)} %select_maximum_fusion), channel_id=1, source_target_pairs={{0,2},{2,0},{1,3},{3,1},{4,6},{6,4},{5,7},{7,5},{8,10},{10,8},{9,1... | collective-permute-start | bytes 27656 | tf_op jit(solution)/shard_map/ppermute | solution.py:662
  14.6 6.9 %collective-permute-start.2 = (f32[2,8,16,128]{3,2,1,0:T(8,128)S(1)}, f32[2,8,16,128]{3,2,1,0:T(8,128)S(1)}, u32[]{:S(2)}, u32[]{:S(2)}) collective-permute-start(f32[2,8,16,128]{3,2,1,0:T(8,128)S(1)} %get-tuple-element.77), channel_id=1, source_target_pairs={{0,4},{4,0},{8,12},{12,8},{1,5},{5,1},{9,13},{13,9},{2,6},{6,2},{1... | collective-permute-start | bytes 393224 | tf_op jit(solution)/shard_map/ppermute | solution.py:662
  18.6 17.6 %collective-permute-start.5 = (f32[2,8,16,128]{3,2,1,0:T(8,128)S(1)}, f32[2,8,16,128]{3,2,1,0:T(8,128)S(1)}, u32[]{:S(2)}, u32[]{:S(2)}) collective-permute-start(f32[2,8,16,128]{3,2,1,0:T(8,128)S(1)} %get-tuple-element.82), channel_id=1, source_target_pairs={{0,8},{4,12},{8,0},{12,4},{1,9},{5,13},{9,1},{13,5},{2,10},{6,14},... | collective-permute-start | bytes 393224 | tf_op jit(solution)/shard_map/ppermute | solution.py:662
  18.8 7.6 %collective-permute-start.8 = (f32[2,8,16,128]{3,2,1,0:T(8,128)S(1)}, f32[2,8,16,128]{3,2,1,0:T(8,128)S(1)}, u32[]{:S(2)}, u32[]{:S(2)}) collective-permute-start(f32[2,8,16,128]{3,2,1,0:T(8,128)S(1)} %get-tuple-element.87), channel_id=1, source_target_pairs={{0,12},{4,8},{8,4},{12,0},{1,13},{5,9},{9,5},{13,1},{2,14},{6,10},... | collective-permute-start | bytes 393224 | tf_op jit(solution)/shard_map/ppermute | solution.py:662
  22.9 16.2 %collective-permute-start.10 = (f32[2,8,48,128]{3,2,1,0:T(8,128)S(1)}, f32[2,8,48,128]{3,2,1,0:T(8,128)S(1)}, u32[]{:S(2)}, u32[]{:S(2)}) collective-permute-start(f32[2,8,48,128]{3,2,1,0:T(8,128)S(1)} %get-tuple-element.97), channel_id=1, source_target_pairs={{0,2},{2,0},{1,3},{3,1},{4,6},{6,4},{5,7},{7,5},{8,10},{10,8},{9,1... | collective-permute-start | bytes 1179656 | tf_op jit(solution)/shard_map/ppermute | solution.py:662
  26.4 18.7 %collective-permute-start.9 = (f32[2,8,16,128]{3,2,1,0:T(8,128)S(1)}, f32[2,8,16,128]{3,2,1,0:T(8,128)S(1)}, u32[]{:S(2)}, u32[]{:S(2)}) collective-permute-start(f32[2,8,16,128]{3,2,1,0:T(8,128)S(1)} %get-tuple-element.88), channel_id=1, source_target_pairs={{0,12},{4,8},{8,4},{12,0},{1,13},{5,9},{9,5},{13,1},{2,14},{6,10},... | collective-permute-start | bytes 393224 | tf_op jit(solution)/shard_map/ppermute | solution.py:662
  27.7 17.4 %collective-permute-start.3 = (f32[2,8,16,128]{3,2,1,0:T(8,128)S(1)}, f32[2,8,16,128]{3,2,1,0:T(8,128)S(1)}, u32[]{:S(2)}, u32[]{:S(2)}) collective-permute-start(f32[2,8,16,128]{3,2,1,0:T(8,128)S(1)} %get-tuple-element.78), channel_id=1, source_target_pairs={{0,4},{4,0},{8,12},{12,8},{1,5},{5,1},{9,13},{13,9},{2,6},{6,2},{1... | collective-permute-start | bytes 393224 | tf_op jit(solution)/shard_map/ppermute | solution.py:662
  36.2 8.9 %collective-permute-start.6 = (f32[2,8,16,128]{3,2,1,0:T(8,128)S(1)}, f32[2,8,16,128]{3,2,1,0:T(8,128)S(1)}, u32[]{:S(2)}, u32[]{:S(2)}) collective-permute-start(f32[2,8,16,128]{3,2,1,0:T(8,128)S(1)} %get-tuple-element.83), channel_id=1, source_target_pairs={{0,8},{4,12},{8,0},{12,4},{1,9},{5,13},{9,1},{13,5},{2,10},{6,14},... | collective-permute-start | bytes 393224 | tf_op jit(solution)/shard_map/ppermute | solution.py:662
  37.5 10.1 %collective-permute-start.12 = (f32[2,8,48,128]{3,2,1,0:T(8,128)S(1)}, f32[2,8,48,128]{3,2,1,0:T(8,128)S(1)}, u32[]{:S(2)}, u32[]{:S(2)}) collective-permute-start(f32[2,8,48,128]{3,2,1,0:T(8,128)S(1)} %get-tuple-element.90), channel_id=1, source_target_pairs={{0,2},{2,0},{1,3},{3,1},{4,6},{6,4},{5,7},{7,5},{8,10},{10,8},{9,1... | collective-permute-start | bytes 1179656 | tf_op jit(solution)/shard_map/ppermute | solution.py:662
  46.5 10.4 %collective-permute-start.11 = (f32[2,8,48,128]{3,2,1,0:T(8,128)S(1)}, f32[2,8,48,128]{3,2,1,0:T(8,128)S(1)}, u32[]{:S(2)}, u32[]{:S(2)}) collective-permute-start(f32[2,8,48,128]{3,2,1,0:T(8,128)S(1)} %get-tuple-element.105), channel_id=1, source_target_pairs={{0,2},{2,0},{1,3},{3,1},{4,6},{6,4},{5,7},{7,5},{8,10},{10,8},{9,1... | collective-permute-start | bytes 1179656 | tf_op jit(solution)/shard_map/ppermute | solution.py:662
  62.1 2.0 %collective-permute-start.13 = (f32[4,264,128]{2,1,0:T(8,128)S(1)}, f32[4,264,128]{2,1,0:T(8,128)S(1)}, u32[]{:S(2)}, u32[]{:S(2)}) collective-permute-start(f32[4,264,128]{2,1,0:T(8,128)S(1)} %get-tuple-element.116), channel_id=1, source_target_pairs={{0,1},{1,0},{2,3},{3,2},{4,5},{5,4},{6,7},{7,6},{8,9},{9,8},{10,11... | collective-permute-start | bytes 1622024 | tf_op jit(solution)/shard_map/ppermute | solution.py:662
  64.9 8.7 %collective-permute-start.14 = (f32[264,128]{1,0:T(8,128)}, f32[264,128]{1,0:T(8,128)}, u32[]{:S(2)}, u32[]{:S(2)}) collective-permute-start(f32[264,128]{1,0:T(8,128)} %get-tuple-element.142), channel_id=1, source_target_pairs={{0,12},{4,8},{8,4},{12,0},{1,13},{5,9},{9,5},{13,1},{2,14},{6,10},... | collective-permute-start | bytes 405512 | tf_op jit(solution)/shard_map/ppermute | solution.py:662
  66.4 13.2 %collective-permute-start.15 = (f32[264,128]{1,0:T(8,128)}, f32[264,128]{1,0:T(8,128)}, u32[]{:S(2)}, u32[]{:S(2)}) collective-permute-start(f32[264,128]{1,0:T(8,128)} %get-tuple-element.141), channel_id=1, source_target_pairs={{0,8},{4,12},{8,0},{12,4},{1,9},{5,13},{9,1},{13,5},{2,10},{6,14},... | collective-permute-start | bytes 405512 | tf_op jit(solution)/shard_map/ppermute | solution.py:662
  67.0 12.6 %collective-permute-start.16 = (f32[264,128]{1,0:T(8,128)}, f32[264,128]{1,0:T(8,128)}, u32[]{:S(2)}, u32[]{:S(2)}) collective-permute-start(f32[264,128]{1,0:T(8,128)} %get-tuple-element.140), channel_id=1, source_target_pairs={{0,4},{4,0},{8,12},{12,8},{1,5},{5,1},{9,13},{13,9},{2,6},{6,2},{1... | collective-permute-start | bytes 405512 | tf_op jit(solution)/shard_map/ppermute | solution.py:662
  81.5 7.6 %collective-permute-start.17 = (f32[512,128]{1,0:T(8,128)S(1)}, f32[512,128]{1,0:T(8,128)S(1)}, u32[]{:S(2)}, u32[]{:S(2)}) collective-permute-start(f32[512,128]{1,0:T(8,128)S(1)} %get-tuple-element.119.lower_ref.refs_2_), channel_id=1, source_target_pairs={{0,2},{2,0},{1,3},{3,1},{4,6},{6,4},{5,7},{7,5},{8,10},{10,8},{9,1... | collective-permute-start | bytes 786440 | tf_op jit(solution)/shard_map/ppermute | solution.py:662
  82.4 8.0 %collective-permute-start.20 = (f32[512,128]{1,0:T(8,128)S(1)}, f32[512,128]{1,0:T(8,128)S(1)}, u32[]{:S(2)}, u32[]{:S(2)}) collective-permute-start(f32[512,128]{1,0:T(8,128)S(1)} %get-tuple-element.119.lower_ref.refs_2_), channel_id=1, source_target_pairs={{0,1},{1,0},{2,3},{3,2},{4,5},{5,4},{6,7},{7,6},{8,9},{9,8},{10,11... | collective-permute-start | bytes 786440 | tf_op jit(solution)/shard_map/ppermute | solution.py:662
  89.0 9.2 %collective-permute-start.19 = (f32[520,128]{1,0:T(8,128)S(1)}, f32[520,128]{1,0:T(8,128)S(1)}, u32[]{:S(2)}, u32[]{:S(2)}) collective-permute-start(f32[520,128]{1,0:T(8,128)S(1)} %statistics.1.refs_2_.upper_ref), channel_id=1, source_target_pairs={{0,1},{1,0},{2,3},{3,2},{4,5},{5,4},{6,7},{7,6},{8,9},{9,8},{10,11... | collective-permute-start | bytes 798728 | tf_op jit(solution)/shard_map/ppermute | solution.py:662
  89.6 8.5 %collective-permute-start.18 = (f32[520,128]{1,0:T(8,128)S(1)}, f32[520,128]{1,0:T(8,128)S(1)}, u32[]{:S(2)}, u32[]{:S(2)}) collective-permute-start(f32[520,128]{1,0:T(8,128)S(1)} %statistics.1.refs_2_.upper_ref), channel_id=1, source_target_pairs={{0,2},{2,0},{1,3},{3,1},{4,6},{6,4},{5,7},{7,5},{8,10},{10,8},{9,1... | collective-permute-start | bytes 798728 | tf_op jit(solution)/shard_map/ppermute | solution.py:662
  109.2 8.4 %collective-permute-start.24 = (f32[264,128]{1,0:T(8,128)S(1)}, f32[264,128]{1,0:T(8,128)S(1)}, u32[]{:S(2)}, u32[]{:S(2)}) collective-permute-start(f32[264,128]{1,0:T(8,128)S(1)} %get-tuple-element.138), channel_id=1, source_target_pairs={{0,12},{4,8},{8,4},{12,0},{1,13},{5,9},{9,5},{13,1},{2,14},{6,10},... | collective-permute-start | bytes 405512 | tf_op jit(solution)/shard_map/ppermute | solution.py:662
  112.0 10.9 %collective-permute-start.25 = (f32[264,128]{1,0:T(8,128)S(1)}, f32[264,128]{1,0:T(8,128)S(1)}, u32[]{:S(2)}, u32[]{:S(2)}) collective-permute-start(f32[264,128]{1,0:T(8,128)S(1)} %get-tuple-element.137), channel_id=1, source_target_pairs={{0,8},{4,12},{8,0},{12,4},{1,9},{5,13},{9,1},{13,5},{2,10},{6,14},... | collective-permute-start | bytes 405512 | tf_op jit(solution)/shard_map/ppermute | solution.py:662
  112.0 10.9 %collective-permute-start.26 = (f32[264,128]{1,0:T(8,128)S(1)}, f32[264,128]{1,0:T(8,128)S(1)}, u32[]{:S(2)}, u32[]{:S(2)}) collective-permute-start(f32[264,128]{1,0:T(8,128)S(1)} %get-tuple-element.136), channel_id=1, source_target_pairs={{0,4},{4,0},{8,12},{12,8},{1,5},{5,1},{9,13},{13,9},{2,6},{6,2},{1... | collective-permute-start | bytes 405512 | tf_op jit(solution)/shard_map/ppermute | solution.py:662
  (42 other events, 401.9 us)

commit v15 on v14

--- a/solution.py
+++ b/solution.py
@@ -688,7 +688,7 @@
     place = 2 * mpo + rep
     info = jnp.stack([place, place ^ 2, place ^ 1, place ^ 3, blk, rep, mpo]).astype(jnp.int32)
     bonds = environment.shape[0]
-    sizes = tuple(bonds * part // 6 for part in (2, 2, 2))
+    sizes = tuple(bonds * part // 6 for part in (3, 2, 1))
     firsts = tuple(sum(sizes[:group]) for group in range(len(sizes)))
     entries = float(blocks * zs * rows * width)
 
@@ -728,7 +728,7 @@
         if group >= 2:
             total = apply_group(group - 2, after(vector, sent[group - 1]))[0]
             pieces[group][3] = after(pieces[group][3], total)
-        if group < 1:
+        if group < 2:
             pieces[group][1] = after(pieces[group][1], pieces[group + 1][1])
         *own_set, send = own_operands(info, pieces[group])
         made.append(own_set)

time: 125 us -> 135 us (1.080)
  waiting for transfers between devices: 37.8 us -> 45 us
  starting transfers between devices: 36 us -> 37.5 us
    ppermute x27, waiting for transfers between devices: 37.8 us -> 45 us  [partner(): return lax.ppermute(x, axis, [(i, i ^ k) for i in range(size)])]
    ppermute x27, starting transfers between devices: 36 us -> 37.5 us  [partner(): return lax.ppermute(x, axis, [(i, i ^ k) for i in range(size)])]
    unnamed x80 -> x86, local copies, waits for them, and re-layouts: 2.89 us -> 3.27 us
  transfers between devices with their start and end apart: 27 -> 27, of which waited for: 13 -> 12; matrix products, arithmetic and copies ran while one was open for 1% -> 1% of each run, Pallas kernels for 23% -> 22%
where the time goes in v15:
time: 135 us
  Pallas kernels  46.9 us (35%)
  waiting for transfers between devices  45 us (33%)
  starting transfers between devices  37.5 us (28%)
  local copies, waits for them, and re-layouts  3.37 us (2%)
  between operations  1.37 us (1%)
    ppermute x27, waiting for transfers between devices, partner(): return lax.ppermute(x, axis, [(i, i ^ k) for i in range(size)])  45 us
    ppermute x27, starting transfers between devices, partner(): return lax.ppermute(x, axis, [(i, i ^ k) for i in range(size)])  37.5 us
    pallas_call x5, Pallas kernels, apply_bonds(): pl.pallas_call(functools.partial(apply_kernel, plan), in_specs=[pl.BlockS...  31.4 us
    pallas_call x3, Pallas kernels, own_operands(): pl.pallas_call(own_operands_kernel, grid_spec=pltpu.PrefetchScalarGridSpe...  3.97 us
    pallas_call x3, Pallas kernels, cut_pieces(): pl.pallas_call(functools.partial(cut_kernel, first), grid_spec=pltpu.Pref...  3.79 us
    unnamed x86, local copies, waits for them, and re-layouts  3.27 us
  transfers between devices with their start and end apart: 27, of which 12 were waited for; matrix products, arithmetic and copies ran while one was open for 1% of the time, Pallas kernels for 22%

profile of v15, /device:TPU:0, one launch (start us, length us, event | category | flops | bytes accessed | tf_op | source)
XLA Modules:
  0.0 135.1 jit_solution(12694721766482283420)
XLA Ops:
  0.7 1.9 %cut_pieces.3 = (f32[3,8,16,128]{3,2,1,0:T(8,128)S(1)}, f32[3,8,16,128]{3,2,1,0:T(8,128)S(1)}, f32[3,8,16,128]{3,2,1,0:T(8,128)S(1)}, f32[3,8,16,128]{3,2,1,0:T(8,128)S(1)}) custom-call(s32[7]{0:T(128)S(1)} %stack.31.info_ref, f32[6,4,8,16,128]{4,3,2,1,0:T(8,128)} %bitcast.34), custom_call_target="tpu_custom_call" | custom-call | flops 1100000000 | bytes 1048576 | tf_op jit(solution)/shard_map/cut_pieces/pallas_call | solution.py:288
  2.7 3.1 %collective-permute-start = (f32[3,8,16,128]{3,2,1,0:T(8,128)S(1)}, f32[3,8,16,128]{3,2,1,0:T(8,128)S(1)}, u32[]{:S(2)}, u32[]{:S(2)}) collective-permute-start(f32[3,8,16,128]{3,2,1,0:T(8,128)S(1)} %get-tuple-element.70), channel_id=1, source_target_pairs={{0,4},{4,0},{8,12},{12,8},{1,5},{5,1},{9,13},{13,9},{2,6},{6,2},{1... | collective-permute-start | bytes 589832 | tf_op jit(solution)/shard_map/ppermute | solution.py:662
  5.8 2.6 %collective-permute-start.4 = (f32[3,8,16,128]{3,2,1,0:T(8,128)S(1)}, f32[3,8,16,128]{3,2,1,0:T(8,128)S(1)}, u32[]{:S(2)}, u32[]{:S(2)}) collective-permute-start(f32[3,8,16,128]{3,2,1,0:T(8,128)S(1)} %get-tuple-element.82), channel_id=1, source_target_pairs={{0,8},{4,12},{8,0},{12,4},{1,9},{5,13},{9,1},{13,5},{2,10},{6,14},... | collective-permute-start | bytes 589832 | tf_op jit(solution)/shard_map/ppermute | solution.py:662
  8.4 2.6 %pack.1 = (bf16[8,128,1024]{2,1,0:T(8,128)(2,1)S(1)}, f32[8,128,128]{2,1,0:T(8,128)S(1)}, f32[8,128,128]{2,1,0:T(8,128)S(1)}) custom-call(s32[7]{0:T(128)S(1)} %stack.31.info_ref, f32[8,64,1024]{2,1,0:T(8,128)S(1)} %copy-done.11, f32[8,64,1024]{2,1,0:T(8,128)S(1)} %copy-done.11, f32[8,64,256]{2,1,0:T(8,128)S(1)} %copy-done.13), custom_call_target="tpu_custom_call" | custom-call | flops 5500000256 | bytes 1048576 | tf_op jit(solution)/shard_map/pack/pallas_call | solution.py:139
  12.0 2.1 %collective-permute-done.refs_1_ = f32[3,8,16,128]{3,2,1,0:T(8,128)S(1)} collective-permute-done((f32[3,8,16,128]{3,2,1,0:T(8,128)S(1)}, f32[3,8,16,128]{3,2,1,0:T(8,128)S(1)}, u32[]{:S(2)}, u32[]{:S(2)}) %collective-permute-start) | collective-permute-done | bytes 196640 | tf_op jit(solution)/shard_map/ppermute | solution.py:662
  16.8 6.2 %collective-permute-done.4.refs_2_ = f32[3,8,16,128]{3,2,1,0:T(8,128)S(1)} collective-permute-done((f32[3,8,16,128]{3,2,1,0:T(8,128)S(1)}, f32[3,8,16,128]{3,2,1,0:T(8,128)S(1)}, u32[]{:S(2)}, u32[]{:S(2)}) %collective-permute-start.4) | collective-permute-done | bytes 196640 | tf_op jit(solution)/shard_map/ppermute | solution.py:662
  23.0 3.5 %collective-permute-start.8 = (f32[2,8,16,128]{3,2,1,0:T(8,128)S(1)}, f32[2,8,16,128]{3,2,1,0:T(8,128)S(1)}, u32[]{:S(2)}, u32[]{:S(2)}) collective-permute-start(f32[2,8,16,128]{3,2,1,0:T(8,128)S(1)} %get-tuple-element.88), channel_id=1, source_target_pairs={{0,12},{4,8},{8,4},{12,0},{1,13},{5,9},{9,5},{13,1},{2,14},{6,10},... | collective-permute-start | bytes 393224 | tf_op jit(solution)/shard_map/ppermute | solution.py:662
  26.8 8.5 %collective-permute-start.3 = (f32[1,8,16,128]{3,2,1,0:T(8,128)S(1)}, f32[1,8,16,128]{3,2,1,0:T(8,128)S(1)}, u32[]{:S(2)}, u32[]{:S(2)}) collective-permute-start(f32[1,8,16,128]{3,2,1,0:T(8,128)S(1)} %get-tuple-element.79), channel_id=1, source_target_pairs={{0,4},{4,0},{8,12},{12,8},{1,5},{5,1},{9,13},{13,9},{2,6},{6,2},{1... | collective-permute-start | bytes 196616 | tf_op jit(solution)/shard_map/ppermute | solution.py:662
  41.8 2.0 %collective-permute-start.12 = (f32[2,8,48,128]{3,2,1,0:T(8,128)S(1)}, f32[2,8,48,128]{3,2,1,0:T(8,128)S(1)}, u32[]{:S(2)}, u32[]{:S(2)}) collective-permute-start(f32[2,8,48,128]{3,2,1,0:T(8,128)S(1)} %get-tuple-element.92), channel_id=1, source_target_pairs={{0,2},{2,0},{1,3},{3,1},{4,6},{6,4},{5,7},{7,5},{8,10},{10,8},{9,1... | collective-permute-start | bytes 1179656 | tf_op jit(solution)/shard_map/ppermute | solution.py:662
  43.9 7.9 %collective-permute-done.10.refs_6_ = f32[3,8,48,128]{3,2,1,0:T(8,128)S(1)} collective-permute-done((f32[3,8,48,128]{3,2,1,0:T(8,128)S(1)}, f32[3,8,48,128]{3,2,1,0:T(8,128)S(1)}, u32[]{:S(2)}, u32[]{:S(2)}) %collective-permute-start.10) | collective-permute-done | bytes 589856 | tf_op jit(solution)/shard_map/ppermute | solution.py:662
  51.8 6.8 %apply_bonds.5 = (f32[2,8,128,128]{3,2,1,0:T(8,128)S(1)}, bf16[3,8,64,128]{3,2,1,0:T(8,128)(2,1)S(1)}, bf16[3,8,64,128]{3,2,1,0:T(8,128)(2,1)S(1)}, bf16[8,96,256]{2,1,0:T(8,128)(2,1)S(1)}) custom-call(s32[7]{0:T(128)S(1)} %stack.31.info_ref, s32[6,8]{1,0:T(8,128)S(1)} %copy-done.10, s32[6,8]{1,0:T(8,128)S(1)} %bitcast.29, ...), custom_call_target="tpu_custom_call" | custom-call | flops 1100000000 | bytes 1048576 | tf_op jit(solution)/shard_map/apply_bonds/pallas_call | solution.py:506
  61.3 5.5 %apply_bonds.6 = (f32[2,8,128,128]{3,2,1,0:T(8,128)S(1)}, bf16[2,8,64,128]{3,2,1,0:T(8,128)(2,1)S(1)}, bf16[2,8,64,128]{3,2,1,0:T(8,128)(2,1)S(1)}, bf16[8,64,256]{2,1,0:T(8,128)(2,1)S(1)}) custom-call(s32[7]{0:T(128)S(1)} %stack.31.info_ref, s32[6,8]{1,0:T(8,128)S(1)} %copy-done.10, s32[6,8]{1,0:T(8,128)S(1)} %bitcast.30, ...), custom_call_target="tpu_custom_call", output_to_operand_aliasing={{0}: (10, {})} | custom-call | flops 1100000000 | bytes 1048576 | tf_op jit(solution)/shard_map/apply_bonds/pallas_call | solution.py:506
  68.3 4.3 %apply_bonds.7 = (f32[4,264,128]{2,1,0:T(8,128)S(1)}, f32[4,264,128]{2,1,0:T(8,128)S(1)}, bf16[1,8,64,128]{3,2,1,0:T(8,128)(2,1)S(1)}, bf16[1,8,64,128]{3,2,1,0:T(8,128)(2,1)S(1)}, bf16[8,32,256]{2,1,0:T(8,128)(2,1)S(1)}) custom-call(s32[7]{0:T(128)S(1)} %stack.31.info_ref, s32[6,8]{1,0:T(8,128)S(1)} %copy-done.10, s32[6,8]{1,0:T(8,128)S(1)} %bitcast.31, ...), custom_call_target="tpu_custom_call" | custom-call | flops 1100000000 | bytes 1048576 | tf_op jit(solution)/shard_map/apply_bonds/pallas_call | solution.py:506
  72.7 1.9 %collective-permute-done.13 = f32[4,264,128]{2,1,0:T(8,128)S(1)} collective-permute-done((f32[4,264,128]{2,1,0:T(8,128)S(1)}, f32[4,264,128]{2,1,0:T(8,128)S(1)}, u32[]{:S(2)}, u32[]{:S(2)}) %collective-permute-start.13) | collective-permute-done | bytes 540704 | tf_op jit(solution)/shard_map/ppermute | solution.py:662
  77.2 2.7 %collective-permute-start.16 = (f32[264,128]{1,0:T(8,128)}, f32[264,128]{1,0:T(8,128)}, u32[]{:S(2)}, u32[]{:S(2)}) collective-permute-start(f32[264,128]{1,0:T(8,128)} %get-tuple-element.142), channel_id=1, source_target_pairs={{0,4},{4,0},{8,12},{12,8},{1,5},{5,1},{9,13},{13,9},{2,6},{6,2},{1... | collective-permute-start | bytes 405512 | tf_op jit(solution)/shard_map/ppermute | solution.py:662
  80.7 3.4 %collective-permute-done.14.a3 = f32[264,128]{1,0:T(8,128)} collective-permute-done((f32[264,128]{1,0:T(8,128)}, f32[264,128]{1,0:T(8,128)}, u32[]{:S(2)}, u32[]{:S(2)}) %collective-permute-start.14) | collective-permute-done | bytes 135200 | tf_op jit(solution)/shard_map/ppermute | solution.py:662
  84.1 5.7 %collective-permute-done.15.a2 = f32[264,128]{1,0:T(8,128)} collective-permute-done((f32[264,128]{1,0:T(8,128)}, f32[264,128]{1,0:T(8,128)}, u32[]{:S(2)}, u32[]{:S(2)}) %collective-permute-start.15) | collective-permute-done | bytes 135200 | tf_op jit(solution)/shard_map/ppermute | solution.py:662
  94.3 5.2 %collective-permute-done.17.refs_3_ = f32[512,128]{1,0:T(8,128)S(1)} collective-permute-done((f32[512,128]{1,0:T(8,128)S(1)}, f32[512,128]{1,0:T(8,128)S(1)}, u32[]{:S(2)}, u32[]{:S(2)}) %collective-permute-start.17) | collective-permute-done | bytes 262176 | tf_op jit(solution)/shard_map/ppermute | solution.py:662
  101.2 7.3 %apply_bonds.8.refs_30_ = f32[2,8,128,128]{3,2,1,0:T(8,128)S(1)} custom-call(s32[7]{0:T(128)S(1)} %stack.31.info_ref, s32[6,8]{1,0:T(8,128)S(1)} %copy-done.10, s32[6,8]{1,0:T(8,128)S(1)} %bitcast.32, f32[512,128]{1,0:T(8,128)S(1)} %get-tuple-element.121.lower_ref.refs_2_, f32[512,128]{1,0:T(8,128)S(1)} %collective-permute-done.17.refs_3_, ...), custom_call_target="tpu_custom_call" | custom-call | flops 11000000512 | bytes 1048576 | tf_op jit(solution)/shard_map/apply_bonds/pallas_call | solution.py:506
  110.2 7.5 %apply_bonds.9 = (f32[4,264,128]{2,1,0:T(8,128)S(1)}, f32[4,264,128]{2,1,0:T(8,128)S(1)}) custom-call(s32[7]{0:T(128)S(1)} %stack.31.info_ref, s32[6,8]{1,0:T(8,128)S(1)} %copy-done.10, s32[6,8]{1,0:T(8,128)S(1)} %bitcast.33, f32[520,128]{1,0:T(8,128)S(1)} %statistics.1.refs_2_.upper_ref, f32[520,128]{1,0:T(8,128)S(1)} %collective-permute-done.18.refs_3_, ...), custom_call_target="tpu_custom_call" | custom-call | flops 11000000512 | bytes 1048576 | tf_op jit(solution)/shard_map/apply_bonds/pallas_call | solution.py:506
  121.1 3.1 %collective-permute-start.26 = (f32[264,128]{1,0:T(8,128)S(1)}, f32[264,128]{1,0:T(8,128)S(1)}, u32[]{:S(2)}, u32[]{:S(2)}) collective-permute-start(f32[264,128]{1,0:T(8,128)S(1)} %get-tuple-element.138), channel_id=1, source_target_pairs={{0,4},{4,0},{8,12},{12,8},{1,5},{5,1},{9,13},{13,9},{2,6},{6,2},{1... | collective-permute-start | bytes 405512 | tf_op jit(solution)/shard_map/ppermute | solution.py:662
  124.2 4.0 %collective-permute-done.24.a3 = f32[264,128]{1,0:T(8,128)S(1)} collective-permute-done((f32[264,128]{1,0:T(8,128)S(1)}, f32[264,128]{1,0:T(8,128)S(1)}, u32[]{:S(2)}, u32[]{:S(2)}) %collective-permute-start.24) | collective-permute-done | bytes 135200 | tf_op jit(solution)/shard_map/ppermute | solution.py:662
  128.1 4.9 %collective-permute-done.25.a2 = f32[264,128]{1,0:T(8,128)S(1)} collective-permute-done((f32[264,128]{1,0:T(8,128)S(1)}, f32[264,128]{1,0:T(8,128)S(1)}, u32[]{:S(2)}, u32[]{:S(2)}) %collective-permute-start.25) | collective-permute-done | bytes 135200 | tf_op jit(solution)/shard_map/ppermute | solution.py:662
  133.0 2.1 %outputs.1 = (f32[8,64,256]{2,1,0:T(8,128)}, f32[8,64,256]{2,1,0:T(8,128)}, f32[8,64,256]{2,1,0:T(8,128)}) custom-call(s32[7]{0:T(128)S(1)} %stack.31.info_ref, s32[4,2]{1,0:T(4,128)S(1)} %copy.12.owner_ref, f32[264,128]{1,0:T(8,128)S(1)} %collective-permute-done.24.a3, f32[264,128]{1,0:T(8,128)S(1)} %collective-permute-done.25.a2, ...), custom_call_target="tpu_custom_call" | custom-call | flops 4400000000 | bytes 1048576 | tf_op jit(solution)/shard_map/outputs/pallas_call | solution.py:639
  (141 shorter events, 29.0 us)
Async XLA Ops:
  2.7 11.4 %collective-permute-start = (f32[3,8,16,128]{3,2,1,0:T(8,128)S(1)}, f32[3,8,16,128]{3,2,1,0:T(8,128)S(1)}, u32[]{:S(2)}, u32[]{:S(2)}) collective-permute-start(f32[3,8,16,128]{3,2,1,0:T(8,128)S(1)} %get-tuple-element.70), channel_id=1, source_target_pairs={{0,4},{4,0},{8,12},{12,8},{1,5},{5,1},{9,13},{13,9},{2,6},{6,2},{1... | collective-permute-start | bytes 589832 | tf_op jit(solution)/shard_map/ppermute | solution.py:662
  5.8 17.2 %collective-permute-start.4 = (f32[3,8,16,128]{3,2,1,0:T(8,128)S(1)}, f32[3,8,16,128]{3,2,1,0:T(8,128)S(1)}, u32[]{:S(2)}, u32[]{:S(2)}) collective-permute-start(f32[3,8,16,128]{3,2,1,0:T(8,128)S(1)} %get-tuple-element.82), channel_id=1, source_target_pairs={{0,8},{4,12},{8,0},{12,4},{1,9},{5,13},{9,1},{13,5},{2,10},{6,14},... | collective-permute-start | bytes 589832 | tf_op jit(solution)/shard_map/ppermute | solution.py:662
  8.4 14.6 %collective-permute-start.7 = (f32[3,8,16,128]{3,2,1,0:T(8,128)S(1)}, f32[3,8,16,128]{3,2,1,0:T(8,128)S(1)}, u32[]{:S(2)}, u32[]{:S(2)}) collective-permute-start(f32[3,8,16,128]{3,2,1,0:T(8,128)S(1)} %get-tuple-element.87), channel_id=1, source_target_pairs={{0,12},{4,8},{8,4},{12,0},{1,13},{5,9},{9,5},{13,1},{2,14},{6,10},... | collective-permute-start | bytes 589832 | tf_op jit(solution)/shard_map/ppermute | solution.py:662
  14.1 12.4 %collective-permute-start.1 = (f32[6,24,16]{2,1,0:T(8,128)S(1)}, f32[6,24,16]{2,1,0:T(8,128)S(1)}, u32[]{:S(2)}, u32[]{:S(2)}) collective-permute-start(f32[6,24,16]{2,1,0:T(8,128)S(1)} %select_maximum_fusion), channel_id=1, source_target_pairs={{0,2},{2,0},{1,3},{3,1},{4,6},{6,4},{5,7},{7,5},{8,10},{10,8},{9,1... | collective-permute-start | bytes 27656 | tf_op jit(solution)/shard_map/ppermute | solution.py:662
  16.7 10.1 %collective-permute-start.2 = (f32[2,8,16,128]{3,2,1,0:T(8,128)S(1)}, f32[2,8,16,128]{3,2,1,0:T(8,128)S(1)}, u32[]{:S(2)}, u32[]{:S(2)}) collective-permute-start(f32[2,8,16,128]{3,2,1,0:T(8,128)S(1)} %get-tuple-element.78), channel_id=1, source_target_pairs={{0,4},{4,0},{8,12},{12,8},{1,5},{5,1},{9,13},{13,9},{2,6},{6,2},{1... | collective-permute-start | bytes 393224 | tf_op jit(solution)/shard_map/ppermute | solution.py:662
  23.0 16.9 %collective-permute-start.5 = (f32[2,8,16,128]{3,2,1,0:T(8,128)S(1)}, f32[2,8,16,128]{3,2,1,0:T(8,128)S(1)}, u32[]{:S(2)}, u32[]{:S(2)}) collective-permute-start(f32[2,8,16,128]{3,2,1,0:T(8,128)S(1)} %get-tuple-element.83), channel_id=1, source_target_pairs={{0,8},{4,12},{8,0},{12,4},{1,9},{5,13},{9,1},{13,5},{2,10},{6,14},... | collective-permute-start | bytes 393224 | tf_op jit(solution)/shard_map/ppermute | solution.py:662
  23.0 15.5 %collective-permute-start.8 = (f32[2,8,16,128]{3,2,1,0:T(8,128)S(1)}, f32[2,8,16,128]{3,2,1,0:T(8,128)S(1)}, u32[]{:S(2)}, u32[]{:S(2)}) collective-permute-start(f32[2,8,16,128]{3,2,1,0:T(8,128)S(1)} %get-tuple-element.88), channel_id=1, source_target_pairs={{0,12},{4,8},{8,4},{12,0},{1,13},{5,9},{9,5},{13,1},{2,14},{6,10},... | collective-permute-start | bytes 393224 | tf_op jit(solution)/shard_map/ppermute | solution.py:662
  26.8 13.6 %collective-permute-start.3 = (f32[1,8,16,128]{3,2,1,0:T(8,128)S(1)}, f32[1,8,16,128]{3,2,1,0:T(8,128)S(1)}, u32[]{:S(2)}, u32[]{:S(2)}) collective-permute-start(f32[1,8,16,128]{3,2,1,0:T(8,128)S(1)} %get-tuple-element.79), channel_id=1, source_target_pairs={{0,4},{4,0},{8,12},{12,8},{1,5},{5,1},{9,13},{13,9},{2,6},{6,2},{1... | collective-permute-start | bytes 196616 | tf_op jit(solution)/shard_map/ppermute | solution.py:662
  37.0 14.8 %collective-permute-start.10 = (f32[3,8,48,128]{3,2,1,0:T(8,128)S(1)}, f32[3,8,48,128]{3,2,1,0:T(8,128)S(1)}, u32[]{:S(2)}, u32[]{:S(2)}) collective-permute-start(f32[3,8,48,128]{3,2,1,0:T(8,128)S(1)} %get-tuple-element.99), channel_id=1, source_target_pairs={{0,2},{2,0},{1,3},{3,1},{4,6},{6,4},{5,7},{7,5},{8,10},{10,8},{9,1... | collective-permute-start | bytes 1769480 | tf_op jit(solution)/shard_map/ppermute | solution.py:662
  38.5 20.1 %collective-permute-start.9 = (f32[1,8,16,128]{3,2,1,0:T(8,128)S(1)}, f32[1,8,16,128]{3,2,1,0:T(8,128)S(1)}, u32[]{:S(2)}, u32[]{:S(2)}) collective-permute-start(f32[1,8,16,128]{3,2,1,0:T(8,128)S(1)} %get-tuple-element.89), channel_id=1, source_target_pairs={{0,12},{4,8},{8,4},{12,0},{1,13},{5,9},{9,5},{13,1},{2,14},{6,10},... | collective-permute-start | bytes 196616 | tf_op jit(solution)/shard_map/ppermute | solution.py:662
  39.9 18.7 %collective-permute-start.6 = (f32[1,8,16,128]{3,2,1,0:T(8,128)S(1)}, f32[1,8,16,128]{3,2,1,0:T(8,128)S(1)}, u32[]{:S(2)}, u32[]{:S(2)}) collective-permute-start(f32[1,8,16,128]{3,2,1,0:T(8,128)S(1)} %get-tuple-element.84), channel_id=1, source_target_pairs={{0,8},{4,12},{8,0},{12,4},{1,9},{5,13},{9,1},{13,5},{2,10},{6,14},... | collective-permute-start | bytes 196616 | tf_op jit(solution)/shard_map/ppermute | solution.py:662
  41.8 19.4 %collective-permute-start.12 = (f32[2,8,48,128]{3,2,1,0:T(8,128)S(1)}, f32[2,8,48,128]{3,2,1,0:T(8,128)S(1)}, u32[]{:S(2)}, u32[]{:S(2)}) collective-permute-start(f32[2,8,48,128]{3,2,1,0:T(8,128)S(1)} %get-tuple-element.92), channel_id=1, source_target_pairs={{0,2},{2,0},{1,3},{3,1},{4,6},{6,4},{5,7},{7,5},{8,10},{10,8},{9,1... | collective-permute-start | bytes 1179656 | tf_op jit(solution)/shard_map/ppermute | solution.py:662
  59.7 8.6 %collective-permute-start.11 = (f32[1,8,48,128]{3,2,1,0:T(8,128)S(1)}, f32[1,8,48,128]{3,2,1,0:T(8,128)S(1)}, u32[]{:S(2)}, u32[]{:S(2)}) collective-permute-start(f32[1,8,48,128]{3,2,1,0:T(8,128)S(1)} %get-tuple-element.107), channel_id=1, source_target_pairs={{0,2},{2,0},{1,3},{3,1},{4,6},{6,4},{5,7},{7,5},{8,10},{10,8},{9,1... | collective-permute-start | bytes 589832 | tf_op jit(solution)/shard_map/ppermute | solution.py:662
  75.4 8.7 %collective-permute-start.14 = (f32[264,128]{1,0:T(8,128)}, f32[264,128]{1,0:T(8,128)}, u32[]{:S(2)}, u32[]{:S(2)}) collective-permute-start(f32[264,128]{1,0:T(8,128)} %get-tuple-element.144), channel_id=1, source_target_pairs={{0,12},{4,8},{8,4},{12,0},{1,13},{5,9},{9,5},{13,1},{2,14},{6,10},... | collective-permute-start | bytes 405512 | tf_op jit(solution)/shard_map/ppermute | solution.py:662
  76.6 13.2 %collective-permute-start.15 = (f32[264,128]{1,0:T(8,128)}, f32[264,128]{1,0:T(8,128)}, u32[]{:S(2)}, u32[]{:S(2)}) collective-permute-start(f32[264,128]{1,0:T(8,128)} %get-tuple-element.143), channel_id=1, source_target_pairs={{0,8},{4,12},{8,0},{12,4},{1,9},{5,13},{9,1},{13,5},{2,10},{6,14},... | collective-permute-start | bytes 405512 | tf_op jit(solution)/shard_map/ppermute | solution.py:662
  77.2 12.6 %collective-permute-start.16 = (f32[264,128]{1,0:T(8,128)}, f32[264,128]{1,0:T(8,128)}, u32[]{:S(2)}, u32[]{:S(2)}) collective-permute-start(f32[264,128]{1,0:T(8,128)} %get-tuple-element.142), channel_id=1, source_target_pairs={{0,4},{4,0},{8,12},{12,8},{1,5},{5,1},{9,13},{13,9},{2,6},{6,2},{1... | collective-permute-start | bytes 405512 | tf_op jit(solution)/shard_map/ppermute | solution.py:662
  91.9 7.6 %collective-permute-start.17 = (f32[512,128]{1,0:T(8,128)S(1)}, f32[512,128]{1,0:T(8,128)S(1)}, u32[]{:S(2)}, u32[]{:S(2)}) collective-permute-start(f32[512,128]{1,0:T(8,128)S(1)} %get-tuple-element.121.lower_ref.refs_2_), channel_id=1, source_target_pairs={{0,2},{2,0},{1,3},{3,1},{4,6},{6,4},{5,7},{7,5},{8,10},{10,8},{9,1... | collective-permute-start | bytes 786440 | tf_op jit(solution)/shard_map/ppermute | solution.py:662
  92.5 8.0 %collective-permute-start.20 = (f32[512,128]{1,0:T(8,128)S(1)}, f32[512,128]{1,0:T(8,128)S(1)}, u32[]{:S(2)}, u32[]{:S(2)}) collective-permute-start(f32[512,128]{1,0:T(8,128)S(1)} %get-tuple-element.121.lower_ref.refs_2_), channel_id=1, source_target_pairs={{0,1},{1,0},{2,3},{3,2},{4,5},{5,4},{6,7},{7,6},{8,9},{9,8},{10,11... | collective-permute-start | bytes 786440 | tf_op jit(solution)/shard_map/ppermute | solution.py:662
  99.5 9.2 %collective-permute-start.19 = (f32[520,128]{1,0:T(8,128)S(1)}, f32[520,128]{1,0:T(8,128)S(1)}, u32[]{:S(2)}, u32[]{:S(2)}) collective-permute-start(f32[520,128]{1,0:T(8,128)S(1)} %statistics.1.refs_2_.upper_ref), channel_id=1, source_target_pairs={{0,1},{1,0},{2,3},{3,2},{4,5},{5,4},{6,7},{7,6},{8,9},{9,8},{10,11... | collective-permute-start | bytes 798728 | tf_op jit(solution)/shard_map/ppermute | solution.py:662
  100.0 8.5 %collective-permute-start.18 = (f32[520,128]{1,0:T(8,128)S(1)}, f32[520,128]{1,0:T(8,128)S(1)}, u32[]{:S(2)}, u32[]{:S(2)}) collective-permute-start(f32[520,128]{1,0:T(8,128)S(1)} %statistics.1.refs_2_.upper_ref), channel_id=1, source_target_pairs={{0,2},{2,0},{1,3},{3,1},{4,6},{6,4},{5,7},{7,5},{8,10},{10,8},{9,1... | collective-permute-start | bytes 798728 | tf_op jit(solution)/shard_map/ppermute | solution.py:662
  117.6 2.0 %collective-permute-start.23 = (f32[4,264,128]{2,1,0:T(8,128)S(1)}, f32[4,264,128]{2,1,0:T(8,128)S(1)}, u32[]{:S(2)}, u32[]{:S(2)}) collective-permute-start(f32[4,264,128]{2,1,0:T(8,128)S(1)} %get-tuple-element.136), channel_id=1, source_target_pairs={{0,1},{1,0},{2,3},{3,2},{4,5},{5,4},{6,7},{7,6},{8,9},{9,8},{10,11... | collective-permute-start | bytes 1622024 | tf_op jit(solution)/shard_map/ppermute | solution.py:662
  119.7 8.4 %collective-permute-start.24 = (f32[264,128]{1,0:T(8,128)S(1)}, f32[264,128]{1,0:T(8,128)S(1)}, u32[]{:S(2)}, u32[]{:S(2)}) collective-permute-start(f32[264,128]{1,0:T(8,128)S(1)} %get-tuple-element.140), channel_id=1, source_target_pairs={{0,12},{4,8},{8,4},{12,0},{1,13},{5,9},{9,5},{13,1},{2,14},{6,10},... | collective-permute-start | bytes 405512 | tf_op jit(solution)/shard_map/ppermute | solution.py:662
  121.1 12.0 %collective-permute-start.25 = (f32[264,128]{1,0:T(8,128)S(1)}, f32[264,128]{1,0:T(8,128)S(1)}, u32[]{:S(2)}, u32[]{:S(2)}) collective-permute-start(f32[264,128]{1,0:T(8,128)S(1)} %get-tuple-element.139), channel_id=1, source_target_pairs={{0,8},{4,12},{8,0},{12,4},{1,9},{5,13},{9,1},{13,5},{2,10},{6,14},... | collective-permute-start | bytes 405512 | tf_op jit(solution)/shard_map/ppermute | solution.py:662
  121.1 12.0 %collective-permute-start.26 = (f32[264,128]{1,0:T(8,128)S(1)}, f32[264,128]{1,0:T(8,128)S(1)}, u32[]{:S(2)}, u32[]{:S(2)}) collective-permute-start(f32[264,128]{1,0:T(8,128)S(1)} %get-tuple-element.138), channel_id=1, source_target_pairs={{0,4},{4,0},{8,12},{12,8},{1,5},{5,1},{9,13},{13,9},{2,6},{6,2},{1... | collective-permute-start | bytes 405512 | tf_op jit(solution)/shard_map/ppermute | solution.py:662
  (45 other events, 466.2 us)

commit v16 on v14

--- a/solution.py
+++ b/solution.py
@@ -612,25 +612,53 @@
 
 
 def final_kernel(
-    entries, info_ref, owner_ref, a3, a2, a1, a0, diag_ref, own_ref, lower_ref, upper_ref,
-    first_ref, vector_ref, second_ref, total,
+    entries, info_ref, owner_ref, a3, a2, a1, a0, diag_any, own_any, lower_any, upper_any,
+    first_any, vector_any, second_any, total, diag_ref, own_ref, image_ref, first_ref, vector_ref,
+    second_ref, fetched, stored,
 ):
     arrived = (a0, a1, a2, a3)
+    blocks = total.shape[0]
+    fetches = []
+    for k in range(blocks):
+        image = (lower_any if k < blocks // 2 else upper_any).at[
+            pl.ds(k % (blocks // 2) * LANES, LANES)
+        ]
+        fetches.append(
+            [
+                pltpu.make_async_copy(source, target.at[k], fetched.at[i, k])
+                for i, (source, target) in enumerate(
+                    ((diag_any.at[k], diag_ref), (own_any.at[k], own_ref), (image, image_ref))
+                )
+            ]
+        )
+    for copies in fetches:
+        for copy in copies:
+            copy.start()
     cross, square, rest = merged([ref[2 * LANES :] for ref in arrived])
     scale = lax.rsqrt(square / entries + 1e-06)
     rayleigh = scale * scale * (cross / entries)
     apart = (cross / jnp.maximum(square, TINY) - rayleigh) * jnp.sqrt(square)
     mean = scale * scale * ((rest + apart * apart) / entries)
     second_scale = scale * lax.rsqrt(mean + 1e-06)
-    for k in range(total.shape[0]):
-        at = k % (total.shape[0] // 2) * LANES
-        image = (lower_ref if k < total.shape[0] // 2 else upper_ref)[at : at + LANES]
-        total[k] = (diag_ref[k] - rayleigh) * image
+    total[...] = jnp.zeros_like(total)
+    add_arrived(info_ref, owner_ref, arrived, total)
+    stores = []
+    for k in range(blocks):
+        for copy in fetches[k]:
+            copy.wait()
+        image = image_ref[k]
         first_ref[k] = unpack_tile(scale * image)
         vector_ref[k] = unpack_tile(second_scale * (image - rayleigh * own_ref[k]))
-    add_arrived(info_ref, owner_ref, arrived, total)
-    for k in range(total.shape[0]):
-        second_ref[k] = unpack_tile(second_scale * total[k])
+        image = (diag_ref[k] - rayleigh) * image + total[k]
+        second_ref[k] = unpack_tile(second_scale * image)
+        for i, (source, target) in enumerate(
+            ((first_ref, first_any), (vector_ref, vector_any), (second_ref, second_any))
+        ):
+            copy = pltpu.make_async_copy(source.at[k], target.at[k], stored.at[i, k])
+            copy.start()
+            stores.append(copy)
+    for copy in stores:
+        copy.wait()
 
 
 def outputs(info, owners, arrived, diagonal, own, images, entries):
@@ -638,14 +666,13 @@
     shape = (blocks, LANES // 2, 2 * LANES)
     return pl.pallas_call(
         functools.partial(final_kernel, entries),
-        grid_spec=pltpu.PrefetchScalarGridSpec(
-            num_scalar_prefetch=2,
-            grid=(1,),
-            in_specs=[whole(*x.shape) for x in (*arrived, diagonal, own)]
-            + [whole(blocks // 2 * LANES, LANES)] * 2,
-            out_specs=[whole(*shape)] * 3,
-            scratch_shapes=[pltpu.VMEM(diagonal.shape, jnp.float32)],
-        ),
+        in_specs=[pl.BlockSpec(memory_space=pltpu.SMEM)] * 2
+        + [pl.BlockSpec(memory_space=pltpu.VMEM)] * 4
+        + [pl.BlockSpec(memory_space=pl.ANY)] * 4,
+        out_specs=[pl.BlockSpec(memory_space=pl.ANY)] * 3,
+        scratch_shapes=[pltpu.VMEM(diagonal.shape, jnp.float32)] * 4
+        + [pltpu.VMEM(shape, jnp.float32)] * 3
+        + [pltpu.SemaphoreType.DMA((3, blocks))] * 2,
         out_shape=[jax.ShapeDtypeStruct(shape, jnp.float32)] * 3,
         compiler_params=pltpu.CompilerParams(vmem_limit_bytes=SMALL_VMEM),
         cost_estimate=micros(4),

time: 125 us -> 128 us (1.024)
  Pallas kernels: 46 us -> 48.8 us
    pallas_call x1, Pallas kernels: 2.09 us -> 4.88 us  [outputs(): pl.pallas_call(functools.partial(final_kernel, entries), in_specs=[pl.Blo...]
  transfers between devices with their start and end apart: 27 -> 27, of which waited for: 13 -> 13; matrix products, arithmetic and copies ran while one was open for 1% -> 1% of each run, Pallas kernels for 23% -> 22%
where the time goes in v16:
time: 128 us
  Pallas kernels  48.8 us (38%)
  waiting for transfers between devices  37.8 us (30%)
  starting transfers between devices  36 us (28%)
  local copies, waits for them, and re-layouts  2.98 us (2%)
  between operations  1.51 us (1%)
    ppermute x27, waiting for transfers between devices, partner(): return lax.ppermute(x, axis, [(i, i ^ k) for i in range(size)])  37.8 us
    ppermute x27, starting transfers between devices, partner(): return lax.ppermute(x, axis, [(i, i ^ k) for i in range(size)])  36 us
    pallas_call x5, Pallas kernels, apply_bonds(): pl.pallas_call(functools.partial(apply_kernel, plan), in_specs=[pl.BlockS...  30.5 us
    pallas_call x1, Pallas kernels, outputs(): pl.pallas_call(functools.partial(final_kernel, entries), in_specs=[pl.Blo...  4.88 us
    pallas_call x3, Pallas kernels, own_operands(): pl.pallas_call(own_operands_kernel, grid_spec=pltpu.PrefetchScalarGridSpe...  4.05 us
    pallas_call x3, Pallas kernels, cut_pieces(): pl.pallas_call(functools.partial(cut_kernel, first), grid_spec=pltpu.Pref...  3.67 us
    unnamed x80, local copies, waits for them, and re-layouts  2.89 us
  transfers between devices with their start and end apart: 27, of which 13 were waited for; matrix products, arithmetic and copies ran while one was open for 1% of the time, Pallas kernels for 22%

profile of v16, /device:TPU:0, one launch (start us, length us, event | category | flops | bytes accessed | tf_op | source)
XLA Modules:
  0.0 128.0 jit_solution(17238966210876570450)
XLA Ops:
  0.7 1.8 %cut_pieces.3 = (f32[2,8,16,128]{3,2,1,0:T(8,128)S(1)}, f32[2,8,16,128]{3,2,1,0:T(8,128)S(1)}, f32[2,8,16,128]{3,2,1,0:T(8,128)S(1)}, f32[2,8,16,128]{3,2,1,0:T(8,128)S(1)}) custom-call(s32[7]{0:T(128)S(1)} %stack.31.info_ref, f32[6,4,8,16,128]{4,3,2,1,0:T(8,128)} %bitcast.34), custom_call_target="tpu_custom_call" | custom-call | flops 1100000000 | bytes 1048576 | tf_op jit(solution)/shard_map/cut_pieces/pallas_call | solution.py:288
  2.6 3.1 %collective-permute-start = (f32[2,8,16,128]{3,2,1,0:T(8,128)S(1)}, f32[2,8,16,128]{3,2,1,0:T(8,128)S(1)}, u32[]{:S(2)}, u32[]{:S(2)}) collective-permute-start(f32[2,8,16,128]{3,2,1,0:T(8,128)S(1)} %get-tuple-element.69), channel_id=1, source_target_pairs={{0,4},{4,0},{8,12},{12,8},{1,5},{5,1},{9,13},{13,9},{2,6},{6,2},{1... | collective-permute-start | bytes 393224 | tf_op jit(solution)/shard_map/ppermute | solution.py:689
  5.7 2.6 %collective-permute-start.4 = (f32[2,8,16,128]{3,2,1,0:T(8,128)S(1)}, f32[2,8,16,128]{3,2,1,0:T(8,128)S(1)}, u32[]{:S(2)}, u32[]{:S(2)}) collective-permute-start(f32[2,8,16,128]{3,2,1,0:T(8,128)S(1)} %get-tuple-element.81), channel_id=1, source_target_pairs={{0,8},{4,12},{8,0},{12,4},{1,9},{5,13},{9,1},{13,5},{2,10},{6,14},... | collective-permute-start | bytes 393224 | tf_op jit(solution)/shard_map/ppermute | solution.py:689
  8.3 2.5 %pack.1 = (bf16[8,128,1024]{2,1,0:T(8,128)(2,1)S(1)}, f32[8,128,128]{2,1,0:T(8,128)S(1)}, f32[8,128,128]{2,1,0:T(8,128)S(1)}) custom-call(s32[7]{0:T(128)S(1)} %stack.31.info_ref, f32[8,64,1024]{2,1,0:T(8,128)S(1)} %copy-done.8, f32[8,64,1024]{2,1,0:T(8,128)S(1)} %copy-done.8, f32[8,64,256]{2,1,0:T(8,128)S(1)} %copy-done.10), custom_call_target="tpu_custom_call" | custom-call | flops 5500000256 | bytes 1048576 | tf_op jit(solution)/shard_map/pack/pallas_call | solution.py:139
  15.3 3.3 %collective-permute-done.4.refs_2_ = f32[2,8,16,128]{3,2,1,0:T(8,128)S(1)} collective-permute-done((f32[2,8,16,128]{3,2,1,0:T(8,128)S(1)}, f32[2,8,16,128]{3,2,1,0:T(8,128)S(1)}, u32[]{:S(2)}, u32[]{:S(2)}) %collective-permute-start.4) | collective-permute-done | bytes 131104 | tf_op jit(solution)/shard_map/ppermute | solution.py:689
  18.8 2.1 %collective-permute-start.8 = (f32[2,8,16,128]{3,2,1,0:T(8,128)S(1)}, f32[2,8,16,128]{3,2,1,0:T(8,128)S(1)}, u32[]{:S(2)}, u32[]{:S(2)}) collective-permute-start(f32[2,8,16,128]{3,2,1,0:T(8,128)S(1)} %get-tuple-element.87), channel_id=1, source_target_pairs={{0,12},{4,8},{8,4},{12,0},{1,13},{5,9},{9,5},{13,1},{2,14},{6,10},... | collective-permute-start | bytes 393224 | tf_op jit(solution)/shard_map/ppermute | solution.py:689
  24.4 2.0 %collective-permute-done.8.refs_3_ = f32[2,8,16,128]{3,2,1,0:T(8,128)S(1)} collective-permute-done((f32[2,8,16,128]{3,2,1,0:T(8,128)S(1)}, f32[2,8,16,128]{3,2,1,0:T(8,128)S(1)}, u32[]{:S(2)}, u32[]{:S(2)}) %collective-permute-start.8) | collective-permute-done | bytes 131104 | tf_op jit(solution)/shard_map/ppermute | solution.py:689
  27.7 8.5 %collective-permute-start.3 = (f32[2,8,16,128]{3,2,1,0:T(8,128)S(1)}, f32[2,8,16,128]{3,2,1,0:T(8,128)S(1)}, u32[]{:S(2)}, u32[]{:S(2)}) collective-permute-start(f32[2,8,16,128]{3,2,1,0:T(8,128)S(1)} %get-tuple-element.78), channel_id=1, source_target_pairs={{0,4},{4,0},{8,12},{12,8},{1,5},{5,1},{9,13},{13,9},{2,6},{6,2},{1... | collective-permute-start | bytes 393224 | tf_op jit(solution)/shard_map/ppermute | solution.py:689
  39.1 5.2 %apply_bonds.5 = (f32[2,8,128,128]{3,2,1,0:T(8,128)S(1)}, bf16[2,8,64,128]{3,2,1,0:T(8,128)(2,1)S(1)}, bf16[2,8,64,128]{3,2,1,0:T(8,128)(2,1)S(1)}, bf16[8,64,256]{2,1,0:T(8,128)(2,1)S(1)}) custom-call(s32[7]{0:T(128)S(1)} %stack.31.info_ref, s32[6,8]{1,0:T(8,128)S(1)} %copy-done.5, s32[6,8]{1,0:T(8,128)S(1)} %bitcast.29, ...), custom_call_target="tpu_custom_call" | custom-call | flops 1100000000 | bytes 1048576 | tf_op jit(solution)/shard_map/apply_bonds/pallas_call | solution.py:506
  47.6 5.4 %apply_bonds.6 = (f32[2,8,128,128]{3,2,1,0:T(8,128)S(1)}, bf16[2,8,64,128]{3,2,1,0:T(8,128)(2,1)S(1)}, bf16[2,8,64,128]{3,2,1,0:T(8,128)(2,1)S(1)}, bf16[8,64,256]{2,1,0:T(8,128)(2,1)S(1)}) custom-call(s32[7]{0:T(128)S(1)} %stack.31.info_ref, s32[6,8]{1,0:T(8,128)S(1)} %copy-done.5, s32[6,8]{1,0:T(8,128)S(1)} %bitcast.30, ...), custom_call_target="tpu_custom_call", output_to_operand_aliasing={{0}: (10, {})} | custom-call | flops 1100000000 | bytes 1048576 | tf_op jit(solution)/shard_map/apply_bonds/pallas_call | solution.py:506
  53.1 3.8 %collective-permute-done.11.refs_6_ = f32[2,8,48,128]{3,2,1,0:T(8,128)S(1)} collective-permute-done((f32[2,8,48,128]{3,2,1,0:T(8,128)S(1)}, f32[2,8,48,128]{3,2,1,0:T(8,128)S(1)}, u32[]{:S(2)}, u32[]{:S(2)}) %collective-permute-start.11) | collective-permute-done | bytes 393248 | tf_op jit(solution)/shard_map/ppermute | solution.py:689
  56.8 5.2 %apply_bonds.7 = (f32[4,264,128]{2,1,0:T(8,128)S(1)}, f32[4,264,128]{2,1,0:T(8,128)S(1)}, bf16[2,8,64,128]{3,2,1,0:T(8,128)(2,1)S(1)}, bf16[2,8,64,128]{3,2,1,0:T(8,128)(2,1)S(1)}, bf16[8,64,256]{2,1,0:T(8,128)(2,1)S(1)}) custom-call(s32[7]{0:T(128)S(1)} %stack.31.info_ref, s32[6,8]{1,0:T(8,128)S(1)} %copy-done.5, s32[6,8]{1,0:T(8,128)S(1)} %bitcast.31, ...), custom_call_target="tpu_custom_call" | custom-call | flops 1100000000 | bytes 1048576 | tf_op jit(solution)/shard_map/apply_bonds/pallas_call | solution.py:506
  62.2 1.9 %collective-permute-done.13 = f32[4,264,128]{2,1,0:T(8,128)S(1)} collective-permute-done((f32[4,264,128]{2,1,0:T(8,128)S(1)}, f32[4,264,128]{2,1,0:T(8,128)S(1)}, u32[]{:S(2)}, u32[]{:S(2)}) %collective-permute-start.13) | collective-permute-done | bytes 540704 | tf_op jit(solution)/shard_map/ppermute | solution.py:689
  67.0 2.3 %collective-permute-start.16 = (f32[264,128]{1,0:T(8,128)}, f32[264,128]{1,0:T(8,128)}, u32[]{:S(2)}, u32[]{:S(2)}) collective-permute-start(f32[264,128]{1,0:T(8,128)} %get-tuple-element.140), channel_id=1, source_target_pairs={{0,4},{4,0},{8,12},{12,8},{1,5},{5,1},{9,13},{13,9},{2,6},{6,2},{1... | collective-permute-start | bytes 405512 | tf_op jit(solution)/shard_map/ppermute | solution.py:689
  70.7 2.9 %collective-permute-done.14.a3 = f32[264,128]{1,0:T(8,128)} collective-permute-done((f32[264,128]{1,0:T(8,128)}, f32[264,128]{1,0:T(8,128)}, u32[]{:S(2)}, u32[]{:S(2)}) %collective-permute-start.14) | collective-permute-done | bytes 135200 | tf_op jit(solution)/shard_map/ppermute | solution.py:689
  73.6 6.0 %collective-permute-done.15.a2 = f32[264,128]{1,0:T(8,128)} collective-permute-done((f32[264,128]{1,0:T(8,128)}, f32[264,128]{1,0:T(8,128)}, u32[]{:S(2)}, u32[]{:S(2)}) %collective-permute-start.15) | collective-permute-done | bytes 135200 | tf_op jit(solution)/shard_map/ppermute | solution.py:689
  84.1 4.9 %collective-permute-done.17.refs_3_ = f32[512,128]{1,0:T(8,128)S(1)} collective-permute-done((f32[512,128]{1,0:T(8,128)S(1)}, f32[512,128]{1,0:T(8,128)S(1)}, u32[]{:S(2)}, u32[]{:S(2)}) %collective-permute-start.17) | collective-permute-done | bytes 262176 | tf_op jit(solution)/shard_map/ppermute | solution.py:689
  90.7 7.3 %apply_bonds.8.refs_30_ = f32[2,8,128,128]{3,2,1,0:T(8,128)S(1)} custom-call(s32[7]{0:T(128)S(1)} %stack.31.info_ref, s32[6,8]{1,0:T(8,128)S(1)} %copy-done.5, s32[6,8]{1,0:T(8,128)S(1)} %bitcast.32, f32[512,128]{1,0:T(8,128)S(1)} %get-tuple-element.119.lower_ref.refs_2_.lower_any, f32[512,128]{1,0:T(8,128)S(1)} %collective-permute-done.17.refs_3_, ...), custom_call_target="tpu_custom_call" | custom-call | flops 11000000512 | bytes 1048576 | tf_op jit(solution)/shard_map/apply_bonds/pallas_call | solution.py:506
  99.7 7.4 %apply_bonds.9 = (f32[4,264,128]{2,1,0:T(8,128)S(1)}, f32[4,264,128]{2,1,0:T(8,128)S(1)}) custom-call(s32[7]{0:T(128)S(1)} %stack.31.info_ref, s32[6,8]{1,0:T(8,128)S(1)} %copy-done.5, s32[6,8]{1,0:T(8,128)S(1)} %bitcast.33, f32[520,128]{1,0:T(8,128)S(1)} %statistics.1.refs_2_.upper_any, f32[520,128]{1,0:T(8,128)S(1)} %collective-permute-done.18.refs_3_, ...), custom_call_target="tpu_custom_call" | custom-call | flops 11000000512 | bytes 1048576 | tf_op jit(solution)/shard_map/apply_bonds/pallas_call | solution.py:506
  107.3 1.8 %collective-permute-done.23 = f32[4,264,128]{2,1,0:T(8,128)S(1)} collective-permute-done((f32[4,264,128]{2,1,0:T(8,128)S(1)}, f32[4,264,128]{2,1,0:T(8,128)S(1)}, u32[]{:S(2)}, u32[]{:S(2)}) %collective-permute-start.23) | collective-permute-done | bytes 540704 | tf_op jit(solution)/shard_map/ppermute | solution.py:689
  109.2 2.8 %collective-permute-start.24 = (f32[264,128]{1,0:T(8,128)S(1)}, f32[264,128]{1,0:T(8,128)S(1)}, u32[]{:S(2)}, u32[]{:S(2)}) collective-permute-start(f32[264,128]{1,0:T(8,128)S(1)} %get-tuple-element.138), channel_id=1, source_target_pairs={{0,12},{4,8},{8,4},{12,0},{1,13},{5,9},{9,5},{13,1},{2,14},{6,10},... | collective-permute-start | bytes 405512 | tf_op jit(solution)/shard_map/ppermute | solution.py:689
  113.6 3.9 %collective-permute-done.24.a3 = f32[264,128]{1,0:T(8,128)S(1)} collective-permute-done((f32[264,128]{1,0:T(8,128)S(1)}, f32[264,128]{1,0:T(8,128)S(1)}, u32[]{:S(2)}, u32[]{:S(2)}) %collective-permute-start.24) | collective-permute-done | bytes 135200 | tf_op jit(solution)/shard_map/ppermute | solution.py:689
  117.6 5.4 %collective-permute-done.25.a2 = f32[264,128]{1,0:T(8,128)S(1)} collective-permute-done((f32[264,128]{1,0:T(8,128)S(1)}, f32[264,128]{1,0:T(8,128)S(1)}, u32[]{:S(2)}, u32[]{:S(2)}) %collective-permute-start.25) | collective-permute-done | bytes 135200 | tf_op jit(solution)/shard_map/ppermute | solution.py:689
  123.0 4.9 %outputs.1 = (f32[8,64,256]{2,1,0:T(8,128)}, f32[8,64,256]{2,1,0:T(8,128)}, f32[8,64,256]{2,1,0:T(8,128)}) custom-call(s32[7]{0:T(128)S(1)} %stack.31.info_ref, s32[4,2]{1,0:T(4,128)S(1)} %copy-done.7, f32[264,128]{1,0:T(8,128)S(1)} %collective-permute-done.24.a3, f32[264,128]{1,0:T(8,128)S(1)} %collective-permute-done.25.a2, ...), custom_call_target="tpu_custom_call" | custom-call | flops 4400000000 | bytes 1048576 | tf_op jit(solution)/shard_map/outputs/pallas_call | solution.py:667
  (135 shorter events, 29.5 us)
Async XLA Ops:
  2.6 9.3 %collective-permute-start = (f32[2,8,16,128]{3,2,1,0:T(8,128)S(1)}, f32[2,8,16,128]{3,2,1,0:T(8,128)S(1)}, u32[]{:S(2)}, u32[]{:S(2)}) collective-permute-start(f32[2,8,16,128]{3,2,1,0:T(8,128)S(1)} %get-tuple-element.69), channel_id=1, source_target_pairs={{0,4},{4,0},{8,12},{12,8},{1,5},{5,1},{9,13},{13,9},{2,6},{6,2},{1... | collective-permute-start | bytes 393224 | tf_op jit(solution)/shard_map/ppermute | solution.py:689
  5.7 12.9 %collective-permute-start.4 = (f32[2,8,16,128]{3,2,1,0:T(8,128)S(1)}, f32[2,8,16,128]{3,2,1,0:T(8,128)S(1)}, u32[]{:S(2)}, u32[]{:S(2)}) collective-permute-start(f32[2,8,16,128]{3,2,1,0:T(8,128)S(1)} %get-tuple-element.81), channel_id=1, source_target_pairs={{0,8},{4,12},{8,0},{12,4},{1,9},{5,13},{9,1},{13,5},{2,10},{6,14},... | collective-permute-start | bytes 393224 | tf_op jit(solution)/shard_map/ppermute | solution.py:689
  8.2 10.6 %collective-permute-start.7 = (f32[2,8,16,128]{3,2,1,0:T(8,128)S(1)}, f32[2,8,16,128]{3,2,1,0:T(8,128)S(1)}, u32[]{:S(2)}, u32[]{:S(2)}) collective-permute-start(f32[2,8,16,128]{3,2,1,0:T(8,128)S(1)} %get-tuple-element.86), channel_id=1, source_target_pairs={{0,12},{4,8},{8,4},{12,0},{1,13},{5,9},{9,5},{13,1},{2,14},{6,10},... | collective-permute-start | bytes 393224 | tf_op jit(solution)/shard_map/ppermute | solution.py:689
  11.9 9.0 %collective-permute-start.1 = (f32[6,24,16]{2,1,0:T(8,128)S(1)}, f32[6,24,16]{2,1,0:T(8,128)S(1)}, u32[]{:S(2)}, u32[]{:S(2)}) collective-permute-start(f32[6,24,16]{2,1,0:T(8,128)S(1)} %select_maximum_fusion), channel_id=1, source_target_pairs={{0,2},{2,0},{1,3},{3,1},{4,6},{6,4},{5,7},{7,5},{8,10},{10,8},{9,1... | collective-permute-start | bytes 27656 | tf_op jit(solution)/shard_map/ppermute | solution.py:689
  14.6 6.9 %collective-permute-start.2 = (f32[2,8,16,128]{3,2,1,0:T(8,128)S(1)}, f32[2,8,16,128]{3,2,1,0:T(8,128)S(1)}, u32[]{:S(2)}, u32[]{:S(2)}) collective-permute-start(f32[2,8,16,128]{3,2,1,0:T(8,128)S(1)} %get-tuple-element.77), channel_id=1, source_target_pairs={{0,4},{4,0},{8,12},{12,8},{1,5},{5,1},{9,13},{13,9},{2,6},{6,2},{1... | collective-permute-start | bytes 393224 | tf_op jit(solution)/shard_map/ppermute | solution.py:689
  18.6 17.6 %collective-permute-start.5 = (f32[2,8,16,128]{3,2,1,0:T(8,128)S(1)}, f32[2,8,16,128]{3,2,1,0:T(8,128)S(1)}, u32[]{:S(2)}, u32[]{:S(2)}) collective-permute-start(f32[2,8,16,128]{3,2,1,0:T(8,128)S(1)} %get-tuple-element.82), channel_id=1, source_target_pairs={{0,8},{4,12},{8,0},{12,4},{1,9},{5,13},{9,1},{13,5},{2,10},{6,14},... | collective-permute-start | bytes 393224 | tf_op jit(solution)/shard_map/ppermute | solution.py:689
  18.8 7.6 %collective-permute-start.8 = (f32[2,8,16,128]{3,2,1,0:T(8,128)S(1)}, f32[2,8,16,128]{3,2,1,0:T(8,128)S(1)}, u32[]{:S(2)}, u32[]{:S(2)}) collective-permute-start(f32[2,8,16,128]{3,2,1,0:T(8,128)S(1)} %get-tuple-element.87), channel_id=1, source_target_pairs={{0,12},{4,8},{8,4},{12,0},{1,13},{5,9},{9,5},{13,1},{2,14},{6,10},... | collective-permute-start | bytes 393224 | tf_op jit(solution)/shard_map/ppermute | solution.py:689
  22.9 16.2 %collective-permute-start.10 = (f32[2,8,48,128]{3,2,1,0:T(8,128)S(1)}, f32[2,8,48,128]{3,2,1,0:T(8,128)S(1)}, u32[]{:S(2)}, u32[]{:S(2)}) collective-permute-start(f32[2,8,48,128]{3,2,1,0:T(8,128)S(1)} %get-tuple-element.97), channel_id=1, source_target_pairs={{0,2},{2,0},{1,3},{3,1},{4,6},{6,4},{5,7},{7,5},{8,10},{10,8},{9,1... | collective-permute-start | bytes 1179656 | tf_op jit(solution)/shard_map/ppermute | solution.py:689
  26.4 18.7 %collective-permute-start.9 = (f32[2,8,16,128]{3,2,1,0:T(8,128)S(1)}, f32[2,8,16,128]{3,2,1,0:T(8,128)S(1)}, u32[]{:S(2)}, u32[]{:S(2)}) collective-permute-start(f32[2,8,16,128]{3,2,1,0:T(8,128)S(1)} %get-tuple-element.88), channel_id=1, source_target_pairs={{0,12},{4,8},{8,4},{12,0},{1,13},{5,9},{9,5},{13,1},{2,14},{6,10},... | collective-permute-start | bytes 393224 | tf_op jit(solution)/shard_map/ppermute | solution.py:689
  27.7 17.4 %collective-permute-start.3 = (f32[2,8,16,128]{3,2,1,0:T(8,128)S(1)}, f32[2,8,16,128]{3,2,1,0:T(8,128)S(1)}, u32[]{:S(2)}, u32[]{:S(2)}) collective-permute-start(f32[2,8,16,128]{3,2,1,0:T(8,128)S(1)} %get-tuple-element.78), channel_id=1, source_target_pairs={{0,4},{4,0},{8,12},{12,8},{1,5},{5,1},{9,13},{13,9},{2,6},{6,2},{1... | collective-permute-start | bytes 393224 | tf_op jit(solution)/shard_map/ppermute | solution.py:689
  36.2 8.9 %collective-permute-start.6 = (f32[2,8,16,128]{3,2,1,0:T(8,128)S(1)}, f32[2,8,16,128]{3,2,1,0:T(8,128)S(1)}, u32[]{:S(2)}, u32[]{:S(2)}) collective-permute-start(f32[2,8,16,128]{3,2,1,0:T(8,128)S(1)} %get-tuple-element.83), channel_id=1, source_target_pairs={{0,8},{4,12},{8,0},{12,4},{1,9},{5,13},{9,1},{13,5},{2,10},{6,14},... | collective-permute-start | bytes 393224 | tf_op jit(solution)/shard_map/ppermute | solution.py:689
  37.5 10.1 %collective-permute-start.12 = (f32[2,8,48,128]{3,2,1,0:T(8,128)S(1)}, f32[2,8,48,128]{3,2,1,0:T(8,128)S(1)}, u32[]{:S(2)}, u32[]{:S(2)}) collective-permute-start(f32[2,8,48,128]{3,2,1,0:T(8,128)S(1)} %get-tuple-element.90), channel_id=1, source_target_pairs={{0,2},{2,0},{1,3},{3,1},{4,6},{6,4},{5,7},{7,5},{8,10},{10,8},{9,1... | collective-permute-start | bytes 1179656 | tf_op jit(solution)/shard_map/ppermute | solution.py:689
  46.5 10.4 %collective-permute-start.11 = (f32[2,8,48,128]{3,2,1,0:T(8,128)S(1)}, f32[2,8,48,128]{3,2,1,0:T(8,128)S(1)}, u32[]{:S(2)}, u32[]{:S(2)}) collective-permute-start(f32[2,8,48,128]{3,2,1,0:T(8,128)S(1)} %get-tuple-element.105), channel_id=1, source_target_pairs={{0,2},{2,0},{1,3},{3,1},{4,6},{6,4},{5,7},{7,5},{8,10},{10,8},{9,1... | collective-permute-start | bytes 1179656 | tf_op jit(solution)/shard_map/ppermute | solution.py:689
  62.1 2.0 %collective-permute-start.13 = (f32[4,264,128]{2,1,0:T(8,128)S(1)}, f32[4,264,128]{2,1,0:T(8,128)S(1)}, u32[]{:S(2)}, u32[]{:S(2)}) collective-permute-start(f32[4,264,128]{2,1,0:T(8,128)S(1)} %get-tuple-element.116), channel_id=1, source_target_pairs={{0,1},{1,0},{2,3},{3,2},{4,5},{5,4},{6,7},{7,6},{8,9},{9,8},{10,11... | collective-permute-start | bytes 1622024 | tf_op jit(solution)/shard_map/ppermute | solution.py:689
  64.9 8.7 %collective-permute-start.14 = (f32[264,128]{1,0:T(8,128)}, f32[264,128]{1,0:T(8,128)}, u32[]{:S(2)}, u32[]{:S(2)}) collective-permute-start(f32[264,128]{1,0:T(8,128)} %get-tuple-element.142), channel_id=1, source_target_pairs={{0,12},{4,8},{8,4},{12,0},{1,13},{5,9},{9,5},{13,1},{2,14},{6,10},... | collective-permute-start | bytes 405512 | tf_op jit(solution)/shard_map/ppermute | solution.py:689
  66.4 13.2 %collective-permute-start.15 = (f32[264,128]{1,0:T(8,128)}, f32[264,128]{1,0:T(8,128)}, u32[]{:S(2)}, u32[]{:S(2)}) collective-permute-start(f32[264,128]{1,0:T(8,128)} %get-tuple-element.141), channel_id=1, source_target_pairs={{0,8},{4,12},{8,0},{12,4},{1,9},{5,13},{9,1},{13,5},{2,10},{6,14},... | collective-permute-start | bytes 405512 | tf_op jit(solution)/shard_map/ppermute | solution.py:689
  67.0 12.6 %collective-permute-start.16 = (f32[264,128]{1,0:T(8,128)}, f32[264,128]{1,0:T(8,128)}, u32[]{:S(2)}, u32[]{:S(2)}) collective-permute-start(f32[264,128]{1,0:T(8,128)} %get-tuple-element.140), channel_id=1, source_target_pairs={{0,4},{4,0},{8,12},{12,8},{1,5},{5,1},{9,13},{13,9},{2,6},{6,2},{1... | collective-permute-start | bytes 405512 | tf_op jit(solution)/shard_map/ppermute | solution.py:689
  81.5 7.6 %collective-permute-start.17 = (f32[512,128]{1,0:T(8,128)S(1)}, f32[512,128]{1,0:T(8,128)S(1)}, u32[]{:S(2)}, u32[]{:S(2)}) collective-permute-start(f32[512,128]{1,0:T(8,128)S(1)} %get-tuple-element.119.lower_ref.refs_2_.lower_any), channel_id=1, source_target_pairs={{0,2},{2,0},{1,3},{3,1},{4,6},{6,4},{5,7},{7,5},{8,10},{10,8},{9,1... | collective-permute-start | bytes 786440 | tf_op jit(solution)/shard_map/ppermute | solution.py:689
  82.4 8.0 %collective-permute-start.20 = (f32[512,128]{1,0:T(8,128)S(1)}, f32[512,128]{1,0:T(8,128)S(1)}, u32[]{:S(2)}, u32[]{:S(2)}) collective-permute-start(f32[512,128]{1,0:T(8,128)S(1)} %get-tuple-element.119.lower_ref.refs_2_.lower_any), channel_id=1, source_target_pairs={{0,1},{1,0},{2,3},{3,2},{4,5},{5,4},{6,7},{7,6},{8,9},{9,8},{10,11... | collective-permute-start | bytes 786440 | tf_op jit(solution)/shard_map/ppermute | solution.py:689
  89.0 9.2 %collective-permute-start.19 = (f32[520,128]{1,0:T(8,128)S(1)}, f32[520,128]{1,0:T(8,128)S(1)}, u32[]{:S(2)}, u32[]{:S(2)}) collective-permute-start(f32[520,128]{1,0:T(8,128)S(1)} %statistics.1.refs_2_.upper_any), channel_id=1, source_target_pairs={{0,1},{1,0},{2,3},{3,2},{4,5},{5,4},{6,7},{7,6},{8,9},{9,8},{10,11... | collective-permute-start | bytes 798728 | tf_op jit(solution)/shard_map/ppermute | solution.py:689
  89.6 8.5 %collective-permute-start.18 = (f32[520,128]{1,0:T(8,128)S(1)}, f32[520,128]{1,0:T(8,128)S(1)}, u32[]{:S(2)}, u32[]{:S(2)}) collective-permute-start(f32[520,128]{1,0:T(8,128)S(1)} %statistics.1.refs_2_.upper_any), channel_id=1, source_target_pairs={{0,2},{2,0},{1,3},{3,1},{4,6},{6,4},{5,7},{7,5},{8,10},{10,8},{9,1... | collective-permute-start | bytes 798728 | tf_op jit(solution)/shard_map/ppermute | solution.py:689
  109.2 8.4 %collective-permute-start.24 = (f32[264,128]{1,0:T(8,128)S(1)}, f32[264,128]{1,0:T(8,128)S(1)}, u32[]{:S(2)}, u32[]{:S(2)}) collective-permute-start(f32[264,128]{1,0:T(8,128)S(1)} %get-tuple-element.138), channel_id=1, source_target_pairs={{0,12},{4,8},{8,4},{12,0},{1,13},{5,9},{9,5},{13,1},{2,14},{6,10},... | collective-permute-start | bytes 405512 | tf_op jit(solution)/shard_map/ppermute | solution.py:689
  112.0 10.9 %collective-permute-start.25 = (f32[264,128]{1,0:T(8,128)S(1)}, f32[264,128]{1,0:T(8,128)S(1)}, u32[]{:S(2)}, u32[]{:S(2)}) collective-permute-start(f32[264,128]{1,0:T(8,128)S(1)} %get-tuple-element.137), channel_id=1, source_target_pairs={{0,8},{4,12},{8,0},{12,4},{1,9},{5,13},{9,1},{13,5},{2,10},{6,14},... | collective-permute-start | bytes 405512 | tf_op jit(solution)/shard_map/ppermute | solution.py:689
  112.0 10.9 %collective-permute-start.26 = (f32[264,128]{1,0:T(8,128)S(1)}, f32[264,128]{1,0:T(8,128)S(1)}, u32[]{:S(2)}, u32[]{:S(2)}) collective-permute-start(f32[264,128]{1,0:T(8,128)S(1)} %get-tuple-element.136), channel_id=1, source_target_pairs={{0,4},{4,0},{8,12},{12,8},{1,5},{5,1},{9,13},{13,9},{2,6},{6,2},{1... | collective-permute-start | bytes 405512 | tf_op jit(solution)/shard_map/ppermute | solution.py:689
  (42 other events, 401.9 us)

commit v17 on v14

--- a/solution.py
+++ b/solution.py
@@ -173,7 +173,7 @@
         for group, size in enumerate(sizes):
             out_ref = outs[n * len(sizes) + group]
             for at in range(size):
-                for place, term in enumerate(split_two(source[start + at, 0:PHYS].T)):
+                for place, term in enumerate(split_two(source[start + at].T)):
                     wide = jnp.dot(term, spread, preferred_element_type=jnp.float32)
                     tall = jnp.concatenate([wide] * SUB, axis=0)
                     tall = jnp.where(same, tall, 0.0).astype(jnp.bfloat16)
@@ -702,13 +702,9 @@
             cuts[1:] = [after(x, y) for x, y in zip(cuts[1:], pieces[-1][1:])]
         pieces.append(cuts[:1] + [partner(cuts[k], "blk", k) for k in range(1, 4)])
     pieces[0][1] = after(pieces[0][1], vector)
-    phys = bond_terms.shape[-1]
-    table = jnp.pad(term_slot.astype(jnp.float32), ((0, 0), (0, phys - blocks)))
-    tables = jnp.pad(table[:, None], ((0, 0), (0, SUB - 1), (0, 0)))
-    both = jnp.concatenate([bond_terms, tables], axis=1)
-    other_terms = partner(after(both, pieces[0][1]), "mpo", 1)
+    other_terms = partner(after(bond_terms, pieces[0][1]), "mpo", 1)
     mixing = mixing_operands([bond_terms, other_terms], sizes)
-    slots = [term_slot, other_terms[:, phys, :blocks].astype(jnp.int32)]
+    slots = [term_slot, partner(after(term_slot, pieces[0][1]), "mpo", 1)]
 
     made, sent = [], []
     total = None

time: 125 us -> 126 us (level)
    unnamed x80 -> x79, local copies, waits for them, and re-layouts: 2.89 us -> 3.6 us
    ppermute x27 -> x28, starting transfers between devices: 36 us -> 35.6 us  [partner(): return lax.ppermute(x, axis, [(i, i ^ k) for i in range(size)])]
    ppermute x27 -> x28, waiting for transfers between devices: 37.8 us -> 38 us  [partner(): return lax.ppermute(x, axis, [(i, i ^ k) for i in range(size)])]
  transfers between devices with their start and end apart: 27 -> 28, of which waited for: 13 -> 12; matrix products, arithmetic and copies ran while one was open for 1% -> 1% of each run, Pallas kernels for 23% -> 23%
where the time goes in v17:
time: 126 us; the launch traced here: 125 us
  Pallas kernels  46 us (37%)
  waiting for transfers between devices  38 us (30%)
  starting transfers between devices  35.6 us (28%)
  local copies, waits for them, and re-layouts  3.68 us (3%)
  between operations  1.28 us (1%)
    ppermute x28, waiting for transfers between devices, partner(): return lax.ppermute(x, axis, [(i, i ^ k) for i in range(size)])  38 us
    ppermute x28, starting transfers between devices, partner(): return lax.ppermute(x, axis, [(i, i ^ k) for i in range(size)])  35.6 us
    pallas_call x5, Pallas kernels, apply_bonds(): pl.pallas_call(functools.partial(apply_kernel, plan), in_specs=[pl.BlockS...  30.6 us
    pallas_call x3, Pallas kernels, own_operands(): pl.pallas_call(own_operands_kernel, grid_spec=pltpu.PrefetchScalarGridSpe...  4.05 us
    pallas_call x3, Pallas kernels, cut_pieces(): pl.pallas_call(functools.partial(cut_kernel, first), grid_spec=pltpu.Pref...  3.66 us
    unnamed x79, local copies, waits for them, and re-layouts  3.6 us
    pallas_call x1, Pallas kernels, pack(): pl.pallas_call(pack_kernel, grid_spec=pltpu.PrefetchScalarGridSpec(num_sc...  2.54 us
  transfers between devices with their start and end apart: 28, of which 12 were waited for; matrix products, arithmetic and copies ran while one was open for 1% of the time, Pallas kernels for 23%

profile of v17, /device:TPU:0, one launch (start us, length us, event | category | flops | bytes accessed | tf_op | source)
XLA Modules:
  0.0 125.5 jit_solution(1054269084377966776)
XLA Ops:
  0.7 1.8 %cut_pieces.3 = (f32[2,8,16,128]{3,2,1,0:T(8,128)S(1)}, f32[2,8,16,128]{3,2,1,0:T(8,128)S(1)}, f32[2,8,16,128]{3,2,1,0:T(8,128)S(1)}, f32[2,8,16,128]{3,2,1,0:T(8,128)S(1)}) custom-call(s32[7]{0:T(128)S(1)} %stack.31.info_ref, f32[6,4,8,16,128]{4,3,2,1,0:T(8,128)} %bitcast.24), custom_call_target="tpu_custom_call" | custom-call | flops 1100000000 | bytes 1048576 | tf_op jit(solution)/shard_map/cut_pieces/pallas_call | solution.py:288
  2.6 3.1 %collective-permute-start = (f32[2,8,16,128]{3,2,1,0:T(8,128)S(1)}, f32[2,8,16,128]{3,2,1,0:T(8,128)S(1)}, u32[]{:S(2)}, u32[]{:S(2)}) collective-permute-start(f32[2,8,16,128]{3,2,1,0:T(8,128)S(1)} %get-tuple-element.70), channel_id=1, source_target_pairs={{0,4},{4,0},{8,12},{12,8},{1,5},{5,1},{9,13},{13,9},{2,6},{6,2},{1... | collective-permute-start | bytes 393224 | tf_op jit(solution)/shard_map/ppermute | solution.py:662
  5.6 2.6 %collective-permute-start.4 = (f32[2,8,16,128]{3,2,1,0:T(8,128)S(1)}, f32[2,8,16,128]{3,2,1,0:T(8,128)S(1)}, u32[]{:S(2)}, u32[]{:S(2)}) collective-permute-start(f32[2,8,16,128]{3,2,1,0:T(8,128)S(1)} %get-tuple-element.82), channel_id=1, source_target_pairs={{0,8},{4,12},{8,0},{12,4},{1,9},{5,13},{9,1},{13,5},{2,10},{6,14},... | collective-permute-start | bytes 393224 | tf_op jit(solution)/shard_map/ppermute | solution.py:662
  8.2 2.5 %pack.1 = (bf16[8,128,1024]{2,1,0:T(8,128)(2,1)S(1)}, f32[8,128,128]{2,1,0:T(8,128)S(1)}, f32[8,128,128]{2,1,0:T(8,128)S(1)}) custom-call(s32[7]{0:T(128)S(1)} %stack.31.info_ref, f32[8,64,1024]{2,1,0:T(8,128)S(1)} %copy-done.7, f32[8,64,1024]{2,1,0:T(8,128)S(1)} %copy-done.7, f32[8,64,256]{2,1,0:T(8,128)S(1)} %copy-done.9), custom_call_target="tpu_custom_call" | custom-call | flops 5500000256 | bytes 1048576 | tf_op jit(solution)/shard_map/pack/pallas_call | solution.py:139
  15.2 3.3 %collective-permute-done.4.refs_2_ = f32[2,8,16,128]{3,2,1,0:T(8,128)S(1)} collective-permute-done((f32[2,8,16,128]{3,2,1,0:T(8,128)S(1)}, f32[2,8,16,128]{3,2,1,0:T(8,128)S(1)}, u32[]{:S(2)}, u32[]{:S(2)}) %collective-permute-start.4) | collective-permute-done | bytes 131104 | tf_op jit(solution)/shard_map/ppermute | solution.py:662
  18.7 2.1 %collective-permute-start.8 = (f32[2,8,16,128]{3,2,1,0:T(8,128)S(1)}, f32[2,8,16,128]{3,2,1,0:T(8,128)S(1)}, u32[]{:S(2)}, u32[]{:S(2)}) collective-permute-start(f32[2,8,16,128]{3,2,1,0:T(8,128)S(1)} %get-tuple-element.88), channel_id=1, source_target_pairs={{0,12},{4,8},{8,4},{12,0},{1,13},{5,9},{9,5},{13,1},{2,14},{6,10},... | collective-permute-start | bytes 393224 | tf_op jit(solution)/shard_map/ppermute | solution.py:662
  27.6 8.5 %collective-permute-start.3 = (f32[2,8,16,128]{3,2,1,0:T(8,128)S(1)}, f32[2,8,16,128]{3,2,1,0:T(8,128)S(1)}, u32[]{:S(2)}, u32[]{:S(2)}) collective-permute-start(f32[2,8,16,128]{3,2,1,0:T(8,128)S(1)} %get-tuple-element.79), channel_id=1, source_target_pairs={{0,4},{4,0},{8,12},{12,8},{1,5},{5,1},{9,13},{13,9},{2,6},{6,2},{1... | collective-permute-start | bytes 393224 | tf_op jit(solution)/shard_map/ppermute | solution.py:662
  39.1 5.2 %apply_bonds.5 = (f32[2,8,128,128]{3,2,1,0:T(8,128)S(1)}, bf16[2,8,64,128]{3,2,1,0:T(8,128)(2,1)S(1)}, bf16[2,8,64,128]{3,2,1,0:T(8,128)(2,1)S(1)}, bf16[8,64,256]{2,1,0:T(8,128)(2,1)S(1)}) custom-call(s32[7]{0:T(128)S(1)} %stack.31.info_ref, s32[6,8]{1,0:T(8,128)S(1)} %copy-done.4, s32[6,8]{1,0:T(8,128)S(1)} %collective-permute-done.1.refs_1_, ...), custom_call_target="tpu_custom_call" | custom-call | flops 1100000000 | bytes 1048576 | tf_op jit(solution)/shard_map/apply_bonds/pallas_call | solution.py:506
  47.8 5.4 %apply_bonds.6 = (f32[2,8,128,128]{3,2,1,0:T(8,128)S(1)}, bf16[2,8,64,128]{3,2,1,0:T(8,128)(2,1)S(1)}, bf16[2,8,64,128]{3,2,1,0:T(8,128)(2,1)S(1)}, bf16[8,64,256]{2,1,0:T(8,128)(2,1)S(1)}) custom-call(s32[7]{0:T(128)S(1)} %stack.31.info_ref, s32[6,8]{1,0:T(8,128)S(1)} %copy-done.4, ...), custom_call_target="tpu_custom_call", output_to_operand_aliasing={{0}: (10, {})} | custom-call | flops 1100000000 | bytes 1048576 | tf_op jit(solution)/shard_map/apply_bonds/pallas_call | solution.py:506
  53.2 3.6 %collective-permute-done.12.refs_6_ = f32[2,8,48,128]{3,2,1,0:T(8,128)S(1)} collective-permute-done((f32[2,8,48,128]{3,2,1,0:T(8,128)S(1)}, f32[2,8,48,128]{3,2,1,0:T(8,128)S(1)}, u32[]{:S(2)}, u32[]{:S(2)}) %collective-permute-start.12) | collective-permute-done | bytes 393248 | tf_op jit(solution)/shard_map/ppermute | solution.py:662
  56.8 5.2 %apply_bonds.7 = (f32[4,264,128]{2,1,0:T(8,128)S(1)}, f32[4,264,128]{2,1,0:T(8,128)S(1)}, bf16[2,8,64,128]{3,2,1,0:T(8,128)(2,1)S(1)}, bf16[2,8,64,128]{3,2,1,0:T(8,128)(2,1)S(1)}, bf16[8,64,256]{2,1,0:T(8,128)(2,1)S(1)}) custom-call(s32[7]{0:T(128)S(1)} %stack.31.info_ref, s32[6,8]{1,0:T(8,128)S(1)} %copy-done.4, ...), custom_call_target="tpu_custom_call" | custom-call | flops 1100000000 | bytes 1048576 | tf_op jit(solution)/shard_map/apply_bonds/pallas_call | solution.py:506
  62.1 1.9 %collective-permute-done.14 = f32[4,264,128]{2,1,0:T(8,128)S(1)} collective-permute-done((f32[4,264,128]{2,1,0:T(8,128)S(1)}, f32[4,264,128]{2,1,0:T(8,128)S(1)}, u32[]{:S(2)}, u32[]{:S(2)}) %collective-permute-start.14) | collective-permute-done | bytes 540704 | tf_op jit(solution)/shard_map/ppermute | solution.py:662
  64.8 1.9 %collective-permute-start.15 = (f32[264,128]{1,0:T(8,128)}, f32[264,128]{1,0:T(8,128)}, u32[]{:S(2)}, u32[]{:S(2)}) collective-permute-start(f32[264,128]{1,0:T(8,128)} %get-tuple-element.144), channel_id=1, source_target_pairs={{0,12},{4,8},{8,4},{12,0},{1,13},{5,9},{9,5},{13,1},{2,14},{6,10},... | collective-permute-start | bytes 405512 | tf_op jit(solution)/shard_map/ppermute | solution.py:662
  70.6 2.9 %collective-permute-done.15.a3 = f32[264,128]{1,0:T(8,128)} collective-permute-done((f32[264,128]{1,0:T(8,128)}, f32[264,128]{1,0:T(8,128)}, u32[]{:S(2)}, u32[]{:S(2)}) %collective-permute-start.15) | collective-permute-done | bytes 135200 | tf_op jit(solution)/shard_map/ppermute | solution.py:662
  73.5 6.9 %collective-permute-done.16.a2 = f32[264,128]{1,0:T(8,128)} collective-permute-done((f32[264,128]{1,0:T(8,128)}, f32[264,128]{1,0:T(8,128)}, u32[]{:S(2)}, u32[]{:S(2)}) %collective-permute-start.16) | collective-permute-done | bytes 135200 | tf_op jit(solution)/shard_map/ppermute | solution.py:662
  84.7 5.1 %collective-permute-done.18.refs_3_ = f32[512,128]{1,0:T(8,128)S(1)} collective-permute-done((f32[512,128]{1,0:T(8,128)S(1)}, f32[512,128]{1,0:T(8,128)S(1)}, u32[]{:S(2)}, u32[]{:S(2)}) %collective-permute-start.18) | collective-permute-done | bytes 262176 | tf_op jit(solution)/shard_map/ppermute | solution.py:662
  91.5 7.3 %apply_bonds.8.refs_30_ = f32[2,8,128,128]{3,2,1,0:T(8,128)S(1)} custom-call(s32[7]{0:T(128)S(1)} %stack.31.info_ref, s32[6,8]{1,0:T(8,128)S(1)} %copy-done.4, s32[6,8]{1,0:T(8,128)S(1)} %collective-permute-done.1.refs_1_, f32[512,128]{1,0:T(8,128)S(1)} %get-tuple-element.121.lower_ref.refs_2_, f32[512,128]{1,0:T(8,128)S(1)} %collective-permute-done.18.refs_3_, ...), custom_call_target="tpu_custom_call" | custom-call | flops 11000000512 | bytes 1048576 | tf_op jit(solution)/shard_map/apply_bonds/pallas_call | solution.py:506
  100.5 7.4 %apply_bonds.9 = (f32[4,264,128]{2,1,0:T(8,128)S(1)}, f32[4,264,128]{2,1,0:T(8,128)S(1)}) custom-call(s32[7]{0:T(128)S(1)} %stack.31.info_ref, s32[6,8]{1,0:T(8,128)S(1)} %copy-done.4, s32[6,8]{1,0:T(8,128)S(1)} %collective-permute-done.1.refs_1_, f32[520,128]{1,0:T(8,128)S(1)} %statistics.1.refs_2_.upper_ref, ...), custom_call_target="tpu_custom_call" | custom-call | flops 11000000512 | bytes 1048576 | tf_op jit(solution)/shard_map/apply_bonds/pallas_call | solution.py:506
  108.1 1.8 %collective-permute-done.24 = f32[4,264,128]{2,1,0:T(8,128)S(1)} collective-permute-done((f32[4,264,128]{2,1,0:T(8,128)S(1)}, f32[4,264,128]{2,1,0:T(8,128)S(1)}, u32[]{:S(2)}, u32[]{:S(2)}) %collective-permute-start.24) | collective-permute-done | bytes 540704 | tf_op jit(solution)/shard_map/ppermute | solution.py:662
  110.0 2.4 %collective-permute-start.25 = (f32[264,128]{1,0:T(8,128)S(1)}, f32[264,128]{1,0:T(8,128)S(1)}, u32[]{:S(2)}, u32[]{:S(2)}) collective-permute-start(f32[264,128]{1,0:T(8,128)S(1)} %get-tuple-element.140), channel_id=1, source_target_pairs={{0,12},{4,8},{8,4},{12,0},{1,13},{5,9},{9,5},{13,1},{2,14},{6,10},... | collective-permute-start | bytes 405512 | tf_op jit(solution)/shard_map/ppermute | solution.py:662
  112.4 2.0 %collective-permute-start.27 = (f32[264,128]{1,0:T(8,128)S(1)}, f32[264,128]{1,0:T(8,128)S(1)}, u32[]{:S(2)}, u32[]{:S(2)}) collective-permute-start(f32[264,128]{1,0:T(8,128)S(1)} %get-tuple-element.138), channel_id=1, source_target_pairs={{0,4},{4,0},{8,12},{12,8},{1,5},{5,1},{9,13},{13,9},{2,6},{6,2},{1... | collective-permute-start | bytes 405512 | tf_op jit(solution)/shard_map/ppermute | solution.py:662
  114.4 4.0 %collective-permute-done.25.a3 = f32[264,128]{1,0:T(8,128)S(1)} collective-permute-done((f32[264,128]{1,0:T(8,128)S(1)}, f32[264,128]{1,0:T(8,128)S(1)}, u32[]{:S(2)}, u32[]{:S(2)}) %collective-permute-start.25) | collective-permute-done | bytes 135200 | tf_op jit(solution)/shard_map/ppermute | solution.py:662
  118.4 5.0 %collective-permute-done.26.a2 = f32[264,128]{1,0:T(8,128)S(1)} collective-permute-done((f32[264,128]{1,0:T(8,128)S(1)}, f32[264,128]{1,0:T(8,128)S(1)}, u32[]{:S(2)}, u32[]{:S(2)}) %collective-permute-start.26) | collective-permute-done | bytes 135200 | tf_op jit(solution)/shard_map/ppermute | solution.py:662
  123.4 2.1 %outputs.1 = (f32[8,64,256]{2,1,0:T(8,128)}, f32[8,64,256]{2,1,0:T(8,128)}, f32[8,64,256]{2,1,0:T(8,128)}) custom-call(s32[7]{0:T(128)S(1)} %stack.31.info_ref, s32[4,2]{1,0:T(4,128)S(1)} %copy-done.6, f32[264,128]{1,0:T(8,128)S(1)} %collective-permute-done.25.a3, f32[264,128]{1,0:T(8,128)S(1)} %collective-permute-done.26.a2, ...), custom_call_target="tpu_custom_call" | custom-call | flops 4400000000 | bytes 1048576 | tf_op jit(solution)/shard_map/outputs/pallas_call | solution.py:639
  (131 shorter events, 30.1 us)
Async XLA Ops:
  2.6 9.2 %collective-permute-start = (f32[2,8,16,128]{3,2,1,0:T(8,128)S(1)}, f32[2,8,16,128]{3,2,1,0:T(8,128)S(1)}, u32[]{:S(2)}, u32[]{:S(2)}) collective-permute-start(f32[2,8,16,128]{3,2,1,0:T(8,128)S(1)} %get-tuple-element.70), channel_id=1, source_target_pairs={{0,4},{4,0},{8,12},{12,8},{1,5},{5,1},{9,13},{13,9},{2,6},{6,2},{1... | collective-permute-start | bytes 393224 | tf_op jit(solution)/shard_map/ppermute | solution.py:662
  5.6 12.9 %collective-permute-start.4 = (f32[2,8,16,128]{3,2,1,0:T(8,128)S(1)}, f32[2,8,16,128]{3,2,1,0:T(8,128)S(1)}, u32[]{:S(2)}, u32[]{:S(2)}) collective-permute-start(f32[2,8,16,128]{3,2,1,0:T(8,128)S(1)} %get-tuple-element.82), channel_id=1, source_target_pairs={{0,8},{4,12},{8,0},{12,4},{1,9},{5,13},{9,1},{13,5},{2,10},{6,14},... | collective-permute-start | bytes 393224 | tf_op jit(solution)/shard_map/ppermute | solution.py:662
  8.2 10.5 %collective-permute-start.7 = (f32[2,8,16,128]{3,2,1,0:T(8,128)S(1)}, f32[2,8,16,128]{3,2,1,0:T(8,128)S(1)}, u32[]{:S(2)}, u32[]{:S(2)}) collective-permute-start(f32[2,8,16,128]{3,2,1,0:T(8,128)S(1)} %get-tuple-element.87), channel_id=1, source_target_pairs={{0,12},{4,8},{8,4},{12,0},{1,13},{5,9},{9,5},{13,1},{2,14},{6,10},... | collective-permute-start | bytes 393224 | tf_op jit(solution)/shard_map/ppermute | solution.py:662
  11.8 10.8 %collective-permute-start.11 = (f32[6,16,16]{2,1,0:T(8,128)S(1)}, f32[6,16,16]{2,1,0:T(8,128)S(1)}, u32[]{:S(2)}, u32[]{:S(2)}) collective-permute-start(f32[6,16,16]{2,1,0:T(8,128)S(1)} %copy-done.22), channel_id=1, source_target_pairs={{0,2},{2,0},{1,3},{3,1},{4,6},{6,4},{5,7},{7,5},{8,10},{10,8},{9,1... | collective-permute-start | bytes 18440 | tf_op jit(solution)/shard_map/ppermute | solution.py:662
  14.5 8.5 %collective-permute-start.2 = (f32[2,8,16,128]{3,2,1,0:T(8,128)S(1)}, f32[2,8,16,128]{3,2,1,0:T(8,128)S(1)}, u32[]{:S(2)}, u32[]{:S(2)}) collective-permute-start(f32[2,8,16,128]{3,2,1,0:T(8,128)S(1)} %get-tuple-element.78), channel_id=1, source_target_pairs={{0,4},{4,0},{8,12},{12,8},{1,5},{5,1},{9,13},{13,9},{2,6},{6,2},{1... | collective-permute-start | bytes 393224 | tf_op jit(solution)/shard_map/ppermute | solution.py:662
  18.6 17.6 %collective-permute-start.5 = (f32[2,8,16,128]{3,2,1,0:T(8,128)S(1)}, f32[2,8,16,128]{3,2,1,0:T(8,128)S(1)}, u32[]{:S(2)}, u32[]{:S(2)}) collective-permute-start(f32[2,8,16,128]{3,2,1,0:T(8,128)S(1)} %get-tuple-element.83), channel_id=1, source_target_pairs={{0,8},{4,12},{8,0},{12,4},{1,9},{5,13},{9,1},{13,5},{2,10},{6,14},... | collective-permute-start | bytes 393224 | tf_op jit(solution)/shard_map/ppermute | solution.py:662
  18.7 7.7 %collective-permute-start.8 = (f32[2,8,16,128]{3,2,1,0:T(8,128)S(1)}, f32[2,8,16,128]{3,2,1,0:T(8,128)S(1)}, u32[]{:S(2)}, u32[]{:S(2)}) collective-permute-start(f32[2,8,16,128]{3,2,1,0:T(8,128)S(1)} %get-tuple-element.88), channel_id=1, source_target_pairs={{0,12},{4,8},{8,4},{12,0},{1,13},{5,9},{9,5},{13,1},{2,14},{6,10},... | collective-permute-start | bytes 393224 | tf_op jit(solution)/shard_map/ppermute | solution.py:662
  20.9 16.6 %collective-permute-start.1 = (s32[6,8]{1,0:T(8,128)S(1)}, s32[6,8]{1,0:T(8,128)S(1)}, u32[]{:S(2)}, u32[]{:S(2)}) collective-permute-start(s32[6,8]{1,0:T(8,128)S(1)} %copy-done.4), channel_id=1, source_target_pairs={{0,2},{2,0},{1,3},{3,1},{4,6},{6,4},{5,7},{7,5},{8,10},{10,8},{9,1... | collective-permute-start | bytes 584 | tf_op jit(solution)/shard_map/ppermute | solution.py:662
  24.4 14.7 %collective-permute-start.10 = (f32[2,8,48,128]{3,2,1,0:T(8,128)S(1)}, f32[2,8,48,128]{3,2,1,0:T(8,128)S(1)}, u32[]{:S(2)}, u32[]{:S(2)}) collective-permute-start(f32[2,8,48,128]{3,2,1,0:T(8,128)S(1)} %get-tuple-element.98), channel_id=1, source_target_pairs={{0,2},{2,0},{1,3},{3,1},{4,6},{6,4},{5,7},{7,5},{8,10},{10,8},{9,1... | collective-permute-start | bytes 1179656 | tf_op jit(solution)/shard_map/ppermute | solution.py:662
  26.4 19.4 %collective-permute-start.9 = (f32[2,8,16,128]{3,2,1,0:T(8,128)S(1)}, f32[2,8,16,128]{3,2,1,0:T(8,128)S(1)}, u32[]{:S(2)}, u32[]{:S(2)}) collective-permute-start(f32[2,8,16,128]{3,2,1,0:T(8,128)S(1)} %get-tuple-element.89), channel_id=1, source_target_pairs={{0,12},{4,8},{8,4},{12,0},{1,13},{5,9},{9,5},{13,1},{2,14},{6,10},... | collective-permute-start | bytes 393224 | tf_op jit(solution)/shard_map/ppermute | solution.py:662
  27.6 18.1 %collective-permute-start.3 = (f32[2,8,16,128]{3,2,1,0:T(8,128)S(1)}, f32[2,8,16,128]{3,2,1,0:T(8,128)S(1)}, u32[]{:S(2)}, u32[]{:S(2)}) collective-permute-start(f32[2,8,16,128]{3,2,1,0:T(8,128)S(1)} %get-tuple-element.79), channel_id=1, source_target_pairs={{0,4},{4,0},{8,12},{12,8},{1,5},{5,1},{9,13},{13,9},{2,6},{6,2},{1... | collective-permute-start | bytes 393224 | tf_op jit(solution)/shard_map/ppermute | solution.py:662
  36.2 9.6 %collective-permute-start.6 = (f32[2,8,16,128]{3,2,1,0:T(8,128)S(1)}, f32[2,8,16,128]{3,2,1,0:T(8,128)S(1)}, u32[]{:S(2)}, u32[]{:S(2)}) collective-permute-start(f32[2,8,16,128]{3,2,1,0:T(8,128)S(1)} %get-tuple-element.84), channel_id=1, source_target_pairs={{0,8},{4,12},{8,0},{12,4},{1,9},{5,13},{9,1},{13,5},{2,10},{6,14},... | collective-permute-start | bytes 393224 | tf_op jit(solution)/shard_map/ppermute | solution.py:662
  37.5 10.2 %collective-permute-start.13 = (f32[2,8,48,128]{3,2,1,0:T(8,128)S(1)}, f32[2,8,48,128]{3,2,1,0:T(8,128)S(1)}, u32[]{:S(2)}, u32[]{:S(2)}) collective-permute-start(f32[2,8,48,128]{3,2,1,0:T(8,128)S(1)} %get-tuple-element.91), channel_id=1, source_target_pairs={{0,2},{2,0},{1,3},{3,1},{4,6},{6,4},{5,7},{7,5},{8,10},{10,8},{9,1... | collective-permute-start | bytes 1179656 | tf_op jit(solution)/shard_map/ppermute | solution.py:662
  47.1 9.6 %collective-permute-start.12 = (f32[2,8,48,128]{3,2,1,0:T(8,128)S(1)}, f32[2,8,48,128]{3,2,1,0:T(8,128)S(1)}, u32[]{:S(2)}, u32[]{:S(2)}) collective-permute-start(f32[2,8,48,128]{3,2,1,0:T(8,128)S(1)} %get-tuple-element.107), channel_id=1, source_target_pairs={{0,2},{2,0},{1,3},{3,1},{4,6},{6,4},{5,7},{7,5},{8,10},{10,8},{9,1... | collective-permute-start | bytes 1179656 | tf_op jit(solution)/shard_map/ppermute | solution.py:662
  64.8 8.7 %collective-permute-start.15 = (f32[264,128]{1,0:T(8,128)}, f32[264,128]{1,0:T(8,128)}, u32[]{:S(2)}, u32[]{:S(2)}) collective-permute-start(f32[264,128]{1,0:T(8,128)} %get-tuple-element.144), channel_id=1, source_target_pairs={{0,12},{4,8},{8,4},{12,0},{1,13},{5,9},{9,5},{13,1},{2,14},{6,10},... | collective-permute-start | bytes 405512 | tf_op jit(solution)/shard_map/ppermute | solution.py:662
  66.7 13.7 %collective-permute-start.16 = (f32[264,128]{1,0:T(8,128)}, f32[264,128]{1,0:T(8,128)}, u32[]{:S(2)}, u32[]{:S(2)}) collective-permute-start(f32[264,128]{1,0:T(8,128)} %get-tuple-element.143), channel_id=1, source_target_pairs={{0,8},{4,12},{8,0},{12,4},{1,9},{5,13},{9,1},{13,5},{2,10},{6,14},... | collective-permute-start | bytes 405512 | tf_op jit(solution)/shard_map/ppermute | solution.py:662
  67.8 12.6 %collective-permute-start.17 = (f32[264,128]{1,0:T(8,128)}, f32[264,128]{1,0:T(8,128)}, u32[]{:S(2)}, u32[]{:S(2)}) collective-permute-start(f32[264,128]{1,0:T(8,128)} %get-tuple-element.142), channel_id=1, source_target_pairs={{0,4},{4,0},{8,12},{12,8},{1,5},{5,1},{9,13},{13,9},{2,6},{6,2},{1... | collective-permute-start | bytes 405512 | tf_op jit(solution)/shard_map/ppermute | solution.py:662
  82.2 7.6 %collective-permute-start.18 = (f32[512,128]{1,0:T(8,128)S(1)}, f32[512,128]{1,0:T(8,128)S(1)}, u32[]{:S(2)}, u32[]{:S(2)}) collective-permute-start(f32[512,128]{1,0:T(8,128)S(1)} %get-tuple-element.121.lower_ref.refs_2_), channel_id=1, source_target_pairs={{0,2},{2,0},{1,3},{3,1},{4,6},{6,4},{5,7},{7,5},{8,10},{10,8},{9,1... | collective-permute-start | bytes 786440 | tf_op jit(solution)/shard_map/ppermute | solution.py:662
  82.9 8.0 %collective-permute-start.21 = (f32[512,128]{1,0:T(8,128)S(1)}, f32[512,128]{1,0:T(8,128)S(1)}, u32[]{:S(2)}, u32[]{:S(2)}) collective-permute-start(f32[512,128]{1,0:T(8,128)S(1)} %get-tuple-element.121.lower_ref.refs_2_), channel_id=1, source_target_pairs={{0,1},{1,0},{2,3},{3,2},{4,5},{5,4},{6,7},{7,6},{8,9},{9,8},{10,11... | collective-permute-start | bytes 786440 | tf_op jit(solution)/shard_map/ppermute | solution.py:662
  89.8 9.2 %collective-permute-start.20 = (f32[520,128]{1,0:T(8,128)S(1)}, f32[520,128]{1,0:T(8,128)S(1)}, u32[]{:S(2)}, u32[]{:S(2)}) collective-permute-start(f32[520,128]{1,0:T(8,128)S(1)} %statistics.1.refs_2_.upper_ref), channel_id=1, source_target_pairs={{0,1},{1,0},{2,3},{3,2},{4,5},{5,4},{6,7},{7,6},{8,9},{9,8},{10,11... | collective-permute-start | bytes 798728 | tf_op jit(solution)/shard_map/ppermute | solution.py:662
  90.3 8.5 %collective-permute-start.19 = (f32[520,128]{1,0:T(8,128)S(1)}, f32[520,128]{1,0:T(8,128)S(1)}, u32[]{:S(2)}, u32[]{:S(2)}) collective-permute-start(f32[520,128]{1,0:T(8,128)S(1)} %statistics.1.refs_2_.upper_ref), channel_id=1, source_target_pairs={{0,2},{2,0},{1,3},{3,1},{4,6},{6,4},{5,7},{7,5},{8,10},{10,8},{9,1... | collective-permute-start | bytes 798728 | tf_op jit(solution)/shard_map/ppermute | solution.py:662
  110.0 8.4 %collective-permute-start.25 = (f32[264,128]{1,0:T(8,128)S(1)}, f32[264,128]{1,0:T(8,128)S(1)}, u32[]{:S(2)}, u32[]{:S(2)}) collective-permute-start(f32[264,128]{1,0:T(8,128)S(1)} %get-tuple-element.140), channel_id=1, source_target_pairs={{0,12},{4,8},{8,4},{12,0},{1,13},{5,9},{9,5},{13,1},{2,14},{6,10},... | collective-permute-start | bytes 405512 | tf_op jit(solution)/shard_map/ppermute | solution.py:662
  112.4 11.0 %collective-permute-start.26 = (f32[264,128]{1,0:T(8,128)S(1)}, f32[264,128]{1,0:T(8,128)S(1)}, u32[]{:S(2)}, u32[]{:S(2)}) collective-permute-start(f32[264,128]{1,0:T(8,128)S(1)} %get-tuple-element.139), channel_id=1, source_target_pairs={{0,8},{4,12},{8,0},{12,4},{1,9},{5,13},{9,1},{13,5},{2,10},{6,14},... | collective-permute-start | bytes 405512 | tf_op jit(solution)/shard_map/ppermute | solution.py:662
  112.4 11.0 %collective-permute-start.27 = (f32[264,128]{1,0:T(8,128)S(1)}, f32[264,128]{1,0:T(8,128)S(1)}, u32[]{:S(2)}, u32[]{:S(2)}) collective-permute-start(f32[264,128]{1,0:T(8,128)S(1)} %get-tuple-element.138), channel_id=1, source_target_pairs={{0,4},{4,0},{8,12},{12,8},{1,5},{5,1},{9,13},{13,9},{2,6},{6,2},{1... | collective-permute-start | bytes 405512 | tf_op jit(solution)/shard_map/ppermute | solution.py:662
  (43 other events, 396.6 us)
